TPU v7x, 32 devices: a whole 2x2x4 slice. The times are simulated.
32 devices in a mesh: parts: 2 (over y), expert: 2 (over x), col: 4 (over z), row: 2 (over core).
Axes of the slice: x: 2, y: 2, z: 4, core: 2. Of those that a mesh axis runs over, the one named last changes fastest.
Arguments:
- tokens: bfloat16 [1024, 6144], P(('parts', 'col'), ('expert', 'row')), parts along dimension 0, may hold values from -6 to 6
- routes: int32 [1024, 2], P(('parts', 'col')), parts along dimension 0, may hold values from 0 to 7, as said below
- route_weight: float32 [1024, 2], P(('parts', 'col')), parts along dimension 0, may hold values from 0.2 to 1
- pad_mask: int32 [1024], P(('parts', 'col')), parts along dimension 0, may hold values 0 or 1
- gate_up: bfloat16 [6144, 2, 12288], P(('expert', 'row'), None, 'col'), may hold values from -0.078125 to 0.078125
- down: bfloat16 [12288, 6144], P('col', ('expert', 'row')), may hold values from -0.0546875 to 0.0546875
Outputs:
- expert_out: bfloat16 [1024, 6144], P(('parts', 'col'), ('expert', 'row')), parts along dimension 0
- gram: float32 [24576, 12288], P(('parts', 'expert', 'row'), 'col'), parts along dimension 0
There are 2 independent parts, one for each index of `parts`. A program takes and returns all parts, laid end to end along the dimension named above; an argument that names none is the same for every part. Nothing has to cross between parts.
Inputs may be any that keep to these rules, and one draw needn't show every extreme that they name: `routes`: each row names two different experts. In each aligned block of 128 rows at most 32 rows name expert 0, and some block has exactly 32.
All inputs are finite; a program needn't handle non-finite values. No bound on the sum of `pad_mask` on one device may be relied on, other than what follows from the above.
Results may differ from a plain program's by a relative error of at most 0.005.
Values may be sent and summed in bfloat16 or wider, within the bound.
No kernel may reach another device: no remote copies, remote signals or barrier semaphores. Data moves between devices by JAX's collectives and lax.ppermute only.
A program may use at most 192 MiB of HBM per device.

v0:
```python
import jax
import jax.numpy as jnp
from jax import lax
from jax.sharding import PartitionSpec as P


def spread(value, axis, source):
    kept = jnp.where(lax.axis_index(axis) == source, value, 0).astype(value.dtype)
    return lax.psum(kept, axis)


def activate(preacts):
    return (jax.nn.silu(preacts[:, 0, :]) * preacts[:, 1, :]).astype(jnp.bfloat16)


def on_device(tokens, routes, route_weight, pad_mask, gate_up, down):
    group_rows = tokens.shape[0]
    slot_count = group_rows // 4
    names_zero = routes == 0
    routed = jnp.any(names_zero, axis=1)
    live_rows = routed & (pad_mask == 1)
    factor = jnp.sum(
        jnp.where(names_zero, route_weight, jnp.float32(0.0)), axis=1
    ) * live_rows.astype(jnp.float32)
    position = jnp.cumsum(routed.astype(jnp.int32)) - 1
    slot_ids = lax.broadcasted_iota(jnp.int32, (slot_count, group_rows), 0)
    placing = ((position[None, :] == slot_ids) & routed[None, :]).astype(jnp.bfloat16)
    masked = tokens * live_rows.astype(jnp.bfloat16)[:, None]
    packed = jnp.dot(placing, masked, preferred_element_type=jnp.float32).astype(jnp.bfloat16)
    gathered = lax.all_gather(packed, "col", axis=0, tiled=True)
    anchor = lax.axis_index(("expert", "row"))
    preacts = lax.psum(
        jnp.einsum("rd,dgf->rgf", gathered, gate_up, preferred_element_type=jnp.float32),
        ("expert", "row"),
    )
    hidden = activate(preacts)
    mirrored = spread(hidden, "col", anchor)
    gram_block = lax.dot_general(
        mirrored, hidden, (((0,), (0,)), ((), ())), preferred_element_type=jnp.float32
    )
    gram_block = gram_block * jnp.float32(2.0 / hidden.shape[0])
    returned = lax.psum_scatter(
        jnp.dot(hidden, down, preferred_element_type=jnp.float32),
        "col",
        scatter_dimension=0,
        tiled=True,
    )
    unpacked = lax.dot_general(
        placing.astype(jnp.float32),
        returned,
        (((0,), (0,)), ((), ())),
        precision=lax.Precision.HIGHEST,
        preferred_element_type=jnp.float32,
    )
    expert_out = (unpacked * factor[:, None]).astype(jnp.bfloat16)
    return (expert_out, gram_block)


def solution(mesh):
    in_specs = (
        P(("parts", "col"), ("expert", "row")),
        P(("parts", "col"), None),
        P(("parts", "col"), None),
        P(("parts", "col")),
        P(("expert", "row"), None, "col"),
        P("col", ("expert", "row")),
    )
    out_specs = (P(("parts", "col"), ("expert", "row")), P(("parts", "expert", "row"), "col"))
    return jax.shard_map(
        on_device, mesh=mesh, in_specs=in_specs, out_specs=out_specs, check_vma=False
    )
```

profile of v0, /device:TPU:0, one launch (start us, length us, event | category | flops | bytes accessed | tf_op | source)
XLA Modules:
  0.0 192.5 jit_solution(47222154096616843)
XLA Ops:
  7.2 0.0 all-reduce.3.cloned.1.call-start
  7.2 0.7 fusion.15
  7.9 0.7 convert_bitcast_fusion
  8.6 0.1 copy.10
  8.7 0.2 reduce-window.8
  8.9 0.1 add_reduce_fusion
  9.0 1.2 convolution_convert_fusion
  10.2 16.2 %all_gather.3 = bf16[128,1536]{1,0:T(8,128)(2,1)S(1)} all-gather(bf16[32,1536]{1,0:T(8,128)(2,1)S(1)} %convolution_convert_fusion), channel_id=1, replica_groups=mesh['parts'=2,'expert'=2,'col'=4,'row'=2] {'col'}, dimensions={0}, use_global_device_ids=true | all-gather | bytes 491520 | tf_op jit(solution)/shard_map/all_gather | solution.py:30
  26.5 14.7 %fusion = f32[128,2,3072]{2,0,1:T(8,128)} fusion(bf16[1536,2,3072]{2,1,0:T(2,128)(2,1)} %param.10, bf16[128,1536]{1,0:T(8,128)(2,1)S(1)} %all_gather.3), kind=kOutput, calls=%fused_computation | convolution fusion | flops 2415919104 | bytes 22413312 | tf_op jit(solution)/shard_map/rd,dgf->rgf/dot_general | solution.py:33
  41.1 0.0 all-reduce.3.cloned.1.call-update
  41.2 0.0 all-reduce.5.cloned.1.call-start
  41.2 0.0 copy-done.1
  41.2 0.0 copy-done.2
  41.3 70.2 %all-reduce.3.cloned.1.call-done = f32[128,2,3072]{2,0,1:T(8,128)} async-done(((f32[128,2,3072]{2,0,1:T(8,128)}), f32[128,2,3072]{2,0,1:T(8,128)}) %all-reduce.3.cloned.1.call-update) | async-done | bytes 3145744 | tf_op jit(solution)/shard_map/psum | solution.py:32
  111.5 3.3 %broadcast_select_fusion = (bf16[128,3072]{1,0:T(8,128)(2,1)}, bf16[128,3072]{1,0:T(8,128)(2,1)S(1)}) fusion(pred[]{:T(512)S(6)} %eq.25, f32[128,2,3072]{2,0,1:T(8,128)} %all-reduce.3.cloned.1.call-done), kind=kLoop, calls=%fused_computation.10 | loop fusion | flops 2752512 | bytes 4718593 | tf_op jit(solution)/shard_map/jit(_where)/select_n | solution.py:8
  114.8 0.0 all-reduce.5.cloned.1.call-update
  114.8 0.0 reduce-scatter.2.cloned.1.call-start
  114.9 0.0 copy-done
  114.9 6.0 %fusion.18 = f32[128,1536]{1,0:T(8,128)} fusion(bf16[128,3072]{1,0:T(8,128)(2,1)S(1)} %get-tuple-element.3, bf16[3072,1536]{1,0:T(8,128)(2,1)} %param.11), kind=kOutput, calls=%fused_computation.28 | convolution fusion | flops 1207959552 | bytes 11010048 | tf_op jit(solution)/shard_map/dot_general | solution.py:43
  120.9 0.0 reduce-scatter.2.cloned.1.call-update
  120.9 37.8 %all-reduce.5.cloned.1.call-done = bf16[128,3072]{1,0:T(8,128)(2,1)} async-done(((bf16[128,3072]{1,0:T(8,128)(2,1)}), bf16[128,3072]{1,0:T(8,128)(2,1)}) %all-reduce.5.cloned.1.call-update) | async-done | bytes 786448 | tf_op jit(solution)/shard_map/psum | solution.py:9
  158.8 16.8 %broadcast_multiply_fusion = f32[3072,3072]{1,0:T(8,128)} fusion(bf16[128,3072]{1,0:T(8,128)(2,1)} %all-reduce.5.cloned.1.call-done, bf16[128,3072]{1,0:T(8,128)(2,1)S(1)} %get-tuple-element.3), kind=kOutput, calls=%fused_computation.2 | convolution fusion | flops 2425356288 | bytes 39321600 | tf_op jit(solution)/shard_map/dot_general | solution.py:38
  175.6 8.2 %reduce-scatter.2.cloned.1.call-done = f32[32,1536]{1,0:T(8,128)} async-done(((f32[128,1536]{1,0:T(8,128)}), f32[32,1536]{1,0:T(8,128)}) %reduce-scatter.2.cloned.1.call-update) | async-done | bytes 196624 | tf_op jit(solution)/shard_map/reduce_scatter | solution.py:42
  183.7 2.2 %fusion.2 = bf16[128,1536]{1,0:T(8,128)(2,1)} fusion(f32[32,1536]{1,0:T(8,128)} %reduce-scatter.2.cloned.1.call-done, f32[128]{0:T(128)S(1)} %broadcast_select_fusion.1, s32[128]{0:T(128)S(1)} %add_reduce_fusion, pred[128]{0:T(512)(128)(4,1)S(1)} %fusion.15), kind=kOutput, calls=%fused_computation.4 | convolution fusion | flops 75898880 | bytes 590976 | tf_op jit(solution)/shard_map/dot_general | solution.py:48
  (5 shorter events, 0.0 us)
Async XLA Ops:
  7.2 104.3 %all-reduce.3.cloned.1.call-start = ((), (), s32[]{:S(2)}) async-start(), calls=%async_computation.1 | async-start | bytes 6291456 | tf_op jit(solution)/shard_map/psum | solution.py:32
  26.4 14.8 %copy-start.1 = (s32[128,2]{0,1:T(2,128)S(1)}, s32[128,2]{0,1:T(2,128)}, u32[]{:S(2)}) copy-start(s32[128,2]{0,1:T(2,128)} %param.7) | copy-start | bytes 3076
  26.5 14.8 %copy-start.2 = (f32[128,2]{0,1:T(2,128)S(1)}, f32[128,2]{0,1:T(2,128)}, u32[]{:S(2)}) copy-start(f32[128,2]{0,1:T(2,128)} %param.8) | copy-start | bytes 3076
  26.5 88.4 %copy-start = (s32[128]{0:T(128)S(1)}, s32[128]{0:T(128)}, u32[]{:S(2)}) copy-start(s32[128]{0:T(128)} %param.9) | copy-start | bytes 1540
  41.2 117.6 %all-reduce.5.cloned.1.call-start = ((), (), s32[]{:S(2)}) async-start(), calls=%async_computation.3 | async-start | bytes 1572864 | tf_op jit(solution)/shard_map/psum | solution.py:9
  114.8 68.9 %reduce-scatter.2.cloned.1.call-start = ((), (), s32[]{:S(2)}) async-start(), calls=%async_computation.2 | async-start | bytes 983040 | tf_op jit(solution)/shard_map/reduce_scatter | solution.py:42
Sparse Core Ops, SparseCore 0:
  41.3 70.1 all-reduce.2
  115.0 43.7 all-reduce.4
  161.1 22.6 reduce-scatter.1
where the time goes:
time: 193 us; the launch traced here: 192 us
  waiting for transfers between devices  116 us (60%)
  matrix products  40.9 us (21%)
  blocking collectives  16.2 us (8%)
  between operations  13.8 us (7%)
  other arithmetic  4.97 us (3%)
    psum x1, waiting for transfers between devices, on_device(): lax.psum(jnp.einsum('rd,dgf->rgf', gathered, gate_up, preferred_element_t...  70.2 us
    psum x1, waiting for transfers between devices, spread(): return lax.psum(kept, axis)  37.8 us
    dot_general x1, matrix products, on_device(): lax.dot_general(mirrored, hidden, (((0,), (0,)), ((), ())), preferred_ele...  16.8 us
    all_gather x1, blocking collectives, on_device(): gathered = lax.all_gather(packed, 'col', axis=0, tiled=True)  16.2 us
    dot_general x1, matrix products, on_device(): jnp.einsum('rd,dgf->rgf', gathered, gate_up, preferred_element_type=jnp.f...  14.7 us
    reduce_scatter x1, waiting for transfers between devices, on_device(): lax.psum_scatter(jnp.dot(hidden, down, preferred_element_type=jnp.float32...  8.15 us
    dot_general x1, matrix products, on_device(): jnp.dot(hidden, down, preferred_element_type=jnp.float32)  5.98 us
  transfers between devices with their start and end apart: 3, of which 3 were waited for; matrix products, arithmetic and copies ran while one was open for 12% of the time, Pallas kernels for 0%

commit v1 on v0

--- a/solution.py
+++ b/solution.py
@@ -1,7 +1,15 @@
+import functools
+
 import jax
 import jax.numpy as jnp
 from jax import lax
+from jax.experimental import pallas as pl
+from jax.experimental.pallas import tpu as pltpu
 from jax.sharding import PartitionSpec as P
+
+F32 = jnp.float32
+BF16 = jnp.bfloat16
+MIB = 1 << 20
 
 
 def spread(value, axis, source):
@@ -13,7 +21,7 @@
     return (jax.nn.silu(preacts[:, 0, :]) * preacts[:, 1, :]).astype(jnp.bfloat16)
 
 
-def on_device(tokens, routes, route_weight, pad_mask, gate_up, down):
+def on_any_device(tokens, routes, route_weight, pad_mask, gate_up, down):
     group_rows = tokens.shape[0]
     slot_count = group_rows // 4
     names_zero = routes == 0
@@ -56,6 +64,280 @@
     return (expert_out, gram_block)
 
 
+def cost(flops, moved):
+    return pl.CostEstimate(flops=int(flops), bytes_accessed=int(moved), transcendentals=0)
+
+
+def params(mib):
+    return pltpu.CompilerParams(vmem_limit_bytes=mib * MIB)
+
+
+def placing_of(routes_t, pad, slots):
+    rows = routes_t.shape[1]
+    routed = (routes_t[0:1, :] == 0) | (routes_t[1:2, :] == 0)
+    live = jnp.where(routed & (pad == 1), 1.0, 0.0)
+    before = lax.broadcasted_iota(jnp.int32, (rows, rows), 0)
+    upto = lax.broadcasted_iota(jnp.int32, (rows, rows), 1)
+    tri = jnp.where(before <= upto, 1.0, 0.0).astype(BF16)
+    routed_rows = jnp.broadcast_to(jnp.where(routed, 1.0, 0.0), (8, rows)).astype(BF16)
+    position = jnp.dot(routed_rows, tri, preferred_element_type=F32)[0:1, :] - 1.0
+    slot_ids = lax.broadcasted_iota(jnp.int32, (slots, rows), 0).astype(F32)
+    return jnp.where(position == slot_ids, jnp.broadcast_to(live, (slots, rows)), 0.0)
+
+
+def pack_kernel(tokens_ref, routes_ref, pad_ref, packed_ref):
+    placing = placing_of(routes_ref[...], pad_ref[...], packed_ref.shape[0])
+    packed_ref[...] = jnp.dot(
+        placing.astype(BF16), tokens_ref[...], preferred_element_type=F32
+    ).astype(BF16)
+
+
+def unpack_kernel(routes_ref, pad_ref, weight_ref, own_ref, r1_ref, r2_ref, r3_ref, out_ref):
+    routes_t = routes_ref[...]
+    placing = placing_of(routes_t, pad_ref[...], own_ref.shape[0])
+    weight = jnp.sum(jnp.where(routes_t == 0, weight_ref[...], 0.0), axis=0, keepdims=True)
+    factor = jnp.sum(placing * weight, axis=1, keepdims=True)
+    total = own_ref[...] + r1_ref[...].astype(F32) + r2_ref[...].astype(F32) + r3_ref[...].astype(F32)
+    scaled = (total * factor).astype(BF16)
+    out_ref[...] = lax.dot_general(
+        placing.astype(BF16), scaled, (((0,), (0,)), ((), ())), preferred_element_type=F32
+    ).astype(BF16)
+
+
+def preact_kernel(first, place_ref, *refs):
+    if first:
+        x0, x1, x2, x3, w0_ref, w1_ref, out_ref, wide_ref = refs
+    else:
+        wide_ref, w0_ref, w1_ref, out_ref = refs
+    depth = w0_ref.shape[0]
+    if first:
+
+        @pl.when(pl.program_id(0) == 0)
+        def _():
+            slots = x0.shape[0]
+            rows = 4 * slots
+            here = place_ref[2]
+            cut = 256
+            into = lax.broadcasted_iota(jnp.int32, (cut, 2 * cut), 1)
+            out_of = lax.broadcasted_iota(jnp.int32, (cut, 2 * cut), 0)
+            for half in range(2):
+                widen = jnp.where(into == 2 * out_of + half, 1.0, 0.0).astype(BF16)
+                for slot, x_ref in enumerate((x0, x1, x2, x3)):
+                    at = pl.multiple_of(half * rows + (here ^ slot) * slots, slots)
+                    for k in range(depth // cut):
+                        wide_ref[pl.ds(at, slots), 2 * cut * k : 2 * cut * (k + 1)] = jnp.dot(
+                            x_ref[:, cut * k : cut * (k + 1)], widen, preferred_element_type=F32
+                        ).astype(BF16)
+
+    wide = wide_ref[...]
+    lanes = w0_ref.shape[-1]
+    for i, w_ref in enumerate((w0_ref, w1_ref)):
+        w = w_ref.reshape(2 * depth, lanes)[...]
+        out_ref[:, lanes * i : lanes * (i + 1)] = jnp.dot(
+            wide, w, preferred_element_type=F32
+        ).astype(out_ref.dtype)
+
+
+def preacts_of(place, lefts, weights, row_flip, out_type):
+    depth, tiles, _, lanes = weights.shape
+    first = len(lefts) > 1
+    rows = 4 * lefts[0].shape[0] if first else lefts[0].shape[0] // 2
+    per = tiles // 4
+    steps = per // 2
+
+    def tile(i, j, place):
+        quarter = (place[0] ^ (1 - j // steps)) * 2 + (place[1] ^ row_flip)
+        return (0, quarter * per + (j % steps) * 2 + i, 0, 0)
+
+    whole = lambda shape: pl.BlockSpec(shape, lambda j, place: (0,) * len(shape))
+    out_shape = [jax.ShapeDtypeStruct((2, 2 * rows, per * lanes), out_type)]
+    out_specs = [pl.BlockSpec((None, 2 * rows, 2 * lanes), lambda j, place: (j // steps, 0, j % steps))]
+    if first:
+        out_shape.append(jax.ShapeDtypeStruct((2 * rows, 2 * depth), BF16))
+        out_specs.append(whole((2 * rows, 2 * depth)))
+    return pl.pallas_call(
+        functools.partial(preact_kernel, first),
+        grid_spec=pltpu.PrefetchScalarGridSpec(
+            num_scalar_prefetch=1,
+            grid=(2 * steps,),
+            in_specs=[whole(left.shape) for left in lefts]
+            + [
+                pl.BlockSpec((depth, None, 2, lanes), functools.partial(tile, 0)),
+                pl.BlockSpec((depth, None, 2, lanes), functools.partial(tile, 1)),
+            ],
+            out_specs=out_specs,
+        ),
+        out_shape=out_shape,
+        compiler_params=params(40),
+        cost_estimate=cost(8 * rows * depth * per * 2 * lanes, depth * tiles * lanes * 2),
+        name="preacts_sent" if first else "preacts_kept",
+    )(place, *lefts, weights, weights)
+
+
+def project_kernel(place_ref, h0, h1, h2, h3, down_ref, own_ref, s1_ref, s2_ref, s3_ref, total_ref):
+    j = pl.program_id(0)
+    slots = own_ref.shape[0]
+    for k, h_ref in enumerate((h0, h1, h2, h3)):
+
+        @pl.when(j == k)
+        def _():
+            part = jnp.dot(h_ref[...], down_ref[...], preferred_element_type=F32)
+            total_ref[...] = part if k == 0 else total_ref[...] + part
+
+    @pl.when(j == 3)
+    def _():
+        here = place_ref[2]
+        for slot, out_ref in enumerate((own_ref, s1_ref, s2_ref, s3_ref)):
+            at = pl.multiple_of((here ^ slot) * slots, slots)
+            out_ref[...] = total_ref[pl.ds(at, slots), :].astype(out_ref.dtype)
+
+
+def project(place, quarters, down):
+    rows, units = quarters[0].shape
+    width = down.shape[1]
+    slots = rows // 4
+    whole = lambda shape: pl.BlockSpec(shape, lambda j, place: (0, 0))
+
+    def quarter(j, place):
+        return ((place[0] ^ (j % 2)) * 2 + (place[1] ^ (j // 2)), 0)
+
+    return pl.pallas_call(
+        project_kernel,
+        grid_spec=pltpu.PrefetchScalarGridSpec(
+            num_scalar_prefetch=1,
+            grid=(4,),
+            in_specs=[whole((rows, units))] * 4 + [pl.BlockSpec((units, width), quarter)],
+            out_specs=[whole((slots, width))] * 4,
+            scratch_shapes=[pltpu.VMEM((rows, width), F32)],
+        ),
+        out_shape=[jax.ShapeDtypeStruct((slots, width), F32)]
+        + [jax.ShapeDtypeStruct((slots, width), BF16)] * 3,
+        compiler_params=params(32),
+        cost_estimate=cost(2 * rows * 4 * units * width, down.size * 2),
+        name="project",
+    )(place, *quarters, down)
+
+
+def gram_kernel(scale, halves, place_ref, a0, a1, a2, a3, c0, c1, c2, c3, out_ref, wide_ref):
+    j = pl.program_id(0)
+    units = a0.shape[1]
+    take = units // halves
+
+    @pl.when(j == 0)
+    def _():
+        for k, c_ref in enumerate((c0, c1, c2, c3)):
+            q = (place_ref[0] ^ (k % 2)) * 2 + (place_ref[1] ^ (k // 2))
+            wide_ref[:, pl.ds(pl.multiple_of(q * units, units), units)] = c_ref[...]
+
+    for k, a_ref in enumerate((a0, a1, a2, a3)):
+        for half in range(halves):
+
+            @pl.when(j == k * halves + half)
+            def _():
+                left = a_ref[:, take * half : take * (half + 1)]
+                cut = 256
+                for n in range(4 * units // cut):
+                    out_ref[:, cut * n : cut * (n + 1)] = scale * lax.dot_general(
+                        left,
+                        wide_ref[:, cut * n : cut * (n + 1)],
+                        (((0,), (0,)), ((), ())),
+                        preferred_element_type=F32,
+                    )
+
+
+def gram_of(place, a_quarters, c_quarters):
+    rows, units = a_quarters[0].shape
+    halves = 2
+    whole = pl.BlockSpec((rows, units), lambda j, place: (0, 0))
+
+    def block(j, place):
+        k = j // halves
+        quarter = (place[0] ^ (k % 2)) * 2 + (place[1] ^ (k // 2))
+        return (quarter * halves + j % halves, 0)
+
+    return pl.pallas_call(
+        functools.partial(gram_kernel, 2.0 / rows, halves),
+        grid_spec=pltpu.PrefetchScalarGridSpec(
+            num_scalar_prefetch=1,
+            grid=(4 * halves,),
+            in_specs=[whole] * 8,
+            out_specs=pl.BlockSpec((units // halves, 4 * units), block),
+            scratch_shapes=[pltpu.VMEM((rows, 4 * units), BF16)],
+        ),
+        out_shape=jax.ShapeDtypeStruct((4 * units, 4 * units), F32),
+        compiler_params=params(32),
+        cost_estimate=cost(2 * rows * 16 * units * units, 64 * units * units),
+        name="gram",
+    )(place, *a_quarters, *c_quarters)
+
+
+def swap(value, axis):
+    return lax.ppermute(value, axis, [(0, 1), (1, 0)])
+
+
+def across(value, slot):
+    return lax.ppermute(value, "col", [(i, i ^ slot) for i in range(4)])
+
+
+def on_device(tokens, routes, route_weight, pad_mask, gate_up, down):
+    group_rows, depth = tokens.shape
+    slots = group_rows // 4
+    units = gate_up.shape[2]
+    lanes = 128
+    e = lax.axis_index("expert").astype(jnp.int32)
+    r = lax.axis_index("row").astype(jnp.int32)
+    c = lax.axis_index("col").astype(jnp.int32)
+    place = jnp.stack([e, r, c])
+    routes_t = routes.T
+    pad = pad_mask[None, :]
+    weights = gate_up.reshape(depth, 2, units // lanes, lanes).transpose(0, 2, 1, 3)
+
+    packed = pl.pallas_call(
+        pack_kernel,
+        out_shape=jax.ShapeDtypeStruct((slots, depth), BF16),
+        name="pack",
+    )(tokens, routes_t, pad)
+    lefts = [packed] + [across(packed, slot) for slot in (1, 2, 3)]
+    sent, wide = preacts_of(place, lefts, weights, 1, BF16)
+    got = swap(sent, "row")
+    (kept,) = preacts_of(place, [wide], weights, 0, F32)
+    got_x = swap((kept[0] + got[0].astype(F32)).astype(BF16), "expert")
+    rows = 4 * slots
+    preacts = kept[1] + got[1].astype(F32) + got_x.astype(F32)
+    hidden = (jax.nn.silu(preacts[:rows]) * preacts[rows:]).astype(BF16)
+
+    z1, z2, z3 = (across(hidden, slot) for slot in (1, 2, 3))
+    near = (c // 2) == e
+    hidden_x = swap(hidden, "expert")
+    x2 = swap(jnp.where(near, z2, z1), "expert")
+    x3 = lax.ppermute(
+        z3,
+        ("expert", "col"),
+        [(ee * 4 + cc, (1 - ee) * 4 + cc) for ee in range(2) for cc in range(4) if cc // 2 == ee],
+    )
+    odd = (c % 2) != r
+
+    def pick(flag):
+        own = jnp.where(near, jnp.where(flag, z1, hidden), jnp.where(flag, z3, z2))
+        other = jnp.where(near, jnp.where(flag, x2, hidden_x), jnp.where(flag, x3, x2))
+        return own, other
+
+    a_own, a_other = pick(odd)
+    b_own, b_other = pick(~odd)
+    a_quarters = [a_own, a_other, swap(b_own, "row"), swap(b_other, "row")]
+    c_quarters = [hidden, hidden_x, swap(hidden, "row"), swap(hidden_x, "row")]
+
+    own, s1, s2, s3 = project(place, c_quarters, down)
+    returned = [across(value, slot) for slot, value in ((1, s1), (2, s2), (3, s3))]
+    gram_block = gram_of(place, a_quarters, c_quarters)
+    expert_out = pl.pallas_call(
+        unpack_kernel,
+        out_shape=jax.ShapeDtypeStruct((group_rows, depth), BF16),
+        name="unpack",
+    )(routes_t, pad, route_weight.T, own, *returned)
+    return (expert_out, gram_block)
+
+
 def solution(mesh):
     in_specs = (
         P(("parts", "col"), ("expert", "row")),
@@ -66,6 +348,11 @@
         P("col", ("expert", "row")),
     )
     out_specs = (P(("parts", "col"), ("expert", "row")), P(("parts", "expert", "row"), "col"))
+    small = mesh.shape["expert"] == 2 and mesh.shape["row"] == 2 and mesh.shape["col"] == 4
     return jax.shard_map(
-        on_device, mesh=mesh, in_specs=in_specs, out_specs=out_specs, check_vma=False
-    )
+        on_device if small else on_any_device,
+        mesh=mesh,
+        in_specs=in_specs,
+        out_specs=out_specs,
+        check_vma=False,
+    )

time: 193 us -> 117 us (0.61)
  waiting for transfers between devices: 116 us -> 44.2 us
  Pallas kernels: 0 us -> 42.7 us
  matrix products: 40.9 us -> 0 us
  starting transfers between devices: 0.12 us -> 22.1 us
  blocking collectives: 16.2 us -> 0 us
  between operations: 13.8 us -> 0.77 us
  local copies, waits for them, and re-layouts: 0.12 us -> 5.88 us
  other arithmetic: 4.97 us -> 0.6 us
    psum x2 -> x0, waiting for transfers between devices: 108 us -> none  [the longest x1 70.2 us: on_device(): lax.psum(jnp.einsum('rd,dgf->rgf', gathered, gate_up, preferred_element_t...]
    ppermute x0 -> x18, waiting for transfers between devices: none -> 44.2 us  [the longest x9 29.7 us: across(): return lax.ppermute(value, 'col', [(i, i ^ slot) for i in range(4)])]
    pallas_call x0 -> x6, Pallas kernels: none -> 42.7 us  [the longest x2 21.5 us: preacts_of(): pl.pallas_call(functools.partial(preact_kernel, first), grid_spec=pltpu.P...]
    dot_general x5 -> x0, matrix products: 40.9 us -> none  [the longest x1 16.8 us: on_device(): lax.dot_general(mirrored, hidden, (((0,), (0,)), ((), ())), preferred_ele...]
    ppermute x0 -> x18, starting transfers between devices: none -> 22.1 us  [the longest x9 14.1 us: across(): return lax.ppermute(value, 'col', [(i, i ^ slot) for i in range(4)])]
    all_gather x1 -> x0, blocking collectives: 16.2 us -> none  [on_device(): gathered = lax.all_gather(packed, 'col', axis=0, tiled=True)]
    reduce_scatter x1 -> x0, waiting for transfers between devices: 8.15 us -> none  [on_device(): lax.psum_scatter(jnp.dot(hidden, down, preferred_element_type=jnp.float32...]
    unnamed x6 -> x12, local copies, waits for them, and re-layouts: 0.01 us -> 5.88 us
  transfers between devices with their start and end apart: 3 -> 18, of which waited for: 3 -> 11; matrix products, arithmetic and copies ran while one was open for 12% -> 0% of each run, Pallas kernels for 0% -> 13%
where the time goes in v1:
time: 117 us; the launch traced here: 116 us
  waiting for transfers between devices  44.2 us (38%)
  Pallas kernels  42.7 us (36%)
  starting transfers between devices  22.1 us (19%)
  local copies, waits for them, and re-layouts  5.88 us (5%)
    ppermute x9, waiting for transfers between devices, across(): return lax.ppermute(value, 'col', [(i, i ^ slot) for i in range(4)])  29.7 us
    pallas_call x2, Pallas kernels, preacts_of(): pl.pallas_call(functools.partial(preact_kernel, first), grid_spec=pltpu.P...  21.5 us
    pallas_call x1, Pallas kernels, gram_of(): pl.pallas_call(functools.partial(gram_kernel, 2.0 / rows, halves), grid_s...  14.2 us
    ppermute x9, starting transfers between devices, across(): return lax.ppermute(value, 'col', [(i, i ^ slot) for i in range(4)])  14.1 us
    ppermute x8, waiting for transfers between devices, swap(): return lax.ppermute(value, axis, [(0, 1), (1, 0)])  12.1 us
    unnamed x12, local copies, waits for them, and re-layouts  5.88 us
    ppermute x8, starting transfers between devices, swap(): return lax.ppermute(value, axis, [(0, 1), (1, 0)])  5.38 us
    pallas_call x1, Pallas kernels, project(): pl.pallas_call(project_kernel, grid_spec=pltpu.PrefetchScalarGridSpec(num...  2.63 us
  transfers between devices with their start and end apart: 18, of which 11 were waited for; matrix products, arithmetic and copies ran while one was open for 0% of the time, Pallas kernels for 13%

profile of v1, /device:TPU:0, one launch (start us, length us, event | category | flops | bytes accessed | tf_op | source)
XLA Modules:
  0.0 116.2 jit_solution(4017421091598971082)
XLA Ops:
  0.6 2.0 %pack.1.refs_0_ = bf16[32,1536]{1,0:T(8,128)(2,1)} custom-call(bf16[128,1536]{1,0:T(8,128)(2,1)} %tokens_ref.1, s32[2,128]{1,0:T(2,128)} %bitcast.19, s32[1,128]{1,0:T(1,128)} %bitcast.21), custom_call_target="tpu_custom_call" | custom-call | tf_op jit(solution)/shard_map/pack/pallas_call | solution.py:295
  2.6 3.0 %collective-permute-start = (bf16[32,1536]{1,0:T(8,128)(2,1)}, bf16[32,1536]{1,0:T(8,128)(2,1)S(1)}, u32[]{:S(2)}, u32[]{:S(2)}) collective-permute-start(bf16[32,1536]{1,0:T(8,128)(2,1)} %pack.1.refs_0_), channel_id=1, source_target_pairs={{0,2},{2,0},{4,6},{6,4},{1,3},{3,1},{5,7},{7,5},{8,10},{10,8},{12,... | collective-permute-start | bytes 294920 | tf_op jit(solution)/shard_map/ppermute | solution.py:279
  5.6 2.6 %collective-permute-start.1 = (bf16[32,1536]{1,0:T(8,128)(2,1)}, bf16[32,1536]{1,0:T(8,128)(2,1)S(1)}, u32[]{:S(2)}, u32[]{:S(2)}) collective-permute-start(bf16[32,1536]{1,0:T(8,128)(2,1)} %pack.1.refs_0_), channel_id=1, source_target_pairs={{0,4},{2,6},{4,0},{6,2},{1,5},{3,7},{5,1},{7,3},{8,12},{10,14},{12... | collective-permute-start | bytes 294920 | tf_op jit(solution)/shard_map/ppermute | solution.py:279
  8.6 7.6 %collective-permute-done.1.refs_2_ = bf16[32,1536]{1,0:T(8,128)(2,1)S(1)} collective-permute-done((bf16[32,1536]{1,0:T(8,128)(2,1)}, bf16[32,1536]{1,0:T(8,128)(2,1)S(1)}, u32[]{:S(2)}, u32[]{:S(2)}) %collective-permute-start.1) | collective-permute-done | bytes 98336 | tf_op jit(solution)/shard_map/ppermute | solution.py:279
  17.2 11.9 %preacts_sent.1 = (bf16[2,256,768]{2,1,0:T(8,128)(2,1)S(1)}, bf16[256,3072]{1,0:T(8,128)(2,1)S(1)}) custom-call(s32[3]{0:T(128)S(1)} %pad_add_fusion.place_ref, bf16[32,1536]{1,0:T(8,128)(2,1)S(1)} %copy-done.1, bf16[32,1536]{1,0:T(8,128)(2,1)S(1)} %collective-permute-done.refs_1_, bf16[32,1536]{1,0:T(8,128)(2,1)S(1)} %collective-permute-done.1.refs_2_, ...), custom_call_target="tpu_custom_call" | custom-call | flops 2415919104 | bytes 9437184 | tf_op jit(solution)/shard_map/preacts_sent/pallas_call | solution.py:158
  29.1 9.6 %preacts_kept.1 = f32[2,256,768]{2,1,0:T(8,128)S(1)} custom-call(s32[3]{0:T(128)S(1)} %pad_add_fusion.place_ref, bf16[256,3072]{1,0:T(8,128)(2,1)S(1)} %get-tuple-element.8.refs_0_, bf16[1536,24,2,128]{3,2,1,0:T(2,128)(2,1)} %bitcast.17, bf16[1536,24,2,128]{3,2,1,0:T(2,128)(2,1)} %bitcast.18), custom_call_target="tpu_custom_call" | custom-call | flops 2415919104 | bytes 9437184 | tf_op jit(solution)/shard_map/preacts_kept/pallas_call | solution.py:158
  38.9 1.6 %collective-permute-start.4 = (bf16[256,768]{1,0:T(8,128)(2,1)S(1)}, bf16[256,768]{1,0:T(8,128)(2,1)S(1)}, u32[]{:S(2)}, u32[]{:S(2)}) collective-permute-start(bf16[256,768]{1,0:T(8,128)(2,1)S(1)} %fusion.3), channel_id=1, source_target_pairs={{0,8},{8,0},{1,9},{9,1},{2,10},{10,2},{3,11},{11,3},{4,12},{12,4},... | collective-permute-start | bytes 1179656 | tf_op jit(solution)/shard_map/ppermute | solution.py:275
  40.4 10.0 %collective-permute-done.4 = bf16[256,768]{1,0:T(8,128)(2,1)S(1)} collective-permute-done((bf16[256,768]{1,0:T(8,128)(2,1)S(1)}, bf16[256,768]{1,0:T(8,128)(2,1)S(1)}, u32[]{:S(2)}, u32[]{:S(2)}) %collective-permute-start.4) | collective-permute-done | bytes 393248 | tf_op jit(solution)/shard_map/ppermute | solution.py:275
  50.7 1.7 %collective-permute-start.11 = (bf16[128,768]{1,0:T(8,128)(2,1)S(1)}, bf16[128,768]{1,0:T(8,128)(2,1)S(1)}, u32[]{:S(2)}, u32[]{:S(2)}) collective-permute-start(bf16[128,768]{1,0:T(8,128)(2,1)S(1)} %fusion.4.h0.c0), channel_id=1, source_target_pairs={{0,2},{2,0},{4,6},{6,4},{1,3},{3,1},{5,7},{7,5},{8,10},{10,8},{12,... | collective-permute-start | bytes 589832 | tf_op jit(solution)/shard_map/ppermute | solution.py:279
  52.4 2.5 %collective-permute-start.12 = (bf16[128,768]{1,0:T(8,128)(2,1)S(1)}, bf16[128,768]{1,0:T(8,128)(2,1)S(1)}, u32[]{:S(2)}, u32[]{:S(2)}) collective-permute-start(bf16[128,768]{1,0:T(8,128)(2,1)S(1)} %fusion.4.h0.c0), channel_id=1, source_target_pairs={{0,6},{2,4},{4,2},{6,0},{1,7},{3,5},{5,3},{7,1},{8,14},{10,12},{12... | collective-permute-start | bytes 589832 | tf_op jit(solution)/shard_map/ppermute | solution.py:279
  54.8 1.5 %collective-permute-start.5 = (bf16[128,768]{1,0:T(8,128)(2,1)S(1)}, bf16[128,768]{1,0:T(8,128)(2,1)S(1)}, u32[]{:S(2)}, u32[]{:S(2)}) collective-permute-start(bf16[128,768]{1,0:T(8,128)(2,1)S(1)} %fusion.4.h0.c0), channel_id=1, source_target_pairs={{0,8},{8,0},{1,9},{9,1},{2,10},{10,2},{3,11},{11,3},{4,12},{12,4},... | collective-permute-start | bytes 589832 | tf_op jit(solution)/shard_map/ppermute | solution.py:275
  57.7 7.2 %collective-permute-done.12 = bf16[128,768]{1,0:T(8,128)(2,1)S(1)} collective-permute-done((bf16[128,768]{1,0:T(8,128)(2,1)S(1)}, bf16[128,768]{1,0:T(8,128)(2,1)S(1)}, u32[]{:S(2)}, u32[]{:S(2)}) %collective-permute-start.12) | collective-permute-done | bytes 196640 | tf_op jit(solution)/shard_map/ppermute | solution.py:279
  64.9 6.2 %collective-permute-done.13 = bf16[128,768]{1,0:T(8,128)(2,1)S(1)} collective-permute-done((bf16[128,768]{1,0:T(8,128)(2,1)S(1)}, bf16[128,768]{1,0:T(8,128)(2,1)S(1)}, u32[]{:S(2)}, u32[]{:S(2)}) %collective-permute-start.13) | collective-permute-done | bytes 196640 | tf_op jit(solution)/shard_map/ppermute | solution.py:279
  71.3 1.6 %collective-permute-start.14 = (bf16[128,768]{1,0:T(8,128)(2,1)S(1)}, bf16[128,768]{1,0:T(8,128)(2,1)S(1)}, u32[]{:S(2)}, u32[]{:S(2)}) collective-permute-start(bf16[128,768]{1,0:T(8,128)(2,1)S(1)} %get-tuple-element.18), channel_id=1, source_target_pairs={{0,8},{8,0},{1,9},{9,1},{2,10},{10,2},{3,11},{11,3},{4,12},{12,4},... | collective-permute-start | bytes 589832 | tf_op jit(solution)/shard_map/ppermute | solution.py:275
  72.8 2.6 %collective-permute-start.15 = (bf16[128,768]{1,0:T(8,128)(2,1)S(1)}, bf16[128,768]{1,0:T(8,128)(2,1)S(1)}, u32[]{:S(2)}, u32[]{:S(2)}) collective-permute-start(bf16[128,768]{1,0:T(8,128)(2,1)S(1)} %collective-permute-done.12), channel_id=1, source_target_pairs={{0,8},{2,10},{12,4},{14,6},{1,9},{3,11},{13,5},{15,7},{16,24},{18,... | collective-permute-start | bytes 589832 | tf_op jit(solution)/shard_map/ppermute | solution.py:313
  76.1 2.1 %collective-permute-done.14 = bf16[128,768]{1,0:T(8,128)(2,1)S(1)} collective-permute-done((bf16[128,768]{1,0:T(8,128)(2,1)S(1)}, bf16[128,768]{1,0:T(8,128)(2,1)S(1)}, u32[]{:S(2)}, u32[]{:S(2)}) %collective-permute-start.14) | collective-permute-done | bytes 196640 | tf_op jit(solution)/shard_map/ppermute | solution.py:275
  78.2 2.3 %collective-permute-done.15 = bf16[128,768]{1,0:T(8,128)(2,1)S(1)} collective-permute-done((bf16[128,768]{1,0:T(8,128)(2,1)S(1)}, bf16[128,768]{1,0:T(8,128)(2,1)S(1)}, u32[]{:S(2)}, u32[]{:S(2)}) %collective-permute-start.15) | collective-permute-done | bytes 196640 | tf_op jit(solution)/shard_map/ppermute | solution.py:313
  80.7 3.7 %copy-done = bf16[3072,1536]{1,0:T(8,128)(2,1)S(1)} copy-done((bf16[3072,1536]{1,0:T(8,128)(2,1)S(1)}, bf16[3072,1536]{1,0:T(8,128)(2,1)}, u32[]{:S(2)}) %copy-start) | copy-done | bytes 9437208
  84.4 2.6 %project.1 = (f32[32,1536]{1,0:T(8,128)S(1)}, bf16[32,1536]{1,0:T(8,128)(2,1)S(1)}, bf16[32,1536]{1,0:T(8,128)(2,1)S(1)}, bf16[32,1536]{1,0:T(8,128)(2,1)S(1)}) custom-call(s32[3]{0:T(128)S(1)} %pad_add_fusion.place_ref, bf16[128,768]{1,0:T(8,128)(2,1)S(1)} %fusion.4.h0.c0, bf16[128,768]{1,0:T(8,128)(2,1)S(1)} %collective-permute-done.5.h1.c1, ...), custom_call_target="tpu_custom_call" | custom-call | flops 1207959552 | bytes 9437184 | tf_op jit(solution)/shard_map/project/pallas_call | solution.py:204
  87.7 3.1 %collective-permute-start.10 = (bf16[32,1536]{1,0:T(8,128)(2,1)S(1)}, bf16[32,1536]{1,0:T(8,128)(2,1)S(1)}, u32[]{:S(2)}, u32[]{:S(2)}) collective-permute-start(bf16[32,1536]{1,0:T(8,128)(2,1)S(1)} %get-tuple-element.13), channel_id=1, source_target_pairs={{0,6},{2,4},{4,2},{6,0},{1,7},{3,5},{5,3},{7,1},{8,14},{10,12},{12... | collective-permute-start | bytes 294920 | tf_op jit(solution)/shard_map/ppermute | solution.py:279
  92.1 3.1 %collective-permute-done.10.r3_ref = bf16[32,1536]{1,0:T(8,128)(2,1)S(1)} collective-permute-done((bf16[32,1536]{1,0:T(8,128)(2,1)S(1)}, bf16[32,1536]{1,0:T(8,128)(2,1)S(1)}, u32[]{:S(2)}, u32[]{:S(2)}) %collective-permute-start.10) | collective-permute-done | bytes 98336 | tf_op jit(solution)/shard_map/ppermute | solution.py:279
  95.1 3.7 %collective-permute-done.8.r1_ref = bf16[32,1536]{1,0:T(8,128)(2,1)S(1)} collective-permute-done((bf16[32,1536]{1,0:T(8,128)(2,1)S(1)}, bf16[32,1536]{1,0:T(8,128)(2,1)S(1)}, u32[]{:S(2)}, u32[]{:S(2)}) %collective-permute-start.8) | collective-permute-done | bytes 98336 | tf_op jit(solution)/shard_map/ppermute | solution.py:279
  99.6 2.3 %unpack.1 = bf16[128,1536]{1,0:T(8,128)(2,1)} custom-call(s32[2,128]{1,0:T(2,128)} %bitcast.20, s32[1,128]{1,0:T(1,128)} %bitcast.22, f32[2,128]{1,0:T(2,128)} %bitcast.23, f32[32,1536]{1,0:T(8,128)} %copy-done.2, bf16[32,1536]{1,0:T(8,128)(2,1)} %copy-done.4, bf16[32,1536]{1,0:T(8,128)(2,1)} %copy-done.5, bf16[32,1536]{1,0:T(8,128)(2,1)} %copy-done.3), custom_call_target="tpu_custom_call" | custom-call | tf_op jit(solution)/shard_map/unpack/pallas_call | solution.py:333
  102.0 14.2 %gram.1 = f32[3072,3072]{1,0:T(8,128)} custom-call(s32[3]{0:T(128)S(1)} %pad_add_fusion.place_ref, bf16[128,768]{1,0:T(8,128)(2,1)S(1)} %get-tuple-element.15.a0, bf16[128,768]{1,0:T(8,128)(2,1)S(1)} %get-tuple-element.17.a1, bf16[128,768]{1,0:T(8,128)(2,1)S(1)} %collective-permute-done.16.a2, bf16[128,768]{1,0:T(8,128)(2,1)S(1)} %collective-permute-done.17.a3, ...), custom_call_target="tpu_custom_call" | custom-call | flops 2415919104 | bytes 37748736 | tf_op jit(solution)/shard_map/gram/pallas_call | solution.py:258
  (36 shorter events, 6.7 us)
Async XLA Ops:
  2.6 6.0 %collective-permute-start = (bf16[32,1536]{1,0:T(8,128)(2,1)}, bf16[32,1536]{1,0:T(8,128)(2,1)S(1)}, u32[]{:S(2)}, u32[]{:S(2)}) collective-permute-start(bf16[32,1536]{1,0:T(8,128)(2,1)} %pack.1.refs_0_), channel_id=1, source_target_pairs={{0,2},{2,0},{4,6},{6,4},{1,3},{3,1},{5,7},{7,5},{8,10},{10,8},{12,... | collective-permute-start | bytes 294920 | tf_op jit(solution)/shard_map/ppermute | solution.py:279
  5.6 10.6 %collective-permute-start.1 = (bf16[32,1536]{1,0:T(8,128)(2,1)}, bf16[32,1536]{1,0:T(8,128)(2,1)S(1)}, u32[]{:S(2)}, u32[]{:S(2)}) collective-permute-start(bf16[32,1536]{1,0:T(8,128)(2,1)} %pack.1.refs_0_), channel_id=1, source_target_pairs={{0,4},{2,6},{4,0},{6,2},{1,5},{3,7},{5,1},{7,3},{8,12},{10,14},{12... | collective-permute-start | bytes 294920 | tf_op jit(solution)/shard_map/ppermute | solution.py:279
  8.2 8.1 %collective-permute-start.2 = (bf16[32,1536]{1,0:T(8,128)(2,1)}, bf16[32,1536]{1,0:T(8,128)(2,1)S(1)}, u32[]{:S(2)}, u32[]{:S(2)}) collective-permute-start(bf16[32,1536]{1,0:T(8,128)(2,1)} %pack.1.refs_0_), channel_id=1, source_target_pairs={{0,6},{2,4},{4,2},{6,0},{1,7},{3,5},{5,3},{7,1},{8,14},{10,12},{12... | collective-permute-start | bytes 294920 | tf_op jit(solution)/shard_map/ppermute | solution.py:279
  16.3 0.9 copy-start.1
  29.1 9.7 %collective-permute-start.3 = (bf16[2,256,768]{2,1,0:T(8,128)(2,1)S(1)}, bf16[2,256,768]{2,1,0:T(8,128)(2,1)S(1)}, u32[]{:S(2)}, u32[]{:S(2)}) collective-permute-start(bf16[2,256,768]{2,1,0:T(8,128)(2,1)S(1)} %get-tuple-element.9), channel_id=1, source_target_pairs={{0,1},{1,0},{2,3},{3,2},{4,5},{5,4},{6,7},{7,6},{8,9},{9,8},{10,11... | collective-permute-start | bytes 2359304 | tf_op jit(solution)/shard_map/ppermute | solution.py:275
  38.9 11.6 %collective-permute-start.4 = (bf16[256,768]{1,0:T(8,128)(2,1)S(1)}, bf16[256,768]{1,0:T(8,128)(2,1)S(1)}, u32[]{:S(2)}, u32[]{:S(2)}) collective-permute-start(bf16[256,768]{1,0:T(8,128)(2,1)S(1)} %fusion.3), channel_id=1, source_target_pairs={{0,8},{8,0},{1,9},{9,1},{2,10},{10,2},{3,11},{11,3},{4,12},{12,4},... | collective-permute-start | bytes 1179656 | tf_op jit(solution)/shard_map/ppermute | solution.py:275
  50.7 7.0 %collective-permute-start.11 = (bf16[128,768]{1,0:T(8,128)(2,1)S(1)}, bf16[128,768]{1,0:T(8,128)(2,1)S(1)}, u32[]{:S(2)}, u32[]{:S(2)}) collective-permute-start(bf16[128,768]{1,0:T(8,128)(2,1)S(1)} %fusion.4.h0.c0), channel_id=1, source_target_pairs={{0,2},{2,0},{4,6},{6,4},{1,3},{3,1},{5,7},{7,5},{8,10},{10,8},{12,... | collective-permute-start | bytes 589832 | tf_op jit(solution)/shard_map/ppermute | solution.py:279
  52.4 12.6 %collective-permute-start.12 = (bf16[128,768]{1,0:T(8,128)(2,1)S(1)}, bf16[128,768]{1,0:T(8,128)(2,1)S(1)}, u32[]{:S(2)}, u32[]{:S(2)}) collective-permute-start(bf16[128,768]{1,0:T(8,128)(2,1)S(1)} %fusion.4.h0.c0), channel_id=1, source_target_pairs={{0,6},{2,4},{4,2},{6,0},{1,7},{3,5},{5,3},{7,1},{8,14},{10,12},{12... | collective-permute-start | bytes 589832 | tf_op jit(solution)/shard_map/ppermute | solution.py:279
  54.8 16.3 %collective-permute-start.13 = (bf16[128,768]{1,0:T(8,128)(2,1)S(1)}, bf16[128,768]{1,0:T(8,128)(2,1)S(1)}, u32[]{:S(2)}, u32[]{:S(2)}) collective-permute-start(bf16[128,768]{1,0:T(8,128)(2,1)S(1)} %fusion.4.h0.c0), channel_id=1, source_target_pairs={{0,4},{2,6},{4,0},{6,2},{1,5},{3,7},{5,1},{7,3},{8,12},{10,14},{12... | collective-permute-start | bytes 589832 | tf_op jit(solution)/shard_map/ppermute | solution.py:279
  54.8 21.2 %collective-permute-start.5 = (bf16[128,768]{1,0:T(8,128)(2,1)S(1)}, bf16[128,768]{1,0:T(8,128)(2,1)S(1)}, u32[]{:S(2)}, u32[]{:S(2)}) collective-permute-start(bf16[128,768]{1,0:T(8,128)(2,1)S(1)} %fusion.4.h0.c0), channel_id=1, source_target_pairs={{0,8},{8,0},{1,9},{9,1},{2,10},{10,2},{3,11},{11,3},{4,12},{12,4},... | collective-permute-start | bytes 589832 | tf_op jit(solution)/shard_map/ppermute | solution.py:275
  71.3 6.9 %collective-permute-start.14 = (bf16[128,768]{1,0:T(8,128)(2,1)S(1)}, bf16[128,768]{1,0:T(8,128)(2,1)S(1)}, u32[]{:S(2)}, u32[]{:S(2)}) collective-permute-start(bf16[128,768]{1,0:T(8,128)(2,1)S(1)} %get-tuple-element.18), channel_id=1, source_target_pairs={{0,8},{8,0},{1,9},{9,1},{2,10},{10,2},{3,11},{11,3},{4,12},{12,4},... | collective-permute-start | bytes 589832 | tf_op jit(solution)/shard_map/ppermute | solution.py:275
  72.8 7.7 %collective-permute-start.15 = (bf16[128,768]{1,0:T(8,128)(2,1)S(1)}, bf16[128,768]{1,0:T(8,128)(2,1)S(1)}, u32[]{:S(2)}, u32[]{:S(2)}) collective-permute-start(bf16[128,768]{1,0:T(8,128)(2,1)S(1)} %collective-permute-done.12), channel_id=1, source_target_pairs={{0,8},{2,10},{12,4},{14,6},{1,9},{3,11},{13,5},{15,7},{16,24},{18,... | collective-permute-start | bytes 589832 | tf_op jit(solution)/shard_map/ppermute | solution.py:313
  75.4 5.2 %collective-permute-start.6 = (bf16[128,768]{1,0:T(8,128)(2,1)S(1)}, bf16[128,768]{1,0:T(8,128)(2,1)S(1)}, u32[]{:S(2)}, u32[]{:S(2)}) collective-permute-start(bf16[128,768]{1,0:T(8,128)(2,1)S(1)} %fusion.4.h0.c0), channel_id=1, source_target_pairs={{0,1},{1,0},{2,3},{3,2},{4,5},{5,4},{6,7},{7,6},{8,9},{9,8},{10,11... | collective-permute-start | bytes 589832 | tf_op jit(solution)/shard_map/ppermute | solution.py:275
  75.5 26.5 %collective-permute-start.16 = (bf16[128,768]{1,0:T(8,128)(2,1)S(1)}, bf16[128,768]{1,0:T(8,128)(2,1)S(1)}, u32[]{:S(2)}, u32[]{:S(2)}) collective-permute-start(bf16[128,768]{1,0:T(8,128)(2,1)S(1)} %get-tuple-element.14), channel_id=1, source_target_pairs={{0,1},{1,0},{2,3},{3,2},{4,5},{5,4},{6,7},{7,6},{8,9},{9,8},{10,11... | collective-permute-start | bytes 589832 | tf_op jit(solution)/shard_map/ppermute | solution.py:275
  76.0 4.7 %collective-permute-start.7 = (bf16[128,768]{1,0:T(8,128)(2,1)S(1)}, bf16[128,768]{1,0:T(8,128)(2,1)S(1)}, u32[]{:S(2)}, u32[]{:S(2)}) collective-permute-start(bf16[128,768]{1,0:T(8,128)(2,1)S(1)} %collective-permute-done.5.h1.c1), channel_id=1, source_target_pairs={{0,1},{1,0},{2,3},{3,2},{4,5},{5,4},{6,7},{7,6},{8,9},{9,8},{10,11... | collective-permute-start | bytes 589832 | tf_op jit(solution)/shard_map/ppermute | solution.py:275
  80.6 21.4 %collective-permute-start.17 = (bf16[128,768]{1,0:T(8,128)(2,1)S(1)}, bf16[128,768]{1,0:T(8,128)(2,1)S(1)}, u32[]{:S(2)}, u32[]{:S(2)}) collective-permute-start(bf16[128,768]{1,0:T(8,128)(2,1)S(1)} %get-tuple-element.16), channel_id=1, source_target_pairs={{0,1},{1,0},{2,3},{3,2},{4,5},{5,4},{6,7},{7,6},{8,9},{9,8},{10,11... | collective-permute-start | bytes 589832 | tf_op jit(solution)/shard_map/ppermute | solution.py:275
  80.7 3.7 %copy-start = (bf16[3072,1536]{1,0:T(8,128)(2,1)S(1)}, bf16[3072,1536]{1,0:T(8,128)(2,1)}, u32[]{:S(2)}) copy-start(bf16[3072,1536]{1,0:T(8,128)(2,1)} %down_ref.1) | copy-start | bytes 28311556
  87.0 0.7 copy-start.2
  87.7 7.4 %collective-permute-start.10 = (bf16[32,1536]{1,0:T(8,128)(2,1)S(1)}, bf16[32,1536]{1,0:T(8,128)(2,1)S(1)}, u32[]{:S(2)}, u32[]{:S(2)}) collective-permute-start(bf16[32,1536]{1,0:T(8,128)(2,1)S(1)} %get-tuple-element.13), channel_id=1, source_target_pairs={{0,6},{2,4},{4,2},{6,0},{1,7},{3,5},{5,3},{7,1},{8,14},{10,12},{12... | collective-permute-start | bytes 294920 | tf_op jit(solution)/shard_map/ppermute | solution.py:279
  90.8 8.0 %collective-permute-start.8 = (bf16[32,1536]{1,0:T(8,128)(2,1)S(1)}, bf16[32,1536]{1,0:T(8,128)(2,1)S(1)}, u32[]{:S(2)}, u32[]{:S(2)}) collective-permute-start(bf16[32,1536]{1,0:T(8,128)(2,1)S(1)} %get-tuple-element.11), channel_id=1, source_target_pairs={{0,2},{2,0},{4,6},{6,4},{1,3},{3,1},{5,7},{7,5},{8,10},{10,8},{12,... | collective-permute-start | bytes 294920 | tf_op jit(solution)/shard_map/ppermute | solution.py:279
  90.8 8.2 %collective-permute-start.9 = (bf16[32,1536]{1,0:T(8,128)(2,1)S(1)}, bf16[32,1536]{1,0:T(8,128)(2,1)S(1)}, u32[]{:S(2)}, u32[]{:S(2)}) collective-permute-start(bf16[32,1536]{1,0:T(8,128)(2,1)S(1)} %get-tuple-element.12), channel_id=1, source_target_pairs={{0,4},{2,6},{4,0},{6,2},{1,5},{3,7},{5,1},{7,3},{8,12},{10,14},{12... | collective-permute-start | bytes 294920 | tf_op jit(solution)/shard_map/ppermute | solution.py:279
  95.1 3.9 %copy-start.3 = (bf16[32,1536]{1,0:T(8,128)(2,1)}, bf16[32,1536]{1,0:T(8,128)(2,1)S(1)}, u32[]{:S(2)}) copy-start(bf16[32,1536]{1,0:T(8,128)(2,1)S(1)} %collective-permute-done.10.r3_ref) | copy-start | bytes 294916
  98.9 0.6 copy-start.4
  99.0 0.6 copy-start.5

commit v2 on v1

--- a/solution.py
+++ b/solution.py
@@ -92,7 +92,10 @@
     ).astype(BF16)
 
 
-def unpack_kernel(routes_ref, pad_ref, weight_ref, own_ref, r1_ref, r2_ref, r3_ref, out_ref):
+def unpack_kernel(
+    after_ref, routes_ref, pad_ref, weight_ref, own_ref, r1_ref, r2_ref, r3_ref, out_ref
+):
+    del after_ref
     routes_t = routes_ref[...]
     placing = placing_of(routes_t, pad_ref[...], own_ref.shape[0])
     weight = jnp.sum(jnp.where(routes_t == 0, weight_ref[...], 0.0), axis=0, keepdims=True)
@@ -104,74 +107,86 @@
     ).astype(BF16)
 
 
-def preact_kernel(first, place_ref, *refs):
+def regroup_kernel(after_ref, weights_ref, out_ref, sems):
+    del after_ref
+    copies = [
+        pltpu.make_async_copy(weights_ref.at[:, t], out_ref.at[t], sems.at[t])
+        for t in range(out_ref.shape[0])
+    ]
+    for copy in copies:
+        copy.start()
+    for copy in copies:
+        copy.wait()
+
+
+def regroup(after, weights):
+    depth, tiles, two, lanes = weights.shape
+    grouped = pl.pallas_call(
+        regroup_kernel,
+        in_specs=[pl.BlockSpec(memory_space=pl.ANY), pl.BlockSpec(memory_space=pltpu.HBM)],
+        out_specs=pl.BlockSpec(memory_space=pltpu.VMEM),
+        out_shape=pltpu.VMEM((tiles, depth, two, lanes), BF16),
+        scratch_shapes=[pltpu.SemaphoreType.DMA((tiles,))],
+        compiler_params=params(8),
+        cost_estimate=cost(0, 4 * weights.size),
+        name="regroup",
+    )(after, weights)
+    return grouped.reshape(tiles, depth * two, lanes)
+
+
+def widen_tokens(place_ref, x_refs, wide_ref):
+    slots, depth = x_refs[0].shape
+    rows = 4 * slots
+    here = place_ref[2]
+    cut = 256
+    into = lax.broadcasted_iota(jnp.int32, (cut, 2 * cut), 1)
+    out_of = lax.broadcasted_iota(jnp.int32, (cut, 2 * cut), 0)
+    for half in range(2):
+        widen = jnp.where(into == 2 * out_of + half, 1.0, 0.0).astype(BF16)
+        for slot, x_ref in enumerate(x_refs):
+            at = pl.multiple_of(half * rows + (here ^ slot) * slots, slots)
+            for k in range(depth // cut):
+                wide_ref[pl.ds(at, slots), 2 * cut * k : 2 * cut * (k + 1)] = jnp.dot(
+                    x_ref[:, cut * k : cut * (k + 1)], widen, preferred_element_type=F32
+                ).astype(BF16)
+
+
+def preact_kernel(first, row_flip, place_ref, *refs):
     if first:
-        x0, x1, x2, x3, w0_ref, w1_ref, out_ref, wide_ref = refs
+        x0, x1, x2, x3, w_ref, out_ref, wide_ref = refs
+        widen_tokens(place_ref, (x0, x1, x2, x3), wide_ref)
     else:
-        wide_ref, w0_ref, w1_ref, out_ref = refs
-    depth = w0_ref.shape[0]
-    if first:
-
-        @pl.when(pl.program_id(0) == 0)
-        def _():
-            slots = x0.shape[0]
-            rows = 4 * slots
-            here = place_ref[2]
-            cut = 256
-            into = lax.broadcasted_iota(jnp.int32, (cut, 2 * cut), 1)
-            out_of = lax.broadcasted_iota(jnp.int32, (cut, 2 * cut), 0)
-            for half in range(2):
-                widen = jnp.where(into == 2 * out_of + half, 1.0, 0.0).astype(BF16)
-                for slot, x_ref in enumerate((x0, x1, x2, x3)):
-                    at = pl.multiple_of(half * rows + (here ^ slot) * slots, slots)
-                    for k in range(depth // cut):
-                        wide_ref[pl.ds(at, slots), 2 * cut * k : 2 * cut * (k + 1)] = jnp.dot(
-                            x_ref[:, cut * k : cut * (k + 1)], widen, preferred_element_type=F32
-                        ).astype(BF16)
-
-    wide = wide_ref[...]
-    lanes = w0_ref.shape[-1]
-    for i, w_ref in enumerate((w0_ref, w1_ref)):
-        w = w_ref.reshape(2 * depth, lanes)[...]
-        out_ref[:, lanes * i : lanes * (i + 1)] = jnp.dot(
-            wide, w, preferred_element_type=F32
-        ).astype(out_ref.dtype)
+        wide_ref, w_ref, out_ref = refs
+    tiles, _, lanes = w_ref.shape
+    per = tiles // 4
+    for i in range(2):
+        quarter = (place_ref[0] ^ (1 - i)) * 2 + (place_ref[1] ^ row_flip)
+        for j in range(per // 2):
+            at = quarter * per + 2 * j
+            w = jnp.concatenate([w_ref[at], w_ref[at + 1]], axis=1)
+            out_ref[i, :, 2 * lanes * j : 2 * lanes * (j + 1)] = jnp.dot(
+                wide_ref[...], w, preferred_element_type=F32
+            ).astype(out_ref.dtype)
 
 
 def preacts_of(place, lefts, weights, row_flip, out_type):
-    depth, tiles, _, lanes = weights.shape
+    tiles, depth2, lanes = weights.shape
     first = len(lefts) > 1
     rows = 4 * lefts[0].shape[0] if first else lefts[0].shape[0] // 2
     per = tiles // 4
-    steps = per // 2
-
-    def tile(i, j, place):
-        quarter = (place[0] ^ (1 - j // steps)) * 2 + (place[1] ^ row_flip)
-        return (0, quarter * per + (j % steps) * 2 + i, 0, 0)
-
-    whole = lambda shape: pl.BlockSpec(shape, lambda j, place: (0,) * len(shape))
+    vmem = pl.BlockSpec(memory_space=pltpu.VMEM)
     out_shape = [jax.ShapeDtypeStruct((2, 2 * rows, per * lanes), out_type)]
-    out_specs = [pl.BlockSpec((None, 2 * rows, 2 * lanes), lambda j, place: (j // steps, 0, j % steps))]
     if first:
-        out_shape.append(jax.ShapeDtypeStruct((2 * rows, 2 * depth), BF16))
-        out_specs.append(whole((2 * rows, 2 * depth)))
+        out_shape.append(jax.ShapeDtypeStruct((2 * rows, depth2), BF16))
     return pl.pallas_call(
-        functools.partial(preact_kernel, first),
-        grid_spec=pltpu.PrefetchScalarGridSpec(
-            num_scalar_prefetch=1,
-            grid=(2 * steps,),
-            in_specs=[whole(left.shape) for left in lefts]
-            + [
-                pl.BlockSpec((depth, None, 2, lanes), functools.partial(tile, 0)),
-                pl.BlockSpec((depth, None, 2, lanes), functools.partial(tile, 1)),
-            ],
-            out_specs=out_specs,
-        ),
+        functools.partial(preact_kernel, first, row_flip),
+        in_specs=[pl.BlockSpec(memory_space=pltpu.SMEM)] + [vmem] * (len(lefts) + 1),
+        out_specs=[vmem] * len(out_shape),
         out_shape=out_shape,
-        compiler_params=params(40),
-        cost_estimate=cost(8 * rows * depth * per * 2 * lanes, depth * tiles * lanes * 2),
+        compiler_params=params(8),
+        cost_estimate=cost(4 * rows * depth2 * per * 2 * lanes, 2 * weights.size // 2),
         name="preacts_sent" if first else "preacts_kept",
-    )(place, *lefts, weights, weights)
+    )(place, *lefts, pltpu.with_memory_space_constraint(weights, pltpu.VMEM))
 
 
 def project_kernel(place_ref, h0, h1, h2, h3, down_ref, own_ref, s1_ref, s2_ref, s3_ref, total_ref):
@@ -215,11 +230,12 @@
         compiler_params=params(32),
         cost_estimate=cost(2 * rows * 4 * units * width, down.size * 2),
         name="project",
-    )(place, *quarters, down)
-
-
-def gram_kernel(scale, halves, place_ref, a0, a1, a2, a3, c0, c1, c2, c3, out_ref, wide_ref):
+    )(place, *quarters, pltpu.with_memory_space_constraint(down, pltpu.HBM))
+
+
+def gram_kernel(scale, halves, place_ref, a0, a1, a2, a3, c0, c1, c2, c3, out_ref, done_ref, wide_ref):
     j = pl.program_id(0)
+    done_ref[...] = jnp.zeros_like(done_ref)
     units = a0.shape[1]
     take = units // halves
 
@@ -261,10 +277,16 @@
             num_scalar_prefetch=1,
             grid=(4 * halves,),
             in_specs=[whole] * 8,
-            out_specs=pl.BlockSpec((units // halves, 4 * units), block),
+            out_specs=[
+                pl.BlockSpec((units // halves, 4 * units), block),
+                pl.BlockSpec((8, 128), lambda j, place: (0, 0)),
+            ],
             scratch_shapes=[pltpu.VMEM((rows, 4 * units), BF16)],
         ),
-        out_shape=jax.ShapeDtypeStruct((4 * units, 4 * units), F32),
+        out_shape=[
+            jax.ShapeDtypeStruct((4 * units, 4 * units), F32),
+            jax.ShapeDtypeStruct((8, 128), F32),
+        ],
         compiler_params=params(32),
         cost_estimate=cost(2 * rows * 16 * units * units, 64 * units * units),
         name="gram",
@@ -298,18 +320,27 @@
         name="pack",
     )(tokens, routes_t, pad)
     lefts = [packed] + [across(packed, slot) for slot in (1, 2, 3)]
-    sent, wide = preacts_of(place, lefts, weights, 1, BF16)
+    grouped = regroup(packed, pltpu.with_memory_space_constraint(weights, pltpu.HBM))
+    sent, wide = preacts_of(place, lefts, grouped, 1, F32)
     got = swap(sent, "row")
-    (kept,) = preacts_of(place, [wide], weights, 0, F32)
-    got_x = swap((kept[0] + got[0].astype(F32)).astype(BF16), "expert")
+    (kept,) = preacts_of(place, [wide], grouped, 0, F32)
+    got_x = swap((kept[0] + got[0]).astype(BF16), "expert")
     rows = 4 * slots
-    preacts = kept[1] + got[1].astype(F32) + got_x.astype(F32)
+    preacts = kept[1] + got[1] + got_x.astype(F32)
     hidden = (jax.nn.silu(preacts[:rows]) * preacts[rows:]).astype(BF16)
 
-    z1, z2, z3 = (across(hidden, slot) for slot in (1, 2, 3))
+    z2 = across(hidden, 2)
+    z1 = across(hidden, 1)
+    hidden_x = swap(hidden, "expert")
+
     near = (c // 2) == e
-    hidden_x = swap(hidden, "expert")
-    x2 = swap(jnp.where(near, z2, z1), "expert")
+    z2, z1, hidden_x = lax.optimization_barrier((z2, z1, hidden_x))
+    onward, x2 = lax.optimization_barrier((z2, jnp.where(near, z2, z1)))
+    z3 = across(onward, 1)
+    x2 = swap(x2, "expert")
+    c_quarters = [hidden, hidden_x, swap(hidden, "row"), swap(hidden_x, "row")]
+    own, s1, s2, s3 = project(place, c_quarters, down)
+    z3, own = lax.optimization_barrier((z3, own))
     x3 = lax.ppermute(
         z3,
         ("expert", "col"),
@@ -325,16 +356,14 @@
     a_own, a_other = pick(odd)
     b_own, b_other = pick(~odd)
     a_quarters = [a_own, a_other, swap(b_own, "row"), swap(b_other, "row")]
-    c_quarters = [hidden, hidden_x, swap(hidden, "row"), swap(hidden_x, "row")]
-
-    own, s1, s2, s3 = project(place, c_quarters, down)
+
     returned = [across(value, slot) for slot, value in ((1, s1), (2, s2), (3, s3))]
-    gram_block = gram_of(place, a_quarters, c_quarters)
+    gram_block, done = gram_of(place, a_quarters, c_quarters)
     expert_out = pl.pallas_call(
         unpack_kernel,
         out_shape=jax.ShapeDtypeStruct((group_rows, depth), BF16),
         name="unpack",
-    )(routes_t, pad, route_weight.T, own, *returned)
+    )(done, routes_t, pad, route_weight.T, own, *returned)
     return (expert_out, gram_block)
 
 

time: 117 us -> 89 us (0.76)
  waiting for transfers between devices: 44.2 us -> 22.5 us
  local copies, waits for them, and re-layouts: 5.88 us -> 2.2 us
  Pallas kernels: 42.7 us -> 40 us
    ppermute x9, waiting for transfers between devices: 29.7 us -> 7.96 us  [across(): return lax.ppermute(value, 'col', [(i, i ^ slot) for i in range(4)])]
    pallas_call x2 -> x3, Pallas kernels: 21.5 us -> 15.6 us  [the longest x2 8.64 us: preacts_of(): pl.pallas_call(functools.partial(preact_kernel, first, row_flip), in_spec...]
    unnamed x12 -> x14, local copies, waits for them, and re-layouts: 5.88 us -> 2.2 us
    pallas_call x1, Pallas kernels: 2.63 us -> 5.83 us  [project(): pl.pallas_call(project_kernel, grid_spec=pltpu.PrefetchScalarGridSpec(num...]
    ppermute x1, waiting for transfers between devices: 2.35 us -> 3.78 us  [on_device(): lax.ppermute(z3, ('expert', 'col'), [(ee * 4 + cc, (1 - ee) * 4 + cc) for...]
    ppermute x8, waiting for transfers between devices: 12.1 us -> 10.8 us  [swap(): return lax.ppermute(value, axis, [(0, 1), (1, 0)])]
  transfers between devices with their start and end apart: 18 -> 18, of which waited for: 11 -> 8; matrix products, arithmetic and copies ran while one was open for 0% -> 0% of each run, Pallas kernels for 13% -> 34%
where the time goes in v2:
time: 89 us; the launch traced here: 88.8 us
  Pallas kernels  40 us (45%)
  starting transfers between devices  22.6 us (25%)
  waiting for transfers between devices  22.5 us (25%)
  local copies, waits for them, and re-layouts  2.2 us (2%)
    ppermute x9, starting transfers between devices, across(): return lax.ppermute(value, 'col', [(i, i ^ slot) for i in range(4)])  15.3 us
    pallas_call x1, Pallas kernels, gram_of(): pl.pallas_call(functools.partial(gram_kernel, 2.0 / rows, halves), grid_s...  14.2 us
    ppermute x8, waiting for transfers between devices, swap(): return lax.ppermute(value, axis, [(0, 1), (1, 0)])  10.8 us
    pallas_call x2, Pallas kernels, preacts_of(): pl.pallas_call(functools.partial(preact_kernel, first, row_flip), in_spec...  8.64 us
    ppermute x9, waiting for transfers between devices, across(): return lax.ppermute(value, 'col', [(i, i ^ slot) for i in range(4)])  7.96 us
    pallas_call x1, Pallas kernels, regroup(): pl.pallas_call(regroup_kernel, in_specs=[pl.BlockSpec(memory_space=pl.ANY...  7 us
    pallas_call x1, Pallas kernels, project(): pl.pallas_call(project_kernel, grid_spec=pltpu.PrefetchScalarGridSpec(num...  5.83 us
    ppermute x8, starting transfers between devices, swap(): return lax.ppermute(value, axis, [(0, 1), (1, 0)])  4.3 us
  transfers between devices with their start and end apart: 18, of which 8 were waited for; matrix products, arithmetic and copies ran while one was open for 0% of the time, Pallas kernels for 34%

profile of v2, /device:TPU:0, one launch (start us, length us, event | category | flops | bytes accessed | tf_op | source)
XLA Modules:
  0.0 88.8 jit_solution(768340804193802974)
XLA Ops:
  0.6 2.0 %pack.1.after_ref.refs_0_ = bf16[32,1536]{1,0:T(8,128)(2,1)} custom-call(bf16[128,1536]{1,0:T(8,128)(2,1)} %tokens_ref.1, s32[2,128]{1,0:T(2,128)} %bitcast.19, s32[1,128]{1,0:T(1,128)} %bitcast.21), custom_call_target="tpu_custom_call" | custom-call | tf_op jit(solution)/shard_map/pack/pallas_call | solution.py:317
  2.6 5.1 %collective-permute-start.2 = (bf16[32,1536]{1,0:T(8,128)(2,1)}, bf16[32,1536]{1,0:T(8,128)(2,1)S(1)}, u32[]{:S(2)}, u32[]{:S(2)}) collective-permute-start(bf16[32,1536]{1,0:T(8,128)(2,1)} %pack.1.after_ref.refs_0_), channel_id=1, source_target_pairs={{0,6},{2,4},{4,2},{6,0},{1,7},{3,5},{5,3},{7,1},{8,14},{10,12},{12... | collective-permute-start | bytes 294920 | tf_op jit(solution)/shard_map/ppermute | solution.py:301
  7.7 0.6 collective-permute-start
  8.2 0.9 %copy-done = bf16[32,1536]{1,0:T(8,128)(2,1)S(1)} copy-done((bf16[32,1536]{1,0:T(8,128)(2,1)S(1)}, bf16[32,1536]{1,0:T(8,128)(2,1)}, u32[]{:S(2)}) %copy-start) | copy-done | bytes 98328
  9.2 7.0 %regroup.1 = bf16[24,1536,2,128]{3,2,1,0:T(2,128)(2,1)S(1)} custom-call(bf16[32,1536]{1,0:T(8,128)(2,1)S(1)} %copy-done, bf16[1536,24,2,128]{3,2,1,0:T(2,128)(2,1)} %bitcast.18), custom_call_target="tpu_custom_call" | custom-call | bytes 37748736 | tf_op jit(solution)/shard_map/regroup/pallas_call | solution.py:124
  16.3 5.4 %preacts_sent.1 = (f32[2,256,768]{2,1,0:T(8,128)S(1)}, bf16[256,3072]{1,0:T(8,128)(2,1)S(1)}) custom-call(s32[3]{0:T(128)S(1)} %pad_add_fusion.place_ref, bf16[32,1536]{1,0:T(8,128)(2,1)S(1)} %copy-done.1, bf16[32,1536]{1,0:T(8,128)(2,1)S(1)} %collective-permute-done.refs_1_, bf16[32,1536]{1,0:T(8,128)(2,1)S(1)} %collective-permute-done.1.refs_2_, ...), custom_call_target="tpu_custom_call" | custom-call | flops 2415919104 | bytes 9437184 | tf_op jit(solution)/shard_map/preacts_sent/pallas_call | solution.py:181
  21.8 3.2 %preacts_kept.1 = f32[2,256,768]{2,1,0:T(8,128)S(1)} custom-call(s32[3]{0:T(128)S(1)} %pad_add_fusion.place_ref, bf16[256,3072]{1,0:T(8,128)(2,1)S(1)} %get-tuple-element.17.refs_0_, bf16[24,3072,128]{2,1,0:T(8,128)(2,1)S(1)} %bitcast.17), custom_call_target="tpu_custom_call" | custom-call | flops 2415919104 | bytes 9437184 | tf_op jit(solution)/shard_map/preacts_kept/pallas_call | solution.py:181
  25.3 1.8 %collective-permute-start.4 = (bf16[256,768]{1,0:T(8,128)(2,1)S(1)}, bf16[256,768]{1,0:T(8,128)(2,1)S(1)}, u32[]{:S(2)}, u32[]{:S(2)}) collective-permute-start(bf16[256,768]{1,0:T(8,128)(2,1)S(1)} %fusion.3), channel_id=1, source_target_pairs={{0,8},{8,0},{1,9},{9,1},{2,10},{10,2},{3,11},{11,3},{4,12},{12,4},... | collective-permute-start | bytes 1179656 | tf_op jit(solution)/shard_map/ppermute | solution.py:297
  27.0 9.7 %collective-permute-done.4 = bf16[256,768]{1,0:T(8,128)(2,1)S(1)} collective-permute-done((bf16[256,768]{1,0:T(8,128)(2,1)S(1)}, bf16[256,768]{1,0:T(8,128)(2,1)S(1)}, u32[]{:S(2)}, u32[]{:S(2)}) %collective-permute-start.4) | collective-permute-done | bytes 393248 | tf_op jit(solution)/shard_map/ppermute | solution.py:297
  36.9 1.8 %collective-permute-start.7 = (bf16[128,768]{1,0:T(8,128)(2,1)S(1)}, bf16[128,768]{1,0:T(8,128)(2,1)S(1)}, u32[]{:S(2)}, u32[]{:S(2)}) collective-permute-start(bf16[128,768]{1,0:T(8,128)(2,1)S(1)} %fusion.4.h0.c0), channel_id=1, source_target_pairs={{0,8},{8,0},{1,9},{9,1},{2,10},{10,2},{3,11},{11,3},{4,12},{12,4},... | collective-permute-start | bytes 589832 | tf_op jit(solution)/shard_map/ppermute | solution.py:297
  38.7 1.2 %collective-permute-start.6 = (bf16[128,768]{1,0:T(8,128)(2,1)S(1)}, bf16[128,768]{1,0:T(8,128)(2,1)S(1)}, u32[]{:S(2)}, u32[]{:S(2)}) collective-permute-start(bf16[128,768]{1,0:T(8,128)(2,1)S(1)} %fusion.4.h0.c0), channel_id=1, source_target_pairs={{0,2},{2,0},{4,6},{6,4},{1,3},{3,1},{5,7},{7,5},{8,10},{10,8},{12,... | collective-permute-start | bytes 589832 | tf_op jit(solution)/shard_map/ppermute | solution.py:301
  39.9 2.9 %collective-permute-start.5 = (bf16[128,768]{1,0:T(8,128)(2,1)S(1)}, bf16[128,768]{1,0:T(8,128)(2,1)S(1)}, u32[]{:S(2)}, u32[]{:S(2)}) collective-permute-start(bf16[128,768]{1,0:T(8,128)(2,1)S(1)} %fusion.4.h0.c0), channel_id=1, source_target_pairs={{0,4},{2,6},{4,0},{6,2},{1,5},{3,7},{5,1},{7,3},{8,12},{10,14},{12... | collective-permute-start | bytes 589832 | tf_op jit(solution)/shard_map/ppermute | solution.py:301
  43.3 5.4 %collective-permute-done.6 = bf16[128,768]{1,0:T(8,128)(2,1)S(1)} collective-permute-done((bf16[128,768]{1,0:T(8,128)(2,1)S(1)}, bf16[128,768]{1,0:T(8,128)(2,1)S(1)}, u32[]{:S(2)}, u32[]{:S(2)}) %collective-permute-start.6) | collective-permute-done | bytes 196640 | tf_op jit(solution)/shard_map/ppermute | solution.py:301
  48.7 2.4 %collective-permute-done.5 = bf16[128,768]{1,0:T(8,128)(2,1)S(1)} collective-permute-done((bf16[128,768]{1,0:T(8,128)(2,1)S(1)}, bf16[128,768]{1,0:T(8,128)(2,1)S(1)}, u32[]{:S(2)}, u32[]{:S(2)}) %collective-permute-start.5) | collective-permute-done | bytes 196640 | tf_op jit(solution)/shard_map/ppermute | solution.py:301
  51.6 0.5 collective-permute-start.11
  52.6 5.8 %project.1 = (f32[32,1536]{1,0:T(8,128)S(1)}, bf16[32,1536]{1,0:T(8,128)(2,1)S(1)}, bf16[32,1536]{1,0:T(8,128)(2,1)S(1)}, bf16[32,1536]{1,0:T(8,128)(2,1)S(1)}) custom-call(s32[3]{0:T(128)S(1)} %pad_add_fusion.place_ref, bf16[128,768]{1,0:T(8,128)(2,1)S(1)} %fusion.4.h0.c0, bf16[128,768]{1,0:T(8,128)(2,1)S(1)} %collective-permute-done.7.h1.c1, ...), custom_call_target="tpu_custom_call" | custom-call | flops 1207959552 | bytes 9437184 | tf_op jit(solution)/shard_map/project/pallas_call | solution.py:219
  58.6 3.0 %collective-permute-start.12 = (bf16[128,768]{1,0:T(8,128)(2,1)S(1)}, bf16[128,768]{1,0:T(8,128)(2,1)S(1)}, u32[]{:S(2)}, u32[]{:S(2)}) collective-permute-start(bf16[128,768]{1,0:T(8,128)(2,1)S(1)} %collective-permute-done.8), channel_id=1, source_target_pairs={{0,8},{2,10},{12,4},{14,6},{1,9},{3,11},{13,5},{15,7},{16,24},{18,... | collective-permute-start | bytes 589832 | tf_op jit(solution)/shard_map/ppermute | solution.py:344
  61.9 3.8 %collective-permute-done.12 = bf16[128,768]{1,0:T(8,128)(2,1)S(1)} collective-permute-done((bf16[128,768]{1,0:T(8,128)(2,1)S(1)}, bf16[128,768]{1,0:T(8,128)(2,1)S(1)}, u32[]{:S(2)}, u32[]{:S(2)}) %collective-permute-start.12) | collective-permute-done | bytes 196640 | tf_op jit(solution)/shard_map/ppermute | solution.py:344
  65.8 1.7 %collective-permute-start.15 = (bf16[32,1536]{1,0:T(8,128)(2,1)S(1)}, bf16[32,1536]{1,0:T(8,128)(2,1)S(1)}, u32[]{:S(2)}, u32[]{:S(2)}) collective-permute-start(bf16[32,1536]{1,0:T(8,128)(2,1)S(1)} %get-tuple-element.28), channel_id=1, source_target_pairs={{0,2},{2,0},{4,6},{6,4},{1,3},{3,1},{5,7},{7,5},{8,10},{10,8},{12,... | collective-permute-start | bytes 294920 | tf_op jit(solution)/shard_map/ppermute | solution.py:301
  67.5 2.9 %collective-permute-start.16 = (bf16[32,1536]{1,0:T(8,128)(2,1)S(1)}, bf16[32,1536]{1,0:T(8,128)(2,1)S(1)}, u32[]{:S(2)}, u32[]{:S(2)}) collective-permute-start(bf16[32,1536]{1,0:T(8,128)(2,1)S(1)} %get-tuple-element.29), channel_id=1, source_target_pairs={{0,4},{2,6},{4,0},{6,2},{1,5},{3,7},{5,1},{7,3},{8,12},{10,14},{12... | collective-permute-start | bytes 294920 | tf_op jit(solution)/shard_map/ppermute | solution.py:301
  70.9 14.2 %gram.1 = (f32[3072,3072]{1,0:T(8,128)}, f32[8,128]{1,0:T(8,128)S(1)}) custom-call(s32[3]{0:T(128)S(1)} %pad_add_fusion.place_ref, bf16[128,768]{1,0:T(8,128)(2,1)S(1)} %get-tuple-element.33.a0, bf16[128,768]{1,0:T(8,128)(2,1)S(1)} %get-tuple-element.35.a1, bf16[128,768]{1,0:T(8,128)(2,1)S(1)} %collective-permute-done.13.a2, ...), custom_call_target="tpu_custom_call" | custom-call | flops 2415919104 | bytes 37748736 | tf_op jit(solution)/shard_map/gram/pallas_call | solution.py:274
  85.1 0.6 copy-done.3
  85.8 0.6 copy-done.4
  86.5 2.3 %unpack.1 = bf16[128,1536]{1,0:T(8,128)(2,1)} custom-call(f32[8,128]{1,0:T(8,128)} %copy-done.3, s32[2,128]{1,0:T(2,128)} %bitcast.20, s32[1,128]{1,0:T(1,128)} %bitcast.22, f32[2,128]{1,0:T(2,128)} %bitcast.23, f32[32,1536]{1,0:T(8,128)} %copy-done.2, bf16[32,1536]{1,0:T(8,128)(2,1)} %copy-done.4, bf16[32,1536]{1,0:T(8,128)(2,1)} %copy-done.5, ...), custom_call_target="tpu_custom_call" | custom-call | tf_op jit(solution)/shard_map/unpack/pallas_call | solution.py:362
  (40 shorter events, 3.2 us)
Async XLA Ops:
  2.6 13.6 %collective-permute-start.2 = (bf16[32,1536]{1,0:T(8,128)(2,1)}, bf16[32,1536]{1,0:T(8,128)(2,1)S(1)}, u32[]{:S(2)}, u32[]{:S(2)}) collective-permute-start(bf16[32,1536]{1,0:T(8,128)(2,1)} %pack.1.after_ref.refs_0_), channel_id=1, source_target_pairs={{0,6},{2,4},{4,2},{6,0},{1,7},{3,5},{5,3},{7,1},{8,14},{10,12},{12... | collective-permute-start | bytes 294920 | tf_op jit(solution)/shard_map/ppermute | solution.py:301
  7.7 8.6 %collective-permute-start.1 = (bf16[32,1536]{1,0:T(8,128)(2,1)}, bf16[32,1536]{1,0:T(8,128)(2,1)S(1)}, u32[]{:S(2)}, u32[]{:S(2)}) collective-permute-start(bf16[32,1536]{1,0:T(8,128)(2,1)} %pack.1.after_ref.refs_0_), channel_id=1, source_target_pairs={{0,4},{2,6},{4,0},{6,2},{1,5},{3,7},{5,1},{7,3},{8,12},{10,14},{12... | collective-permute-start | bytes 294920 | tf_op jit(solution)/shard_map/ppermute | solution.py:301
  7.7 8.6 %collective-permute-start = (bf16[32,1536]{1,0:T(8,128)(2,1)}, bf16[32,1536]{1,0:T(8,128)(2,1)S(1)}, u32[]{:S(2)}, u32[]{:S(2)}) collective-permute-start(bf16[32,1536]{1,0:T(8,128)(2,1)} %pack.1.after_ref.refs_0_), channel_id=1, source_target_pairs={{0,2},{2,0},{4,6},{6,4},{1,3},{3,1},{5,7},{7,5},{8,10},{10,8},{12,... | collective-permute-start | bytes 294920 | tf_op jit(solution)/shard_map/ppermute | solution.py:301
  8.2 0.9 %copy-start = (bf16[32,1536]{1,0:T(8,128)(2,1)S(1)}, bf16[32,1536]{1,0:T(8,128)(2,1)}, u32[]{:S(2)}) copy-start(bf16[32,1536]{1,0:T(8,128)(2,1)} %pack.1.after_ref.refs_0_) | copy-start | bytes 294916
  9.1 7.1 %copy-start.1 = (bf16[32,1536]{1,0:T(8,128)(2,1)S(1)}, bf16[32,1536]{1,0:T(8,128)(2,1)}, u32[]{:S(2)}) copy-start(bf16[32,1536]{1,0:T(8,128)(2,1)} %pack.1.after_ref.refs_0_) | copy-start | bytes 294916
  21.7 3.5 %collective-permute-start.3 = (f32[2,256,768]{2,1,0:T(8,128)S(1)}, f32[2,256,768]{2,1,0:T(8,128)S(1)}, u32[]{:S(2)}, u32[]{:S(2)}) collective-permute-start(f32[2,256,768]{2,1,0:T(8,128)S(1)} %get-tuple-element.18), channel_id=1, source_target_pairs={{0,1},{1,0},{2,3},{3,2},{4,5},{5,4},{6,7},{7,6},{8,9},{9,8},{10,11... | collective-permute-start | bytes 4718600 | tf_op jit(solution)/shard_map/ppermute | solution.py:297
  25.3 11.4 %collective-permute-start.4 = (bf16[256,768]{1,0:T(8,128)(2,1)S(1)}, bf16[256,768]{1,0:T(8,128)(2,1)S(1)}, u32[]{:S(2)}, u32[]{:S(2)}) collective-permute-start(bf16[256,768]{1,0:T(8,128)(2,1)S(1)} %fusion.3), channel_id=1, source_target_pairs={{0,8},{8,0},{1,9},{9,1},{2,10},{10,2},{3,11},{11,3},{4,12},{12,4},... | collective-permute-start | bytes 1179656 | tf_op jit(solution)/shard_map/ppermute | solution.py:297
  36.9 6.4 %collective-permute-start.7 = (bf16[128,768]{1,0:T(8,128)(2,1)S(1)}, bf16[128,768]{1,0:T(8,128)(2,1)S(1)}, u32[]{:S(2)}, u32[]{:S(2)}) collective-permute-start(bf16[128,768]{1,0:T(8,128)(2,1)S(1)} %fusion.4.h0.c0), channel_id=1, source_target_pairs={{0,8},{8,0},{1,9},{9,1},{2,10},{10,2},{3,11},{11,3},{4,12},{12,4},... | collective-permute-start | bytes 589832 | tf_op jit(solution)/shard_map/ppermute | solution.py:297
  38.7 10.0 %collective-permute-start.6 = (bf16[128,768]{1,0:T(8,128)(2,1)S(1)}, bf16[128,768]{1,0:T(8,128)(2,1)S(1)}, u32[]{:S(2)}, u32[]{:S(2)}) collective-permute-start(bf16[128,768]{1,0:T(8,128)(2,1)S(1)} %fusion.4.h0.c0), channel_id=1, source_target_pairs={{0,2},{2,0},{4,6},{6,4},{1,3},{3,1},{5,7},{7,5},{8,10},{10,8},{12,... | collective-permute-start | bytes 589832 | tf_op jit(solution)/shard_map/ppermute | solution.py:301
  39.9 11.2 %collective-permute-start.5 = (bf16[128,768]{1,0:T(8,128)(2,1)S(1)}, bf16[128,768]{1,0:T(8,128)(2,1)S(1)}, u32[]{:S(2)}, u32[]{:S(2)}) collective-permute-start(bf16[128,768]{1,0:T(8,128)(2,1)S(1)} %fusion.4.h0.c0), channel_id=1, source_target_pairs={{0,4},{2,6},{4,0},{6,2},{1,5},{3,7},{5,1},{7,3},{8,12},{10,14},{12... | collective-permute-start | bytes 589832 | tf_op jit(solution)/shard_map/ppermute | solution.py:301
  42.9 9.3 %collective-permute-start.9 = (bf16[128,768]{1,0:T(8,128)(2,1)S(1)}, bf16[128,768]{1,0:T(8,128)(2,1)S(1)}, u32[]{:S(2)}, u32[]{:S(2)}) collective-permute-start(bf16[128,768]{1,0:T(8,128)(2,1)S(1)} %fusion.4.h0.c0), channel_id=1, source_target_pairs={{0,1},{1,0},{2,3},{3,2},{4,5},{5,4},{6,7},{7,6},{8,9},{9,8},{10,11... | collective-permute-start | bytes 589832 | tf_op jit(solution)/shard_map/ppermute | solution.py:297
  51.1 1.4 %collective-permute-start.10 = (bf16[128,768]{1,0:T(8,128)(2,1)S(1)}, bf16[128,768]{1,0:T(8,128)(2,1)S(1)}, u32[]{:S(2)}, u32[]{:S(2)}) collective-permute-start(bf16[128,768]{1,0:T(8,128)(2,1)S(1)} %collective-permute-done.7.h1.c1), channel_id=1, source_target_pairs={{0,1},{1,0},{2,3},{3,2},{4,5},{5,4},{6,7},{7,6},{8,9},{9,8},{10,11... | collective-permute-start | bytes 589832 | tf_op jit(solution)/shard_map/ppermute | solution.py:297
  51.2 7.4 %collective-permute-start.8 = (bf16[128,768]{1,0:T(8,128)(2,1)S(1)}, bf16[128,768]{1,0:T(8,128)(2,1)S(1)}, u32[]{:S(2)}, u32[]{:S(2)}) collective-permute-start(bf16[128,768]{1,0:T(8,128)(2,1)S(1)} %collective-permute-done.5), channel_id=1, source_target_pairs={{0,2},{2,0},{4,6},{6,4},{1,3},{3,1},{5,7},{7,5},{8,10},{10,8},{12,... | collective-permute-start | bytes 589832 | tf_op jit(solution)/shard_map/ppermute | solution.py:301
  51.6 10.3 %collective-permute-start.11 = (bf16[128,768]{1,0:T(8,128)(2,1)S(1)}, bf16[128,768]{1,0:T(8,128)(2,1)S(1)}, u32[]{:S(2)}, u32[]{:S(2)}) collective-permute-start(bf16[128,768]{1,0:T(8,128)(2,1)S(1)} %broadcast_select_fusion), channel_id=1, source_target_pairs={{0,8},{8,0},{1,9},{9,1},{2,10},{10,2},{3,11},{11,3},{4,12},{12,4},... | collective-permute-start | bytes 589832 | tf_op jit(solution)/shard_map/ppermute | solution.py:297
  58.4 26.7 %copy-start.2 = (f32[32,1536]{1,0:T(8,128)}, f32[32,1536]{1,0:T(8,128)S(1)}, u32[]{:S(2)}) copy-start(f32[32,1536]{1,0:T(8,128)S(1)} %get-tuple-element.27.own_ref) | copy-start | bytes 589828
  58.6 7.1 %collective-permute-start.12 = (bf16[128,768]{1,0:T(8,128)(2,1)S(1)}, bf16[128,768]{1,0:T(8,128)(2,1)S(1)}, u32[]{:S(2)}, u32[]{:S(2)}) collective-permute-start(bf16[128,768]{1,0:T(8,128)(2,1)S(1)} %collective-permute-done.8), channel_id=1, source_target_pairs={{0,8},{2,10},{12,4},{14,6},{1,9},{3,11},{13,5},{15,7},{16,24},{18,... | collective-permute-start | bytes 589832 | tf_op jit(solution)/shard_map/ppermute | solution.py:344
  61.8 9.1 %collective-permute-start.13 = (bf16[128,768]{1,0:T(8,128)(2,1)S(1)}, bf16[128,768]{1,0:T(8,128)(2,1)S(1)}, u32[]{:S(2)}, u32[]{:S(2)}) collective-permute-start(bf16[128,768]{1,0:T(8,128)(2,1)S(1)} %get-tuple-element.32), channel_id=1, source_target_pairs={{0,1},{1,0},{2,3},{3,2},{4,5},{5,4},{6,7},{7,6},{8,9},{9,8},{10,11... | collective-permute-start | bytes 589832 | tf_op jit(solution)/shard_map/ppermute | solution.py:297
  65.7 5.2 %collective-permute-start.14 = (bf16[128,768]{1,0:T(8,128)(2,1)S(1)}, bf16[128,768]{1,0:T(8,128)(2,1)S(1)}, u32[]{:S(2)}, u32[]{:S(2)}) collective-permute-start(bf16[128,768]{1,0:T(8,128)(2,1)S(1)} %get-tuple-element.34), channel_id=1, source_target_pairs={{0,1},{1,0},{2,3},{3,2},{4,5},{5,4},{6,7},{7,6},{8,9},{9,8},{10,11... | collective-permute-start | bytes 589832 | tf_op jit(solution)/shard_map/ppermute | solution.py:297
  65.8 19.9 %collective-permute-start.15 = (bf16[32,1536]{1,0:T(8,128)(2,1)S(1)}, bf16[32,1536]{1,0:T(8,128)(2,1)S(1)}, u32[]{:S(2)}, u32[]{:S(2)}) collective-permute-start(bf16[32,1536]{1,0:T(8,128)(2,1)S(1)} %get-tuple-element.28), channel_id=1, source_target_pairs={{0,2},{2,0},{4,6},{6,4},{1,3},{3,1},{5,7},{7,5},{8,10},{10,8},{12,... | collective-permute-start | bytes 294920 | tf_op jit(solution)/shard_map/ppermute | solution.py:301
  67.5 18.2 %collective-permute-start.16 = (bf16[32,1536]{1,0:T(8,128)(2,1)S(1)}, bf16[32,1536]{1,0:T(8,128)(2,1)S(1)}, u32[]{:S(2)}, u32[]{:S(2)}) collective-permute-start(bf16[32,1536]{1,0:T(8,128)(2,1)S(1)} %get-tuple-element.29), channel_id=1, source_target_pairs={{0,4},{2,6},{4,0},{6,2},{1,5},{3,7},{5,1},{7,3},{8,12},{10,14},{12... | collective-permute-start | bytes 294920 | tf_op jit(solution)/shard_map/ppermute | solution.py:301
  70.4 15.4 %collective-permute-start.17 = (bf16[32,1536]{1,0:T(8,128)(2,1)S(1)}, bf16[32,1536]{1,0:T(8,128)(2,1)S(1)}, u32[]{:S(2)}, u32[]{:S(2)}) collective-permute-start(bf16[32,1536]{1,0:T(8,128)(2,1)S(1)} %get-tuple-element.30), channel_id=1, source_target_pairs={{0,6},{2,4},{4,2},{6,0},{1,7},{3,5},{5,3},{7,1},{8,14},{10,12},{12... | collective-permute-start | bytes 294920 | tf_op jit(solution)/shard_map/ppermute | solution.py:301
  85.7 0.6 copy-start.4
  85.7 0.7 copy-start.5
  85.8 0.7 copy-start.6
  (1 other events, 0.6 us)

commit v3 on v0

--- a/solution.py
+++ b/solution.py
@@ -1,7 +1,15 @@
+import functools
+
 import jax
 import jax.numpy as jnp
 from jax import lax
+from jax.experimental import pallas as pl
+from jax.experimental.pallas import tpu as pltpu
 from jax.sharding import PartitionSpec as P
+
+F32 = jnp.float32
+BF16 = jnp.bfloat16
+MIB = 1 << 20
 
 
 def spread(value, axis, source):
@@ -13,7 +21,7 @@
     return (jax.nn.silu(preacts[:, 0, :]) * preacts[:, 1, :]).astype(jnp.bfloat16)
 
 
-def on_device(tokens, routes, route_weight, pad_mask, gate_up, down):
+def on_any_device(tokens, routes, route_weight, pad_mask, gate_up, down):
     group_rows = tokens.shape[0]
     slot_count = group_rows // 4
     names_zero = routes == 0
@@ -56,6 +64,425 @@
     return (expert_out, gram_block)
 
 
+def cost(flops, moved):
+    return pl.CostEstimate(flops=int(flops), bytes_accessed=int(moved), transcendentals=0)
+
+
+def params(mib):
+    return pltpu.CompilerParams(vmem_limit_bytes=mib * MIB)
+
+
+VMEM = pl.BlockSpec(memory_space=pltpu.VMEM)
+HBM = pl.BlockSpec(memory_space=pltpu.HBM)
+SMEM = pl.BlockSpec(memory_space=pltpu.SMEM)
+ANY = pl.BlockSpec(memory_space=pl.ANY)
+
+
+def in_vmem(value):
+    return pltpu.with_memory_space_constraint(value, pltpu.VMEM)
+
+
+def in_hbm(value):
+    return pltpu.with_memory_space_constraint(value, pltpu.HBM)
+
+
+def tie(*values):
+    return lax.optimization_barrier(values)
+
+
+def pack_kernel(
+    tokens_ref, routes_ref, pad_ref, weight_ref, packed_ref, placing_ref, factor_ref, held_ref, sem
+):
+    copy = pltpu.make_async_copy(tokens_ref, held_ref, sem)
+    copy.start()
+    slots, rows = placing_ref.shape
+    routes_t = routes_ref[...]
+    routed = (routes_t[0:1, :] == 0) | (routes_t[1:2, :] == 0)
+    live = jnp.where(routed & (pad_ref[...] == 1), 1.0, 0.0)
+    before = lax.broadcasted_iota(jnp.int32, (rows, rows), 0)
+    upto = lax.broadcasted_iota(jnp.int32, (rows, rows), 1)
+    tri = jnp.where(before <= upto, 1.0, 0.0).astype(BF16)
+    routed_rows = jnp.broadcast_to(jnp.where(routed, 1.0, 0.0), (8, rows)).astype(BF16)
+    position = jnp.dot(routed_rows, tri, preferred_element_type=F32)[0:1, :] - 1.0
+    slot_ids = lax.broadcasted_iota(jnp.int32, (slots, rows), 0).astype(F32)
+    placing = jnp.where(position == slot_ids, jnp.broadcast_to(live, (slots, rows)), 0.0)
+    placing_ref[...] = placing.astype(BF16)
+    weight = jnp.sum(jnp.where(routes_t == 0, weight_ref[...], 0.0), axis=0, keepdims=True)
+    factor = jnp.sum(placing * weight, axis=1, keepdims=True)
+    factor_ref[...] = jnp.broadcast_to(factor, factor_ref.shape)
+    copy.wait()
+    packed_ref[...] = jnp.dot(
+        placing.astype(BF16), held_ref[...], preferred_element_type=F32
+    ).astype(BF16)
+
+
+def pack(tokens, routes_t, pad, weight_t):
+    rows, depth = tokens.shape
+    slots = rows // 4
+    return pl.pallas_call(
+        pack_kernel,
+        in_specs=[HBM, VMEM, VMEM, VMEM],
+        out_specs=[VMEM] * 3,
+        out_shape=[
+            pltpu.VMEM((slots, depth), BF16),
+            pltpu.VMEM((slots, rows), BF16),
+            pltpu.VMEM((slots, 128), F32),
+        ],
+        scratch_shapes=[pltpu.VMEM((rows, depth), BF16), pltpu.SemaphoreType.DMA],
+        compiler_params=params(4),
+        name="pack",
+    )(tokens, routes_t, pad, weight_t)
+
+
+def unpack_kernel(after_ref, placing_ref, factor_ref, own_ref, r1_ref, r2_ref, r3_ref, out_ref):
+    del after_ref
+    total = own_ref[...] + r1_ref[...].astype(F32) + r2_ref[...].astype(F32) + r3_ref[...].astype(F32)
+    scaled = (total * factor_ref[:, 0:1]).astype(BF16)
+    out_ref[...] = lax.dot_general(
+        placing_ref[...], scaled, (((0,), (0,)), ((), ())), preferred_element_type=F32
+    ).astype(BF16)
+
+
+def unpack(done, placing, factor, own, returned):
+    slots, rows = placing.shape
+    return pl.pallas_call(
+        unpack_kernel,
+        in_specs=[ANY] + [VMEM] * 6,
+        out_specs=VMEM,
+        out_shape=jax.ShapeDtypeStruct((rows, own.shape[1]), BF16),
+        compiler_params=params(4),
+        name="unpack",
+    )(done, placing, factor, own, *returned)
+
+
+def regroup_kernel(after_ref, weights_ref, out_ref, sems):
+    del after_ref
+    copies = [
+        pltpu.make_async_copy(weights_ref.at[:, t], out_ref.at[t], sems.at[t])
+        for t in range(out_ref.shape[0])
+    ]
+    for copy in copies:
+        copy.start()
+    for copy in copies:
+        copy.wait()
+
+
+def regroup(behind, weights):
+    depth, tiles, two, lanes = weights.shape
+    grouped = pl.pallas_call(
+        regroup_kernel,
+        in_specs=[ANY, HBM],
+        out_specs=VMEM,
+        out_shape=pltpu.VMEM((tiles, depth, two, lanes), BF16),
+        scratch_shapes=[pltpu.SemaphoreType.DMA((tiles,))],
+        compiler_params=params(4),
+        cost_estimate=cost(0, 4 * weights.size),
+        name="regroup",
+    )(behind, in_hbm(weights))
+    return grouped.reshape(tiles, depth * two, lanes)
+
+
+def fetch_kernel(after_ref, down_ref, out_ref, done_ref, sems):
+    del after_ref
+    parts = sems.shape[0]
+    size = down_ref.shape[0] // parts
+    copies = [
+        pltpu.make_async_copy(
+            down_ref.at[pl.ds(size * i, size)], out_ref.at[pl.ds(size * i, size)], sems.at[i]
+        )
+        for i in range(parts)
+    ]
+    for copy in copies:
+        copy.start()
+    done_ref[...] = jnp.zeros_like(done_ref)
+    for copy in copies:
+        copy.wait()
+
+
+def fetch(behind, down):
+    return pl.pallas_call(
+        fetch_kernel,
+        in_specs=[ANY, HBM],
+        out_specs=[VMEM, VMEM],
+        out_shape=[pltpu.VMEM(down.shape, BF16), pltpu.VMEM((8, 128), F32)],
+        scratch_shapes=[pltpu.SemaphoreType.DMA((4,))],
+        compiler_params=params(4),
+        cost_estimate=cost(0, 4 * down.size),
+        name="fetch_down",
+    )(behind, in_hbm(down))
+
+
+def widen_tokens(place_ref, x_refs, wide_ref):
+    slots, depth = x_refs[0].shape
+    rows = 4 * slots
+    here = place_ref[2]
+    cut = 256
+    into = lax.broadcasted_iota(jnp.int32, (cut, 4 * cut), 1)
+    out_of = lax.broadcasted_iota(jnp.int32, (cut, 4 * cut), 0)
+    half = jnp.where(into < 2 * cut, 0, 1)
+    widen = jnp.where(into - 2 * cut * half == 2 * out_of + half, 1.0, 0.0).astype(BF16)
+    for slot, x_ref in enumerate(x_refs):
+        stacked = jnp.concatenate(
+            [x_ref[:, cut * k : cut * (k + 1)] for k in range(depth // cut)], axis=0
+        )
+        spaced = jnp.dot(stacked, widen, preferred_element_type=F32).astype(BF16)
+        for h in range(2):
+            at = pl.multiple_of(h * rows + (here ^ slot) * slots, slots)
+            for k in range(depth // cut):
+                wide_ref[pl.ds(at, slots), 2 * cut * k : 2 * cut * (k + 1)] = spaced[
+                    slots * k : slots * (k + 1), 2 * cut * h : 2 * cut * (h + 1)
+                ]
+
+
+def preact_kernel(first, row_flip, chunk, chunks, place_ref, *refs):
+    if first:
+        x0, x1, x2, x3, w_ref, out_ref, wide_ref = refs
+        widen_tokens(place_ref, (x0, x1, x2, x3), wide_ref)
+    else:
+        wide_ref, w_ref, out_ref = refs
+    tiles, _, lanes = w_ref.shape
+    per = tiles // 4
+    take = per // chunks
+    at = []
+    for i in range(2):
+        quarter = (place_ref[0] ^ (1 - i)) * 2 + (place_ref[1] ^ row_flip)
+        at += [quarter * per + chunk * take + j for j in range(take)]
+    for j in range(take):
+        w = jnp.concatenate([w_ref[at[2 * j]], w_ref[at[2 * j + 1]]], axis=1)
+        out_ref[:, 2 * lanes * j : 2 * lanes * (j + 1)] = jnp.dot(
+            wide_ref[...], w, preferred_element_type=F32
+        )
+
+
+def preacts_of(place, lefts, weights, row_flip, chunk, chunks):
+    tiles, depth2, lanes = weights.shape
+    first = len(lefts) > 1
+    rows = 4 * lefts[0].shape[0] if first else lefts[0].shape[0] // 2
+    units = tiles // 4 // chunks * lanes
+    out_shape = [jax.ShapeDtypeStruct((2 * rows, 2 * units), F32)]
+    if first:
+        out_shape.append(pltpu.VMEM((2 * rows, depth2), BF16))
+    return pl.pallas_call(
+        functools.partial(preact_kernel, first, row_flip, chunk, chunks),
+        in_specs=[SMEM] + [VMEM] * (len(lefts) + 1),
+        out_specs=[VMEM] * len(out_shape),
+        out_shape=out_shape,
+        compiler_params=params(8),
+        cost_estimate=cost(8 * rows * depth2 * units, 0),
+        name="preacts_" + ("sent" if row_flip else "kept"),
+    )(place, *lefts, in_vmem(weights))
+
+
+def project_kernel(tick_ref, place_ref, hidden_ref, down_ref, own_ref, s1_ref, s2_ref, s3_ref, total_ref):
+    del tick_ref
+    slots, width = own_ref.shape
+    cut = 512
+    for n in range(width // cut):
+        total_ref[:, cut * n : cut * (n + 1)] = jnp.dot(
+            hidden_ref[...], down_ref[:, cut * n : cut * (n + 1)], preferred_element_type=F32
+        )
+    here = place_ref[2]
+    for slot, out_ref in enumerate((own_ref, s1_ref, s2_ref, s3_ref)):
+        at = pl.multiple_of((here ^ slot) * slots, slots)
+        out_ref[...] = total_ref[pl.ds(at, slots), :].astype(out_ref.dtype)
+
+
+def project(tick, place, hidden, down):
+    rows, units = hidden.shape
+    width = down.shape[1]
+    slots = rows // 4
+    return pl.pallas_call(
+        project_kernel,
+        in_specs=[ANY, SMEM, VMEM, VMEM],
+        out_specs=[VMEM] * 4,
+        out_shape=[jax.ShapeDtypeStruct((slots, width), F32)]
+        + [jax.ShapeDtypeStruct((slots, width), BF16)] * 3,
+        scratch_shapes=[pltpu.VMEM((rows, width), F32)],
+        compiler_params=params(8),
+        cost_estimate=cost(2 * rows * units * width, 0),
+        name="project",
+    )(tick, place, in_vmem(hidden), in_vmem(down))
+
+
+def gram_kernel(scale, first, flip, chunk, chunks, tick_ref, place_ref, a0, a1, *refs):
+    del tick_ref
+    if first:
+        c_refs = refs[: 4 * chunks]
+        out_ref, done_ref, wide_ref, held_ref, sems = refs[4 * chunks :]
+    else:
+        wide_ref, _, out_ref, done_ref, held_ref, sems = refs
+    done_ref[...] = jnp.zeros_like(done_ref)
+    units = a0.shape[1]
+    quarter = chunks * units
+    if first:
+        for k in range(4):
+            q = (place_ref[0] ^ (k % 2)) * 2 + (place_ref[1] ^ (k // 2))
+            for h in range(chunks):
+                at = pl.multiple_of(q * quarter + h * units, units)
+                wide_ref[:, pl.ds(at, units)] = c_refs[k * chunks + h][...]
+    cut = held_ref.shape[-1]
+    copies = []
+    for k, a_ref in enumerate((a0, a1)):
+        q = (place_ref[0] ^ flip) * 2 + (place_ref[1] ^ k)
+        rows = pl.ds(pl.multiple_of(q * quarter + chunk * units, units), units)
+        left = a_ref[...].T
+        for n in range(4 * quarter // cut):
+            columns = pl.ds(cut * n, cut)
+            held_ref[k, n] = scale * jnp.dot(
+                left, wide_ref[:, cut * n : cut * (n + 1)], preferred_element_type=F32
+            )
+            copy = pltpu.make_async_copy(
+                held_ref.at[k, n], out_ref.at[rows, columns], sems.at[k, n]
+            )
+            copy.start()
+            copies.append(copy)
+    for copy in copies:
+        copy.wait()
+
+
+def gram_piece(tick, place, pieces, flip, chunk, chunks, c_parts=None, wide=None, gram=None):
+    rows, units = pieces[0].shape
+    quarter = chunks * units
+    first = gram is None
+    cut = 512
+    steps = 4 * quarter // cut
+    out_specs = [HBM, VMEM]
+    out_shape = [
+        jax.ShapeDtypeStruct((4 * quarter, 4 * quarter), F32),
+        pltpu.VMEM((8, 128), F32),
+    ]
+    if first:
+        operands = [tick, place, *pieces, *c_parts]
+        in_specs = [ANY, SMEM] + [VMEM] * (2 + 4 * chunks)
+        out_specs.append(VMEM)
+        out_shape.append(pltpu.VMEM((rows, 4 * quarter), BF16))
+        aliases = {}
+    else:
+        operands = [tick, place, *pieces, in_vmem(wide), gram]
+        in_specs = [ANY, SMEM] + [VMEM] * 3 + [HBM]
+        aliases = {5: 0}
+    return pl.pallas_call(
+        functools.partial(gram_kernel, 2.0 / rows, first, flip, chunk, chunks),
+        in_specs=in_specs,
+        out_specs=out_specs,
+        out_shape=out_shape,
+        input_output_aliases=aliases,
+        scratch_shapes=[
+            pltpu.VMEM((2, steps, units, cut), F32),
+            pltpu.SemaphoreType.DMA((2, steps)),
+        ],
+        compiler_params=params(24),
+        cost_estimate=cost(16 * rows * units * quarter, 32 * units * quarter),
+        name="gram",
+    )(*operands)
+
+
+def swap(value, axis):
+    return lax.ppermute(value, axis, [(0, 1), (1, 0)])
+
+
+def across(value, slot):
+    return lax.ppermute(value, "col", [(i, i ^ slot) for i in range(4)])
+
+
+def on_device(tokens, routes, route_weight, pad_mask, gate_up, down):
+    group_rows, depth = tokens.shape
+    slots = group_rows // 4
+    rows = 4 * slots
+    units = gate_up.shape[2]
+    lanes = 128
+    chunks = 2
+    width = units // 4 // chunks
+    e = lax.axis_index("expert").astype(jnp.int32)
+    r = lax.axis_index("row").astype(jnp.int32)
+    c = lax.axis_index("col").astype(jnp.int32)
+    place = jnp.stack([e, r, c])
+    near = (c // 2) == e
+    odd = (c % 2) != r
+    weights = gate_up.reshape(depth, 2, units // lanes, lanes).transpose(0, 2, 1, 3)
+
+    packed, placing, factor = pack(tokens, routes.T, pad_mask[None, :], route_weight.T)
+    lefts = [packed] + [across(packed, slot) for slot in (1, 2, 3)]
+    grouped = regroup(packed, weights)
+
+    first_sent, wide = preacts_of(place, lefts, grouped, 1, 0, chunks)
+    (last_sent,) = preacts_of(place, [wide], grouped, 1, 1, chunks)
+    got = [swap(first_sent, "row"), swap(last_sent, "row")]
+    sums, got_x = [], []
+    for h in range(chunks):
+        (kept,) = preacts_of(place, [wide], grouped, 0, h, chunks)
+        leaves = (kept[:, :width] + got[h][:, :width]).astype(BF16)
+        wide, leaves = tie(wide, leaves)
+        sums.append(kept[:, width:] + got[h][:, width:])
+        got_x.append(swap(leaves, "expert"))
+    down_held, tick = fetch(wide, down)
+
+    hidden, z1, z2, z3, hidden_x, x2, x3 = ([None] * chunks for _ in range(7))
+    for h in range(chunks):
+        tick, arrived = tie(tick, got_x[h])
+        preacts = sums[h] + arrived.astype(F32)
+        hidden[h] = (jax.nn.silu(preacts[:rows]) * preacts[rows:]).astype(BF16)
+        z2[h] = across(hidden[h], 2)
+        z1[h] = across(hidden[h], 1)
+        hidden_x[h] = swap(hidden[h], "expert")
+
+    def pass_on(tick, h):
+        tick, z2[h], z1[h], hidden[-1] = tie(tick, z2[h], z1[h], hidden[-1])
+        tick, onward, leaves = tie(tick, z2[h], jnp.where(near, z2[h], z1[h]))
+        z3[h] = across(onward, 1)
+        x2[h] = swap(leaves, "expert")
+        return tick
+
+    def pass_last(tick, h):
+        tick, z3[h] = tie(tick, z3[h])
+        x3[h] = lax.ppermute(
+            z3[h],
+            ("expert", "col"),
+            [
+                (ee * 4 + cc, (1 - ee) * 4 + cc)
+                for ee in range(2)
+                for cc in range(4)
+                if cc // 2 == ee
+            ],
+        )
+        return tick
+
+    def own_plane(h, flag):
+        return jnp.where(near, jnp.where(flag, z1[h], hidden[h]), jnp.where(flag, z3[h], z2[h]))
+
+    def other_plane(h, flag):
+        return jnp.where(near, jnp.where(flag, x2[h], hidden_x[h]), jnp.where(flag, x3[h], x2[h]))
+
+    def pieces_of(plane, h):
+        return [plane(h, odd), swap(plane(h, ~odd), "row")]
+
+    tick = pass_on(tick, 0)
+    tick, hidden_x[0] = tie(tick, hidden_x[0])
+    c_parts = [*hidden, *hidden_x, swap(hidden[0], "row"), swap(hidden[1], "row")]
+    c_parts.append(swap(hidden_x[0], "row"))
+    tick = pass_last(tick, 0)
+    own_first = pieces_of(own_plane, 0)
+    tick = pass_on(tick, 1)
+    tick, hidden_x[1] = tie(tick, hidden_x[1])
+    c_parts[3] = hidden_x[1]
+    c_parts.append(swap(hidden_x[1], "row"))
+    gram, tick, hidden_c = gram_piece(tick, place, own_first, 0, 0, chunks, c_parts=c_parts)
+
+    tick = pass_last(tick, 1)
+    own_last = pieces_of(own_plane, 1)
+    own, s1, s2, s3 = project(tick, place, hidden_c, down_held)
+    tick, own = tie(tick, own)
+    returned = [across(value, slot) for slot, value in ((1, s1), (2, s2), (3, s3))]
+    tick, x2[0], x3[0] = tie(tick, x2[0], x3[0])
+    other_first = pieces_of(other_plane, 0)
+    gram, tick = gram_piece(tick, place, own_last, 0, 1, chunks, wide=hidden_c, gram=gram)
+    tick, x2[1], x3[1] = tie(tick, x2[1], x3[1])
+    other_last = pieces_of(other_plane, 1)
+    gram, tick = gram_piece(tick, place, other_first, 1, 0, chunks, wide=hidden_c, gram=gram)
+    gram, tick = gram_piece(tick, place, other_last, 1, 1, chunks, wide=hidden_c, gram=gram)
+    return (unpack(tick, placing, factor, own, returned), gram)
+
+
 def solution(mesh):
     in_specs = (
         P(("parts", "col"), ("expert", "row")),
@@ -66,6 +493,11 @@
         P("col", ("expert", "row")),
     )
     out_specs = (P(("parts", "col"), ("expert", "row")), P(("parts", "expert", "row"), "col"))
+    small = mesh.shape["expert"] == 2 and mesh.shape["row"] == 2 and mesh.shape["col"] == 4
     return jax.shard_map(
-        on_device, mesh=mesh, in_specs=in_specs, out_specs=out_specs, check_vma=False
+        on_device if small else on_any_device,
+        mesh=mesh,
+        in_specs=in_specs,
+        out_specs=out_specs,
+        check_vma=False,
     )

time: 193 us -> 112 us (0.58)
  waiting for transfers between devices: 116 us -> 11.3 us
  Pallas kernels: 0 us -> 41 us
  matrix products: 40.9 us -> 0 us
  starting transfers between devices: 0.12 us -> 33 us
  local copies, waits for them, and re-layouts: 0.12 us -> 19.3 us
  blocking collectives: 16.2 us -> 0 us
  between operations: 13.8 us -> 1 us
    psum x2 -> x0, waiting for transfers between devices: 108 us -> none  [the longest x1 70.2 us: on_device(): lax.psum(jnp.einsum('rd,dgf->rgf', gathered, gate_up, preferred_element_t...]
    pallas_call x0 -> x13, Pallas kernels: none -> 41 us  [the longest x4 18.2 us: gram_piece(): pl.pallas_call(functools.partial(gram_kernel, 2.0 / rows, first, flip, ch...]
    dot_general x5 -> x0, matrix products: 40.9 us -> none  [the longest x1 16.8 us: on_device(): lax.dot_general(mirrored, hidden, (((0,), (0,)), ((), ())), preferred_ele...]
    ppermute x0 -> x30, starting transfers between devices: none -> 33 us  [the longest x12 18.1 us: across(): return lax.ppermute(value, 'col', [(i, i ^ slot) for i in range(4)])]
    unnamed x6 -> x18, local copies, waits for them, and re-layouts: 0.01 us -> 19.3 us
    all_gather x1 -> x0, blocking collectives: 16.2 us -> none  [on_device(): gathered = lax.all_gather(packed, 'col', axis=0, tiled=True)]
    ppermute x0 -> x30, waiting for transfers between devices: none -> 11.3 us  [the longest x12 10.6 us: across(): return lax.ppermute(value, 'col', [(i, i ^ slot) for i in range(4)])]
    reduce_scatter x1 -> x0, waiting for transfers between devices: 8.15 us -> none  [on_device(): lax.psum_scatter(jnp.dot(hidden, down, preferred_element_type=jnp.float32...]
  transfers between devices with their start and end apart: 3 -> 30, of which waited for: 3 -> 5; matrix products, arithmetic and copies ran while one was open for 12% -> 5% of each run, Pallas kernels for 0% -> 33%
where the time goes in v3:
time: 112 us; the launch traced here: 111 us
  Pallas kernels  41 us (37%)
  starting transfers between devices  33 us (29%)
  local copies, waits for them, and re-layouts  19.3 us (17%)
  waiting for transfers between devices  11.3 us (10%)
  other arithmetic  5.45 us (5%)
    unnamed x18, local copies, waits for them, and re-layouts  19.3 us
    pallas_call x4, Pallas kernels, gram_piece(): pl.pallas_call(functools.partial(gram_kernel, 2.0 / rows, first, flip, ch...  18.2 us
    ppermute x12, starting transfers between devices, across(): return lax.ppermute(value, 'col', [(i, i ^ slot) for i in range(4)])  18.1 us
    ppermute x12, waiting for transfers between devices, across(): return lax.ppermute(value, 'col', [(i, i ^ slot) for i in range(4)])  10.6 us
    pallas_call x4, Pallas kernels, preacts_of(): pl.pallas_call(functools.partial(preact_kernel, first, row_flip, chunk, c...  8.4 us
    ppermute x2, starting transfers between devices, pass_last(): lax.ppermute(z3[h], ('expert', 'col'), [(ee * 4 + cc, (1 - ee) * 4 + cc)...  7.47 us
    ppermute x16, starting transfers between devices, swap(): return lax.ppermute(value, axis, [(0, 1), (1, 0)])  7.47 us
    pallas_call x1, Pallas kernels, regroup(): pl.pallas_call(regroup_kernel, in_specs=[ANY, HBM], out_specs=VMEM, out_s...  6.97 us
  transfers between devices with their start and end apart: 30, of which 5 were waited for; matrix products, arithmetic and copies ran while one was open for 5% of the time, Pallas kernels for 33%

profile of v3, /device:TPU:0, one launch (start us, length us, event | category | flops | bytes accessed | tf_op | source)
XLA Modules:
  0.0 111.1 jit_solution(6435094318473802351)
XLA Ops:
  4.3 5.1 %collective-permute-start.2 = (bf16[32,1536]{1,0:T(8,128)(2,1)S(1)}, bf16[32,1536]{1,0:T(8,128)(2,1)S(1)}, u32[]{:S(2)}, u32[]{:S(2)}) collective-permute-start(bf16[32,1536]{1,0:T(8,128)(2,1)S(1)} %get-tuple-element.60.after_ref.refs_0_), channel_id=1, source_target_pairs={{0,6},{2,4},{4,2},{6,0},{1,7},{3,5},{5,3},{7,1},{8,14},{10,12},{12... | collective-permute-start | bytes 294920 | tf_op jit(solution)/shard_map/ppermute | solution.py:385
  10.0 7.0 %regroup.1 = bf16[24,1536,2,128]{3,2,1,0:T(2,128)(2,1)S(1)} custom-call(bf16[32,1536]{1,0:T(8,128)(2,1)S(1)} %get-tuple-element.60.after_ref.refs_0_, bf16[1536,24,2,128]{3,2,1,0:T(2,128)(2,1)} %bitcast.17), custom_call_target="tpu_custom_call" | custom-call | bytes 37748736 | tf_op jit(solution)/shard_map/regroup/pallas_call | solution.py:172
  17.6 2.5 %preacts_sent.2 = (f32[256,768]{1,0:T(8,128)S(1)}, bf16[256,3072]{1,0:T(8,128)(2,1)S(1)}) custom-call(s32[3]{0:T(128)S(1)} %pad_add_fusion.place_ref, bf16[32,1536]{1,0:T(8,128)(2,1)S(1)} %get-tuple-element.60.after_ref.refs_0_, bf16[32,1536]{1,0:T(8,128)(2,1)S(1)} %collective-permute-done.refs_1_, bf16[32,1536]{1,0:T(8,128)(2,1)S(1)} %collective-permute-done.1.refs_2_, ...), custom_call_target="tpu_custom_call" | custom-call | flops 1207959552 | tf_op jit(solution)/shard_map/preacts_sent/pallas_call | solution.py:265
  20.3 2.0 %preacts_sent.3 = f32[256,768]{1,0:T(8,128)S(1)} custom-call(s32[3]{0:T(128)S(1)} %pad_add_fusion.place_ref, bf16[256,3072]{1,0:T(8,128)(2,1)S(1)} %get-tuple-element.64.refs_0_.after_ref, bf16[24,3072,128]{2,1,0:T(8,128)(2,1)S(1)} %bitcast.11), custom_call_target="tpu_custom_call" | custom-call | flops 1207959552 | tf_op jit(solution)/shard_map/preacts_sent/pallas_call | solution.py:265
  23.8 6.4 %copy-done.1 = bf16[24,1536,2,128]{3,2,1,0:T(2,128)(2,1)S(1)} copy-done((bf16[24,1536,2,128]{3,2,1,0:T(2,128)(2,1)S(1)}, bf16[24,1536,2,128]{3,2,1,0:T(2,128)(2,1)}, u32[]{:S(2)}) %copy-start.1) | copy-done | bytes 18874392
  30.2 1.9 %preacts_kept.2 = f32[256,768]{1,0:T(8,128)S(1)} custom-call(s32[3]{0:T(128)S(1)} %pad_add_fusion.place_ref, bf16[256,3072]{1,0:T(8,128)(2,1)S(1)} %get-tuple-element.64.refs_0_.after_ref, bf16[24,3072,128]{2,1,0:T(8,128)(2,1)S(1)} %bitcast.12), custom_call_target="tpu_custom_call" | custom-call | flops 1207959552 | tf_op jit(solution)/shard_map/preacts_kept/pallas_call | solution.py:265
  32.2 1.8 %fusion.3 = bf16[256,384]{1,0:T(8,128)(2,1)S(1)} fusion(f32[256,768]{1,0:T(8,128)} %collective-permute-done.3, f32[256,768]{1,0:T(8,128)S(1)} %preacts_kept.2), kind=kLoop, calls=%fused_computation.7 | loop fusion | flops 196608 | bytes 983040 | tf_op jit(solution)/shard_map/convert_element_type | solution.py:414
  34.0 1.7 %collective-permute-start.5 = (bf16[256,384]{1,0:T(8,128)(2,1)S(1)}, bf16[256,384]{1,0:T(8,128)(2,1)S(1)}, u32[]{:S(2)}, u32[]{:S(2)}) collective-permute-start(bf16[256,384]{1,0:T(8,128)(2,1)S(1)} %fusion.3), channel_id=1, source_target_pairs={{0,8},{8,0},{1,9},{9,1},{2,10},{10,2},{3,11},{11,3},{4,12},{12,4},... | collective-permute-start | bytes 589832 | tf_op jit(solution)/shard_map/ppermute | solution.py:381
  36.7 2.0 %preacts_kept.3 = f32[256,768]{1,0:T(8,128)S(1)} custom-call(s32[3]{0:T(128)S(1)} %pad_add_fusion.place_ref, bf16[256,3072]{1,0:T(8,128)(2,1)S(1)} %get-tuple-element.64.refs_0_.after_ref, bf16[24,3072,128]{2,1,0:T(8,128)(2,1)S(1)} %bitcast.13), custom_call_target="tpu_custom_call" | custom-call | flops 1207959552 | tf_op jit(solution)/shard_map/preacts_kept/pallas_call | solution.py:265
  41.4 3.8 %fetch_down.1 = (bf16[3072,1536]{1,0:T(8,128)(2,1)S(1)}, f32[8,128]{1,0:T(8,128)S(1)}) custom-call(bf16[256,3072]{1,0:T(8,128)(2,1)S(1)} %get-tuple-element.64.refs_0_.after_ref, bf16[3072,1536]{1,0:T(8,128)(2,1)} %down_ref.1), custom_call_target="tpu_custom_call" | custom-call | bytes 18874368 | tf_op jit(solution)/shard_map/fetch_down/pallas_call | solution.py:203
  45.2 3.7 %copy-done.3 = bf16[3072,1536]{1,0:T(8,128)(2,1)} copy-done((bf16[3072,1536]{1,0:T(8,128)(2,1)}, bf16[3072,1536]{1,0:T(8,128)(2,1)S(1)}, u32[]{:S(2)}) %copy-start.3) | copy-done | bytes 9437208
  51.9 2.9 %collective-permute-start.7 = (bf16[128,384]{1,0:T(8,128)(2,1)S(1)}, bf16[128,384]{1,0:T(8,128)(2,1)S(1)}, u32[]{:S(2)}, u32[]{:S(2)}) collective-permute-start(bf16[128,384]{1,0:T(8,128)(2,1)S(1)} %fusion.5.refs_0_), channel_id=1, source_target_pairs={{0,4},{2,6},{4,0},{6,2},{1,5},{3,7},{5,1},{7,3},{8,12},{10,14},{12... | collective-permute-start | bytes 294920 | tf_op jit(solution)/shard_map/ppermute | solution.py:385
  56.0 3.6 %collective-permute-done.7 = bf16[128,384]{1,0:T(8,128)(2,1)S(1)} collective-permute-done((bf16[128,384]{1,0:T(8,128)(2,1)S(1)}, bf16[128,384]{1,0:T(8,128)(2,1)S(1)}, u32[]{:S(2)}, u32[]{:S(2)}) %collective-permute-start.7) | collective-permute-done | bytes 98336 | tf_op jit(solution)/shard_map/ppermute | solution.py:385
  64.4 2.0 %collective-permute-done.12 = bf16[128,384]{1,0:T(8,128)(2,1)S(1)} collective-permute-done((bf16[128,384]{1,0:T(8,128)(2,1)S(1)}, bf16[128,384]{1,0:T(8,128)(2,1)S(1)}, u32[]{:S(2)}, u32[]{:S(2)}) %collective-permute-start.12) | collective-permute-done | bytes 98336 | tf_op jit(solution)/shard_map/ppermute | solution.py:385
  66.4 4.4 %collective-permute-done.11 = bf16[128,384]{1,0:T(8,128)(2,1)S(1)} collective-permute-done((bf16[128,384]{1,0:T(8,128)(2,1)S(1)}, bf16[128,384]{1,0:T(8,128)(2,1)S(1)}, u32[]{:S(2)}, u32[]{:S(2)}) %collective-permute-start.11) | collective-permute-done | bytes 98336 | tf_op jit(solution)/shard_map/ppermute | solution.py:385
  72.4 3.4 %collective-permute-start.21 = (bf16[128,384]{1,0:T(8,128)(2,1)S(1)}, bf16[128,384]{1,0:T(8,128)(2,1)S(1)}, u32[]{:S(2)}, u32[]{:S(2)}) collective-permute-start(bf16[128,384]{1,0:T(8,128)(2,1)S(1)} %collective-permute-done.10), channel_id=1, source_target_pairs={{0,8},{2,10},{12,4},{14,6},{1,9},{3,11},{13,5},{15,7},{16,24},{18,... | collective-permute-start | bytes 294920 | tf_op jit(solution)/shard_map/ppermute | solution.py:438
  75.9 4.6 %gram.4 = (f32[3072,3072]{1,0:T(8,128)}, f32[8,128]{1,0:T(8,128)S(1)}, bf16[128,3072]{1,0:T(8,128)(2,1)S(1)}) custom-call(f32[8,128]{1,0:T(8,128)S(1)} %get-tuple-element.84.tick_ref, s32[3]{0:T(128)S(1)} %pad_add_fusion.place_ref, bf16[128,384]{1,0:T(8,128)(2,1)S(1)} %get-tuple-element.121.a0, bf16[128,384]{1,0:T(8,128)(2,1)S(1)} %collective-permute-done.14.a1, ...), custom_call_target="tpu_custom_call" | custom-call | flops 603979776 | bytes 9437184 | tf_op jit(solution)/shard_map/gram/pallas_call | solution.py:364
  80.5 4.1 %collective-permute-start.24 = (bf16[128,384]{1,0:T(8,128)(2,1)S(1)}, bf16[128,384]{1,0:T(8,128)(2,1)S(1)}, u32[]{:S(2)}, u32[]{:S(2)}) collective-permute-start(bf16[128,384]{1,0:T(8,128)(2,1)S(1)} %collective-permute-done.19), channel_id=1, source_target_pairs={{0,8},{2,10},{12,4},{14,6},{1,9},{3,11},{13,5},{15,7},{16,24},{18,... | collective-permute-start | bytes 294920 | tf_op jit(solution)/shard_map/ppermute | solution.py:438
  84.7 3.7 %copy-done.4 = bf16[3072,1536]{1,0:T(8,128)(2,1)S(1)} copy-done((bf16[3072,1536]{1,0:T(8,128)(2,1)S(1)}, bf16[3072,1536]{1,0:T(8,128)(2,1)}, u32[]{:S(2)}) %copy-start.4) | copy-done | bytes 9437208
  88.3 2.0 %project.1 = (f32[32,1536]{1,0:T(8,128)S(1)}, bf16[32,1536]{1,0:T(8,128)(2,1)S(1)}, bf16[32,1536]{1,0:T(8,128)(2,1)S(1)}, bf16[32,1536]{1,0:T(8,128)(2,1)S(1)}) custom-call(f32[8,128]{1,0:T(8,128)S(1)} %get-tuple-element.96.tick_ref, s32[3]{0:T(128)S(1)} %pad_add_fusion.place_ref, bf16[128,3072]{1,0:T(8,128)(2,1)S(1)} %get-tuple-element.91.hidden_ref.refs_0_, ...), custom_call_target="tpu_custom_call" | custom-call | flops 1207959552 | tf_op jit(solution)/shard_map/project/pallas_call | solution.py:294
  91.7 4.5 %gram.5 = (f32[3072,3072]{1,0:T(8,128)}, f32[8,128]{1,0:T(8,128)S(1)}) custom-call(f32[8,128]{1,0:T(8,128)S(1)} %get-tuple-element.96.tick_ref, s32[3]{0:T(128)S(1)} %pad_add_fusion.place_ref, bf16[128,384]{1,0:T(8,128)(2,1)S(1)} %get-tuple-element.119.a0, bf16[128,384]{1,0:T(8,128)(2,1)S(1)} %collective-permute-done.22.a1, ...), custom_call_target="tpu_custom_call", output_to_operand_aliasing={{0}: (5, {})} | custom-call | flops 603979776 | bytes 9437184 | tf_op jit(solution)/shard_map/gram/pallas_call | solution.py:364
  98.2 2.8 %collective-permute-start.29 = (bf16[32,1536]{1,0:T(8,128)(2,1)S(1)}, bf16[32,1536]{1,0:T(8,128)(2,1)S(1)}, u32[]{:S(2)}, u32[]{:S(2)}) collective-permute-start(bf16[32,1536]{1,0:T(8,128)(2,1)S(1)} %get-tuple-element.116), channel_id=1, source_target_pairs={{0,6},{2,4},{4,2},{6,0},{1,7},{3,5},{5,3},{7,1},{8,14},{10,12},{12... | collective-permute-start | bytes 294920 | tf_op jit(solution)/shard_map/ppermute | solution.py:385
  100.9 4.5 %gram.6 = (f32[3072,3072]{1,0:T(8,128)}, f32[8,128]{1,0:T(8,128)S(1)}) custom-call(f32[8,128]{1,0:T(8,128)S(1)} %get-tuple-element.102.tick_ref, s32[3]{0:T(128)S(1)} %pad_add_fusion.place_ref, bf16[128,384]{1,0:T(8,128)(2,1)S(1)} %get-tuple-element.125.a0, bf16[128,384]{1,0:T(8,128)(2,1)S(1)} %collective-permute-done.25.a1, ...), custom_call_target="tpu_custom_call", output_to_operand_aliasing={{0}: (5, {})} | custom-call | flops 603979776 | bytes 9437184 | tf_op jit(solution)/shard_map/gram/pallas_call | solution.py:364
  105.5 4.6 %gram.7 = (f32[3072,3072]{1,0:T(8,128)}, f32[8,128]{1,0:T(8,128)S(1)}) custom-call(f32[8,128]{1,0:T(8,128)S(1)} %get-tuple-element.106.tick_ref, s32[3]{0:T(128)S(1)} %pad_add_fusion.place_ref, bf16[128,384]{1,0:T(8,128)(2,1)S(1)} %get-tuple-element.123.a0, bf16[128,384]{1,0:T(8,128)(2,1)S(1)} %collective-permute-done.26.a1, ...), custom_call_target="tpu_custom_call", output_to_operand_aliasing={{0}: (5, {})} | custom-call | flops 603979776 | bytes 9437184 | tf_op jit(solution)/shard_map/gram/pallas_call | solution.py:364
  (80 shorter events, 25.3 us)
Async XLA Ops:
  4.3 12.8 %collective-permute-start.2 = (bf16[32,1536]{1,0:T(8,128)(2,1)S(1)}, bf16[32,1536]{1,0:T(8,128)(2,1)S(1)}, u32[]{:S(2)}, u32[]{:S(2)}) collective-permute-start(bf16[32,1536]{1,0:T(8,128)(2,1)S(1)} %get-tuple-element.60.after_ref.refs_0_), channel_id=1, source_target_pairs={{0,6},{2,4},{4,2},{6,0},{1,7},{3,5},{5,3},{7,1},{8,14},{10,12},{12... | collective-permute-start | bytes 294920 | tf_op jit(solution)/shard_map/ppermute | solution.py:385
  9.4 8.3 %collective-permute-start.1 = (bf16[32,1536]{1,0:T(8,128)(2,1)S(1)}, bf16[32,1536]{1,0:T(8,128)(2,1)S(1)}, u32[]{:S(2)}, u32[]{:S(2)}) collective-permute-start(bf16[32,1536]{1,0:T(8,128)(2,1)S(1)} %get-tuple-element.60.after_ref.refs_0_), channel_id=1, source_target_pairs={{0,4},{2,6},{4,0},{6,2},{1,5},{3,7},{5,1},{7,3},{8,12},{10,14},{12... | collective-permute-start | bytes 294920 | tf_op jit(solution)/shard_map/ppermute | solution.py:385
  9.4 8.3 %collective-permute-start = (bf16[32,1536]{1,0:T(8,128)(2,1)S(1)}, bf16[32,1536]{1,0:T(8,128)(2,1)S(1)}, u32[]{:S(2)}, u32[]{:S(2)}) collective-permute-start(bf16[32,1536]{1,0:T(8,128)(2,1)S(1)} %get-tuple-element.60.after_ref.refs_0_), channel_id=1, source_target_pairs={{0,2},{2,0},{4,6},{6,4},{1,3},{3,1},{5,7},{7,5},{8,10},{10,8},{12,... | collective-permute-start | bytes 294920 | tf_op jit(solution)/shard_map/ppermute | solution.py:385
  20.2 12.0 %collective-permute-start.3 = (f32[256,768]{1,0:T(8,128)S(1)}, f32[256,768]{1,0:T(8,128)}, u32[]{:S(2)}, u32[]{:S(2)}) collective-permute-start(f32[256,768]{1,0:T(8,128)S(1)} %get-tuple-element.62), channel_id=1, source_target_pairs={{0,1},{1,0},{2,3},{3,2},{4,5},{5,4},{6,7},{7,6},{8,9},{9,8},{10,11... | collective-permute-start | bytes 2359304 | tf_op jit(solution)/shard_map/ppermute | solution.py:381
  23.8 14.8 %collective-permute-start.4 = (f32[256,768]{1,0:T(8,128)S(1)}, f32[256,768]{1,0:T(8,128)}, u32[]{:S(2)}, u32[]{:S(2)}) collective-permute-start(f32[256,768]{1,0:T(8,128)S(1)} %preacts_sent.3), channel_id=1, source_target_pairs={{0,1},{1,0},{2,3},{3,2},{4,5},{5,4},{6,7},{7,6},{8,9},{9,8},{10,11... | collective-permute-start | bytes 2359304 | tf_op jit(solution)/shard_map/ppermute | solution.py:381
  34.0 14.9 %collective-permute-start.5 = (bf16[256,384]{1,0:T(8,128)(2,1)S(1)}, bf16[256,384]{1,0:T(8,128)(2,1)S(1)}, u32[]{:S(2)}, u32[]{:S(2)}) collective-permute-start(bf16[256,384]{1,0:T(8,128)(2,1)S(1)} %fusion.3), channel_id=1, source_target_pairs={{0,8},{8,0},{1,9},{9,1},{2,10},{10,2},{3,11},{11,3},{4,12},{12,4},... | collective-permute-start | bytes 589832 | tf_op jit(solution)/shard_map/ppermute | solution.py:381
  39.7 15.1 %collective-permute-start.6 = (bf16[256,384]{1,0:T(8,128)(2,1)S(1)}, bf16[256,384]{1,0:T(8,128)(2,1)S(1)}, u32[]{:S(2)}, u32[]{:S(2)}) collective-permute-start(bf16[256,384]{1,0:T(8,128)(2,1)S(1)} %fusion.2), channel_id=1, source_target_pairs={{0,8},{8,0},{1,9},{9,1},{2,10},{10,2},{3,11},{11,3},{4,12},{12,4},... | collective-permute-start | bytes 589832 | tf_op jit(solution)/shard_map/ppermute | solution.py:381
  50.0 13.1 %collective-permute-start.9 = (bf16[128,384]{1,0:T(8,128)(2,1)S(1)}, bf16[128,384]{1,0:T(8,128)(2,1)S(1)}, u32[]{:S(2)}, u32[]{:S(2)}) collective-permute-start(bf16[128,384]{1,0:T(8,128)(2,1)S(1)} %fusion.5.refs_0_), channel_id=1, source_target_pairs={{0,8},{8,0},{1,9},{9,1},{2,10},{10,2},{3,11},{11,3},{4,12},{12,4},... | collective-permute-start | bytes 294920 | tf_op jit(solution)/shard_map/ppermute | solution.py:381
  51.9 7.7 %collective-permute-start.7 = (bf16[128,384]{1,0:T(8,128)(2,1)S(1)}, bf16[128,384]{1,0:T(8,128)(2,1)S(1)}, u32[]{:S(2)}, u32[]{:S(2)}) collective-permute-start(bf16[128,384]{1,0:T(8,128)(2,1)S(1)} %fusion.5.refs_0_), channel_id=1, source_target_pairs={{0,4},{2,6},{4,0},{6,2},{1,5},{3,7},{5,1},{7,3},{8,12},{10,14},{12... | collective-permute-start | bytes 294920 | tf_op jit(solution)/shard_map/ppermute | solution.py:385
  60.0 11.4 %collective-permute-start.15 = (bf16[128,384]{1,0:T(8,128)(2,1)S(1)}, bf16[128,384]{1,0:T(8,128)(2,1)S(1)}, u32[]{:S(2)}, u32[]{:S(2)}) collective-permute-start(bf16[128,384]{1,0:T(8,128)(2,1)S(1)} %fusion.5.refs_0_), channel_id=1, source_target_pairs={{0,1},{1,0},{2,3},{3,2},{4,5},{5,4},{6,7},{7,6},{8,9},{9,8},{10,11... | collective-permute-start | bytes 294920 | tf_op jit(solution)/shard_map/ppermute | solution.py:381
  60.0 10.8 %collective-permute-start.13 = (bf16[128,384]{1,0:T(8,128)(2,1)S(1)}, bf16[128,384]{1,0:T(8,128)(2,1)S(1)}, u32[]{:S(2)}, u32[]{:S(2)}) collective-permute-start(bf16[128,384]{1,0:T(8,128)(2,1)S(1)} %fusion.4.refs_1_), channel_id=1, source_target_pairs={{0,8},{8,0},{1,9},{9,1},{2,10},{10,2},{3,11},{11,3},{4,12},{12,4},... | collective-permute-start | bytes 294920 | tf_op jit(solution)/shard_map/ppermute | solution.py:381
  63.2 7.7 %collective-permute-start.11 = (bf16[128,384]{1,0:T(8,128)(2,1)S(1)}, bf16[128,384]{1,0:T(8,128)(2,1)S(1)}, u32[]{:S(2)}, u32[]{:S(2)}) collective-permute-start(bf16[128,384]{1,0:T(8,128)(2,1)S(1)} %fusion.4.refs_1_), channel_id=1, source_target_pairs={{0,4},{2,6},{4,0},{6,2},{1,5},{3,7},{5,1},{7,3},{8,12},{10,14},{12... | collective-permute-start | bytes 294920 | tf_op jit(solution)/shard_map/ppermute | solution.py:385
  64.3 7.6 %collective-permute-start.17 = (bf16[128,384]{1,0:T(8,128)(2,1)S(1)}, bf16[128,384]{1,0:T(8,128)(2,1)S(1)}, u32[]{:S(2)}, u32[]{:S(2)}) collective-permute-start(bf16[128,384]{1,0:T(8,128)(2,1)S(1)} %collective-permute-done.9.refs_2_), channel_id=1, source_target_pairs={{0,1},{1,0},{2,3},{3,2},{4,5},{5,4},{6,7},{7,6},{8,9},{9,8},{10,11... | collective-permute-start | bytes 294920 | tf_op jit(solution)/shard_map/ppermute | solution.py:381
  66.4 6.0 %collective-permute-start.16 = (bf16[128,384]{1,0:T(8,128)(2,1)S(1)}, bf16[128,384]{1,0:T(8,128)(2,1)S(1)}, u32[]{:S(2)}, u32[]{:S(2)}) collective-permute-start(bf16[128,384]{1,0:T(8,128)(2,1)S(1)} %fusion.4.refs_1_), channel_id=1, source_target_pairs={{0,1},{1,0},{2,3},{3,2},{4,5},{5,4},{6,7},{7,6},{8,9},{9,8},{10,11... | collective-permute-start | bytes 294920 | tf_op jit(solution)/shard_map/ppermute | solution.py:381
  71.4 9.1 %collective-permute-start.19 = (bf16[128,384]{1,0:T(8,128)(2,1)S(1)}, bf16[128,384]{1,0:T(8,128)(2,1)S(1)}, u32[]{:S(2)}, u32[]{:S(2)}) collective-permute-start(bf16[128,384]{1,0:T(8,128)(2,1)S(1)} %collective-permute-done.11), channel_id=1, source_target_pairs={{0,2},{2,0},{4,6},{6,4},{1,3},{3,1},{5,7},{7,5},{8,10},{10,8},{12,... | collective-permute-start | bytes 294920 | tf_op jit(solution)/shard_map/ppermute | solution.py:385
  71.8 18.5 %collective-permute-start.20 = (bf16[128,384]{1,0:T(8,128)(2,1)S(1)}, bf16[128,384]{1,0:T(8,128)(2,1)S(1)}, u32[]{:S(2)}, u32[]{:S(2)}) collective-permute-start(bf16[128,384]{1,0:T(8,128)(2,1)S(1)} %broadcast_select_fusion.1), channel_id=1, source_target_pairs={{0,8},{8,0},{1,9},{9,1},{2,10},{10,2},{3,11},{11,3},{4,12},{12,4},... | collective-permute-start | bytes 294920 | tf_op jit(solution)/shard_map/ppermute | solution.py:381
  72.4 17.9 %collective-permute-start.21 = (bf16[128,384]{1,0:T(8,128)(2,1)S(1)}, bf16[128,384]{1,0:T(8,128)(2,1)S(1)}, u32[]{:S(2)}, u32[]{:S(2)}) collective-permute-start(bf16[128,384]{1,0:T(8,128)(2,1)S(1)} %collective-permute-done.10), channel_id=1, source_target_pairs={{0,8},{2,10},{12,4},{14,6},{1,9},{3,11},{13,5},{15,7},{16,24},{18,... | collective-permute-start | bytes 294920 | tf_op jit(solution)/shard_map/ppermute | solution.py:438
  75.8 20.5 %collective-permute-start.23 = (bf16[128,384]{1,0:T(8,128)(2,1)S(1)}, bf16[128,384]{1,0:T(8,128)(2,1)S(1)}, u32[]{:S(2)}, u32[]{:S(2)}) collective-permute-start(bf16[128,384]{1,0:T(8,128)(2,1)S(1)} %broadcast_select_fusion), channel_id=1, source_target_pairs={{0,8},{8,0},{1,9},{9,1},{2,10},{10,2},{3,11},{11,3},{4,12},{12,4},... | collective-permute-start | bytes 294920 | tf_op jit(solution)/shard_map/ppermute | solution.py:381
  80.5 15.8 %collective-permute-start.24 = (bf16[128,384]{1,0:T(8,128)(2,1)S(1)}, bf16[128,384]{1,0:T(8,128)(2,1)S(1)}, u32[]{:S(2)}, u32[]{:S(2)}) collective-permute-start(bf16[128,384]{1,0:T(8,128)(2,1)S(1)} %collective-permute-done.19), channel_id=1, source_target_pairs={{0,8},{2,10},{12,4},{14,6},{1,9},{3,11},{13,5},{15,7},{16,24},{18,... | collective-permute-start | bytes 294920 | tf_op jit(solution)/shard_map/ppermute | solution.py:438
  90.4 10.5 %collective-permute-start.25 = (bf16[128,384]{1,0:T(8,128)(2,1)S(1)}, bf16[128,384]{1,0:T(8,128)(2,1)S(1)}, u32[]{:S(2)}, u32[]{:S(2)}) collective-permute-start(bf16[128,384]{1,0:T(8,128)(2,1)S(1)} %get-tuple-element.124), channel_id=1, source_target_pairs={{0,1},{1,0},{2,3},{3,2},{4,5},{5,4},{6,7},{7,6},{8,9},{9,8},{10,11... | collective-permute-start | bytes 294920 | tf_op jit(solution)/shard_map/ppermute | solution.py:381
  96.3 9.2 %collective-permute-start.26 = (bf16[128,384]{1,0:T(8,128)(2,1)S(1)}, bf16[128,384]{1,0:T(8,128)(2,1)S(1)}, u32[]{:S(2)}, u32[]{:S(2)}) collective-permute-start(bf16[128,384]{1,0:T(8,128)(2,1)S(1)} %get-tuple-element.122), channel_id=1, source_target_pairs={{0,1},{1,0},{2,3},{3,2},{4,5},{5,4},{6,7},{7,6},{8,9},{9,8},{10,11... | collective-permute-start | bytes 294920 | tf_op jit(solution)/shard_map/ppermute | solution.py:381
  96.5 13.5 %collective-permute-start.27 = (bf16[32,1536]{1,0:T(8,128)(2,1)S(1)}, bf16[32,1536]{1,0:T(8,128)(2,1)S(1)}, u32[]{:S(2)}, u32[]{:S(2)}) collective-permute-start(bf16[32,1536]{1,0:T(8,128)(2,1)S(1)} %get-tuple-element.114), channel_id=1, source_target_pairs={{0,2},{2,0},{4,6},{6,4},{1,3},{3,1},{5,7},{7,5},{8,10},{10,8},{12,... | collective-permute-start | bytes 294920 | tf_op jit(solution)/shard_map/ppermute | solution.py:385
  98.2 11.9 %collective-permute-start.28 = (bf16[32,1536]{1,0:T(8,128)(2,1)S(1)}, bf16[32,1536]{1,0:T(8,128)(2,1)S(1)}, u32[]{:S(2)}, u32[]{:S(2)}) collective-permute-start(bf16[32,1536]{1,0:T(8,128)(2,1)S(1)} %get-tuple-element.115), channel_id=1, source_target_pairs={{0,4},{2,6},{4,0},{6,2},{1,5},{3,7},{5,1},{7,3},{8,12},{10,14},{12... | collective-permute-start | bytes 294920 | tf_op jit(solution)/shard_map/ppermute | solution.py:385
  98.2 11.9 %collective-permute-start.29 = (bf16[32,1536]{1,0:T(8,128)(2,1)S(1)}, bf16[32,1536]{1,0:T(8,128)(2,1)S(1)}, u32[]{:S(2)}, u32[]{:S(2)}) collective-permute-start(bf16[32,1536]{1,0:T(8,128)(2,1)S(1)} %get-tuple-element.116), channel_id=1, source_target_pairs={{0,6},{2,4},{4,2},{6,0},{1,7},{3,5},{5,3},{7,1},{8,14},{10,12},{12... | collective-permute-start | bytes 294920 | tf_op jit(solution)/shard_map/ppermute | solution.py:385
  (15 other events, 56.5 us)

commit v4 on v3

v4 whole, which is shorter than its diff:
```python
import functools

import jax
import jax.numpy as jnp
from jax import lax
from jax.experimental import pallas as pl
from jax.experimental.pallas import tpu as pltpu
from jax.sharding import PartitionSpec as P

F32 = jnp.float32
BF16 = jnp.bfloat16
MIB = 1 << 20


def spread(value, axis, source):
    kept = jnp.where(lax.axis_index(axis) == source, value, 0).astype(value.dtype)
    return lax.psum(kept, axis)


def activate(preacts):
    return (jax.nn.silu(preacts[:, 0, :]) * preacts[:, 1, :]).astype(jnp.bfloat16)


def on_any_device(tokens, routes, route_weight, pad_mask, gate_up, down):
    group_rows = tokens.shape[0]
    slot_count = group_rows // 4
    names_zero = routes == 0
    routed = jnp.any(names_zero, axis=1)
    live_rows = routed & (pad_mask == 1)
    factor = jnp.sum(
        jnp.where(names_zero, route_weight, jnp.float32(0.0)), axis=1
    ) * live_rows.astype(jnp.float32)
    position = jnp.cumsum(routed.astype(jnp.int32)) - 1
    slot_ids = lax.broadcasted_iota(jnp.int32, (slot_count, group_rows), 0)
    placing = ((position[None, :] == slot_ids) & routed[None, :]).astype(jnp.bfloat16)
    masked = tokens * live_rows.astype(jnp.bfloat16)[:, None]
    packed = jnp.dot(placing, masked, preferred_element_type=jnp.float32).astype(jnp.bfloat16)
    gathered = lax.all_gather(packed, "col", axis=0, tiled=True)
    anchor = lax.axis_index(("expert", "row"))
    preacts = lax.psum(
        jnp.einsum("rd,dgf->rgf", gathered, gate_up, preferred_element_type=jnp.float32),
        ("expert", "row"),
    )
    hidden = activate(preacts)
    mirrored = spread(hidden, "col", anchor)
    gram_block = lax.dot_general(
        mirrored, hidden, (((0,), (0,)), ((), ())), preferred_element_type=jnp.float32
    )
    gram_block = gram_block * jnp.float32(2.0 / hidden.shape[0])
    returned = lax.psum_scatter(
        jnp.dot(hidden, down, preferred_element_type=jnp.float32),
        "col",
        scatter_dimension=0,
        tiled=True,
    )
    unpacked = lax.dot_general(
        placing.astype(jnp.float32),
        returned,
        (((0,), (0,)), ((), ())),
        precision=lax.Precision.HIGHEST,
        preferred_element_type=jnp.float32,
    )
    expert_out = (unpacked * factor[:, None]).astype(jnp.bfloat16)
    return (expert_out, gram_block)


def cost(flops, moved):
    return pl.CostEstimate(flops=int(flops), bytes_accessed=int(moved), transcendentals=0)


def params(mib):
    return pltpu.CompilerParams(vmem_limit_bytes=mib * MIB)


VMEM = pl.BlockSpec(memory_space=pltpu.VMEM)
HBM = pl.BlockSpec(memory_space=pltpu.HBM)
SMEM = pl.BlockSpec(memory_space=pltpu.SMEM)
ANY = pl.BlockSpec(memory_space=pl.ANY)


def in_vmem(value):
    return pltpu.with_memory_space_constraint(value, pltpu.VMEM)


def in_hbm(value):
    return pltpu.with_memory_space_constraint(value, pltpu.HBM)


def quarter_of(expert_flip, row_flip):
    return (lax.axis_index("expert") ^ expert_flip) * 2 + (lax.axis_index("row") ^ row_flip)


def tie(*values):
    return lax.optimization_barrier(values)


def pack_kernel(
    tokens_ref, routes_ref, pad_ref, weight_ref, packed_ref, placing_ref, factor_ref,
    tokens_held, routes_held, pad_held, weight_held, sems,
):
    pairs = (
        (routes_ref, routes_held),
        (pad_ref, pad_held),
        (weight_ref, weight_held),
        (tokens_ref, tokens_held),
    )
    copies = [pltpu.make_async_copy(a, b, sems.at[i]) for i, (a, b) in enumerate(pairs)]
    for copy in copies:
        copy.start()
    slots, rows = placing_ref.shape
    before = lax.broadcasted_iota(jnp.int32, (rows, rows), 0)
    upto = lax.broadcasted_iota(jnp.int32, (rows, rows), 1)
    tri = jnp.where(before <= upto, 1.0, 0.0).astype(BF16)
    slot_ids = lax.broadcasted_iota(jnp.int32, (slots, rows), 0).astype(F32)
    for copy in copies[:3]:
        copy.wait()
    routes_t = routes_held[...]
    routed = (routes_t[0:1, :] == 0) | (routes_t[1:2, :] == 0)
    live = jnp.where(routed & (pad_held[...] == 1), 1.0, 0.0)
    routed_rows = jnp.broadcast_to(jnp.where(routed, 1.0, 0.0), (8, rows)).astype(BF16)
    position = jnp.dot(routed_rows, tri, preferred_element_type=F32)[0:1, :] - 1.0
    placing = jnp.where(position == slot_ids, jnp.broadcast_to(live, (slots, rows)), 0.0)
    placing_ref[...] = placing.astype(BF16)
    weight = jnp.sum(jnp.where(routes_t == 0, weight_held[...], 0.0), axis=0, keepdims=True)
    factor = jnp.sum(placing * weight, axis=1, keepdims=True)
    factor_ref[...] = jnp.broadcast_to(factor, factor_ref.shape)
    copies[3].wait()
    packed_ref[...] = jnp.dot(
        placing.astype(BF16), tokens_held[...], preferred_element_type=F32
    ).astype(BF16)


def pack(tokens, routes_t, pad, weight_t):
    rows, depth = tokens.shape
    slots = rows // 4
    operands = (tokens, routes_t, pad, weight_t)
    return pl.pallas_call(
        pack_kernel,
        in_specs=[HBM] * 4,
        out_specs=[VMEM] * 3,
        out_shape=[
            pltpu.VMEM((slots, depth), BF16),
            pltpu.VMEM((slots, rows), BF16),
            pltpu.VMEM((slots, 128), F32),
        ],
        scratch_shapes=[pltpu.VMEM(x.shape, x.dtype) for x in operands]
        + [pltpu.SemaphoreType.DMA((4,))],
        compiler_params=params(3),
        name="pack",
    )(*(in_hbm(x) for x in operands))


def unpack_kernel(after_ref, placing_ref, factor_ref, own_ref, r1_ref, r2_ref, r3_ref, out_ref):
    del after_ref
    total = own_ref[...] + r1_ref[...].astype(F32) + r2_ref[...].astype(F32) + r3_ref[...].astype(F32)
    scaled = (total * factor_ref[:, 0:1]).astype(BF16)
    out_ref[...] = lax.dot_general(
        placing_ref[...], scaled, (((0,), (0,)), ((), ())), preferred_element_type=F32
    ).astype(BF16)


def unpack(done, placing, factor, own, returned):
    slots, rows = placing.shape
    return pl.pallas_call(
        unpack_kernel,
        in_specs=[ANY] + [VMEM] * 6,
        out_specs=VMEM,
        out_shape=jax.ShapeDtypeStruct((rows, own.shape[1]), BF16),
        compiler_params=params(4),
        name="unpack",
    )(done, placing, factor, own, *returned)


def regroup_kernel(after_ref, weights_ref, out_ref, sems):
    del after_ref
    copies = [
        pltpu.make_async_copy(weights_ref.at[:, t], out_ref.at[t], sems.at[t])
        for t in range(out_ref.shape[0])
    ]
    for copy in copies:
        copy.start()
    for copy in copies:
        copy.wait()


def regroup(behind, weights):
    depth, tiles, two, lanes = weights.shape
    grouped = pl.pallas_call(
        regroup_kernel,
        in_specs=[ANY, HBM],
        out_specs=VMEM,
        out_shape=pltpu.VMEM((tiles, depth, two, lanes), BF16),
        scratch_shapes=[pltpu.SemaphoreType.DMA((tiles,))],
        compiler_params=params(4),
        cost_estimate=cost(0, 4 * weights.size),
        name="regroup",
    )(behind, in_hbm(weights))
    return grouped.reshape(tiles, depth * two, lanes)


def fetch_kernel(after_ref, down_ref, out_ref, done_ref, sems):
    del after_ref
    parts = sems.shape[0]
    size = down_ref.shape[0] // parts
    copies = [
        pltpu.make_async_copy(
            down_ref.at[pl.ds(size * i, size)], out_ref.at[pl.ds(size * i, size)], sems.at[i]
        )
        for i in range(parts)
    ]
    for copy in copies:
        copy.start()
    done_ref[...] = jnp.zeros_like(done_ref)
    for copy in copies:
        copy.wait()


def fetch(behind, down):
    return pl.pallas_call(
        fetch_kernel,
        in_specs=[ANY, HBM],
        out_specs=[VMEM, VMEM],
        out_shape=[pltpu.VMEM(down.shape, BF16), pltpu.VMEM((8, 128), F32)],
        scratch_shapes=[pltpu.SemaphoreType.DMA((4,))],
        compiler_params=params(4),
        cost_estimate=cost(0, 4 * down.size),
        name="fetch_down",
    )(behind, in_hbm(down))


def widen_tokens(x_refs, wide_ref):
    slots, depth = x_refs[0].shape
    rows = 4 * slots
    here = lax.axis_index("col")
    cut = 256
    into = lax.broadcasted_iota(jnp.int32, (cut, 4 * cut), 1)
    out_of = lax.broadcasted_iota(jnp.int32, (cut, 4 * cut), 0)
    half = jnp.where(into < 2 * cut, 0, 1)
    widen = jnp.where(into - 2 * cut * half == 2 * out_of + half, 1.0, 0.0).astype(BF16)
    for slot, x_ref in enumerate(x_refs):
        stacked = jnp.concatenate(
            [x_ref[:, cut * k : cut * (k + 1)] for k in range(depth // cut)], axis=0
        )
        spaced = jnp.dot(stacked, widen, preferred_element_type=F32).astype(BF16)
        for h in range(2):
            at = pl.multiple_of(h * rows + (here ^ slot) * slots, slots)
            for k in range(depth // cut):
                wide_ref[pl.ds(at, slots), 2 * cut * k : 2 * cut * (k + 1)] = spaced[
                    slots * k : slots * (k + 1), 2 * cut * h : 2 * cut * (h + 1)
                ]


def preact_kernel(first, row_flip, chunk, chunks, *refs):
    if first:
        x0, x1, x2, x3, w_ref, out_ref, wide_ref = refs
        widen_tokens((x0, x1, x2, x3), wide_ref)
    else:
        wide_ref, w_ref, out_ref = refs
    tiles, _, lanes = w_ref.shape
    per = tiles // 4
    take = per // chunks
    at = []
    for i in range(2):
        quarter = quarter_of(1 - i, row_flip)
        at += [quarter * per + chunk * take + j for j in range(take)]
    for j in range(take):
        w = jnp.concatenate([w_ref[at[2 * j]], w_ref[at[2 * j + 1]]], axis=1)
        out_ref[:, 2 * lanes * j : 2 * lanes * (j + 1)] = jnp.dot(
            wide_ref[...], w, preferred_element_type=F32
        )


def preacts_of(lefts, weights, row_flip, chunk, chunks):
    tiles, depth2, lanes = weights.shape
    first = len(lefts) > 1
    rows = 4 * lefts[0].shape[0] if first else lefts[0].shape[0] // 2
    units = tiles // 4 // chunks * lanes
    out_shape = [jax.ShapeDtypeStruct((2 * rows, 2 * units), F32)]
    if first:
        out_shape.append(pltpu.VMEM((2 * rows, depth2), BF16))
    return pl.pallas_call(
        functools.partial(preact_kernel, first, row_flip, chunk, chunks),
        in_specs=[VMEM] * (len(lefts) + 1),
        out_specs=[VMEM] * len(out_shape),
        out_shape=out_shape,
        compiler_params=params(4),
        cost_estimate=cost(8 * rows * depth2 * units, 0),
        name="preacts_" + ("sent" if row_flip else "kept"),
    )(*lefts, in_vmem(weights))


def leave_kernel(kept_ref, got_ref, leaves_ref, stays_ref):
    units = stays_ref.shape[1]
    leaves_ref[...] = (kept_ref[:, :units] + got_ref[:, :units]).astype(BF16)
    stays_ref[...] = kept_ref[:, units:] + got_ref[:, units:]


def leave(kept, got):
    rows, units = kept.shape[0], kept.shape[1] // 2
    return pl.pallas_call(
        leave_kernel,
        in_specs=[VMEM] * 2,
        out_specs=[VMEM] * 2,
        out_shape=[
            jax.ShapeDtypeStruct((rows, units), BF16),
            jax.ShapeDtypeStruct((rows, units), F32),
        ],
        compiler_params=params(2),
        name="leave",
    )(kept, got)


def act_kernel(tick_ref, stays_ref, got_ref, *refs):
    del tick_ref
    out_ref = refs[-1]
    rows = out_ref.shape[0]
    done = out_ref.shape[1] - stays_ref.shape[1]
    if done:
        out_ref[:, :done] = refs[0][...]
    gate = stays_ref[:rows, :] + got_ref[:rows, :].astype(F32)
    up = stays_ref[rows:, :] + got_ref[rows:, :].astype(F32)
    out_ref[:, done:] = (jax.nn.silu(gate) * up).astype(BF16)


def act(tick, stays, got, *before):
    rows, units = stays.shape
    units += sum(x.shape[1] for x in before)
    return pl.pallas_call(
        act_kernel,
        in_specs=[ANY] + [VMEM] * (2 + len(before)),
        out_specs=VMEM,
        out_shape=jax.ShapeDtypeStruct((rows // 2, units), BF16),
        compiler_params=params(2),
        name="act",
    )(tick, stays, got, *before)


def is_near():
    return (lax.axis_index("col") // 2) == lax.axis_index("expert")


def is_odd():
    return (lax.axis_index("col") % 2) != lax.axis_index("row")


def choose_kernel(near_ref, far_ref, out_ref):
    @pl.when(is_near())
    def _():
        out_ref[...] = near_ref[...]

    @pl.when(jnp.logical_not(is_near()))
    def _():
        out_ref[...] = far_ref[...]


def choose(if_near, if_far):
    return pl.pallas_call(
        choose_kernel,
        in_specs=[VMEM] * 2,
        out_specs=VMEM,
        out_shape=jax.ShapeDtypeStruct(if_near.shape, if_near.dtype),
        compiler_params=params(2),
        name="choose",
    )(if_near, if_far)


def pick_kernel(n0, n1, f2, f3, mine_ref, other_ref):
    for near, pair in ((True, (n0, n1)), (False, (f2, f3))):
        for odd in (False, True):

            @pl.when((is_near() == near) & (is_odd() == odd))
            def _():
                mine_ref[...] = pair[int(odd)][...]
                other_ref[...] = pair[1 - int(odd)][...]


def pick(*slots):
    same = jax.ShapeDtypeStruct(slots[0].shape, slots[0].dtype)
    return pl.pallas_call(
        pick_kernel,
        in_specs=[VMEM] * 4,
        out_specs=[VMEM] * 2,
        out_shape=[same, same],
        compiler_params=params(2),
        name="pick",
    )(*slots)


def project_kernel(
    tick_ref, h0, h1, h2, h3, down_ref, own_ref, s1_ref, s2_ref, s3_ref, wide_ref, done_ref, total_ref
):
    del tick_ref
    units = h0.shape[1]
    for k, h_ref in enumerate((h0, h1, h2, h3)):
        at = pl.multiple_of(quarter_of(k % 2, k // 2) * units, units)
        wide_ref[:, pl.ds(at, units)] = h_ref[...]
    done_ref[...] = jnp.zeros_like(done_ref)
    slots, width = own_ref.shape
    cut = 512
    for n in range(width // cut):
        total_ref[:, cut * n : cut * (n + 1)] = jnp.dot(
            wide_ref[...], down_ref[:, cut * n : cut * (n + 1)], preferred_element_type=F32
        )
    here = lax.axis_index("col")
    for slot, out_ref in enumerate((own_ref, s1_ref, s2_ref, s3_ref)):
        at = pl.multiple_of((here ^ slot) * slots, slots)
        out_ref[...] = total_ref[pl.ds(at, slots), :].astype(out_ref.dtype)


def project(tick, quarters, down):
    rows, units = quarters[0].shape
    width = down.shape[1]
    slots = rows // 4
    return pl.pallas_call(
        project_kernel,
        in_specs=[ANY] + [VMEM] * 5,
        out_specs=[VMEM] * 6,
        out_shape=[jax.ShapeDtypeStruct((slots, width), F32)]
        + [jax.ShapeDtypeStruct((slots, width), BF16)] * 3
        + [pltpu.VMEM((rows, 4 * units), BF16), pltpu.VMEM((8, 128), F32)],
        scratch_shapes=[pltpu.VMEM((rows, width), F32)],
        compiler_params=params(4),
        cost_estimate=cost(8 * rows * units * width, 0),
        name="project",
    )(tick, *quarters, in_vmem(down))


def gram_kernel(scale, flips, *refs):
    count = len(flips)
    pieces = refs[1 : 1 + count]
    wide_ref = refs[1 + count]
    out_ref, done_ref, ring_ref, sems = refs[-4:]
    done_ref[...] = jnp.zeros_like(done_ref)
    units = pieces[0].shape[1]
    depth, _, cut = ring_ref.shape
    copies = []
    for (expert_flip, row_flip), a_ref in zip(flips, pieces):
        at = pl.multiple_of(quarter_of(expert_flip, row_flip) * units, units)
        left = a_ref[...].T
        for n in range(4 * units // cut):
            spot = len(copies) % depth
            if len(copies) >= depth:
                copies[-depth].wait()
            ring_ref[spot] = scale * jnp.dot(
                left, wide_ref[:, cut * n : cut * (n + 1)], preferred_element_type=F32
            )
            copy = pltpu.make_async_copy(
                ring_ref.at[spot], out_ref.at[pl.ds(at, units), pl.ds(cut * n, cut)], sems.at[spot]
            )
            copy.start()
            copies.append(copy)
    for copy in copies[-depth:]:
        copy.wait()


def gram_piece(tick, pieces, flips, wide, gram=None):
    rows, units = pieces[0].shape
    cut, depth = 512, 4
    operands = [tick, *pieces, in_vmem(wide)]
    in_specs = [ANY] + [VMEM] * (len(pieces) + 1)
    aliases = {}
    if gram is not None:
        aliases = {len(operands): 0}
        operands.append(gram)
        in_specs.append(HBM)
    return pl.pallas_call(
        functools.partial(gram_kernel, 2.0 / rows, flips),
        in_specs=in_specs,
        out_specs=[HBM, VMEM],
        out_shape=[
            jax.ShapeDtypeStruct((4 * units, 4 * units), F32),
            pltpu.VMEM((8, 128), F32),
        ],
        input_output_aliases=aliases,
        scratch_shapes=[
            pltpu.VMEM((depth, units, cut), F32),
            pltpu.SemaphoreType.DMA((depth,)),
        ],
        compiler_params=params(10),
        cost_estimate=cost(8 * rows * units * units * len(pieces), 16 * units * units * len(pieces)),
        name="gram",
    )(*operands)


def swap(value, axis):
    return lax.ppermute(value, axis, [(0, 1), (1, 0)])


def across(value, slot):
    return lax.ppermute(value, "col", [(i, i ^ slot) for i in range(4)])


def on_device(tokens, routes, route_weight, pad_mask, gate_up, down):
    depth = tokens.shape[1]
    units = gate_up.shape[2]
    lanes = 128
    chunks = 2
    weights = gate_up.reshape(depth, 2, units // lanes, lanes).transpose(0, 2, 1, 3)

    packed, placing, factor = pack(tokens, routes.T, pad_mask[None, :], route_weight.T)
    lefts = [packed] + [across(packed, slot) for slot in (1, 2, 3)]
    grouped = regroup(packed, weights)

    first_sent, wide = preacts_of(lefts, grouped, 1, 0, chunks)
    (last_sent,) = preacts_of([wide], grouped, 1, 1, chunks)
    got = [swap(first_sent, "row"), swap(last_sent, "row")]
    stays, got_x = [], []
    for h in range(chunks):
        (kept,) = preacts_of([wide], grouped, 0, h, chunks)
        leaves, stay = leave(kept, got[h])
        wide, leaves = tie(wide, leaves)
        stays.append(stay)
        got_x.append(swap(leaves, "expert"))
    down_held, tick = fetch(wide, down)
    tick, got_x[0] = tie(tick, got_x[0])
    hidden = act(tick, stays[0], got_x[0])
    tick, got_x[1], hidden = tie(tick, got_x[1], hidden)
    hidden = act(tick, stays[1], got_x[1], hidden)

    z2 = across(hidden, 2)
    z1 = across(hidden, 1)
    hidden_x = swap(hidden, "expert")
    c_near = swap(hidden, "row")
    tick, z2, z1, hidden_x = tie(tick, z2, z1, hidden_x)

    tick, onward, leaves, sent_x = tie(tick, z2, choose(z2, z1), hidden_x)
    z3 = across(onward, 1)
    x2 = swap(leaves, "expert")
    c_far = swap(sent_x, "row")
    own, s1, s2, s3, hidden_c, tick = project(
        tick, [hidden, hidden_x, c_near, c_far], down_held
    )
    tick, z3 = tie(tick, z3)
    x3 = lax.ppermute(
        z3,
        ("expert", "col"),
        [(ee * 4 + cc, (1 - ee) * 4 + cc) for ee in range(2) for cc in range(4) if cc // 2 == ee],
    )
    mine, passed = pick(hidden, z1, z2, z3)
    mine_near = swap(passed, "row")
    tick, s1, s2, s3 = tie(tick, s1, s2, s3)
    returned = [across(value, slot) for slot, value in ((1, s1), (2, s2), (3, s3))]
    gram, tick = gram_piece(tick, [mine], [(0, 0)], hidden_c)
    tick, x2, x3 = tie(tick, x2, x3)
    mine_x, passed = pick(hidden_x, x2, x2, x3)
    mine_far = swap(passed, "row")
    tick, mine_near = tie(tick, mine_near)
    gram, tick = gram_piece(tick, [mine_near], [(0, 1)], hidden_c, gram)
    tick, mine_far = tie(tick, mine_far)
    gram, tick = gram_piece(tick, [mine_x, mine_far], [(1, 0), (1, 1)], hidden_c, gram)
    return (unpack(tick, placing, factor, own, returned), gram)


def solution(mesh):
    in_specs = (
        P(("parts", "col"), ("expert", "row")),
        P(("parts", "col"), None),
        P(("parts", "col"), None),
        P(("parts", "col")),
        P(("expert", "row"), None, "col"),
        P("col", ("expert", "row")),
    )
    out_specs = (P(("parts", "col"), ("expert", "row")), P(("parts", "expert", "row"), "col"))
    small = mesh.shape["expert"] == 2 and mesh.shape["row"] == 2 and mesh.shape["col"] == 4
    return jax.shard_map(
        on_device if small else on_any_device,
        mesh=mesh,
        in_specs=in_specs,
        out_specs=out_specs,
        check_vma=False,
    )
```

time: 112 us -> 76.2 us (0.68)
  local copies, waits for them, and re-layouts: 19.3 us -> 0 us
  starting transfers between devices: 33 us -> 25.1 us
  other arithmetic: 5.45 us -> 0 us
  Pallas kernels: 41 us -> 36.6 us
  waiting for transfers between devices: 11.3 us -> 13.4 us
    unnamed x18 -> x0, local copies, waits for them, and re-layouts: 19.3 us -> none
    ppermute x2 -> x1, starting transfers between devices: 7.47 us -> 3.42 us  [on_device(): lax.ppermute(z3, ('expert', 'col'), [(ee * 4 + cc, (1 - ee) * 4 + cc) for...]
    convert_element_type x4 -> x0, other arithmetic: 2.97 us -> none  [the longest x2 2.84 us: on_device(): leaves = (kept[:, :width] + got[h][:, :width]).astype(BF16)]
    ppermute x16 -> x10, waiting for transfers between devices: 0.72 us -> 3.58 us  [swap(): return lax.ppermute(value, axis, [(0, 1), (1, 0)])]
    ppermute x12 -> x9, starting transfers between devices: 18.1 us -> 15.2 us  [across(): return lax.ppermute(value, 'col', [(i, i ^ slot) for i in range(4)])]
    pallas_call x6 -> x12, Pallas kernels: 20.8 us -> 18.5 us  [the longest x3 15 us: gram_piece(): pl.pallas_call(functools.partial(gram_kernel, 2.0 / rows, flips), in_spec...]
    pallas_call x4, Pallas kernels: 8.4 us -> 6.26 us  [preacts_of(): pl.pallas_call(functools.partial(preact_kernel, first, row_flip, chunk, c...]
    add x2 -> x0, other arithmetic: 2.12 us -> none  [on_device(): preacts = sums[h] + arrived.astype(F32)]
  transfers between devices with their start and end apart: 30 -> 20, of which waited for: 5 -> 6; matrix products, arithmetic and copies ran while one was open for 5% -> 0% of each run, Pallas kernels for 33% -> 42%
where the time goes in v4:
time: 76.2 us; the launch traced here: 76 us
  Pallas kernels  36.6 us (48%)
  starting transfers between devices  25.1 us (33%)
  waiting for transfers between devices  13.4 us (18%)
  between operations  0.88 us (1%)
    ppermute x9, starting transfers between devices, across(): return lax.ppermute(value, 'col', [(i, i ^ slot) for i in range(4)])  15.2 us
    pallas_call x3, Pallas kernels, gram_piece(): pl.pallas_call(functools.partial(gram_kernel, 2.0 / rows, flips), in_spec...  15 us
    ppermute x9, waiting for transfers between devices, across(): return lax.ppermute(value, 'col', [(i, i ^ slot) for i in range(4)])  9.85 us
    pallas_call x1, Pallas kernels, regroup(): pl.pallas_call(regroup_kernel, in_specs=[ANY, HBM], out_specs=VMEM, out_s...  6.97 us
    ppermute x10, starting transfers between devices, swap(): return lax.ppermute(value, axis, [(0, 1), (1, 0)])  6.47 us
    pallas_call x4, Pallas kernels, preacts_of(): pl.pallas_call(functools.partial(preact_kernel, first, row_flip, chunk, c...  6.26 us
    pallas_call x1, Pallas kernels, fetch(): pl.pallas_call(fetch_kernel, in_specs=[ANY, HBM], out_specs=[VMEM, VMEM],...  3.8 us
    ppermute x10, waiting for transfers between devices, swap(): return lax.ppermute(value, axis, [(0, 1), (1, 0)])  3.58 us
  transfers between devices with their start and end apart: 20, of which 6 were waited for; matrix products, arithmetic and copies ran while one was open for 0% of the time, Pallas kernels for 42%

profile of v4, /device:TPU:0, one launch (start us, length us, event | category | flops | bytes accessed | tf_op | source)
XLA Modules:
  0.0 76.0 jit_solution(16427326947467164834)
XLA Ops:
  0.6 1.3 %pack.1 = (bf16[32,1536]{1,0:T(8,128)(2,1)S(1)}, bf16[32,128]{1,0:T(8,128)(2,1)S(1)}, f32[32,128]{1,0:T(8,128)S(1)}) custom-call(bf16[128,1536]{1,0:T(8,128)(2,1)} %tokens_ref.1, s32[2,128]{1,0:T(2,128)} %bitcast.12, s32[1,128]{1,0:T(1,128)} %bitcast.14, f32[2,128]{1,0:T(2,128)} %bitcast.13), custom_call_target="tpu_custom_call" | custom-call | tf_op jit(solution)/shard_map/pack/pallas_call | solution.py:137
  1.9 3.1 %collective-permute-start = (bf16[32,1536]{1,0:T(8,128)(2,1)S(1)}, bf16[32,1536]{1,0:T(8,128)(2,1)S(1)}, u32[]{:S(2)}, u32[]{:S(2)}) collective-permute-start(bf16[32,1536]{1,0:T(8,128)(2,1)S(1)} %get-tuple-element.59.after_ref.refs_0_), channel_id=1, source_target_pairs={{0,2},{2,0},{4,6},{6,4},{1,3},{3,1},{5,7},{7,5},{8,10},{10,8},{12,... | collective-permute-start | bytes 294920 | tf_op jit(solution)/shard_map/ppermute | solution.py:490
  5.0 2.6 %collective-permute-start.1 = (bf16[32,1536]{1,0:T(8,128)(2,1)S(1)}, bf16[32,1536]{1,0:T(8,128)(2,1)S(1)}, u32[]{:S(2)}, u32[]{:S(2)}) collective-permute-start(bf16[32,1536]{1,0:T(8,128)(2,1)S(1)} %get-tuple-element.59.after_ref.refs_0_), channel_id=1, source_target_pairs={{0,4},{2,6},{4,0},{6,2},{1,5},{3,7},{5,1},{7,3},{8,12},{10,14},{12... | collective-permute-start | bytes 294920 | tf_op jit(solution)/shard_map/ppermute | solution.py:490
  7.6 7.0 %regroup.1 = bf16[24,1536,2,128]{3,2,1,0:T(2,128)(2,1)S(1)} custom-call(bf16[32,1536]{1,0:T(8,128)(2,1)S(1)} %get-tuple-element.59.after_ref.refs_0_, bf16[1536,24,2,128]{3,2,1,0:T(2,128)(2,1)} %bitcast.11), custom_call_target="tpu_custom_call" | custom-call | bytes 37748736 | tf_op jit(solution)/shard_map/regroup/pallas_call | solution.py:188
  15.4 2.0 %preacts_sent.2 = (f32[256,768]{1,0:T(8,128)S(1)}, bf16[256,3072]{1,0:T(8,128)(2,1)S(1)}) custom-call(bf16[32,1536]{1,0:T(8,128)(2,1)S(1)} %get-tuple-element.59.after_ref.refs_0_, bf16[32,1536]{1,0:T(8,128)(2,1)S(1)} %collective-permute-done.refs_1_, bf16[32,1536]{1,0:T(8,128)(2,1)S(1)} %collective-permute-done.1.refs_2_, ...), custom_call_target="tpu_custom_call" | custom-call | flops 1207959552 | tf_op jit(solution)/shard_map/preacts_sent/pallas_call | solution.py:281
  17.5 1.4 %preacts_sent.3 = f32[256,768]{1,0:T(8,128)S(1)} custom-call(bf16[256,3072]{1,0:T(8,128)(2,1)S(1)} %get-tuple-element.65.refs_0_.after_ref, bf16[24,3072,128]{2,1,0:T(8,128)(2,1)S(1)} %bitcast.8), custom_call_target="tpu_custom_call" | custom-call | flops 1207959552 | tf_op jit(solution)/shard_map/preacts_sent/pallas_call | solution.py:281
  19.5 1.4 %preacts_kept.2.kept_ref = f32[256,768]{1,0:T(8,128)S(1)} custom-call(bf16[256,3072]{1,0:T(8,128)(2,1)S(1)} %get-tuple-element.65.refs_0_.after_ref, bf16[24,3072,128]{2,1,0:T(8,128)(2,1)S(1)} %bitcast.9), custom_call_target="tpu_custom_call" | custom-call | flops 1207959552 | tf_op jit(solution)/shard_map/preacts_kept/pallas_call | solution.py:281
  21.0 1.6 %collective-permute-start.5 = (bf16[256,384]{1,0:T(8,128)(2,1)S(1)}, bf16[256,384]{1,0:T(8,128)(2,1)S(1)}, u32[]{:S(2)}, u32[]{:S(2)}) collective-permute-start(bf16[256,384]{1,0:T(8,128)(2,1)S(1)} %get-tuple-element.67), channel_id=1, source_target_pairs={{0,8},{8,0},{1,9},{9,1},{2,10},{10,2},{3,11},{11,3},{4,12},{12,4},... | collective-permute-start | bytes 589832 | tf_op jit(solution)/shard_map/ppermute | solution.py:486
  22.6 1.4 %preacts_kept.3.kept_ref = f32[256,768]{1,0:T(8,128)S(1)} custom-call(bf16[256,3072]{1,0:T(8,128)(2,1)S(1)} %get-tuple-element.65.refs_0_.after_ref, bf16[24,3072,128]{2,1,0:T(8,128)(2,1)S(1)} %bitcast.10), custom_call_target="tpu_custom_call" | custom-call | flops 1207959552 | tf_op jit(solution)/shard_map/preacts_kept/pallas_call | solution.py:281
  24.7 3.8 %fetch_down.1 = (bf16[3072,1536]{1,0:T(8,128)(2,1)S(1)}, f32[8,128]{1,0:T(8,128)S(1)}) custom-call(bf16[256,3072]{1,0:T(8,128)(2,1)S(1)} %get-tuple-element.65.refs_0_.after_ref, bf16[3072,1536]{1,0:T(8,128)(2,1)} %down_ref.1), custom_call_target="tpu_custom_call" | custom-call | bytes 18874368 | tf_op jit(solution)/shard_map/fetch_down/pallas_call | solution.py:219
  28.9 3.2 %collective-permute-done.6.got_ref = bf16[256,384]{1,0:T(8,128)(2,1)S(1)} collective-permute-done((bf16[256,384]{1,0:T(8,128)(2,1)S(1)}, bf16[256,384]{1,0:T(8,128)(2,1)S(1)}, u32[]{:S(2)}, u32[]{:S(2)}) %collective-permute-start.6) | collective-permute-done | bytes 196640 | tf_op jit(solution)/shard_map/ppermute | solution.py:486
  32.2 2.7 %collective-permute-start.7 = (bf16[128,768]{1,0:T(8,128)(2,1)S(1)}, bf16[128,768]{1,0:T(8,128)(2,1)S(1)}, u32[]{:S(2)}, u32[]{:S(2)}) collective-permute-start(bf16[128,768]{1,0:T(8,128)(2,1)S(1)} %act.3.h0.n0), channel_id=1, source_target_pairs={{0,4},{2,6},{4,0},{6,2},{1,5},{3,7},{5,1},{7,3},{8,12},{10,14},{12... | collective-permute-start | bytes 589832 | tf_op jit(solution)/shard_map/ppermute | solution.py:490
  35.8 1.5 %collective-permute-start.9 = (bf16[128,768]{1,0:T(8,128)(2,1)S(1)}, bf16[128,768]{1,0:T(8,128)(2,1)S(1)}, u32[]{:S(2)}, u32[]{:S(2)}) collective-permute-start(bf16[128,768]{1,0:T(8,128)(2,1)S(1)} %act.3.h0.n0), channel_id=1, source_target_pairs={{0,8},{8,0},{1,9},{9,1},{2,10},{10,2},{3,11},{11,3},{4,12},{12,4},... | collective-permute-start | bytes 589832 | tf_op jit(solution)/shard_map/ppermute | solution.py:486
  37.3 6.1 %collective-permute-done.7.near_ref.f2 = bf16[128,768]{1,0:T(8,128)(2,1)S(1)} collective-permute-done((bf16[128,768]{1,0:T(8,128)(2,1)S(1)}, bf16[128,768]{1,0:T(8,128)(2,1)S(1)}, u32[]{:S(2)}, u32[]{:S(2)}) %collective-permute-start.7) | collective-permute-done | bytes 196640 | tf_op jit(solution)/shard_map/ppermute | solution.py:490
  43.8 1.5 %collective-permute-start.12 = (bf16[128,768]{1,0:T(8,128)(2,1)S(1)}, bf16[128,768]{1,0:T(8,128)(2,1)S(1)}, u32[]{:S(2)}, u32[]{:S(2)}) collective-permute-start(bf16[128,768]{1,0:T(8,128)(2,1)S(1)} %collective-permute-done.7.near_ref.f2), channel_id=1, source_target_pairs={{0,2},{2,0},{4,6},{6,4},{1,3},{3,1},{5,7},{7,5},{8,10},{10,8},{12,... | collective-permute-start | bytes 589832 | tf_op jit(solution)/shard_map/ppermute | solution.py:490
  45.3 1.5 %collective-permute-start.13 = (bf16[128,768]{1,0:T(8,128)(2,1)S(1)}, bf16[128,768]{1,0:T(8,128)(2,1)S(1)}, u32[]{:S(2)}, u32[]{:S(2)}) collective-permute-start(bf16[128,768]{1,0:T(8,128)(2,1)S(1)} %choose.1), channel_id=1, source_target_pairs={{0,8},{8,0},{1,9},{9,1},{2,10},{10,2},{3,11},{11,3},{4,12},{12,4},... | collective-permute-start | bytes 589832 | tf_op jit(solution)/shard_map/ppermute | solution.py:486
  46.8 1.6 %project.1 = (f32[32,1536]{1,0:T(8,128)S(1)}, bf16[32,1536]{1,0:T(8,128)(2,1)S(1)}, bf16[32,1536]{1,0:T(8,128)(2,1)S(1)}, bf16[32,1536]{1,0:T(8,128)(2,1)S(1)}, ...) custom-call(f32[8,128]{1,0:T(8,128)S(1)} %get-tuple-element.80.tick_ref, bf16[128,768]{1,0:T(8,128)(2,1)S(1)} %act.3.h0.n0, ...), custom_call_target="tpu_custom_call" | custom-call | flops 1207959552 | tf_op jit(solution)/shard_map/project/pallas_call | solution.py:414
  48.4 2.7 %collective-permute-done.12.f3 = bf16[128,768]{1,0:T(8,128)(2,1)S(1)} collective-permute-done((bf16[128,768]{1,0:T(8,128)(2,1)S(1)}, bf16[128,768]{1,0:T(8,128)(2,1)S(1)}, u32[]{:S(2)}, u32[]{:S(2)}) %collective-permute-start.12) | collective-permute-done | bytes 196640 | tf_op jit(solution)/shard_map/ppermute | solution.py:490
  51.1 3.4 %collective-permute-start.14 = (bf16[128,768]{1,0:T(8,128)(2,1)S(1)}, bf16[128,768]{1,0:T(8,128)(2,1)S(1)}, u32[]{:S(2)}, u32[]{:S(2)}) collective-permute-start(bf16[128,768]{1,0:T(8,128)(2,1)S(1)} %collective-permute-done.12.f3), channel_id=1, source_target_pairs={{0,8},{2,10},{12,4},{14,6},{1,9},{3,11},{13,5},{15,7},{16,24},{18,... | collective-permute-start | bytes 589832 | tf_op jit(solution)/shard_map/ppermute | solution.py:534
  54.7 4.1 %gram.3 = (f32[3072,3072]{1,0:T(8,128)}, f32[8,128]{1,0:T(8,128)S(1)}) custom-call(f32[8,128]{1,0:T(8,128)S(1)} %get-tuple-element.89.refs_0_, bf16[128,768]{1,0:T(8,128)(2,1)S(1)} %get-tuple-element.91.refs_1_, bf16[128,3072]{1,0:T(8,128)(2,1)S(1)} %get-tuple-element.92.refs_2_.refs_3_), custom_call_target="tpu_custom_call" | custom-call | flops 603979776 | bytes 9437184 | tf_op jit(solution)/shard_map/gram/pallas_call | solution.py:466
  59.6 1.5 %collective-permute-start.17 = (bf16[32,1536]{1,0:T(8,128)(2,1)S(1)}, bf16[32,1536]{1,0:T(8,128)(2,1)S(1)}, u32[]{:S(2)}, u32[]{:S(2)}) collective-permute-start(bf16[32,1536]{1,0:T(8,128)(2,1)S(1)} %get-tuple-element.112), channel_id=1, source_target_pairs={{0,2},{2,0},{4,6},{6,4},{1,3},{3,1},{5,7},{7,5},{8,10},{10,8},{12,... | collective-permute-start | bytes 294920 | tf_op jit(solution)/shard_map/ppermute | solution.py:490
  61.0 2.0 %collective-permute-start.18 = (bf16[32,1536]{1,0:T(8,128)(2,1)S(1)}, bf16[32,1536]{1,0:T(8,128)(2,1)S(1)}, u32[]{:S(2)}, u32[]{:S(2)}) collective-permute-start(bf16[32,1536]{1,0:T(8,128)(2,1)S(1)} %get-tuple-element.113), channel_id=1, source_target_pairs={{0,4},{2,6},{4,0},{6,2},{1,5},{3,7},{5,1},{7,3},{8,12},{10,14},{12... | collective-permute-start | bytes 294920 | tf_op jit(solution)/shard_map/ppermute | solution.py:490
  64.0 4.1 %gram.4 = (f32[3072,3072]{1,0:T(8,128)}, f32[8,128]{1,0:T(8,128)S(1)}) custom-call(f32[8,128]{1,0:T(8,128)S(1)} %get-tuple-element.97.refs_0_, bf16[128,768]{1,0:T(8,128)(2,1)S(1)} %collective-permute-done.15.refs_1_, bf16[128,3072]{1,0:T(8,128)(2,1)S(1)} %get-tuple-element.92.refs_2_.refs_3_, ...), custom_call_target="tpu_custom_call", output_to_operand_aliasing={{0}: (3, {})} | custom-call | flops 603979776 | bytes 9437184 | tf_op jit(solution)/shard_map/gram/pallas_call | solution.py:466
  68.1 6.9 %gram.5 = (f32[3072,3072]{1,0:T(8,128)}, f32[8,128]{1,0:T(8,128)S(1)}) custom-call(f32[8,128]{1,0:T(8,128)S(1)} %get-tuple-element.104.refs_0_, bf16[128,768]{1,0:T(8,128)(2,1)S(1)} %get-tuple-element.105.refs_1_, bf16[128,768]{1,0:T(8,128)(2,1)S(1)} %collective-permute-done.16.refs_2_, ...), custom_call_target="tpu_custom_call", output_to_operand_aliasing={{0}: (4, {})} | custom-call | flops 1207959552 | bytes 18874368 | tf_op jit(solution)/shard_map/gram/pallas_call | solution.py:466
  (35 shorter events, 6.8 us)
Async XLA Ops:
  1.9 12.7 %collective-permute-start = (bf16[32,1536]{1,0:T(8,128)(2,1)S(1)}, bf16[32,1536]{1,0:T(8,128)(2,1)S(1)}, u32[]{:S(2)}, u32[]{:S(2)}) collective-permute-start(bf16[32,1536]{1,0:T(8,128)(2,1)S(1)} %get-tuple-element.59.after_ref.refs_0_), channel_id=1, source_target_pairs={{0,2},{2,0},{4,6},{6,4},{1,3},{3,1},{5,7},{7,5},{8,10},{10,8},{12,... | collective-permute-start | bytes 294920 | tf_op jit(solution)/shard_map/ppermute | solution.py:490
  5.0 10.4 %collective-permute-start.1 = (bf16[32,1536]{1,0:T(8,128)(2,1)S(1)}, bf16[32,1536]{1,0:T(8,128)(2,1)S(1)}, u32[]{:S(2)}, u32[]{:S(2)}) collective-permute-start(bf16[32,1536]{1,0:T(8,128)(2,1)S(1)} %get-tuple-element.59.after_ref.refs_0_), channel_id=1, source_target_pairs={{0,4},{2,6},{4,0},{6,2},{1,5},{3,7},{5,1},{7,3},{8,12},{10,14},{12... | collective-permute-start | bytes 294920 | tf_op jit(solution)/shard_map/ppermute | solution.py:490
  7.6 7.8 %collective-permute-start.2 = (bf16[32,1536]{1,0:T(8,128)(2,1)S(1)}, bf16[32,1536]{1,0:T(8,128)(2,1)S(1)}, u32[]{:S(2)}, u32[]{:S(2)}) collective-permute-start(bf16[32,1536]{1,0:T(8,128)(2,1)S(1)} %get-tuple-element.59.after_ref.refs_0_), channel_id=1, source_target_pairs={{0,6},{2,4},{4,2},{6,0},{1,7},{3,5},{5,3},{7,1},{8,14},{10,12},{12... | collective-permute-start | bytes 294920 | tf_op jit(solution)/shard_map/ppermute | solution.py:490
  17.4 3.5 %collective-permute-start.3 = (f32[256,768]{1,0:T(8,128)S(1)}, f32[256,768]{1,0:T(8,128)S(1)}, u32[]{:S(2)}, u32[]{:S(2)}) collective-permute-start(f32[256,768]{1,0:T(8,128)S(1)} %get-tuple-element.61), channel_id=1, source_target_pairs={{0,1},{1,0},{2,3},{3,2},{4,5},{5,4},{6,7},{7,6},{8,9},{9,8},{10,11... | collective-permute-start | bytes 2359304 | tf_op jit(solution)/shard_map/ppermute | solution.py:486
  18.9 5.1 %collective-permute-start.4 = (f32[256,768]{1,0:T(8,128)S(1)}, f32[256,768]{1,0:T(8,128)S(1)}, u32[]{:S(2)}, u32[]{:S(2)}) collective-permute-start(f32[256,768]{1,0:T(8,128)S(1)} %preacts_sent.3), channel_id=1, source_target_pairs={{0,1},{1,0},{2,3},{3,2},{4,5},{5,4},{6,7},{7,6},{8,9},{9,8},{10,11... | collective-permute-start | bytes 2359304 | tf_op jit(solution)/shard_map/ppermute | solution.py:486
  21.0 7.8 %collective-permute-start.5 = (bf16[256,384]{1,0:T(8,128)(2,1)S(1)}, bf16[256,384]{1,0:T(8,128)(2,1)S(1)}, u32[]{:S(2)}, u32[]{:S(2)}) collective-permute-start(bf16[256,384]{1,0:T(8,128)(2,1)S(1)} %get-tuple-element.67), channel_id=1, source_target_pairs={{0,8},{8,0},{1,9},{9,1},{2,10},{10,2},{3,11},{11,3},{4,12},{12,4},... | collective-permute-start | bytes 589832 | tf_op jit(solution)/shard_map/ppermute | solution.py:486
  24.1 8.0 %collective-permute-start.6 = (bf16[256,384]{1,0:T(8,128)(2,1)S(1)}, bf16[256,384]{1,0:T(8,128)(2,1)S(1)}, u32[]{:S(2)}, u32[]{:S(2)}) collective-permute-start(bf16[256,384]{1,0:T(8,128)(2,1)S(1)} %get-tuple-element.69), channel_id=1, source_target_pairs={{0,8},{8,0},{1,9},{9,1},{2,10},{10,2},{3,11},{11,3},{4,12},{12,4},... | collective-permute-start | bytes 589832 | tf_op jit(solution)/shard_map/ppermute | solution.py:486
  32.2 11.3 %collective-permute-start.7 = (bf16[128,768]{1,0:T(8,128)(2,1)S(1)}, bf16[128,768]{1,0:T(8,128)(2,1)S(1)}, u32[]{:S(2)}, u32[]{:S(2)}) collective-permute-start(bf16[128,768]{1,0:T(8,128)(2,1)S(1)} %act.3.h0.n0), channel_id=1, source_target_pairs={{0,4},{2,6},{4,0},{6,2},{1,5},{3,7},{5,1},{7,3},{8,12},{10,14},{12... | collective-permute-start | bytes 589832 | tf_op jit(solution)/shard_map/ppermute | solution.py:490
  34.9 8.8 %collective-permute-start.8 = (bf16[128,768]{1,0:T(8,128)(2,1)S(1)}, bf16[128,768]{1,0:T(8,128)(2,1)S(1)}, u32[]{:S(2)}, u32[]{:S(2)}) collective-permute-start(bf16[128,768]{1,0:T(8,128)(2,1)S(1)} %act.3.h0.n0), channel_id=1, source_target_pairs={{0,2},{2,0},{4,6},{6,4},{1,3},{3,1},{5,7},{7,5},{8,10},{10,8},{12,... | collective-permute-start | bytes 589832 | tf_op jit(solution)/shard_map/ppermute | solution.py:490
  35.8 7.8 %collective-permute-start.9 = (bf16[128,768]{1,0:T(8,128)(2,1)S(1)}, bf16[128,768]{1,0:T(8,128)(2,1)S(1)}, u32[]{:S(2)}, u32[]{:S(2)}) collective-permute-start(bf16[128,768]{1,0:T(8,128)(2,1)S(1)} %act.3.h0.n0), channel_id=1, source_target_pairs={{0,8},{8,0},{1,9},{9,1},{2,10},{10,2},{3,11},{11,3},{4,12},{12,4},... | collective-permute-start | bytes 589832 | tf_op jit(solution)/shard_map/ppermute | solution.py:486
  37.3 9.5 %collective-permute-start.10 = (bf16[128,768]{1,0:T(8,128)(2,1)S(1)}, bf16[128,768]{1,0:T(8,128)(2,1)S(1)}, u32[]{:S(2)}, u32[]{:S(2)}) collective-permute-start(bf16[128,768]{1,0:T(8,128)(2,1)S(1)} %act.3.h0.n0), channel_id=1, source_target_pairs={{0,1},{1,0},{2,3},{3,2},{4,5},{5,4},{6,7},{7,6},{8,9},{9,8},{10,11... | collective-permute-start | bytes 589832 | tf_op jit(solution)/shard_map/ppermute | solution.py:486
  43.7 3.1 %collective-permute-start.11 = (bf16[128,768]{1,0:T(8,128)(2,1)S(1)}, bf16[128,768]{1,0:T(8,128)(2,1)S(1)}, u32[]{:S(2)}, u32[]{:S(2)}) collective-permute-start(bf16[128,768]{1,0:T(8,128)(2,1)S(1)} %collective-permute-done.9.h1.n0), channel_id=1, source_target_pairs={{0,1},{1,0},{2,3},{3,2},{4,5},{5,4},{6,7},{7,6},{8,9},{9,8},{10,11... | collective-permute-start | bytes 589832 | tf_op jit(solution)/shard_map/ppermute | solution.py:486
  43.8 7.3 %collective-permute-start.12 = (bf16[128,768]{1,0:T(8,128)(2,1)S(1)}, bf16[128,768]{1,0:T(8,128)(2,1)S(1)}, u32[]{:S(2)}, u32[]{:S(2)}) collective-permute-start(bf16[128,768]{1,0:T(8,128)(2,1)S(1)} %collective-permute-done.7.near_ref.f2), channel_id=1, source_target_pairs={{0,2},{2,0},{4,6},{6,4},{1,3},{3,1},{5,7},{7,5},{8,10},{10,8},{12,... | collective-permute-start | bytes 589832 | tf_op jit(solution)/shard_map/ppermute | solution.py:490
  45.3 13.4 %collective-permute-start.13 = (bf16[128,768]{1,0:T(8,128)(2,1)S(1)}, bf16[128,768]{1,0:T(8,128)(2,1)S(1)}, u32[]{:S(2)}, u32[]{:S(2)}) collective-permute-start(bf16[128,768]{1,0:T(8,128)(2,1)S(1)} %choose.1), channel_id=1, source_target_pairs={{0,8},{8,0},{1,9},{9,1},{2,10},{10,2},{3,11},{11,3},{4,12},{12,4},... | collective-permute-start | bytes 589832 | tf_op jit(solution)/shard_map/ppermute | solution.py:486
  51.1 7.7 %collective-permute-start.14 = (bf16[128,768]{1,0:T(8,128)(2,1)S(1)}, bf16[128,768]{1,0:T(8,128)(2,1)S(1)}, u32[]{:S(2)}, u32[]{:S(2)}) collective-permute-start(bf16[128,768]{1,0:T(8,128)(2,1)S(1)} %collective-permute-done.12.f3), channel_id=1, source_target_pairs={{0,8},{2,10},{12,4},{14,6},{1,9},{3,11},{13,5},{15,7},{16,24},{18,... | collective-permute-start | bytes 589832 | tf_op jit(solution)/shard_map/ppermute | solution.py:534
  54.6 9.4 %collective-permute-start.15 = (bf16[128,768]{1,0:T(8,128)(2,1)S(1)}, bf16[128,768]{1,0:T(8,128)(2,1)S(1)}, u32[]{:S(2)}, u32[]{:S(2)}) collective-permute-start(bf16[128,768]{1,0:T(8,128)(2,1)S(1)} %get-tuple-element.96), channel_id=1, source_target_pairs={{0,1},{1,0},{2,3},{3,2},{4,5},{5,4},{6,7},{7,6},{8,9},{9,8},{10,11... | collective-permute-start | bytes 589832 | tf_op jit(solution)/shard_map/ppermute | solution.py:486
  59.0 9.0 %collective-permute-start.16 = (bf16[128,768]{1,0:T(8,128)(2,1)S(1)}, bf16[128,768]{1,0:T(8,128)(2,1)S(1)}, u32[]{:S(2)}, u32[]{:S(2)}) collective-permute-start(bf16[128,768]{1,0:T(8,128)(2,1)S(1)} %get-tuple-element.103), channel_id=1, source_target_pairs={{0,1},{1,0},{2,3},{3,2},{4,5},{5,4},{6,7},{7,6},{8,9},{9,8},{10,11... | collective-permute-start | bytes 589832 | tf_op jit(solution)/shard_map/ppermute | solution.py:486
  59.6 15.4 %collective-permute-start.17 = (bf16[32,1536]{1,0:T(8,128)(2,1)S(1)}, bf16[32,1536]{1,0:T(8,128)(2,1)S(1)}, u32[]{:S(2)}, u32[]{:S(2)}) collective-permute-start(bf16[32,1536]{1,0:T(8,128)(2,1)S(1)} %get-tuple-element.112), channel_id=1, source_target_pairs={{0,2},{2,0},{4,6},{6,4},{1,3},{3,1},{5,7},{7,5},{8,10},{10,8},{12,... | collective-permute-start | bytes 294920 | tf_op jit(solution)/shard_map/ppermute | solution.py:490
  61.0 13.9 %collective-permute-start.18 = (bf16[32,1536]{1,0:T(8,128)(2,1)S(1)}, bf16[32,1536]{1,0:T(8,128)(2,1)S(1)}, u32[]{:S(2)}, u32[]{:S(2)}) collective-permute-start(bf16[32,1536]{1,0:T(8,128)(2,1)S(1)} %get-tuple-element.113), channel_id=1, source_target_pairs={{0,4},{2,6},{4,0},{6,2},{1,5},{3,7},{5,1},{7,3},{8,12},{10,14},{12... | collective-permute-start | bytes 294920 | tf_op jit(solution)/shard_map/ppermute | solution.py:490
  63.1 11.9 %collective-permute-start.19 = (bf16[32,1536]{1,0:T(8,128)(2,1)S(1)}, bf16[32,1536]{1,0:T(8,128)(2,1)S(1)}, u32[]{:S(2)}, u32[]{:S(2)}) collective-permute-start(bf16[32,1536]{1,0:T(8,128)(2,1)S(1)} %get-tuple-element.114), channel_id=1, source_target_pairs={{0,6},{2,4},{4,2},{6,0},{1,7},{3,5},{5,3},{7,1},{8,14},{10,12},{12... | collective-permute-start | bytes 294920 | tf_op jit(solution)/shard_map/ppermute | solution.py:490

commit v5 on v4

--- a/solution.py
+++ b/solution.py
@@ -314,22 +314,29 @@
     del tick_ref
     out_ref = refs[-1]
     rows = out_ref.shape[0]
-    done = out_ref.shape[1] - stays_ref.shape[1]
-    if done:
-        out_ref[:, :done] = refs[0][...]
     gate = stays_ref[:rows, :] + got_ref[:rows, :].astype(F32)
     up = stays_ref[rows:, :] + got_ref[rows:, :].astype(F32)
-    out_ref[:, done:] = (jax.nn.silu(gate) * up).astype(BF16)
+    hidden = (jax.nn.silu(gate) * up).astype(BF16)
+    if len(refs) == 1:
+        out_ref[...] = hidden
+    else:
+        before_ref, part_ref, _ = refs
+        done = before_ref.shape[1]
+        part_ref[...] = hidden
+        out_ref[:, :done] = before_ref[...]
+        out_ref[:, done:] = hidden
 
 
 def act(tick, stays, got, *before):
     rows, units = stays.shape
-    units += sum(x.shape[1] for x in before)
+    shapes = [(rows // 2, units)]
+    if before:
+        shapes.append((rows // 2, units + before[0].shape[1]))
     return pl.pallas_call(
         act_kernel,
         in_specs=[ANY] + [VMEM] * (2 + len(before)),
-        out_specs=VMEM,
-        out_shape=jax.ShapeDtypeStruct((rows // 2, units), BF16),
+        out_specs=[VMEM] * len(shapes),
+        out_shape=[jax.ShapeDtypeStruct(shape, BF16) for shape in shapes],
         compiler_params=params(2),
         name="act",
     )(tick, stays, got, *before)
@@ -343,28 +350,41 @@
     return (lax.axis_index("col") % 2) != lax.axis_index("row")
 
 
-def choose_kernel(near_ref, far_ref, out_ref):
+def choose_kernel(n0, n1, far_ref, leaves_ref, joined_ref):
+    units = n0.shape[1]
+    joined_ref[:, :units] = n0[...]
+    joined_ref[:, units:] = n1[...]
+
     @pl.when(is_near())
     def _():
-        out_ref[...] = near_ref[...]
+        leaves_ref[:, :units] = n0[...]
+        leaves_ref[:, units:] = n1[...]
 
     @pl.when(jnp.logical_not(is_near()))
     def _():
-        out_ref[...] = far_ref[...]
-
-
-def choose(if_near, if_far):
+        leaves_ref[...] = far_ref[...]
+
+
+def choose(near_parts, if_far):
+    same = jax.ShapeDtypeStruct(if_far.shape, if_far.dtype)
     return pl.pallas_call(
         choose_kernel,
-        in_specs=[VMEM] * 2,
-        out_specs=VMEM,
-        out_shape=jax.ShapeDtypeStruct(if_near.shape, if_near.dtype),
+        in_specs=[VMEM] * 3,
+        out_specs=[VMEM] * 2,
+        out_shape=[same, same],
         compiler_params=params(2),
         name="choose",
-    )(if_near, if_far)
-
-
-def pick_kernel(n0, n1, f2, f3, mine_ref, other_ref):
+    )(*near_parts, if_far)
+
+
+def pick_kernel(n0, n1, f2, *refs):
+    if len(refs) == 3:
+        f3, mine_ref, other_ref = refs
+    else:
+        h0, h1, mine_ref, other_ref, f3 = refs
+        units = h0.shape[1]
+        f3[:, :units] = h0[...]
+        f3[:, units:] = h1[...]
     for near, pair in ((True, (n0, n1)), (False, (f2, f3))):
         for odd in (False, True):
 
@@ -378,9 +398,9 @@
     same = jax.ShapeDtypeStruct(slots[0].shape, slots[0].dtype)
     return pl.pallas_call(
         pick_kernel,
-        in_specs=[VMEM] * 4,
-        out_specs=[VMEM] * 2,
-        out_shape=[same, same],
+        in_specs=[VMEM] * len(slots),
+        out_specs=[VMEM] * (len(slots) - 2),
+        out_shape=[same] * (len(slots) - 2),
         compiler_params=params(2),
         name="pick",
     )(*slots)
@@ -455,7 +475,7 @@
 
 def gram_piece(tick, pieces, flips, wide, gram=None):
     rows, units = pieces[0].shape
-    cut, depth = 512, 4
+    cut, depth = 256, 8
     operands = [tick, *pieces, in_vmem(wide)]
     in_specs = [ANY] + [VMEM] * (len(pieces) + 1)
     aliases = {}
@@ -513,33 +533,36 @@
         got_x.append(swap(leaves, "expert"))
     down_held, tick = fetch(wide, down)
     tick, got_x[0] = tie(tick, got_x[0])
-    hidden = act(tick, stays[0], got_x[0])
-    tick, got_x[1], hidden = tie(tick, got_x[1], hidden)
-    hidden = act(tick, stays[1], got_x[1], hidden)
-
-    z2 = across(hidden, 2)
+    (hidden_a,) = act(tick, stays[0], got_x[0])
+
+    z2a = across(hidden_a, 2)
+    tick, got_x[1], hidden_a = tie(tick, got_x[1], hidden_a)
+    hidden_b, hidden = act(tick, stays[1], got_x[1], hidden_a)
     z1 = across(hidden, 1)
     hidden_x = swap(hidden, "expert")
     c_near = swap(hidden, "row")
-    tick, z2, z1, hidden_x = tie(tick, z2, z1, hidden_x)
-
-    tick, onward, leaves, sent_x = tie(tick, z2, choose(z2, z1), hidden_x)
-    z3 = across(onward, 1)
+    tick, z2a, hidden_b = tie(tick, z2a, hidden_b)
+    z2b = across(hidden_b, 2)
+    z3a = across(z2a, 1)
+    tick, z2b, z1, hidden_x, z3a = tie(tick, z2b, z1, hidden_x, z3a)
+
+    leaves, z2 = choose((z2a, z2b), z1)
+    tick, z2b, leaves, sent_x = tie(tick, z2b, leaves, hidden_x)
+    z3b = across(z2b, 1)
     x2 = swap(leaves, "expert")
     c_far = swap(sent_x, "row")
     own, s1, s2, s3, hidden_c, tick = project(
         tick, [hidden, hidden_x, c_near, c_far], down_held
     )
-    tick, z3 = tie(tick, z3)
+    returned = [across(value, slot) for slot, value in ((1, s1), (2, s2), (3, s3))]
+    tick, z3b = tie(tick, z3b)
+    mine, passed, z3 = pick(hidden, z1, z2, z3a, z3b)
     x3 = lax.ppermute(
         z3,
         ("expert", "col"),
         [(ee * 4 + cc, (1 - ee) * 4 + cc) for ee in range(2) for cc in range(4) if cc // 2 == ee],
     )
-    mine, passed = pick(hidden, z1, z2, z3)
     mine_near = swap(passed, "row")
-    tick, s1, s2, s3 = tie(tick, s1, s2, s3)
-    returned = [across(value, slot) for slot, value in ((1, s1), (2, s2), (3, s3))]
     gram, tick = gram_piece(tick, [mine], [(0, 0)], hidden_c)
     tick, x2, x3 = tie(tick, x2, x3)
     mine_x, passed = pick(hidden_x, x2, x2, x3)

time: 76.2 us -> 74.9 us (0.983)
  waiting for transfers between devices: 13.4 us -> 7.98 us
  starting transfers between devices: 25.1 us -> 28.5 us
  Pallas kernels: 36.6 us -> 37.4 us
    ppermute x9 -> x11, starting transfers between devices: 15.2 us -> 20.5 us  [across(): return lax.ppermute(value, 'col', [(i, i ^ slot) for i in range(4)])]
    ppermute x9 -> x11, waiting for transfers between devices: 9.85 us -> 7.09 us  [across(): return lax.ppermute(value, 'col', [(i, i ^ slot) for i in range(4)])]
    ppermute x10, waiting for transfers between devices: 3.58 us -> 0.88 us  [swap(): return lax.ppermute(value, axis, [(0, 1), (1, 0)])]
    ppermute x1, starting transfers between devices: 3.42 us -> 2.43 us  [on_device(): lax.ppermute(z3, ('expert', 'col'), [(ee * 4 + cc, (1 - ee) * 4 + cc) for...]
    ppermute x10, starting transfers between devices: 6.47 us -> 5.56 us  [swap(): return lax.ppermute(value, axis, [(0, 1), (1, 0)])]
  transfers between devices with their start and end apart: 20 -> 22, of which waited for: 6 -> 7; matrix products, arithmetic and copies ran while one was open for 0% -> 0% of each run, Pallas kernels for 42% -> 44%
where the time goes in v5:
time: 74.9 us; the launch traced here: 74.8 us
  Pallas kernels  37.4 us (50%)
  starting transfers between devices  28.5 us (38%)
  waiting for transfers between devices  7.98 us (11%)
  between operations  0.88 us (1%)
    ppermute x11, starting transfers between devices, across(): return lax.ppermute(value, 'col', [(i, i ^ slot) for i in range(4)])  20.5 us
    pallas_call x3, Pallas kernels, gram_piece(): pl.pallas_call(functools.partial(gram_kernel, 2.0 / rows, flips), in_spec...  15.8 us
    ppermute x11, waiting for transfers between devices, across(): return lax.ppermute(value, 'col', [(i, i ^ slot) for i in range(4)])  7.09 us
    pallas_call x1, Pallas kernels, regroup(): pl.pallas_call(regroup_kernel, in_specs=[ANY, HBM], out_specs=VMEM, out_s...  6.97 us
    pallas_call x4, Pallas kernels, preacts_of(): pl.pallas_call(functools.partial(preact_kernel, first, row_flip, chunk, c...  6.26 us
    ppermute x10, starting transfers between devices, swap(): return lax.ppermute(value, axis, [(0, 1), (1, 0)])  5.56 us
    pallas_call x1, Pallas kernels, fetch(): pl.pallas_call(fetch_kernel, in_specs=[ANY, HBM], out_specs=[VMEM, VMEM],...  3.8 us
    ppermute x1, starting transfers between devices, on_device(): lax.ppermute(z3, ('expert', 'col'), [(ee * 4 + cc, (1 - ee) * 4 + cc) for...  2.43 us
  transfers between devices with their start and end apart: 22, of which 7 were waited for; matrix products, arithmetic and copies ran while one was open for 0% of the time, Pallas kernels for 44%

profile of v5, /device:TPU:0, one launch (start us, length us, event | category | flops | bytes accessed | tf_op | source)
XLA Modules:
  0.0 74.8 jit_solution(9155670821136331805)
XLA Ops:
  0.6 1.3 %pack.1 = (bf16[32,1536]{1,0:T(8,128)(2,1)S(1)}, bf16[32,128]{1,0:T(8,128)(2,1)S(1)}, f32[32,128]{1,0:T(8,128)S(1)}) custom-call(bf16[128,1536]{1,0:T(8,128)(2,1)} %tokens_ref.1, s32[2,128]{1,0:T(2,128)} %bitcast.12, s32[1,128]{1,0:T(1,128)} %bitcast.14, f32[2,128]{1,0:T(2,128)} %bitcast.13), custom_call_target="tpu_custom_call" | custom-call | tf_op jit(solution)/shard_map/pack/pallas_call | solution.py:137
  1.9 3.1 %collective-permute-start = (bf16[32,1536]{1,0:T(8,128)(2,1)S(1)}, bf16[32,1536]{1,0:T(8,128)(2,1)S(1)}, u32[]{:S(2)}, u32[]{:S(2)}) collective-permute-start(bf16[32,1536]{1,0:T(8,128)(2,1)S(1)} %get-tuple-element.64.after_ref.refs_0_), channel_id=1, source_target_pairs={{0,2},{2,0},{4,6},{6,4},{1,3},{3,1},{5,7},{7,5},{8,10},{10,8},{12,... | collective-permute-start | bytes 294920 | tf_op jit(solution)/shard_map/ppermute | solution.py:510
  5.0 2.6 %collective-permute-start.1 = (bf16[32,1536]{1,0:T(8,128)(2,1)S(1)}, bf16[32,1536]{1,0:T(8,128)(2,1)S(1)}, u32[]{:S(2)}, u32[]{:S(2)}) collective-permute-start(bf16[32,1536]{1,0:T(8,128)(2,1)S(1)} %get-tuple-element.64.after_ref.refs_0_), channel_id=1, source_target_pairs={{0,4},{2,6},{4,0},{6,2},{1,5},{3,7},{5,1},{7,3},{8,12},{10,14},{12... | collective-permute-start | bytes 294920 | tf_op jit(solution)/shard_map/ppermute | solution.py:510
  7.6 7.0 %regroup.1 = bf16[24,1536,2,128]{3,2,1,0:T(2,128)(2,1)S(1)} custom-call(bf16[32,1536]{1,0:T(8,128)(2,1)S(1)} %get-tuple-element.64.after_ref.refs_0_, bf16[1536,24,2,128]{3,2,1,0:T(2,128)(2,1)} %bitcast.11), custom_call_target="tpu_custom_call" | custom-call | bytes 37748736 | tf_op jit(solution)/shard_map/regroup/pallas_call | solution.py:188
  15.4 2.0 %preacts_sent.2 = (f32[256,768]{1,0:T(8,128)S(1)}, bf16[256,3072]{1,0:T(8,128)(2,1)S(1)}) custom-call(bf16[32,1536]{1,0:T(8,128)(2,1)S(1)} %get-tuple-element.64.after_ref.refs_0_, bf16[32,1536]{1,0:T(8,128)(2,1)S(1)} %collective-permute-done.refs_1_, bf16[32,1536]{1,0:T(8,128)(2,1)S(1)} %collective-permute-done.1.refs_2_, ...), custom_call_target="tpu_custom_call" | custom-call | flops 1207959552 | tf_op jit(solution)/shard_map/preacts_sent/pallas_call | solution.py:281
  17.5 1.4 %preacts_sent.3 = f32[256,768]{1,0:T(8,128)S(1)} custom-call(bf16[256,3072]{1,0:T(8,128)(2,1)S(1)} %get-tuple-element.70.refs_0_.after_ref, bf16[24,3072,128]{2,1,0:T(8,128)(2,1)S(1)} %bitcast.8), custom_call_target="tpu_custom_call" | custom-call | flops 1207959552 | tf_op jit(solution)/shard_map/preacts_sent/pallas_call | solution.py:281
  19.5 1.4 %preacts_kept.2.kept_ref = f32[256,768]{1,0:T(8,128)S(1)} custom-call(bf16[256,3072]{1,0:T(8,128)(2,1)S(1)} %get-tuple-element.70.refs_0_.after_ref, bf16[24,3072,128]{2,1,0:T(8,128)(2,1)S(1)} %bitcast.9), custom_call_target="tpu_custom_call" | custom-call | flops 1207959552 | tf_op jit(solution)/shard_map/preacts_kept/pallas_call | solution.py:281
  21.0 1.6 %collective-permute-start.5 = (bf16[256,384]{1,0:T(8,128)(2,1)S(1)}, bf16[256,384]{1,0:T(8,128)(2,1)S(1)}, u32[]{:S(2)}, u32[]{:S(2)}) collective-permute-start(bf16[256,384]{1,0:T(8,128)(2,1)S(1)} %get-tuple-element.72), channel_id=1, source_target_pairs={{0,8},{8,0},{1,9},{9,1},{2,10},{10,2},{3,11},{11,3},{4,12},{12,4},... | collective-permute-start | bytes 589832 | tf_op jit(solution)/shard_map/ppermute | solution.py:506
  22.6 1.4 %preacts_kept.3.kept_ref = f32[256,768]{1,0:T(8,128)S(1)} custom-call(bf16[256,3072]{1,0:T(8,128)(2,1)S(1)} %get-tuple-element.70.refs_0_.after_ref, bf16[24,3072,128]{2,1,0:T(8,128)(2,1)S(1)} %bitcast.10), custom_call_target="tpu_custom_call" | custom-call | flops 1207959552 | tf_op jit(solution)/shard_map/preacts_kept/pallas_call | solution.py:281
  24.7 3.8 %fetch_down.1 = (bf16[3072,1536]{1,0:T(8,128)(2,1)S(1)}, f32[8,128]{1,0:T(8,128)S(1)}) custom-call(bf16[256,3072]{1,0:T(8,128)(2,1)S(1)} %get-tuple-element.70.refs_0_.after_ref, bf16[3072,1536]{1,0:T(8,128)(2,1)} %down_ref.1), custom_call_target="tpu_custom_call" | custom-call | bytes 18874368 | tf_op jit(solution)/shard_map/fetch_down/pallas_call | solution.py:219
  28.9 2.7 %collective-permute-start.7 = (bf16[128,384]{1,0:T(8,128)(2,1)S(1)}, bf16[128,384]{1,0:T(8,128)(2,1)S(1)}, u32[]{:S(2)}, u32[]{:S(2)}) collective-permute-start(bf16[128,384]{1,0:T(8,128)(2,1)S(1)} %act.2.refs_0_), channel_id=1, source_target_pairs={{0,4},{2,6},{4,0},{6,2},{1,5},{3,7},{5,1},{7,3},{8,12},{10,14},{12... | collective-permute-start | bytes 294920 | tf_op jit(solution)/shard_map/ppermute | solution.py:510
  32.2 1.6 %collective-permute-start.10 = (bf16[128,768]{1,0:T(8,128)(2,1)S(1)}, bf16[128,768]{1,0:T(8,128)(2,1)S(1)}, u32[]{:S(2)}, u32[]{:S(2)}) collective-permute-start(bf16[128,768]{1,0:T(8,128)(2,1)S(1)} %get-tuple-element.84.h0.n0), channel_id=1, source_target_pairs={{0,8},{8,0},{1,9},{9,1},{2,10},{10,2},{3,11},{11,3},{4,12},{12,4},... | collective-permute-start | bytes 589832 | tf_op jit(solution)/shard_map/ppermute | solution.py:506
  33.8 1.6 %collective-permute-start.9 = (bf16[128,768]{1,0:T(8,128)(2,1)S(1)}, bf16[128,768]{1,0:T(8,128)(2,1)S(1)}, u32[]{:S(2)}, u32[]{:S(2)}) collective-permute-start(bf16[128,768]{1,0:T(8,128)(2,1)S(1)} %get-tuple-element.84.h0.n0), channel_id=1, source_target_pairs={{0,2},{2,0},{4,6},{6,4},{1,3},{3,1},{5,7},{7,5},{8,10},{10,8},{12,... | collective-permute-start | bytes 589832 | tf_op jit(solution)/shard_map/ppermute | solution.py:510
  36.2 3.2 %collective-permute-start.8 = (bf16[128,384]{1,0:T(8,128)(2,1)S(1)}, bf16[128,384]{1,0:T(8,128)(2,1)S(1)}, u32[]{:S(2)}, u32[]{:S(2)}) collective-permute-start(bf16[128,384]{1,0:T(8,128)(2,1)S(1)} %get-tuple-element.83), channel_id=1, source_target_pairs={{0,4},{2,6},{4,0},{6,2},{1,5},{3,7},{5,1},{7,3},{8,12},{10,14},{12... | collective-permute-start | bytes 294920 | tf_op jit(solution)/shard_map/ppermute | solution.py:510
  39.5 3.4 %collective-permute-done.9.far_ref.n1 = bf16[128,768]{1,0:T(8,128)(2,1)S(1)} collective-permute-done((bf16[128,768]{1,0:T(8,128)(2,1)S(1)}, bf16[128,768]{1,0:T(8,128)(2,1)S(1)}, u32[]{:S(2)}, u32[]{:S(2)}) %collective-permute-start.9) | collective-permute-done | bytes 196640 | tf_op jit(solution)/shard_map/ppermute | solution.py:510
  44.0 2.5 %collective-permute-start.14 = (bf16[128,384]{1,0:T(8,128)(2,1)S(1)}, bf16[128,384]{1,0:T(8,128)(2,1)S(1)}, u32[]{:S(2)}, u32[]{:S(2)}) collective-permute-start(bf16[128,384]{1,0:T(8,128)(2,1)S(1)} %collective-permute-done.8.n1), channel_id=1, source_target_pairs={{0,2},{2,0},{4,6},{6,4},{1,3},{3,1},{5,7},{7,5},{8,10},{10,8},{12,... | collective-permute-start | bytes 294920 | tf_op jit(solution)/shard_map/ppermute | solution.py:510
  47.0 1.6 %project.1 = (f32[32,1536]{1,0:T(8,128)S(1)}, bf16[32,1536]{1,0:T(8,128)(2,1)S(1)}, bf16[32,1536]{1,0:T(8,128)(2,1)S(1)}, bf16[32,1536]{1,0:T(8,128)(2,1)S(1)}, ...) custom-call(f32[8,128]{1,0:T(8,128)S(1)} %get-tuple-element.91.tick_ref, ...), custom_call_target="tpu_custom_call" | custom-call | flops 1207959552 | tf_op jit(solution)/shard_map/project/pallas_call | solution.py:434
  48.7 1.3 %collective-permute-done.14.refs_1_ = bf16[128,384]{1,0:T(8,128)(2,1)S(1)} collective-permute-done((bf16[128,384]{1,0:T(8,128)(2,1)S(1)}, bf16[128,384]{1,0:T(8,128)(2,1)S(1)}, u32[]{:S(2)}, u32[]{:S(2)}) %collective-permute-start.14) | collective-permute-done | bytes 98336 | tf_op jit(solution)/shard_map/ppermute | solution.py:510
  50.0 2.4 %collective-permute-start.16 = (bf16[128,768]{1,0:T(8,128)(2,1)S(1)}, bf16[128,768]{1,0:T(8,128)(2,1)S(1)}, u32[]{:S(2)}, u32[]{:S(2)}) collective-permute-start(bf16[128,768]{1,0:T(8,128)(2,1)S(1)} %get-tuple-element.104), channel_id=1, source_target_pairs={{0,8},{2,10},{12,4},{14,6},{1,9},{3,11},{13,5},{15,7},{16,24},{18,... | collective-permute-start | bytes 589832 | tf_op jit(solution)/shard_map/ppermute | solution.py:560
  52.5 4.1 %gram.3 = (f32[3072,3072]{1,0:T(8,128)}, f32[8,128]{1,0:T(8,128)S(1)}) custom-call(f32[8,128]{1,0:T(8,128)S(1)} %get-tuple-element.96.refs_0_, bf16[128,768]{1,0:T(8,128)(2,1)S(1)} %get-tuple-element.100.refs_1_, bf16[128,3072]{1,0:T(8,128)(2,1)S(1)} %get-tuple-element.101.refs_2_.refs_3_), custom_call_target="tpu_custom_call" | custom-call | flops 603979776 | bytes 9437184 | tf_op jit(solution)/shard_map/gram/pallas_call | solution.py:486
  57.4 1.8 %collective-permute-start.19 = (bf16[32,1536]{1,0:T(8,128)(2,1)S(1)}, bf16[32,1536]{1,0:T(8,128)(2,1)S(1)}, u32[]{:S(2)}, u32[]{:S(2)}) collective-permute-start(bf16[32,1536]{1,0:T(8,128)(2,1)S(1)} %get-tuple-element.122), channel_id=1, source_target_pairs={{0,2},{2,0},{4,6},{6,4},{1,3},{3,1},{5,7},{7,5},{8,10},{10,8},{12,... | collective-permute-start | bytes 294920 | tf_op jit(solution)/shard_map/ppermute | solution.py:510
  59.2 2.8 %collective-permute-start.20 = (bf16[32,1536]{1,0:T(8,128)(2,1)S(1)}, bf16[32,1536]{1,0:T(8,128)(2,1)S(1)}, u32[]{:S(2)}, u32[]{:S(2)}) collective-permute-start(bf16[32,1536]{1,0:T(8,128)(2,1)S(1)} %get-tuple-element.123), channel_id=1, source_target_pairs={{0,4},{2,6},{4,0},{6,2},{1,5},{3,7},{5,1},{7,3},{8,12},{10,14},{12... | collective-permute-start | bytes 294920 | tf_op jit(solution)/shard_map/ppermute | solution.py:510
  62.0 4.1 %gram.4 = (f32[3072,3072]{1,0:T(8,128)}, f32[8,128]{1,0:T(8,128)S(1)}) custom-call(f32[8,128]{1,0:T(8,128)S(1)} %get-tuple-element.107.refs_0_, bf16[128,768]{1,0:T(8,128)(2,1)S(1)} %collective-permute-done.17.refs_1_, bf16[128,3072]{1,0:T(8,128)(2,1)S(1)} %get-tuple-element.101.refs_2_.refs_3_, ...), custom_call_target="tpu_custom_call", output_to_operand_aliasing={{0}: (3, {})} | custom-call | flops 603979776 | bytes 9437184 | tf_op jit(solution)/shard_map/gram/pallas_call | solution.py:486
  66.1 7.6 %gram.5 = (f32[3072,3072]{1,0:T(8,128)}, f32[8,128]{1,0:T(8,128)S(1)}) custom-call(f32[8,128]{1,0:T(8,128)S(1)} %get-tuple-element.114.refs_0_, bf16[128,768]{1,0:T(8,128)(2,1)S(1)} %get-tuple-element.115.refs_1_, bf16[128,768]{1,0:T(8,128)(2,1)S(1)} %collective-permute-done.18.refs_2_, ...), custom_call_target="tpu_custom_call", output_to_operand_aliasing={{0}: (4, {})} | custom-call | flops 1207959552 | bytes 18874368 | tf_op jit(solution)/shard_map/gram/pallas_call | solution.py:486
  (39 shorter events, 7.8 us)
Async XLA Ops:
  1.9 12.7 %collective-permute-start = (bf16[32,1536]{1,0:T(8,128)(2,1)S(1)}, bf16[32,1536]{1,0:T(8,128)(2,1)S(1)}, u32[]{:S(2)}, u32[]{:S(2)}) collective-permute-start(bf16[32,1536]{1,0:T(8,128)(2,1)S(1)} %get-tuple-element.64.after_ref.refs_0_), channel_id=1, source_target_pairs={{0,2},{2,0},{4,6},{6,4},{1,3},{3,1},{5,7},{7,5},{8,10},{10,8},{12,... | collective-permute-start | bytes 294920 | tf_op jit(solution)/shard_map/ppermute | solution.py:510
  5.0 10.4 %collective-permute-start.1 = (bf16[32,1536]{1,0:T(8,128)(2,1)S(1)}, bf16[32,1536]{1,0:T(8,128)(2,1)S(1)}, u32[]{:S(2)}, u32[]{:S(2)}) collective-permute-start(bf16[32,1536]{1,0:T(8,128)(2,1)S(1)} %get-tuple-element.64.after_ref.refs_0_), channel_id=1, source_target_pairs={{0,4},{2,6},{4,0},{6,2},{1,5},{3,7},{5,1},{7,3},{8,12},{10,14},{12... | collective-permute-start | bytes 294920 | tf_op jit(solution)/shard_map/ppermute | solution.py:510
  7.6 7.8 %collective-permute-start.2 = (bf16[32,1536]{1,0:T(8,128)(2,1)S(1)}, bf16[32,1536]{1,0:T(8,128)(2,1)S(1)}, u32[]{:S(2)}, u32[]{:S(2)}) collective-permute-start(bf16[32,1536]{1,0:T(8,128)(2,1)S(1)} %get-tuple-element.64.after_ref.refs_0_), channel_id=1, source_target_pairs={{0,6},{2,4},{4,2},{6,0},{1,7},{3,5},{5,3},{7,1},{8,14},{10,12},{12... | collective-permute-start | bytes 294920 | tf_op jit(solution)/shard_map/ppermute | solution.py:510
  17.4 3.5 %collective-permute-start.3 = (f32[256,768]{1,0:T(8,128)S(1)}, f32[256,768]{1,0:T(8,128)S(1)}, u32[]{:S(2)}, u32[]{:S(2)}) collective-permute-start(f32[256,768]{1,0:T(8,128)S(1)} %get-tuple-element.66), channel_id=1, source_target_pairs={{0,1},{1,0},{2,3},{3,2},{4,5},{5,4},{6,7},{7,6},{8,9},{9,8},{10,11... | collective-permute-start | bytes 2359304 | tf_op jit(solution)/shard_map/ppermute | solution.py:506
  18.9 5.1 %collective-permute-start.4 = (f32[256,768]{1,0:T(8,128)S(1)}, f32[256,768]{1,0:T(8,128)S(1)}, u32[]{:S(2)}, u32[]{:S(2)}) collective-permute-start(f32[256,768]{1,0:T(8,128)S(1)} %preacts_sent.3), channel_id=1, source_target_pairs={{0,1},{1,0},{2,3},{3,2},{4,5},{5,4},{6,7},{7,6},{8,9},{9,8},{10,11... | collective-permute-start | bytes 2359304 | tf_op jit(solution)/shard_map/ppermute | solution.py:506
  21.0 7.8 %collective-permute-start.5 = (bf16[256,384]{1,0:T(8,128)(2,1)S(1)}, bf16[256,384]{1,0:T(8,128)(2,1)S(1)}, u32[]{:S(2)}, u32[]{:S(2)}) collective-permute-start(bf16[256,384]{1,0:T(8,128)(2,1)S(1)} %get-tuple-element.72), channel_id=1, source_target_pairs={{0,8},{8,0},{1,9},{9,1},{2,10},{10,2},{3,11},{11,3},{4,12},{12,4},... | collective-permute-start | bytes 589832 | tf_op jit(solution)/shard_map/ppermute | solution.py:506
  24.1 8.0 %collective-permute-start.6 = (bf16[256,384]{1,0:T(8,128)(2,1)S(1)}, bf16[256,384]{1,0:T(8,128)(2,1)S(1)}, u32[]{:S(2)}, u32[]{:S(2)}) collective-permute-start(bf16[256,384]{1,0:T(8,128)(2,1)S(1)} %get-tuple-element.74), channel_id=1, source_target_pairs={{0,8},{8,0},{1,9},{9,1},{2,10},{10,2},{3,11},{11,3},{4,12},{12,4},... | collective-permute-start | bytes 589832 | tf_op jit(solution)/shard_map/ppermute | solution.py:506
  28.9 7.0 %collective-permute-start.7 = (bf16[128,384]{1,0:T(8,128)(2,1)S(1)}, bf16[128,384]{1,0:T(8,128)(2,1)S(1)}, u32[]{:S(2)}, u32[]{:S(2)}) collective-permute-start(bf16[128,384]{1,0:T(8,128)(2,1)S(1)} %act.2.refs_0_), channel_id=1, source_target_pairs={{0,4},{2,6},{4,0},{6,2},{1,5},{3,7},{5,1},{7,3},{8,12},{10,14},{12... | collective-permute-start | bytes 294920 | tf_op jit(solution)/shard_map/ppermute | solution.py:510
  32.2 7.3 %collective-permute-start.10 = (bf16[128,768]{1,0:T(8,128)(2,1)S(1)}, bf16[128,768]{1,0:T(8,128)(2,1)S(1)}, u32[]{:S(2)}, u32[]{:S(2)}) collective-permute-start(bf16[128,768]{1,0:T(8,128)(2,1)S(1)} %get-tuple-element.84.h0.n0), channel_id=1, source_target_pairs={{0,8},{8,0},{1,9},{9,1},{2,10},{10,2},{3,11},{11,3},{4,12},{12,4},... | collective-permute-start | bytes 589832 | tf_op jit(solution)/shard_map/ppermute | solution.py:506
  33.8 9.1 %collective-permute-start.9 = (bf16[128,768]{1,0:T(8,128)(2,1)S(1)}, bf16[128,768]{1,0:T(8,128)(2,1)S(1)}, u32[]{:S(2)}, u32[]{:S(2)}) collective-permute-start(bf16[128,768]{1,0:T(8,128)(2,1)S(1)} %get-tuple-element.84.h0.n0), channel_id=1, source_target_pairs={{0,2},{2,0},{4,6},{6,4},{1,3},{3,1},{5,7},{7,5},{8,10},{10,8},{12,... | collective-permute-start | bytes 589832 | tf_op jit(solution)/shard_map/ppermute | solution.py:510
  36.0 7.9 %collective-permute-start.11 = (bf16[128,384]{1,0:T(8,128)(2,1)S(1)}, bf16[128,384]{1,0:T(8,128)(2,1)S(1)}, u32[]{:S(2)}, u32[]{:S(2)}) collective-permute-start(bf16[128,384]{1,0:T(8,128)(2,1)S(1)} %collective-permute-done.7.n0), channel_id=1, source_target_pairs={{0,2},{2,0},{4,6},{6,4},{1,3},{3,1},{5,7},{7,5},{8,10},{10,8},{12,... | collective-permute-start | bytes 294920 | tf_op jit(solution)/shard_map/ppermute | solution.py:510
  36.2 7.7 %collective-permute-start.8 = (bf16[128,384]{1,0:T(8,128)(2,1)S(1)}, bf16[128,384]{1,0:T(8,128)(2,1)S(1)}, u32[]{:S(2)}, u32[]{:S(2)}) collective-permute-start(bf16[128,384]{1,0:T(8,128)(2,1)S(1)} %get-tuple-element.83), channel_id=1, source_target_pairs={{0,4},{2,6},{4,0},{6,2},{1,5},{3,7},{5,1},{7,3},{8,12},{10,14},{12... | collective-permute-start | bytes 294920 | tf_op jit(solution)/shard_map/ppermute | solution.py:510
  39.5 7.6 %collective-permute-start.12 = (bf16[128,768]{1,0:T(8,128)(2,1)S(1)}, bf16[128,768]{1,0:T(8,128)(2,1)S(1)}, u32[]{:S(2)}, u32[]{:S(2)}) collective-permute-start(bf16[128,768]{1,0:T(8,128)(2,1)S(1)} %get-tuple-element.84.h0.n0), channel_id=1, source_target_pairs={{0,1},{1,0},{2,3},{3,2},{4,5},{5,4},{6,7},{7,6},{8,9},{9,8},{10,11... | collective-permute-start | bytes 589832 | tf_op jit(solution)/shard_map/ppermute | solution.py:506
  43.9 3.1 %collective-permute-start.13 = (bf16[128,768]{1,0:T(8,128)(2,1)S(1)}, bf16[128,768]{1,0:T(8,128)(2,1)S(1)}, u32[]{:S(2)}, u32[]{:S(2)}) collective-permute-start(bf16[128,768]{1,0:T(8,128)(2,1)S(1)} %collective-permute-done.10.h1.n0), channel_id=1, source_target_pairs={{0,1},{1,0},{2,3},{3,2},{4,5},{5,4},{6,7},{7,6},{8,9},{9,8},{10,11... | collective-permute-start | bytes 589832 | tf_op jit(solution)/shard_map/ppermute | solution.py:506
  44.0 5.9 %collective-permute-start.14 = (bf16[128,384]{1,0:T(8,128)(2,1)S(1)}, bf16[128,384]{1,0:T(8,128)(2,1)S(1)}, u32[]{:S(2)}, u32[]{:S(2)}) collective-permute-start(bf16[128,384]{1,0:T(8,128)(2,1)S(1)} %collective-permute-done.8.n1), channel_id=1, source_target_pairs={{0,2},{2,0},{4,6},{6,4},{1,3},{3,1},{5,7},{7,5},{8,10},{10,8},{12,... | collective-permute-start | bytes 294920 | tf_op jit(solution)/shard_map/ppermute | solution.py:510
  46.5 10.1 %collective-permute-start.15 = (bf16[128,768]{1,0:T(8,128)(2,1)S(1)}, bf16[128,768]{1,0:T(8,128)(2,1)S(1)}, u32[]{:S(2)}, u32[]{:S(2)}) collective-permute-start(bf16[128,768]{1,0:T(8,128)(2,1)S(1)} %get-tuple-element.103), channel_id=1, source_target_pairs={{0,8},{8,0},{1,9},{9,1},{2,10},{10,2},{3,11},{11,3},{4,12},{12,4},... | collective-permute-start | bytes 589832 | tf_op jit(solution)/shard_map/ppermute | solution.py:506
  50.0 6.6 %collective-permute-start.16 = (bf16[128,768]{1,0:T(8,128)(2,1)S(1)}, bf16[128,768]{1,0:T(8,128)(2,1)S(1)}, u32[]{:S(2)}, u32[]{:S(2)}) collective-permute-start(bf16[128,768]{1,0:T(8,128)(2,1)S(1)} %get-tuple-element.104), channel_id=1, source_target_pairs={{0,8},{2,10},{12,4},{14,6},{1,9},{3,11},{13,5},{15,7},{16,24},{18,... | collective-permute-start | bytes 589832 | tf_op jit(solution)/shard_map/ppermute | solution.py:560
  52.4 9.5 %collective-permute-start.17 = (bf16[128,768]{1,0:T(8,128)(2,1)S(1)}, bf16[128,768]{1,0:T(8,128)(2,1)S(1)}, u32[]{:S(2)}, u32[]{:S(2)}) collective-permute-start(bf16[128,768]{1,0:T(8,128)(2,1)S(1)} %get-tuple-element.106), channel_id=1, source_target_pairs={{0,1},{1,0},{2,3},{3,2},{4,5},{5,4},{6,7},{7,6},{8,9},{9,8},{10,11... | collective-permute-start | bytes 589832 | tf_op jit(solution)/shard_map/ppermute | solution.py:506
  56.9 9.2 %collective-permute-start.18 = (bf16[128,768]{1,0:T(8,128)(2,1)S(1)}, bf16[128,768]{1,0:T(8,128)(2,1)S(1)}, u32[]{:S(2)}, u32[]{:S(2)}) collective-permute-start(bf16[128,768]{1,0:T(8,128)(2,1)S(1)} %get-tuple-element.113), channel_id=1, source_target_pairs={{0,1},{1,0},{2,3},{3,2},{4,5},{5,4},{6,7},{7,6},{8,9},{9,8},{10,11... | collective-permute-start | bytes 589832 | tf_op jit(solution)/shard_map/ppermute | solution.py:506
  57.4 16.3 %collective-permute-start.19 = (bf16[32,1536]{1,0:T(8,128)(2,1)S(1)}, bf16[32,1536]{1,0:T(8,128)(2,1)S(1)}, u32[]{:S(2)}, u32[]{:S(2)}) collective-permute-start(bf16[32,1536]{1,0:T(8,128)(2,1)S(1)} %get-tuple-element.122), channel_id=1, source_target_pairs={{0,2},{2,0},{4,6},{6,4},{1,3},{3,1},{5,7},{7,5},{8,10},{10,8},{12,... | collective-permute-start | bytes 294920 | tf_op jit(solution)/shard_map/ppermute | solution.py:510
  59.2 14.5 %collective-permute-start.20 = (bf16[32,1536]{1,0:T(8,128)(2,1)S(1)}, bf16[32,1536]{1,0:T(8,128)(2,1)S(1)}, u32[]{:S(2)}, u32[]{:S(2)}) collective-permute-start(bf16[32,1536]{1,0:T(8,128)(2,1)S(1)} %get-tuple-element.123), channel_id=1, source_target_pairs={{0,4},{2,6},{4,0},{6,2},{1,5},{3,7},{5,1},{7,3},{8,12},{10,14},{12... | collective-permute-start | bytes 294920 | tf_op jit(solution)/shard_map/ppermute | solution.py:510
  62.0 11.7 %collective-permute-start.21 = (bf16[32,1536]{1,0:T(8,128)(2,1)S(1)}, bf16[32,1536]{1,0:T(8,128)(2,1)S(1)}, u32[]{:S(2)}, u32[]{:S(2)}) collective-permute-start(bf16[32,1536]{1,0:T(8,128)(2,1)S(1)} %get-tuple-element.124), channel_id=1, source_target_pairs={{0,6},{2,4},{4,2},{6,0},{1,7},{3,5},{5,3},{7,1},{8,14},{10,12},{12... | collective-permute-start | bytes 294920 | tf_op jit(solution)/shard_map/ppermute | solution.py:510

commit v6 on v5

--- a/solution.py
+++ b/solution.py
@@ -171,31 +171,41 @@
     )(done, placing, factor, own, *returned)
 
 
-def regroup_kernel(after_ref, weights_ref, out_ref, sems):
+def regroup_kernel(row_flip, after_ref, weights_ref, out_ref, done_ref, sems):
     del after_ref
-    copies = [
-        pltpu.make_async_copy(weights_ref.at[:, t], out_ref.at[t], sems.at[t])
-        for t in range(out_ref.shape[0])
-    ]
+    per = out_ref.shape[0] // 2
+    copies = []
+    for i in range(2):
+        start = quarter_of(1 - i, row_flip) * per
+        for t in range(per):
+            copies.append(
+                pltpu.make_async_copy(
+                    weights_ref.at[:, start + t], out_ref.at[per * i + t], sems.at[per * i + t]
+                )
+            )
     for copy in copies:
         copy.start()
+    done_ref[...] = jnp.zeros_like(done_ref)
     for copy in copies:
         copy.wait()
 
 
-def regroup(behind, weights):
+def regroup(behind, weights, row_flip):
     depth, tiles, two, lanes = weights.shape
-    grouped = pl.pallas_call(
-        regroup_kernel,
+    grouped, done = pl.pallas_call(
+        functools.partial(regroup_kernel, row_flip),
         in_specs=[ANY, HBM],
-        out_specs=VMEM,
-        out_shape=pltpu.VMEM((tiles, depth, two, lanes), BF16),
-        scratch_shapes=[pltpu.SemaphoreType.DMA((tiles,))],
-        compiler_params=params(4),
-        cost_estimate=cost(0, 4 * weights.size),
+        out_specs=[VMEM] * 2,
+        out_shape=[
+            pltpu.VMEM((tiles // 2, depth, two, lanes), BF16),
+            pltpu.VMEM((8, 128), F32),
+        ],
+        scratch_shapes=[pltpu.SemaphoreType.DMA((tiles // 2,))],
+        compiler_params=params(2),
+        cost_estimate=cost(0, 2 * weights.size),
         name="regroup",
     )(behind, in_hbm(weights))
-    return grouped.reshape(tiles, depth * two, lanes)
+    return grouped.reshape(tiles // 2, depth * two, lanes), done
 
 
 def fetch_kernel(after_ref, down_ref, out_ref, done_ref, sems):
@@ -250,19 +260,16 @@
                 ]
 
 
-def preact_kernel(first, row_flip, chunk, chunks, *refs):
+def preact_kernel(first, chunk, chunks, *refs):
     if first:
         x0, x1, x2, x3, w_ref, out_ref, wide_ref = refs
         widen_tokens((x0, x1, x2, x3), wide_ref)
     else:
         wide_ref, w_ref, out_ref = refs
     tiles, _, lanes = w_ref.shape
-    per = tiles // 4
+    per = tiles // 2
     take = per // chunks
-    at = []
-    for i in range(2):
-        quarter = quarter_of(1 - i, row_flip)
-        at += [quarter * per + chunk * take + j for j in range(take)]
+    at = [i * per + chunk * take + j for i in range(2) for j in range(take)]
     for j in range(take):
         w = jnp.concatenate([w_ref[at[2 * j]], w_ref[at[2 * j + 1]]], axis=1)
         out_ref[:, 2 * lanes * j : 2 * lanes * (j + 1)] = jnp.dot(
@@ -270,22 +277,22 @@
         )
 
 
-def preacts_of(lefts, weights, row_flip, chunk, chunks):
+def preacts_of(lefts, weights, chunk, chunks):
     tiles, depth2, lanes = weights.shape
     first = len(lefts) > 1
     rows = 4 * lefts[0].shape[0] if first else lefts[0].shape[0] // 2
-    units = tiles // 4 // chunks * lanes
+    units = tiles // 2 // chunks * lanes
     out_shape = [jax.ShapeDtypeStruct((2 * rows, 2 * units), F32)]
     if first:
         out_shape.append(pltpu.VMEM((2 * rows, depth2), BF16))
     return pl.pallas_call(
-        functools.partial(preact_kernel, first, row_flip, chunk, chunks),
+        functools.partial(preact_kernel, first, chunk, chunks),
         in_specs=[VMEM] * (len(lefts) + 1),
         out_specs=[VMEM] * len(out_shape),
         out_shape=out_shape,
         compiler_params=params(4),
         cost_estimate=cost(8 * rows * depth2 * units, 0),
-        name="preacts_" + ("sent" if row_flip else "kept"),
+        name="preacts",
     )(*lefts, in_vmem(weights))
 
 
@@ -406,14 +413,33 @@
     )(*slots)
 
 
+def join_kernel(left_ref, right_ref, out_ref):
+    units = left_ref.shape[1]
+    out_ref[:, :units] = left_ref[...]
+    out_ref[:, units:] = right_ref[...]
+
+
+def join(left, right):
+    rows, units = left.shape
+    return pl.pallas_call(
+        join_kernel,
+        in_specs=[VMEM] * 2,
+        out_specs=VMEM,
+        out_shape=jax.ShapeDtypeStruct((rows, 2 * units), left.dtype),
+        compiler_params=params(2),
+        name="join",
+    )(left, right)
+
+
 def project_kernel(
-    tick_ref, h0, h1, h2, h3, down_ref, own_ref, s1_ref, s2_ref, s3_ref, wide_ref, done_ref, total_ref
+    tick_ref, here_ref, there_ref, down_ref, own_ref, s1_ref, s2_ref, s3_ref, wide_ref, done_ref, total_ref
 ):
     del tick_ref
-    units = h0.shape[1]
-    for k, h_ref in enumerate((h0, h1, h2, h3)):
-        at = pl.multiple_of(quarter_of(k % 2, k // 2) * units, units)
-        wide_ref[:, pl.ds(at, units)] = h_ref[...]
+    units = here_ref.shape[1] // 2
+    for row_flip, pair_ref in enumerate((here_ref, there_ref)):
+        for expert_flip in range(2):
+            at = pl.multiple_of(quarter_of(expert_flip, row_flip) * units, units)
+            wide_ref[:, pl.ds(at, units)] = pair_ref[:, units * expert_flip : units * (expert_flip + 1)]
     done_ref[...] = jnp.zeros_like(done_ref)
     slots, width = own_ref.shape
     cut = 512
@@ -427,13 +453,13 @@
         out_ref[...] = total_ref[pl.ds(at, slots), :].astype(out_ref.dtype)
 
 
-def project(tick, quarters, down):
-    rows, units = quarters[0].shape
+def project(tick, here, there, down):
+    rows, units = here.shape[0], here.shape[1] // 2
     width = down.shape[1]
     slots = rows // 4
     return pl.pallas_call(
         project_kernel,
-        in_specs=[ANY] + [VMEM] * 5,
+        in_specs=[ANY] + [VMEM] * 3,
         out_specs=[VMEM] * 6,
         out_shape=[jax.ShapeDtypeStruct((slots, width), F32)]
         + [jax.ShapeDtypeStruct((slots, width), BF16)] * 3
@@ -442,7 +468,7 @@
         compiler_params=params(4),
         cost_estimate=cost(8 * rows * units * width, 0),
         name="project",
-    )(tick, *quarters, in_vmem(down))
+    )(tick, here, there, in_vmem(down))
 
 
 def gram_kernel(scale, flips, *refs):
@@ -475,7 +501,7 @@
 
 def gram_piece(tick, pieces, flips, wide, gram=None):
     rows, units = pieces[0].shape
-    cut, depth = 256, 8
+    cut, depth = 512, 4
     operands = [tick, *pieces, in_vmem(wide)]
     in_specs = [ANY] + [VMEM] * (len(pieces) + 1)
     aliases = {}
@@ -518,15 +544,20 @@
     weights = gate_up.reshape(depth, 2, units // lanes, lanes).transpose(0, 2, 1, 3)
 
     packed, placing, factor = pack(tokens, routes.T, pad_mask[None, :], route_weight.T)
-    lefts = [packed] + [across(packed, slot) for slot in (1, 2, 3)]
-    grouped = regroup(packed, weights)
-
-    first_sent, wide = preacts_of(lefts, grouped, 1, 0, chunks)
-    (last_sent,) = preacts_of([wide], grouped, 1, 1, chunks)
+    t2 = across(packed, 2)
+    t1 = across(packed, 1)
+    sent_weights, tick = regroup(packed, weights, 1)
+    tick, t2 = tie(tick, t2)
+    t3 = across(t2, 1)
+    kept_weights, tick = regroup(tick, weights, 0)
+    t1, t3, kept_weights = tie(t1, t3, kept_weights)
+
+    first_sent, wide = preacts_of([packed, t1, t2, t3], sent_weights, 0, chunks)
+    (last_sent,) = preacts_of([wide], sent_weights, 1, chunks)
     got = [swap(first_sent, "row"), swap(last_sent, "row")]
     stays, got_x = [], []
     for h in range(chunks):
-        (kept,) = preacts_of([wide], grouped, 0, h, chunks)
+        (kept,) = preacts_of([wide], kept_weights, h, chunks)
         leaves, stay = leave(kept, got[h])
         wide, leaves = tie(wide, leaves)
         stays.append(stay)
@@ -538,24 +569,22 @@
     z2a = across(hidden_a, 2)
     tick, got_x[1], hidden_a = tie(tick, got_x[1], hidden_a)
     hidden_b, hidden = act(tick, stays[1], got_x[1], hidden_a)
-    z1 = across(hidden, 1)
+    z2b = across(hidden_b, 2)
     hidden_x = swap(hidden, "expert")
-    c_near = swap(hidden, "row")
-    tick, z2a, hidden_b = tie(tick, z2a, hidden_b)
-    z2b = across(hidden_b, 2)
+    tick, z2a, leaves = tie(tick, z2a, hidden)
     z3a = across(z2a, 1)
+    z1 = across(leaves, 1)
     tick, z2b, z1, hidden_x, z3a = tie(tick, z2b, z1, hidden_x, z3a)
 
     leaves, z2 = choose((z2a, z2b), z1)
-    tick, z2b, leaves, sent_x = tie(tick, z2b, leaves, hidden_x)
+    here = join(hidden, hidden_x)
+    tick, z2b, leaves, here = tie(tick, z2b, leaves, here)
     z3b = across(z2b, 1)
     x2 = swap(leaves, "expert")
-    c_far = swap(sent_x, "row")
-    own, s1, s2, s3, hidden_c, tick = project(
-        tick, [hidden, hidden_x, c_near, c_far], down_held
-    )
-    returned = [across(value, slot) for slot, value in ((1, s1), (2, s2), (3, s3))]
-    tick, z3b = tie(tick, z3b)
+    there = swap(here, "row")
+    tick, there = tie(tick, there)
+    own, s1, s2, s3, hidden_c, tick = project(tick, here, there, down_held)
+    tick, z3b, s3 = tie(tick, z3b, s3)
     mine, passed, z3 = pick(hidden, z1, z2, z3a, z3b)
     x3 = lax.ppermute(
         z3,
@@ -563,15 +592,20 @@
         [(ee * 4 + cc, (1 - ee) * 4 + cc) for ee in range(2) for cc in range(4) if cc // 2 == ee],
     )
     mine_near = swap(passed, "row")
+    s3 = across(s3, 3)
     gram, tick = gram_piece(tick, [mine], [(0, 0)], hidden_c)
+    tick, s3, s2 = tie(tick, s3, s2)
+    s2 = across(s2, 2)
     tick, x2, x3 = tie(tick, x2, x3)
     mine_x, passed = pick(hidden_x, x2, x2, x3)
     mine_far = swap(passed, "row")
     tick, mine_near = tie(tick, mine_near)
     gram, tick = gram_piece(tick, [mine_near], [(0, 1)], hidden_c, gram)
+    tick, s2, s1 = tie(tick, s2, s1)
+    s1 = across(s1, 1)
     tick, mine_far = tie(tick, mine_far)
     gram, tick = gram_piece(tick, [mine_x, mine_far], [(1, 0), (1, 1)], hidden_c, gram)
-    return (unpack(tick, placing, factor, own, returned), gram)
+    return (unpack(tick, placing, factor, own, [s1, s2, s3]), gram)
 
 
 def solution(mesh):

time: 74.9 us -> 77.6 us (1.036)
  waiting for transfers between devices: 7.98 us -> 15.9 us
  starting transfers between devices: 28.5 us -> 22.6 us
    ppermute x11, waiting for transfers between devices: 7.09 us -> 15.3 us  [across(): return lax.ppermute(value, 'col', [(i, i ^ slot) for i in range(4)])]
    ppermute x11, starting transfers between devices: 20.5 us -> 13.2 us  [across(): return lax.ppermute(value, 'col', [(i, i ^ slot) for i in range(4)])]
    pallas_call x6 -> x8, Pallas kernels: 14.8 us -> 16.2 us  [the longest x2 8.54 us: regroup(): pl.pallas_call(functools.partial(regroup_kernel, row_flip), in_specs=[ANY...]
    ppermute x1, starting transfers between devices: 2.43 us -> 3.4 us  [on_device(): lax.ppermute(z3, ('expert', 'col'), [(ee * 4 + cc, (1 - ee) * 4 + cc) for...]
    ppermute x10 -> x9, starting transfers between devices: 5.56 us -> 6.02 us  [swap(): return lax.ppermute(value, axis, [(0, 1), (1, 0)])]
  transfers between devices with their start and end apart: 22 -> 21, of which waited for: 7 -> 8; matrix products, arithmetic and copies ran while one was open for 0% -> 0% of each run, Pallas kernels for 44% -> 44%
where the time goes in v6:
time: 77.6 us; the launch traced here: 77.4 us
  Pallas kernels  38 us (49%)
  starting transfers between devices  22.6 us (29%)
  waiting for transfers between devices  15.9 us (20%)
  between operations  0.9 us (1%)
    ppermute x11, waiting for transfers between devices, across(): return lax.ppermute(value, 'col', [(i, i ^ slot) for i in range(4)])  15.3 us
    pallas_call x3, Pallas kernels, gram_piece(): pl.pallas_call(functools.partial(gram_kernel, 2.0 / rows, flips), in_spec...  15 us
    ppermute x11, starting transfers between devices, across(): return lax.ppermute(value, 'col', [(i, i ^ slot) for i in range(4)])  13.2 us
    pallas_call x2, Pallas kernels, regroup(): pl.pallas_call(functools.partial(regroup_kernel, row_flip), in_specs=[ANY...  8.54 us
    pallas_call x4, Pallas kernels, preacts_of(): pl.pallas_call(functools.partial(preact_kernel, first, chunk, chunks), in...  6.08 us
    ppermute x9, starting transfers between devices, swap(): return lax.ppermute(value, axis, [(0, 1), (1, 0)])  6.02 us
    pallas_call x1, Pallas kernels, fetch(): pl.pallas_call(fetch_kernel, in_specs=[ANY, HBM], out_specs=[VMEM, VMEM],...  3.8 us
    ppermute x1, starting transfers between devices, on_device(): lax.ppermute(z3, ('expert', 'col'), [(ee * 4 + cc, (1 - ee) * 4 + cc) for...  3.4 us
  transfers between devices with their start and end apart: 21, of which 8 were waited for; matrix products, arithmetic and copies ran while one was open for 0% of the time, Pallas kernels for 44%

profile of v6, /device:TPU:0, one launch (start us, length us, event | category | flops | bytes accessed | tf_op | source)
XLA Modules:
  0.0 77.4 jit_solution(5948307462630952554)
XLA Ops:
  1.9 4.1 %collective-permute-start.1 = (bf16[32,1536]{1,0:T(8,128)(2,1)S(1)}, bf16[32,1536]{1,0:T(8,128)(2,1)S(1)}, u32[]{:S(2)}, u32[]{:S(2)}) collective-permute-start(bf16[32,1536]{1,0:T(8,128)(2,1)S(1)} %get-tuple-element.81.after_ref.refs_0_), channel_id=1, source_target_pairs={{0,4},{2,6},{4,0},{6,2},{1,5},{3,7},{5,1},{7,3},{8,12},{10,14},{12... | collective-permute-start | bytes 294920 | tf_op jit(solution)/shard_map/ppermute | solution.py:536
  6.0 1.6 %collective-permute-start = (bf16[32,1536]{1,0:T(8,128)(2,1)S(1)}, bf16[32,1536]{1,0:T(8,128)(2,1)S(1)}, u32[]{:S(2)}, u32[]{:S(2)}) collective-permute-start(bf16[32,1536]{1,0:T(8,128)(2,1)S(1)} %get-tuple-element.81.after_ref.refs_0_), channel_id=1, source_target_pairs={{0,2},{2,0},{4,6},{6,4},{1,3},{3,1},{5,7},{7,5},{8,10},{10,8},{12,... | collective-permute-start | bytes 294920 | tf_op jit(solution)/shard_map/ppermute | solution.py:536
  7.6 4.0 %regroup.2 = (bf16[12,1536,2,128]{3,2,1,0:T(2,128)(2,1)S(1)}, f32[8,128]{1,0:T(8,128)S(1)}) custom-call(bf16[32,1536]{1,0:T(8,128)(2,1)S(1)} %get-tuple-element.81.after_ref.refs_0_, bf16[1536,24,2,128]{3,2,1,0:T(2,128)(2,1)} %bitcast.12), custom_call_target="tpu_custom_call" | custom-call | bytes 18874368 | tf_op jit(solution)/shard_map/regroup/pallas_call | solution.py:195
  12.1 4.6 %regroup.3 = (bf16[12,1536,2,128]{3,2,1,0:T(2,128)(2,1)S(1)}, f32[8,128]{1,0:T(8,128)}) custom-call(f32[8,128]{1,0:T(8,128)S(1)} %get-tuple-element.84.after_ref, bf16[1536,24,2,128]{3,2,1,0:T(2,128)(2,1)} %bitcast.13), custom_call_target="tpu_custom_call" | custom-call | bytes 18874368 | tf_op jit(solution)/shard_map/regroup/pallas_call | solution.py:195
  16.7 1.9 %preacts.4 = (f32[256,768]{1,0:T(8,128)S(1)}, bf16[256,3072]{1,0:T(8,128)(2,1)S(1)}) custom-call(bf16[32,1536]{1,0:T(8,128)(2,1)S(1)} %get-tuple-element.81.after_ref.refs_0_, bf16[32,1536]{1,0:T(8,128)(2,1)S(1)} %collective-permute-done.refs_1_, bf16[32,1536]{1,0:T(8,128)(2,1)S(1)} %collective-permute-done.1.refs_2_, ...), custom_call_target="tpu_custom_call" | custom-call | flops 1207959552 | tf_op jit(solution)/shard_map/preacts/pallas_call | solution.py:288
  18.7 1.4 %preacts.7 = f32[256,768]{1,0:T(8,128)S(1)} custom-call(bf16[256,3072]{1,0:T(8,128)(2,1)S(1)} %get-tuple-element.95.refs_0_.after_ref, bf16[12,3072,128]{2,1,0:T(8,128)(2,1)S(1)} %bitcast.11), custom_call_target="tpu_custom_call" | custom-call | flops 1207959552 | tf_op jit(solution)/shard_map/preacts/pallas_call | solution.py:288
  20.7 1.4 %preacts.5.kept_ref = f32[256,768]{1,0:T(8,128)S(1)} custom-call(bf16[256,3072]{1,0:T(8,128)(2,1)S(1)} %get-tuple-element.95.refs_0_.after_ref, bf16[12,3072,128]{2,1,0:T(8,128)(2,1)S(1)} %bitcast.8), custom_call_target="tpu_custom_call" | custom-call | flops 1207959552 | tf_op jit(solution)/shard_map/preacts/pallas_call | solution.py:288
  22.2 1.6 %collective-permute-start.5 = (bf16[256,384]{1,0:T(8,128)(2,1)S(1)}, bf16[256,384]{1,0:T(8,128)(2,1)S(1)}, u32[]{:S(2)}, u32[]{:S(2)}) collective-permute-start(bf16[256,384]{1,0:T(8,128)(2,1)S(1)} %get-tuple-element.97), channel_id=1, source_target_pairs={{0,8},{8,0},{1,9},{9,1},{2,10},{10,2},{3,11},{11,3},{4,12},{12,4},... | collective-permute-start | bytes 589832 | tf_op jit(solution)/shard_map/ppermute | solution.py:532
  25.8 3.8 %fetch_down.1 = (bf16[3072,1536]{1,0:T(8,128)(2,1)S(1)}, f32[8,128]{1,0:T(8,128)S(1)}) custom-call(bf16[256,3072]{1,0:T(8,128)(2,1)S(1)} %get-tuple-element.95.refs_0_.after_ref, bf16[3072,1536]{1,0:T(8,128)(2,1)} %down_ref.1), custom_call_target="tpu_custom_call" | custom-call | bytes 18874368 | tf_op jit(solution)/shard_map/fetch_down/pallas_call | solution.py:229
  30.0 3.0 %collective-permute-start.7 = (bf16[128,384]{1,0:T(8,128)(2,1)S(1)}, bf16[128,384]{1,0:T(8,128)(2,1)S(1)}, u32[]{:S(2)}, u32[]{:S(2)}) collective-permute-start(bf16[128,384]{1,0:T(8,128)(2,1)S(1)} %act.2.refs_0_), channel_id=1, source_target_pairs={{0,4},{2,6},{4,0},{6,2},{1,5},{3,7},{5,1},{7,3},{8,12},{10,14},{12... | collective-permute-start | bytes 294920 | tf_op jit(solution)/shard_map/ppermute | solution.py:536
  33.3 1.6 %collective-permute-start.10 = (bf16[128,768]{1,0:T(8,128)(2,1)S(1)}, bf16[128,768]{1,0:T(8,128)(2,1)S(1)}, u32[]{:S(2)}, u32[]{:S(2)}) collective-permute-start(bf16[128,768]{1,0:T(8,128)(2,1)S(1)} %get-tuple-element.109.left_ref.n0), channel_id=1, source_target_pairs={{0,8},{8,0},{1,9},{9,1},{2,10},{10,2},{3,11},{11,3},{4,12},{12,4},... | collective-permute-start | bytes 589832 | tf_op jit(solution)/shard_map/ppermute | solution.py:532
  34.9 2.3 %collective-permute-done.7.n0 = bf16[128,384]{1,0:T(8,128)(2,1)S(1)} collective-permute-done((bf16[128,384]{1,0:T(8,128)(2,1)S(1)}, bf16[128,384]{1,0:T(8,128)(2,1)S(1)}, u32[]{:S(2)}, u32[]{:S(2)}) %collective-permute-start.7) | collective-permute-done | bytes 98336 | tf_op jit(solution)/shard_map/ppermute | solution.py:536
  37.3 3.0 %collective-permute-start.8 = (bf16[128,384]{1,0:T(8,128)(2,1)S(1)}, bf16[128,384]{1,0:T(8,128)(2,1)S(1)}, u32[]{:S(2)}, u32[]{:S(2)}) collective-permute-start(bf16[128,384]{1,0:T(8,128)(2,1)S(1)} %get-tuple-element.108), channel_id=1, source_target_pairs={{0,4},{2,6},{4,0},{6,2},{1,5},{3,7},{5,1},{7,3},{8,12},{10,14},{12... | collective-permute-start | bytes 294920 | tf_op jit(solution)/shard_map/ppermute | solution.py:536
  40.7 2.5 %collective-permute-done.8.n1 = bf16[128,384]{1,0:T(8,128)(2,1)S(1)} collective-permute-done((bf16[128,384]{1,0:T(8,128)(2,1)S(1)}, bf16[128,384]{1,0:T(8,128)(2,1)S(1)}, u32[]{:S(2)}, u32[]{:S(2)}) %collective-permute-start.8) | collective-permute-done | bytes 98336 | tf_op jit(solution)/shard_map/ppermute | solution.py:536
  43.1 3.2 %collective-permute-done.11.refs_0_ = bf16[128,384]{1,0:T(8,128)(2,1)S(1)} collective-permute-done((bf16[128,384]{1,0:T(8,128)(2,1)S(1)}, bf16[128,384]{1,0:T(8,128)(2,1)S(1)}, u32[]{:S(2)}, u32[]{:S(2)}) %collective-permute-start.11) | collective-permute-done | bytes 98336 | tf_op jit(solution)/shard_map/ppermute | solution.py:536
  46.9 1.5 %collective-permute-start.15 = (bf16[128,768]{1,0:T(8,128)(2,1)S(1)}, bf16[128,768]{1,0:T(8,128)(2,1)S(1)}, u32[]{:S(2)}, u32[]{:S(2)}) collective-permute-start(bf16[128,768]{1,0:T(8,128)(2,1)S(1)} %get-tuple-element.134), channel_id=1, source_target_pairs={{0,8},{8,0},{1,9},{9,1},{2,10},{10,2},{3,11},{11,3},{4,12},{12,4},... | collective-permute-start | bytes 589832 | tf_op jit(solution)/shard_map/ppermute | solution.py:532
  48.4 1.6 %project.1 = (f32[32,1536]{1,0:T(8,128)S(1)}, bf16[32,1536]{1,0:T(8,128)(2,1)S(1)}, bf16[32,1536]{1,0:T(8,128)(2,1)S(1)}, bf16[32,1536]{1,0:T(8,128)(2,1)S(1)}, ...) custom-call(f32[8,128]{1,0:T(8,128)S(1)} %get-tuple-element.118.tick_ref, bf16[128,1536]{1,0:T(8,128)(2,1)S(1)} %join.1.here_ref, ...), custom_call_target="tpu_custom_call" | custom-call | flops 1207959552 | tf_op jit(solution)/shard_map/project/pallas_call | solution.py:460
  50.0 1.8 %collective-permute-done.13.refs_1_ = bf16[128,384]{1,0:T(8,128)(2,1)S(1)} collective-permute-done((bf16[128,384]{1,0:T(8,128)(2,1)S(1)}, bf16[128,384]{1,0:T(8,128)(2,1)S(1)}, u32[]{:S(2)}, u32[]{:S(2)}) %collective-permute-start.13) | collective-permute-done | bytes 98336 | tf_op jit(solution)/shard_map/ppermute | solution.py:536
  51.8 3.4 %collective-permute-start.16 = (bf16[128,768]{1,0:T(8,128)(2,1)S(1)}, bf16[128,768]{1,0:T(8,128)(2,1)S(1)}, u32[]{:S(2)}, u32[]{:S(2)}) collective-permute-start(bf16[128,768]{1,0:T(8,128)(2,1)S(1)} %get-tuple-element.135), channel_id=1, source_target_pairs={{0,8},{2,10},{12,4},{14,6},{1,9},{3,11},{13,5},{15,7},{16,24},{18,... | collective-permute-start | bytes 589832 | tf_op jit(solution)/shard_map/ppermute | solution.py:589
  55.4 4.1 %gram.3 = (f32[3072,3072]{1,0:T(8,128)}, f32[8,128]{1,0:T(8,128)S(1)}) custom-call(f32[8,128]{1,0:T(8,128)S(1)} %get-tuple-element.124.refs_0_, bf16[128,768]{1,0:T(8,128)(2,1)S(1)} %get-tuple-element.128.refs_1_, bf16[128,3072]{1,0:T(8,128)(2,1)S(1)} %get-tuple-element.129.refs_2_.refs_3_), custom_call_target="tpu_custom_call" | custom-call | flops 603979776 | bytes 9437184 | tf_op jit(solution)/shard_map/gram/pallas_call | solution.py:512
  59.5 2.3 %collective-permute-done.14.r3_ref = bf16[32,1536]{1,0:T(8,128)(2,1)S(1)} collective-permute-done((bf16[32,1536]{1,0:T(8,128)(2,1)S(1)}, bf16[32,1536]{1,0:T(8,128)(2,1)S(1)}, u32[]{:S(2)}, u32[]{:S(2)}) %collective-permute-start.14) | collective-permute-done | bytes 98336 | tf_op jit(solution)/shard_map/ppermute | solution.py:536
  62.1 4.1 %gram.4 = (f32[3072,3072]{1,0:T(8,128)}, f32[8,128]{1,0:T(8,128)S(1)}) custom-call(f32[8,128]{1,0:T(8,128)S(1)} %get-tuple-element.138.refs_0_, bf16[128,768]{1,0:T(8,128)(2,1)S(1)} %collective-permute-done.17.refs_1_, bf16[128,3072]{1,0:T(8,128)(2,1)S(1)} %get-tuple-element.129.refs_2_.refs_3_, ...), custom_call_target="tpu_custom_call", output_to_operand_aliasing={{0}: (3, {})} | custom-call | flops 603979776 | bytes 9437184 | tf_op jit(solution)/shard_map/gram/pallas_call | solution.py:512
  66.2 3.2 %collective-permute-done.18.r2_ref = bf16[32,1536]{1,0:T(8,128)(2,1)S(1)} collective-permute-done((bf16[32,1536]{1,0:T(8,128)(2,1)S(1)}, bf16[32,1536]{1,0:T(8,128)(2,1)S(1)}, u32[]{:S(2)}, u32[]{:S(2)}) %collective-permute-start.18) | collective-permute-done | bytes 98336 | tf_op jit(solution)/shard_map/ppermute | solution.py:536
  69.5 6.9 %gram.5 = (f32[3072,3072]{1,0:T(8,128)}, f32[8,128]{1,0:T(8,128)S(1)}) custom-call(f32[8,128]{1,0:T(8,128)S(1)} %get-tuple-element.148.refs_0_, bf16[128,768]{1,0:T(8,128)(2,1)S(1)} %get-tuple-element.149.refs_1_, bf16[128,768]{1,0:T(8,128)(2,1)S(1)} %collective-permute-done.19.refs_2_, ...), custom_call_target="tpu_custom_call", output_to_operand_aliasing={{0}: (4, {})} | custom-call | flops 1207959552 | bytes 18874368 | tf_op jit(solution)/shard_map/gram/pallas_call | solution.py:512
  (39 shorter events, 7.9 us)
Async XLA Ops:
  1.9 9.7 %collective-permute-start.1 = (bf16[32,1536]{1,0:T(8,128)(2,1)S(1)}, bf16[32,1536]{1,0:T(8,128)(2,1)S(1)}, u32[]{:S(2)}, u32[]{:S(2)}) collective-permute-start(bf16[32,1536]{1,0:T(8,128)(2,1)S(1)} %get-tuple-element.81.after_ref.refs_0_), channel_id=1, source_target_pairs={{0,4},{2,6},{4,0},{6,2},{1,5},{3,7},{5,1},{7,3},{8,12},{10,14},{12... | collective-permute-start | bytes 294920 | tf_op jit(solution)/shard_map/ppermute | solution.py:536
  6.0 10.7 %collective-permute-start = (bf16[32,1536]{1,0:T(8,128)(2,1)S(1)}, bf16[32,1536]{1,0:T(8,128)(2,1)S(1)}, u32[]{:S(2)}, u32[]{:S(2)}) collective-permute-start(bf16[32,1536]{1,0:T(8,128)(2,1)S(1)} %get-tuple-element.81.after_ref.refs_0_), channel_id=1, source_target_pairs={{0,2},{2,0},{4,6},{6,4},{1,3},{3,1},{5,7},{7,5},{8,10},{10,8},{12,... | collective-permute-start | bytes 294920 | tf_op jit(solution)/shard_map/ppermute | solution.py:536
  11.6 5.1 %collective-permute-start.2 = (bf16[32,1536]{1,0:T(8,128)(2,1)S(1)}, bf16[32,1536]{1,0:T(8,128)(2,1)S(1)}, u32[]{:S(2)}, u32[]{:S(2)}) collective-permute-start(bf16[32,1536]{1,0:T(8,128)(2,1)S(1)} %collective-permute-done.1.refs_2_), channel_id=1, source_target_pairs={{0,2},{2,0},{4,6},{6,4},{1,3},{3,1},{5,7},{7,5},{8,10},{10,8},{12,... | collective-permute-start | bytes 294920 | tf_op jit(solution)/shard_map/ppermute | solution.py:536
  18.6 3.4 %collective-permute-start.3 = (f32[256,768]{1,0:T(8,128)S(1)}, f32[256,768]{1,0:T(8,128)S(1)}, u32[]{:S(2)}, u32[]{:S(2)}) collective-permute-start(f32[256,768]{1,0:T(8,128)S(1)} %get-tuple-element.91), channel_id=1, source_target_pairs={{0,1},{1,0},{2,3},{3,2},{4,5},{5,4},{6,7},{7,6},{8,9},{9,8},{10,11... | collective-permute-start | bytes 2359304 | tf_op jit(solution)/shard_map/ppermute | solution.py:532
  20.1 5.0 %collective-permute-start.4 = (f32[256,768]{1,0:T(8,128)S(1)}, f32[256,768]{1,0:T(8,128)S(1)}, u32[]{:S(2)}, u32[]{:S(2)}) collective-permute-start(f32[256,768]{1,0:T(8,128)S(1)} %preacts.7), channel_id=1, source_target_pairs={{0,1},{1,0},{2,3},{3,2},{4,5},{5,4},{6,7},{7,6},{8,9},{9,8},{10,11... | collective-permute-start | bytes 2359304 | tf_op jit(solution)/shard_map/ppermute | solution.py:532
  22.2 7.8 %collective-permute-start.5 = (bf16[256,384]{1,0:T(8,128)(2,1)S(1)}, bf16[256,384]{1,0:T(8,128)(2,1)S(1)}, u32[]{:S(2)}, u32[]{:S(2)}) collective-permute-start(bf16[256,384]{1,0:T(8,128)(2,1)S(1)} %get-tuple-element.97), channel_id=1, source_target_pairs={{0,8},{8,0},{1,9},{9,1},{2,10},{10,2},{3,11},{11,3},{4,12},{12,4},... | collective-permute-start | bytes 589832 | tf_op jit(solution)/shard_map/ppermute | solution.py:532
  25.2 8.1 %collective-permute-start.6 = (bf16[256,384]{1,0:T(8,128)(2,1)S(1)}, bf16[256,384]{1,0:T(8,128)(2,1)S(1)}, u32[]{:S(2)}, u32[]{:S(2)}) collective-permute-start(bf16[256,384]{1,0:T(8,128)(2,1)S(1)} %get-tuple-element.99), channel_id=1, source_target_pairs={{0,8},{8,0},{1,9},{9,1},{2,10},{10,2},{3,11},{11,3},{4,12},{12,4},... | collective-permute-start | bytes 589832 | tf_op jit(solution)/shard_map/ppermute | solution.py:532
  30.0 7.1 %collective-permute-start.7 = (bf16[128,384]{1,0:T(8,128)(2,1)S(1)}, bf16[128,384]{1,0:T(8,128)(2,1)S(1)}, u32[]{:S(2)}, u32[]{:S(2)}) collective-permute-start(bf16[128,384]{1,0:T(8,128)(2,1)S(1)} %act.2.refs_0_), channel_id=1, source_target_pairs={{0,4},{2,6},{4,0},{6,2},{1,5},{3,7},{5,1},{7,3},{8,12},{10,14},{12... | collective-permute-start | bytes 294920 | tf_op jit(solution)/shard_map/ppermute | solution.py:536
  33.3 9.8 %collective-permute-start.10 = (bf16[128,768]{1,0:T(8,128)(2,1)S(1)}, bf16[128,768]{1,0:T(8,128)(2,1)S(1)}, u32[]{:S(2)}, u32[]{:S(2)}) collective-permute-start(bf16[128,768]{1,0:T(8,128)(2,1)S(1)} %get-tuple-element.109.left_ref.n0), channel_id=1, source_target_pairs={{0,8},{8,0},{1,9},{9,1},{2,10},{10,2},{3,11},{11,3},{4,12},{12,4},... | collective-permute-start | bytes 589832 | tf_op jit(solution)/shard_map/ppermute | solution.py:532
  37.2 9.2 %collective-permute-start.9 = (bf16[128,768]{1,0:T(8,128)(2,1)S(1)}, bf16[128,768]{1,0:T(8,128)(2,1)S(1)}, u32[]{:S(2)}, u32[]{:S(2)}) collective-permute-start(bf16[128,768]{1,0:T(8,128)(2,1)S(1)} %get-tuple-element.109.left_ref.n0), channel_id=1, source_target_pairs={{0,2},{2,0},{4,6},{6,4},{1,3},{3,1},{5,7},{7,5},{8,10},{10,8},{12,... | collective-permute-start | bytes 589832 | tf_op jit(solution)/shard_map/ppermute | solution.py:536
  37.3 5.8 %collective-permute-start.8 = (bf16[128,384]{1,0:T(8,128)(2,1)S(1)}, bf16[128,384]{1,0:T(8,128)(2,1)S(1)}, u32[]{:S(2)}, u32[]{:S(2)}) collective-permute-start(bf16[128,384]{1,0:T(8,128)(2,1)S(1)} %get-tuple-element.108), channel_id=1, source_target_pairs={{0,4},{2,6},{4,0},{6,2},{1,5},{3,7},{5,1},{7,3},{8,12},{10,14},{12... | collective-permute-start | bytes 294920 | tf_op jit(solution)/shard_map/ppermute | solution.py:536
  40.3 6.0 %collective-permute-start.11 = (bf16[128,384]{1,0:T(8,128)(2,1)S(1)}, bf16[128,384]{1,0:T(8,128)(2,1)S(1)}, u32[]{:S(2)}, u32[]{:S(2)}) collective-permute-start(bf16[128,384]{1,0:T(8,128)(2,1)S(1)} %collective-permute-done.7.n0), channel_id=1, source_target_pairs={{0,2},{2,0},{4,6},{6,4},{1,3},{3,1},{5,7},{7,5},{8,10},{10,8},{12,... | collective-permute-start | bytes 294920 | tf_op jit(solution)/shard_map/ppermute | solution.py:536
  46.5 1.9 %collective-permute-start.12 = (bf16[128,1536]{1,0:T(8,128)(2,1)S(1)}, bf16[128,1536]{1,0:T(8,128)(2,1)S(1)}, u32[]{:S(2)}, u32[]{:S(2)}) collective-permute-start(bf16[128,1536]{1,0:T(8,128)(2,1)S(1)} %join.1.here_ref), channel_id=1, source_target_pairs={{0,1},{1,0},{2,3},{3,2},{4,5},{5,4},{6,7},{7,6},{8,9},{9,8},{10,11... | collective-permute-start | bytes 1179656 | tf_op jit(solution)/shard_map/ppermute | solution.py:532
  46.5 5.2 %collective-permute-start.13 = (bf16[128,384]{1,0:T(8,128)(2,1)S(1)}, bf16[128,384]{1,0:T(8,128)(2,1)S(1)}, u32[]{:S(2)}, u32[]{:S(2)}) collective-permute-start(bf16[128,384]{1,0:T(8,128)(2,1)S(1)} %collective-permute-done.8.n1), channel_id=1, source_target_pairs={{0,2},{2,0},{4,6},{6,4},{1,3},{3,1},{5,7},{7,5},{8,10},{10,8},{12,... | collective-permute-start | bytes 294920 | tf_op jit(solution)/shard_map/ppermute | solution.py:536
  46.9 14.8 %collective-permute-start.15 = (bf16[128,768]{1,0:T(8,128)(2,1)S(1)}, bf16[128,768]{1,0:T(8,128)(2,1)S(1)}, u32[]{:S(2)}, u32[]{:S(2)}) collective-permute-start(bf16[128,768]{1,0:T(8,128)(2,1)S(1)} %get-tuple-element.134), channel_id=1, source_target_pairs={{0,8},{8,0},{1,9},{9,1},{2,10},{10,2},{3,11},{11,3},{4,12},{12,4},... | collective-permute-start | bytes 589832 | tf_op jit(solution)/shard_map/ppermute | solution.py:532
  51.8 9.9 %collective-permute-start.16 = (bf16[128,768]{1,0:T(8,128)(2,1)S(1)}, bf16[128,768]{1,0:T(8,128)(2,1)S(1)}, u32[]{:S(2)}, u32[]{:S(2)}) collective-permute-start(bf16[128,768]{1,0:T(8,128)(2,1)S(1)} %get-tuple-element.135), channel_id=1, source_target_pairs={{0,8},{2,10},{12,4},{14,6},{1,9},{3,11},{13,5},{15,7},{16,24},{18,... | collective-permute-start | bytes 589832 | tf_op jit(solution)/shard_map/ppermute | solution.py:589
  55.2 6.5 %collective-permute-start.14 = (bf16[32,1536]{1,0:T(8,128)(2,1)S(1)}, bf16[32,1536]{1,0:T(8,128)(2,1)S(1)}, u32[]{:S(2)}, u32[]{:S(2)}) collective-permute-start(bf16[32,1536]{1,0:T(8,128)(2,1)S(1)} %get-tuple-element.131), channel_id=1, source_target_pairs={{0,6},{2,4},{4,2},{6,0},{1,7},{3,5},{5,3},{7,1},{8,14},{10,12},{12... | collective-permute-start | bytes 294920 | tf_op jit(solution)/shard_map/ppermute | solution.py:536
  55.3 6.8 %collective-permute-start.17 = (bf16[128,768]{1,0:T(8,128)(2,1)S(1)}, bf16[128,768]{1,0:T(8,128)(2,1)S(1)}, u32[]{:S(2)}, u32[]{:S(2)}) collective-permute-start(bf16[128,768]{1,0:T(8,128)(2,1)S(1)} %get-tuple-element.137), channel_id=1, source_target_pairs={{0,1},{1,0},{2,3},{3,2},{4,5},{5,4},{6,7},{7,6},{8,9},{9,8},{10,11... | collective-permute-start | bytes 589832 | tf_op jit(solution)/shard_map/ppermute | solution.py:532
  62.0 7.5 %collective-permute-start.19 = (bf16[128,768]{1,0:T(8,128)(2,1)S(1)}, bf16[128,768]{1,0:T(8,128)(2,1)S(1)}, u32[]{:S(2)}, u32[]{:S(2)}) collective-permute-start(bf16[128,768]{1,0:T(8,128)(2,1)S(1)} %get-tuple-element.147), channel_id=1, source_target_pairs={{0,1},{1,0},{2,3},{3,2},{4,5},{5,4},{6,7},{7,6},{8,9},{9,8},{10,11... | collective-permute-start | bytes 589832 | tf_op jit(solution)/shard_map/ppermute | solution.py:532
  62.1 7.4 %collective-permute-start.18 = (bf16[32,1536]{1,0:T(8,128)(2,1)S(1)}, bf16[32,1536]{1,0:T(8,128)(2,1)S(1)}, u32[]{:S(2)}, u32[]{:S(2)}) collective-permute-start(bf16[32,1536]{1,0:T(8,128)(2,1)S(1)} %get-tuple-element.142), channel_id=1, source_target_pairs={{0,4},{2,6},{4,0},{6,2},{1,5},{3,7},{5,1},{7,3},{8,12},{10,14},{12... | collective-permute-start | bytes 294920 | tf_op jit(solution)/shard_map/ppermute | solution.py:536
  69.5 6.9 %collective-permute-start.20 = (bf16[32,1536]{1,0:T(8,128)(2,1)S(1)}, bf16[32,1536]{1,0:T(8,128)(2,1)S(1)}, u32[]{:S(2)}, u32[]{:S(2)}) collective-permute-start(bf16[32,1536]{1,0:T(8,128)(2,1)S(1)} %get-tuple-element.156), channel_id=1, source_target_pairs={{0,2},{2,0},{4,6},{6,4},{1,3},{3,1},{5,7},{7,5},{8,10},{10,8},{12,... | collective-permute-start | bytes 294920 | tf_op jit(solution)/shard_map/ppermute | solution.py:536

commit v7 on v5

--- a/solution.py
+++ b/solution.py
@@ -125,9 +125,11 @@
     factor = jnp.sum(placing * weight, axis=1, keepdims=True)
     factor_ref[...] = jnp.broadcast_to(factor, factor_ref.shape)
     copies[3].wait()
-    packed_ref[...] = jnp.dot(
+    packed = jnp.dot(
         placing.astype(BF16), tokens_held[...], preferred_element_type=F32
     ).astype(BF16)
+    for i in range(packed_ref.shape[0] // slots):
+        packed_ref[slots * i : slots * (i + 1), :] = packed
 
 
 def pack(tokens, routes_t, pad, weight_t):
@@ -139,7 +141,7 @@
         in_specs=[HBM] * 4,
         out_specs=[VMEM] * 3,
         out_shape=[
-            pltpu.VMEM((slots, depth), BF16),
+            pltpu.VMEM((4 * slots, depth), BF16),
             pltpu.VMEM((slots, rows), BF16),
             pltpu.VMEM((slots, 128), F32),
         ],
@@ -150,25 +152,30 @@
     )(*(in_hbm(x) for x in operands))
 
 
-def unpack_kernel(after_ref, placing_ref, factor_ref, own_ref, r1_ref, r2_ref, r3_ref, out_ref):
+def unpack_kernel(after_ref, placing_ref, factor_ref, own_ref, parts_ref, out_ref):
     del after_ref
-    total = own_ref[...] + r1_ref[...].astype(F32) + r2_ref[...].astype(F32) + r3_ref[...].astype(F32)
+    slots = own_ref.shape[0]
+    here = lax.axis_index("col")
+    total = own_ref[...]
+    for slot in range(1, parts_ref.shape[0] // slots):
+        at = pl.multiple_of((here ^ slot) * slots, slots)
+        total = total + parts_ref[pl.ds(at, slots), :].astype(F32)
     scaled = (total * factor_ref[:, 0:1]).astype(BF16)
     out_ref[...] = lax.dot_general(
         placing_ref[...], scaled, (((0,), (0,)), ((), ())), preferred_element_type=F32
     ).astype(BF16)
 
 
-def unpack(done, placing, factor, own, returned):
+def unpack(done, placing, factor, own, parts):
     slots, rows = placing.shape
     return pl.pallas_call(
         unpack_kernel,
-        in_specs=[ANY] + [VMEM] * 6,
+        in_specs=[ANY] + [VMEM] * 4,
         out_specs=VMEM,
         out_shape=jax.ShapeDtypeStruct((rows, own.shape[1]), BF16),
         compiler_params=params(4),
         name="unpack",
-    )(done, placing, factor, own, *returned)
+    )(done, placing, factor, own, parts)
 
 
 def regroup_kernel(after_ref, weights_ref, out_ref, sems):
@@ -228,32 +235,27 @@
     )(behind, in_hbm(down))
 
 
-def widen_tokens(x_refs, wide_ref):
-    slots, depth = x_refs[0].shape
-    rows = 4 * slots
-    here = lax.axis_index("col")
+def widen_tokens(x_ref, wide_ref):
+    rows, depth = x_ref.shape
     cut = 256
     into = lax.broadcasted_iota(jnp.int32, (cut, 4 * cut), 1)
     out_of = lax.broadcasted_iota(jnp.int32, (cut, 4 * cut), 0)
     half = jnp.where(into < 2 * cut, 0, 1)
     widen = jnp.where(into - 2 * cut * half == 2 * out_of + half, 1.0, 0.0).astype(BF16)
-    for slot, x_ref in enumerate(x_refs):
-        stacked = jnp.concatenate(
-            [x_ref[:, cut * k : cut * (k + 1)] for k in range(depth // cut)], axis=0
-        )
-        spaced = jnp.dot(stacked, widen, preferred_element_type=F32).astype(BF16)
+    for k in range(depth // cut):
+        spaced = jnp.dot(
+            x_ref[:, cut * k : cut * (k + 1)], widen, preferred_element_type=F32
+        ).astype(BF16)
         for h in range(2):
-            at = pl.multiple_of(h * rows + (here ^ slot) * slots, slots)
-            for k in range(depth // cut):
-                wide_ref[pl.ds(at, slots), 2 * cut * k : 2 * cut * (k + 1)] = spaced[
-                    slots * k : slots * (k + 1), 2 * cut * h : 2 * cut * (h + 1)
-                ]
+            wide_ref[rows * h : rows * (h + 1), 2 * cut * k : 2 * cut * (k + 1)] = spaced[
+                :, 2 * cut * h : 2 * cut * (h + 1)
+            ]
 
 
 def preact_kernel(first, row_flip, chunk, chunks, *refs):
     if first:
-        x0, x1, x2, x3, w_ref, out_ref, wide_ref = refs
-        widen_tokens((x0, x1, x2, x3), wide_ref)
+        x_ref, w_ref, out_ref, wide_ref = refs
+        widen_tokens(x_ref, wide_ref)
     else:
         wide_ref, w_ref, out_ref = refs
     tiles, _, lanes = w_ref.shape
@@ -270,23 +272,22 @@
         )
 
 
-def preacts_of(lefts, weights, row_flip, chunk, chunks):
+def preacts_of(left, weights, row_flip, chunk, chunks, first=False):
     tiles, depth2, lanes = weights.shape
-    first = len(lefts) > 1
-    rows = 4 * lefts[0].shape[0] if first else lefts[0].shape[0] // 2
+    rows = left.shape[0] if first else left.shape[0] // 2
     units = tiles // 4 // chunks * lanes
     out_shape = [jax.ShapeDtypeStruct((2 * rows, 2 * units), F32)]
     if first:
         out_shape.append(pltpu.VMEM((2 * rows, depth2), BF16))
     return pl.pallas_call(
         functools.partial(preact_kernel, first, row_flip, chunk, chunks),
-        in_specs=[VMEM] * (len(lefts) + 1),
+        in_specs=[VMEM] * 2,
         out_specs=[VMEM] * len(out_shape),
         out_shape=out_shape,
         compiler_params=params(4),
         cost_estimate=cost(8 * rows * depth2 * units, 0),
         name="preacts_" + ("sent" if row_flip else "kept"),
-    )(*lefts, in_vmem(weights))
+    )(left, in_vmem(weights))
 
 
 def leave_kernel(kept_ref, got_ref, leaves_ref, stays_ref):
@@ -407,7 +408,7 @@
 
 
 def project_kernel(
-    tick_ref, h0, h1, h2, h3, down_ref, own_ref, s1_ref, s2_ref, s3_ref, wide_ref, done_ref, total_ref
+    tick_ref, h0, h1, h2, h3, down_ref, own_ref, parts_ref, wide_ref, done_ref
 ):
     del tick_ref
     units = h0.shape[1]
@@ -417,14 +418,16 @@
     done_ref[...] = jnp.zeros_like(done_ref)
     slots, width = own_ref.shape
     cut = 512
+    here = lax.axis_index("col")
     for n in range(width // cut):
-        total_ref[:, cut * n : cut * (n + 1)] = jnp.dot(
-            wide_ref[...], down_ref[:, cut * n : cut * (n + 1)], preferred_element_type=F32
-        )
-    here = lax.axis_index("col")
-    for slot, out_ref in enumerate((own_ref, s1_ref, s2_ref, s3_ref)):
-        at = pl.multiple_of((here ^ slot) * slots, slots)
-        out_ref[...] = total_ref[pl.ds(at, slots), :].astype(out_ref.dtype)
+        columns = slice(cut * n, cut * (n + 1))
+        total = jnp.dot(wide_ref[...], down_ref[:, columns], preferred_element_type=F32)
+        parts_ref[:, columns] = total.astype(BF16)
+        for col in range(parts_ref.shape[0] // slots):
+
+            @pl.when(here == col)
+            def _():
+                own_ref[:, columns] = total[slots * col : slots * (col + 1), :]
 
 
 def project(tick, quarters, down):
@@ -434,11 +437,13 @@
     return pl.pallas_call(
         project_kernel,
         in_specs=[ANY] + [VMEM] * 5,
-        out_specs=[VMEM] * 6,
-        out_shape=[jax.ShapeDtypeStruct((slots, width), F32)]
-        + [jax.ShapeDtypeStruct((slots, width), BF16)] * 3
-        + [pltpu.VMEM((rows, 4 * units), BF16), pltpu.VMEM((8, 128), F32)],
-        scratch_shapes=[pltpu.VMEM((rows, width), F32)],
+        out_specs=[VMEM] * 4,
+        out_shape=[
+            jax.ShapeDtypeStruct((slots, width), F32),
+            jax.ShapeDtypeStruct((rows, width), BF16),
+            pltpu.VMEM((rows, 4 * units), BF16),
+            pltpu.VMEM((8, 128), F32),
+        ],
         compiler_params=params(4),
         cost_estimate=cost(8 * rows * units * width, 0),
         name="project",
@@ -475,7 +480,7 @@
 
 def gram_piece(tick, pieces, flips, wide, gram=None):
     rows, units = pieces[0].shape
-    cut, depth = 256, 8
+    cut, depth = 512, 4
     operands = [tick, *pieces, in_vmem(wide)]
     in_specs = [ANY] + [VMEM] * (len(pieces) + 1)
     aliases = {}
@@ -518,15 +523,15 @@
     weights = gate_up.reshape(depth, 2, units // lanes, lanes).transpose(0, 2, 1, 3)
 
     packed, placing, factor = pack(tokens, routes.T, pad_mask[None, :], route_weight.T)
-    lefts = [packed] + [across(packed, slot) for slot in (1, 2, 3)]
+    gathered = lax.all_to_all(packed, "col", 0, 0, tiled=True)
     grouped = regroup(packed, weights)
 
-    first_sent, wide = preacts_of(lefts, grouped, 1, 0, chunks)
-    (last_sent,) = preacts_of([wide], grouped, 1, 1, chunks)
+    first_sent, wide = preacts_of(gathered, grouped, 1, 0, chunks, True)
+    (last_sent,) = preacts_of(wide, grouped, 1, 1, chunks)
     got = [swap(first_sent, "row"), swap(last_sent, "row")]
     stays, got_x = [], []
     for h in range(chunks):
-        (kept,) = preacts_of([wide], grouped, 0, h, chunks)
+        (kept,) = preacts_of(wide, grouped, 0, h, chunks)
         leaves, stay = leave(kept, got[h])
         wide, leaves = tie(wide, leaves)
         stays.append(stay)
@@ -551,10 +556,10 @@
     z3b = across(z2b, 1)
     x2 = swap(leaves, "expert")
     c_far = swap(sent_x, "row")
-    own, s1, s2, s3, hidden_c, tick = project(
+    own, parts, hidden_c, tick = project(
         tick, [hidden, hidden_x, c_near, c_far], down_held
     )
-    returned = [across(value, slot) for slot, value in ((1, s1), (2, s2), (3, s3))]
+    returned = lax.all_to_all(parts, "col", 0, 0, tiled=True)
     tick, z3b = tie(tick, z3b)
     mine, passed, z3 = pick(hidden, z1, z2, z3a, z3b)
     x3 = lax.ppermute(

time: 74.9 us -> 91.6 us (1.22)
  local copies, waits for them, and re-layouts: 0 us -> 14.9 us
    unnamed x0 -> x14, local copies, waits for them, and re-layouts: none -> 14.9 us
    ppermute x11 -> x5, starting transfers between devices: 20.5 us -> 9.59 us  [across(): return lax.ppermute(value, 'col', [(i, i ^ slot) for i in range(4)])]
    all_to_all x0 -> x2, starting transfers between devices: none -> 10.1 us  [the longest x1 6.33 us: on_device(): gathered = lax.all_to_all(packed, 'col', 0, 0, tiled=True)]
    ppermute x1, waiting for transfers between devices: 0.01 us -> 1.6 us  [on_device(): lax.ppermute(z3, ('expert', 'col'), [(ee * 4 + cc, (1 - ee) * 4 + cc) for...]
    pallas_call x1, Pallas kernels: 1.61 us -> 2.55 us  [project(): pl.pallas_call(project_kernel, in_specs=[ANY] + [VMEM] * 5, out_specs=[VM...]
    ppermute x11 -> x5, waiting for transfers between devices: 7.09 us -> 6.49 us  [across(): return lax.ppermute(value, 'col', [(i, i ^ slot) for i in range(4)])]
  transfers between devices with their start and end apart: 22 -> 18, of which waited for: 7 -> 5; matrix products, arithmetic and copies ran while one was open for 0% -> 0% of each run, Pallas kernels for 44% -> 36%
where the time goes in v7:
time: 91.6 us; the launch traced here: 90.9 us
  Pallas kernels  38 us (41%)
  starting transfers between devices  28.6 us (31%)
  local copies, waits for them, and re-layouts  14.9 us (16%)
  waiting for transfers between devices  8.56 us (9%)
  between operations  0.92 us (1%)
    pallas_call x3, Pallas kernels, gram_piece(): pl.pallas_call(functools.partial(gram_kernel, 2.0 / rows, flips), in_spec...  15 us
    unnamed x14, local copies, waits for them, and re-layouts  14.9 us
    ppermute x5, starting transfers between devices, across(): return lax.ppermute(value, 'col', [(i, i ^ slot) for i in range(4)])  9.59 us
    pallas_call x1, Pallas kernels, regroup(): pl.pallas_call(regroup_kernel, in_specs=[ANY, HBM], out_specs=VMEM, out_s...  6.97 us
    ppermute x5, waiting for transfers between devices, across(): return lax.ppermute(value, 'col', [(i, i ^ slot) for i in range(4)])  6.49 us
    all_to_all x1, starting transfers between devices, on_device(): gathered = lax.all_to_all(packed, 'col', 0, 0, tiled=True)  6.33 us
    ppermute x10, starting transfers between devices, swap(): return lax.ppermute(value, axis, [(0, 1), (1, 0)])  6.31 us
    pallas_call x4, Pallas kernels, preacts_of(): pl.pallas_call(functools.partial(preact_kernel, first, row_flip, chunk, c...  5.96 us
  transfers between devices with their start and end apart: 18, of which 5 were waited for; matrix products, arithmetic and copies ran while one was open for 0% of the time, Pallas kernels for 36%

profile of v7, /device:TPU:0, one launch (start us, length us, event | category | flops | bytes accessed | tf_op | source)
XLA Modules:
  0.0 90.9 jit_solution(16848273068244513996)
XLA Ops:
  0.6 2.0 %pack.1 = (bf16[128,1536]{1,0:T(8,128)(2,1)}, bf16[32,128]{1,0:T(8,128)(2,1)S(1)}, f32[32,128]{1,0:T(8,128)S(1)}) custom-call(bf16[128,1536]{1,0:T(8,128)(2,1)} %tokens_ref.1, s32[2,128]{1,0:T(2,128)} %bitcast.20, s32[1,128]{1,0:T(1,128)} %bitcast.22, f32[2,128]{1,0:T(2,128)} %bitcast.21), custom_call_target="tpu_custom_call" | custom-call | tf_op jit(solution)/shard_map/pack/pallas_call | solution.py:139
  2.7 6.3 %all-to-all-start = ((bf16[4,32,1536]{2,1,0:T(8,128)(2,1)}), bf16[4,32,1536]{2,1,0:T(8,128)(2,1)S(1)}, u32[]{:S(2)}, u32[]{:S(2)}) async-start(bf16[4,32,1536]{2,1,0:T(8,128)(2,1)} %bitcast.3), calls=%async_computation | async-start | bytes 786432 | tf_op jit(solution)/shard_map/all_to_all | solution.py:526
  9.0 7.0 %regroup.1 = bf16[24,1536,2,128]{3,2,1,0:T(2,128)(2,1)S(1)} custom-call(bf16[128,1536]{1,0:T(8,128)(2,1)} %get-tuple-element.62.after_ref, bf16[1536,24,2,128]{3,2,1,0:T(2,128)(2,1)} %bitcast.19), custom_call_target="tpu_custom_call" | custom-call | bytes 37748736 | tf_op jit(solution)/shard_map/regroup/pallas_call | solution.py:195
  16.0 6.8 %copy-done = bf16[24,1536,2,128]{3,2,1,0:T(2,128)(2,1)} copy-done((bf16[24,1536,2,128]{3,2,1,0:T(2,128)(2,1)}, bf16[24,1536,2,128]{3,2,1,0:T(2,128)(2,1)S(1)}, u32[]{:S(2)}) %copy-start) | copy-done | bytes 18874392
  22.8 6.4 %copy-done.1 = bf16[24,1536,2,128]{3,2,1,0:T(2,128)(2,1)S(1)} copy-done((bf16[24,1536,2,128]{3,2,1,0:T(2,128)(2,1)S(1)}, bf16[24,1536,2,128]{3,2,1,0:T(2,128)(2,1)}, u32[]{:S(2)}) %copy-start.1) | copy-done | bytes 18874392
  29.2 1.8 %preacts_sent.2 = (f32[256,768]{1,0:T(8,128)S(1)}, bf16[256,3072]{1,0:T(8,128)(2,1)S(1)}) custom-call(bf16[128,1536]{1,0:T(8,128)(2,1)S(1)} %bitcast.18, bf16[24,3072,128]{2,1,0:T(8,128)(2,1)S(1)} %bitcast.11), custom_call_target="tpu_custom_call" | custom-call | flops 1207959552 | tf_op jit(solution)/shard_map/preacts_sent/pallas_call | solution.py:282
  31.1 1.4 %preacts_sent.3 = f32[256,768]{1,0:T(8,128)S(1)} custom-call(bf16[256,3072]{1,0:T(8,128)(2,1)S(1)} %get-tuple-element.68.refs_0_.after_ref, bf16[24,3072,128]{2,1,0:T(8,128)(2,1)S(1)} %bitcast.12), custom_call_target="tpu_custom_call" | custom-call | flops 1207959552 | tf_op jit(solution)/shard_map/preacts_sent/pallas_call | solution.py:282
  34.6 1.6 %collective-permute-start.2 = (bf16[256,384]{1,0:T(8,128)(2,1)S(1)}, bf16[256,384]{1,0:T(8,128)(2,1)S(1)}, u32[]{:S(2)}, u32[]{:S(2)}) collective-permute-start(bf16[256,384]{1,0:T(8,128)(2,1)S(1)} %get-tuple-element.70), channel_id=1, source_target_pairs={{0,8},{8,0},{1,9},{9,1},{2,10},{10,2},{3,11},{11,3},{4,12},{12,4},... | collective-permute-start | bytes 589832 | tf_op jit(solution)/shard_map/ppermute | solution.py:511
  37.8 1.4 %preacts_kept.3.kept_ref = f32[256,768]{1,0:T(8,128)S(1)} custom-call(bf16[256,3072]{1,0:T(8,128)(2,1)S(1)} %get-tuple-element.68.refs_0_.after_ref, bf16[24,3072,128]{2,1,0:T(8,128)(2,1)S(1)} %bitcast.16), custom_call_target="tpu_custom_call" | custom-call | flops 1207959552 | tf_op jit(solution)/shard_map/preacts_kept/pallas_call | solution.py:282
  39.2 1.6 %collective-permute-start.3 = (bf16[256,384]{1,0:T(8,128)(2,1)S(1)}, bf16[256,384]{1,0:T(8,128)(2,1)S(1)}, u32[]{:S(2)}, u32[]{:S(2)}) collective-permute-start(bf16[256,384]{1,0:T(8,128)(2,1)S(1)} %get-tuple-element.72), channel_id=1, source_target_pairs={{0,8},{8,0},{1,9},{9,1},{2,10},{10,2},{3,11},{11,3},{4,12},{12,4},... | collective-permute-start | bytes 589832 | tf_op jit(solution)/shard_map/ppermute | solution.py:511
  40.8 3.8 %fetch_down.1 = (bf16[3072,1536]{1,0:T(8,128)(2,1)S(1)}, f32[8,128]{1,0:T(8,128)S(1)}) custom-call(bf16[256,3072]{1,0:T(8,128)(2,1)S(1)} %get-tuple-element.68.refs_0_.after_ref, bf16[3072,1536]{1,0:T(8,128)(2,1)} %down_ref.1), custom_call_target="tpu_custom_call" | custom-call | bytes 18874368 | tf_op jit(solution)/shard_map/fetch_down/pallas_call | solution.py:226
  44.7 3.0 %collective-permute-start.4 = (bf16[128,384]{1,0:T(8,128)(2,1)S(1)}, bf16[128,384]{1,0:T(8,128)(2,1)S(1)}, u32[]{:S(2)}, u32[]{:S(2)}) collective-permute-start(bf16[128,384]{1,0:T(8,128)(2,1)S(1)} %act.2.refs_0_), channel_id=1, source_target_pairs={{0,4},{2,6},{4,0},{6,2},{1,5},{3,7},{5,1},{7,3},{8,12},{10,14},{12... | collective-permute-start | bytes 294920 | tf_op jit(solution)/shard_map/ppermute | solution.py:515
  47.7 1.5 %collective-permute-start.6 = (bf16[128,768]{1,0:T(8,128)(2,1)S(1)}, bf16[128,768]{1,0:T(8,128)(2,1)S(1)}, u32[]{:S(2)}, u32[]{:S(2)}) collective-permute-start(bf16[128,768]{1,0:T(8,128)(2,1)S(1)} %get-tuple-element.82.h0.n0), channel_id=1, source_target_pairs={{0,2},{2,0},{4,6},{6,4},{1,3},{3,1},{5,7},{7,5},{8,10},{10,8},{12,... | collective-permute-start | bytes 589832 | tf_op jit(solution)/shard_map/ppermute | solution.py:515
  50.3 2.8 %collective-permute-done.4.n0 = bf16[128,384]{1,0:T(8,128)(2,1)S(1)} collective-permute-done((bf16[128,384]{1,0:T(8,128)(2,1)S(1)}, bf16[128,384]{1,0:T(8,128)(2,1)S(1)}, u32[]{:S(2)}, u32[]{:S(2)}) %collective-permute-start.4) | collective-permute-done | bytes 98336 | tf_op jit(solution)/shard_map/ppermute | solution.py:515
  54.2 3.0 %collective-permute-start.8 = (bf16[128,384]{1,0:T(8,128)(2,1)S(1)}, bf16[128,384]{1,0:T(8,128)(2,1)S(1)}, u32[]{:S(2)}, u32[]{:S(2)}) collective-permute-start(bf16[128,384]{1,0:T(8,128)(2,1)S(1)} %collective-permute-done.4.n0), channel_id=1, source_target_pairs={{0,2},{2,0},{4,6},{6,4},{1,3},{3,1},{5,7},{7,5},{8,10},{10,8},{12,... | collective-permute-start | bytes 294920 | tf_op jit(solution)/shard_map/ppermute | solution.py:515
  57.2 3.5 %collective-permute-done.5.n1 = bf16[128,384]{1,0:T(8,128)(2,1)S(1)} collective-permute-done((bf16[128,384]{1,0:T(8,128)(2,1)S(1)}, bf16[128,384]{1,0:T(8,128)(2,1)S(1)}, u32[]{:S(2)}, u32[]{:S(2)}) %collective-permute-start.5) | collective-permute-done | bytes 98336 | tf_op jit(solution)/shard_map/ppermute | solution.py:515
  62.4 2.5 %project.1 = (f32[32,1536]{1,0:T(8,128)S(1)}, bf16[128,1536]{1,0:T(8,128)(2,1)}, bf16[128,3072]{1,0:T(8,128)(2,1)S(1)}, f32[8,128]{1,0:T(8,128)S(1)}) custom-call(f32[8,128]{1,0:T(8,128)S(1)} %get-tuple-element.89.tick_ref, bf16[128,768]{1,0:T(8,128)(2,1)S(1)} %get-tuple-element.82.h0.n0, bf16[128,768]{1,0:T(8,128)(2,1)S(1)} %collective-permute-done.7.h1.n0, ...), custom_call_target="tpu_custom_call" | custom-call | flops 1207959552 | tf_op jit(solution)/shard_map/project/pallas_call | solution.py:437
  65.0 3.8 %all-to-all-start.1 = ((bf16[4,32,1536]{2,1,0:T(8,128)(2,1)}), bf16[4,32,1536]{2,1,0:T(8,128)(2,1)S(1)}, u32[]{:S(2)}, u32[]{:S(2)}) async-start(bf16[4,32,1536]{2,1,0:T(8,128)(2,1)} %bitcast.8), calls=%async_computation.1 | async-start | bytes 786432 | tf_op jit(solution)/shard_map/all_to_all | solution.py:562
  68.8 1.4 %collective-permute-start.12 = (bf16[128,768]{1,0:T(8,128)(2,1)S(1)}, bf16[128,768]{1,0:T(8,128)(2,1)S(1)}, u32[]{:S(2)}, u32[]{:S(2)}) collective-permute-start(bf16[128,768]{1,0:T(8,128)(2,1)S(1)} %get-tuple-element.101), channel_id=1, source_target_pairs={{0,8},{8,0},{1,9},{9,1},{2,10},{10,2},{3,11},{11,3},{4,12},{12,4},... | collective-permute-start | bytes 589832 | tf_op jit(solution)/shard_map/ppermute | solution.py:511
  70.2 2.5 %collective-permute-start.13 = (bf16[128,768]{1,0:T(8,128)(2,1)S(1)}, bf16[128,768]{1,0:T(8,128)(2,1)S(1)}, u32[]{:S(2)}, u32[]{:S(2)}) collective-permute-start(bf16[128,768]{1,0:T(8,128)(2,1)S(1)} %get-tuple-element.102), channel_id=1, source_target_pairs={{0,8},{2,10},{12,4},{14,6},{1,9},{3,11},{13,5},{15,7},{16,24},{18,... | collective-permute-start | bytes 589832 | tf_op jit(solution)/shard_map/ppermute | solution.py:565
  72.9 4.1 %gram.3 = (f32[3072,3072]{1,0:T(8,128)}, f32[8,128]{1,0:T(8,128)S(1)}) custom-call(f32[8,128]{1,0:T(8,128)S(1)} %get-tuple-element.94.refs_0_, bf16[128,768]{1,0:T(8,128)(2,1)S(1)} %get-tuple-element.98.refs_1_, bf16[128,3072]{1,0:T(8,128)(2,1)S(1)} %get-tuple-element.99.refs_2_.refs_3_), custom_call_target="tpu_custom_call" | custom-call | flops 603979776 | bytes 9437184 | tf_op jit(solution)/shard_map/gram/pallas_call | solution.py:491
  77.0 1.6 %collective-permute-done.13.refs_0_ = bf16[128,768]{1,0:T(8,128)(2,1)S(1)} collective-permute-done((bf16[128,768]{1,0:T(8,128)(2,1)S(1)}, bf16[128,768]{1,0:T(8,128)(2,1)S(1)}, u32[]{:S(2)}, u32[]{:S(2)}) %collective-permute-start.13) | collective-permute-done | bytes 196640 | tf_op jit(solution)/shard_map/ppermute | solution.py:565
  78.9 4.1 %gram.4 = (f32[3072,3072]{1,0:T(8,128)}, f32[8,128]{1,0:T(8,128)S(1)}) custom-call(f32[8,128]{1,0:T(8,128)S(1)} %get-tuple-element.105.refs_0_, bf16[128,768]{1,0:T(8,128)(2,1)S(1)} %collective-permute-done.14.refs_1_, bf16[128,3072]{1,0:T(8,128)(2,1)S(1)} %get-tuple-element.99.refs_2_.refs_3_, ...), custom_call_target="tpu_custom_call", output_to_operand_aliasing={{0}: (3, {})} | custom-call | flops 603979776 | bytes 9437184 | tf_op jit(solution)/shard_map/gram/pallas_call | solution.py:491
  83.0 6.9 %gram.5 = (f32[3072,3072]{1,0:T(8,128)}, f32[8,128]{1,0:T(8,128)S(1)}) custom-call(f32[8,128]{1,0:T(8,128)S(1)} %get-tuple-element.112.refs_0_, bf16[128,768]{1,0:T(8,128)(2,1)S(1)} %get-tuple-element.113.refs_1_, bf16[128,768]{1,0:T(8,128)(2,1)S(1)} %collective-permute-done.15.refs_2_, ...), custom_call_target="tpu_custom_call", output_to_operand_aliasing={{0}: (4, {})} | custom-call | flops 1207959552 | bytes 18874368 | tf_op jit(solution)/shard_map/gram/pallas_call | solution.py:491
  (46 shorter events, 9.2 us)
Async XLA Ops:
  2.7 20.2 %all-to-all-start = ((bf16[4,32,1536]{2,1,0:T(8,128)(2,1)}), bf16[4,32,1536]{2,1,0:T(8,128)(2,1)S(1)}, u32[]{:S(2)}, u32[]{:S(2)}) async-start(bf16[4,32,1536]{2,1,0:T(8,128)(2,1)} %bitcast.3), calls=%async_computation | async-start | bytes 786432 | tf_op jit(solution)/shard_map/all_to_all | solution.py:526
  16.0 6.9 %copy-start = (bf16[24,1536,2,128]{3,2,1,0:T(2,128)(2,1)}, bf16[24,1536,2,128]{3,2,1,0:T(2,128)(2,1)S(1)}, u32[]{:S(2)}) copy-start(bf16[24,1536,2,128]{3,2,1,0:T(2,128)(2,1)S(1)} %regroup.1) | copy-start | bytes 56623108
  22.8 6.4 %copy-start.1 = (bf16[24,1536,2,128]{3,2,1,0:T(2,128)(2,1)S(1)}, bf16[24,1536,2,128]{3,2,1,0:T(2,128)(2,1)}, u32[]{:S(2)}) copy-start(bf16[24,1536,2,128]{3,2,1,0:T(2,128)(2,1)} %copy-done) | copy-start | bytes 56623108
  31.0 3.5 %collective-permute-start = (f32[256,768]{1,0:T(8,128)S(1)}, f32[256,768]{1,0:T(8,128)S(1)}, u32[]{:S(2)}, u32[]{:S(2)}) collective-permute-start(f32[256,768]{1,0:T(8,128)S(1)} %get-tuple-element.64), channel_id=1, source_target_pairs={{0,1},{1,0},{2,3},{3,2},{4,5},{5,4},{6,7},{7,6},{8,9},{9,8},{10,11... | collective-permute-start | bytes 2359304 | tf_op jit(solution)/shard_map/ppermute | solution.py:511
  31.1 5.0 %slice-start = ((s8[18874368]{0:T(1024)(128)(4,1)}), s8[4194304]{0:T(1024)(128)(4,1)S(1)}, s32[]{:S(2)}) async-start(s8[18874368]{0:T(1024)(128)(4,1)} %bitcast.14), calls=%async_computation.2 | async-start | bytes 8388608
  31.1 5.0 %slice-start.1 = ((s8[18874368]{0:T(1024)(128)(4,1)}), s8[4194304]{0:T(1024)(128)(4,1)S(1)}, s32[]{:S(2)}) async-start(s8[18874368]{0:T(1024)(128)(4,1)} %bitcast.14), calls=%async_computation.3 | async-start | bytes 8388608
  31.1 5.0 %slice-start.2 = ((s8[18874368]{0:T(1024)(128)(4,1)}), s8[4194304]{0:T(1024)(128)(4,1)S(1)}, s32[]{:S(2)}) async-start(s8[18874368]{0:T(1024)(128)(4,1)} %bitcast.14), calls=%async_computation.4 | async-start | bytes 8388608
  32.5 5.2 %slice-start.4 = ((s8[18874368]{0:T(1024)(128)(4,1)}), s8[2097152]{0:T(1024)(128)(4,1)S(1)}, s32[]{:S(2)}) async-start(s8[18874368]{0:T(1024)(128)(4,1)} %bitcast.14), calls=%async_computation.6 | async-start | bytes 4194304
  32.6 6.6 %collective-permute-start.1 = (f32[256,768]{1,0:T(8,128)S(1)}, f32[256,768]{1,0:T(8,128)S(1)}, u32[]{:S(2)}, u32[]{:S(2)}) collective-permute-start(f32[256,768]{1,0:T(8,128)S(1)} %preacts_sent.3), channel_id=1, source_target_pairs={{0,1},{1,0},{2,3},{3,2},{4,5},{5,4},{6,7},{7,6},{8,9},{9,8},{10,11... | collective-permute-start | bytes 2359304 | tf_op jit(solution)/shard_map/ppermute | solution.py:511
  34.6 10.0 %collective-permute-start.2 = (bf16[256,384]{1,0:T(8,128)(2,1)S(1)}, bf16[256,384]{1,0:T(8,128)(2,1)S(1)}, u32[]{:S(2)}, u32[]{:S(2)}) collective-permute-start(bf16[256,384]{1,0:T(8,128)(2,1)S(1)} %get-tuple-element.70), channel_id=1, source_target_pairs={{0,8},{8,0},{1,9},{9,1},{2,10},{10,2},{3,11},{11,3},{4,12},{12,4},... | collective-permute-start | bytes 589832 | tf_op jit(solution)/shard_map/ppermute | solution.py:511
  39.2 8.4 %collective-permute-start.3 = (bf16[256,384]{1,0:T(8,128)(2,1)S(1)}, bf16[256,384]{1,0:T(8,128)(2,1)S(1)}, u32[]{:S(2)}, u32[]{:S(2)}) collective-permute-start(bf16[256,384]{1,0:T(8,128)(2,1)S(1)} %get-tuple-element.72), channel_id=1, source_target_pairs={{0,8},{8,0},{1,9},{9,1},{2,10},{10,2},{3,11},{11,3},{4,12},{12,4},... | collective-permute-start | bytes 589832 | tf_op jit(solution)/shard_map/ppermute | solution.py:511
  44.7 8.4 %collective-permute-start.4 = (bf16[128,384]{1,0:T(8,128)(2,1)S(1)}, bf16[128,384]{1,0:T(8,128)(2,1)S(1)}, u32[]{:S(2)}, u32[]{:S(2)}) collective-permute-start(bf16[128,384]{1,0:T(8,128)(2,1)S(1)} %act.2.refs_0_), channel_id=1, source_target_pairs={{0,4},{2,6},{4,0},{6,2},{1,5},{3,7},{5,1},{7,3},{8,12},{10,14},{12... | collective-permute-start | bytes 294920 | tf_op jit(solution)/shard_map/ppermute | solution.py:515
  47.7 9.4 %collective-permute-start.6 = (bf16[128,768]{1,0:T(8,128)(2,1)S(1)}, bf16[128,768]{1,0:T(8,128)(2,1)S(1)}, u32[]{:S(2)}, u32[]{:S(2)}) collective-permute-start(bf16[128,768]{1,0:T(8,128)(2,1)S(1)} %get-tuple-element.82.h0.n0), channel_id=1, source_target_pairs={{0,2},{2,0},{4,6},{6,4},{1,3},{3,1},{5,7},{7,5},{8,10},{10,8},{12,... | collective-permute-start | bytes 589832 | tf_op jit(solution)/shard_map/ppermute | solution.py:515
  49.3 7.9 %collective-permute-start.7 = (bf16[128,768]{1,0:T(8,128)(2,1)S(1)}, bf16[128,768]{1,0:T(8,128)(2,1)S(1)}, u32[]{:S(2)}, u32[]{:S(2)}) collective-permute-start(bf16[128,768]{1,0:T(8,128)(2,1)S(1)} %get-tuple-element.82.h0.n0), channel_id=1, source_target_pairs={{0,8},{8,0},{1,9},{9,1},{2,10},{10,2},{3,11},{11,3},{4,12},{12,4},... | collective-permute-start | bytes 589832 | tf_op jit(solution)/shard_map/ppermute | solution.py:511
  53.1 7.6 %collective-permute-start.5 = (bf16[128,384]{1,0:T(8,128)(2,1)S(1)}, bf16[128,384]{1,0:T(8,128)(2,1)S(1)}, u32[]{:S(2)}, u32[]{:S(2)}) collective-permute-start(bf16[128,384]{1,0:T(8,128)(2,1)S(1)} %get-tuple-element.81), channel_id=1, source_target_pairs={{0,4},{2,6},{4,0},{6,2},{1,5},{3,7},{5,1},{7,3},{8,12},{10,14},{12... | collective-permute-start | bytes 294920 | tf_op jit(solution)/shard_map/ppermute | solution.py:515
  54.2 6.7 %collective-permute-start.8 = (bf16[128,384]{1,0:T(8,128)(2,1)S(1)}, bf16[128,384]{1,0:T(8,128)(2,1)S(1)}, u32[]{:S(2)}, u32[]{:S(2)}) collective-permute-start(bf16[128,384]{1,0:T(8,128)(2,1)S(1)} %collective-permute-done.4.n0), channel_id=1, source_target_pairs={{0,2},{2,0},{4,6},{6,4},{1,3},{3,1},{5,7},{7,5},{8,10},{10,8},{12,... | collective-permute-start | bytes 294920 | tf_op jit(solution)/shard_map/ppermute | solution.py:515
  57.2 4.8 %collective-permute-start.9 = (bf16[128,768]{1,0:T(8,128)(2,1)S(1)}, bf16[128,768]{1,0:T(8,128)(2,1)S(1)}, u32[]{:S(2)}, u32[]{:S(2)}) collective-permute-start(bf16[128,768]{1,0:T(8,128)(2,1)S(1)} %get-tuple-element.82.h0.n0), channel_id=1, source_target_pairs={{0,1},{1,0},{2,3},{3,2},{4,5},{5,4},{6,7},{7,6},{8,9},{9,8},{10,11... | collective-permute-start | bytes 589832 | tf_op jit(solution)/shard_map/ppermute | solution.py:511
  60.9 1.5 %collective-permute-start.10 = (bf16[128,768]{1,0:T(8,128)(2,1)S(1)}, bf16[128,768]{1,0:T(8,128)(2,1)S(1)}, u32[]{:S(2)}, u32[]{:S(2)}) collective-permute-start(bf16[128,768]{1,0:T(8,128)(2,1)S(1)} %collective-permute-done.7.h1.n0), channel_id=1, source_target_pairs={{0,1},{1,0},{2,3},{3,2},{4,5},{5,4},{6,7},{7,6},{8,9},{9,8},{10,11... | collective-permute-start | bytes 589832 | tf_op jit(solution)/shard_map/ppermute | solution.py:511
  61.0 9.2 %collective-permute-start.11 = (bf16[128,384]{1,0:T(8,128)(2,1)S(1)}, bf16[128,384]{1,0:T(8,128)(2,1)S(1)}, u32[]{:S(2)}, u32[]{:S(2)}) collective-permute-start(bf16[128,384]{1,0:T(8,128)(2,1)S(1)} %collective-permute-done.5.n1), channel_id=1, source_target_pairs={{0,2},{2,0},{4,6},{6,4},{1,3},{3,1},{5,7},{7,5},{8,10},{10,8},{12,... | collective-permute-start | bytes 294920 | tf_op jit(solution)/shard_map/ppermute | solution.py:515
  65.0 24.9 %all-to-all-start.1 = ((bf16[4,32,1536]{2,1,0:T(8,128)(2,1)}), bf16[4,32,1536]{2,1,0:T(8,128)(2,1)S(1)}, u32[]{:S(2)}, u32[]{:S(2)}) async-start(bf16[4,32,1536]{2,1,0:T(8,128)(2,1)} %bitcast.8), calls=%async_computation.1 | async-start | bytes 786432 | tf_op jit(solution)/shard_map/all_to_all | solution.py:562
  68.8 8.2 %collective-permute-start.12 = (bf16[128,768]{1,0:T(8,128)(2,1)S(1)}, bf16[128,768]{1,0:T(8,128)(2,1)S(1)}, u32[]{:S(2)}, u32[]{:S(2)}) collective-permute-start(bf16[128,768]{1,0:T(8,128)(2,1)S(1)} %get-tuple-element.101), channel_id=1, source_target_pairs={{0,8},{8,0},{1,9},{9,1},{2,10},{10,2},{3,11},{11,3},{4,12},{12,4},... | collective-permute-start | bytes 589832 | tf_op jit(solution)/shard_map/ppermute | solution.py:511
  70.2 8.3 %collective-permute-start.13 = (bf16[128,768]{1,0:T(8,128)(2,1)S(1)}, bf16[128,768]{1,0:T(8,128)(2,1)S(1)}, u32[]{:S(2)}, u32[]{:S(2)}) collective-permute-start(bf16[128,768]{1,0:T(8,128)(2,1)S(1)} %get-tuple-element.102), channel_id=1, source_target_pairs={{0,8},{2,10},{12,4},{14,6},{1,9},{3,11},{13,5},{15,7},{16,24},{18,... | collective-permute-start | bytes 589832 | tf_op jit(solution)/shard_map/ppermute | solution.py:565
  72.8 6.1 %collective-permute-start.14 = (bf16[128,768]{1,0:T(8,128)(2,1)S(1)}, bf16[128,768]{1,0:T(8,128)(2,1)S(1)}, u32[]{:S(2)}, u32[]{:S(2)}) collective-permute-start(bf16[128,768]{1,0:T(8,128)(2,1)S(1)} %get-tuple-element.104), channel_id=1, source_target_pairs={{0,1},{1,0},{2,3},{3,2},{4,5},{5,4},{6,7},{7,6},{8,9},{9,8},{10,11... | collective-permute-start | bytes 589832 | tf_op jit(solution)/shard_map/ppermute | solution.py:511
  78.8 4.2 %collective-permute-start.15 = (bf16[128,768]{1,0:T(8,128)(2,1)S(1)}, bf16[128,768]{1,0:T(8,128)(2,1)S(1)}, u32[]{:S(2)}, u32[]{:S(2)}) collective-permute-start(bf16[128,768]{1,0:T(8,128)(2,1)S(1)} %get-tuple-element.111), channel_id=1, source_target_pairs={{0,1},{1,0},{2,3},{3,2},{4,5},{5,4},{6,7},{7,6},{8,9},{9,8},{10,11... | collective-permute-start | bytes 589832 | tf_op jit(solution)/shard_map/ppermute | solution.py:511
  (1 other events, 4.6 us)

commit v8 on v5

--- a/solution.py
+++ b/solution.py
@@ -150,27 +150,6 @@
     )(*(in_hbm(x) for x in operands))
 
 
-def unpack_kernel(after_ref, placing_ref, factor_ref, own_ref, r1_ref, r2_ref, r3_ref, out_ref):
-    del after_ref
-    total = own_ref[...] + r1_ref[...].astype(F32) + r2_ref[...].astype(F32) + r3_ref[...].astype(F32)
-    scaled = (total * factor_ref[:, 0:1]).astype(BF16)
-    out_ref[...] = lax.dot_general(
-        placing_ref[...], scaled, (((0,), (0,)), ((), ())), preferred_element_type=F32
-    ).astype(BF16)
-
-
-def unpack(done, placing, factor, own, returned):
-    slots, rows = placing.shape
-    return pl.pallas_call(
-        unpack_kernel,
-        in_specs=[ANY] + [VMEM] * 6,
-        out_specs=VMEM,
-        out_shape=jax.ShapeDtypeStruct((rows, own.shape[1]), BF16),
-        compiler_params=params(4),
-        name="unpack",
-    )(done, placing, factor, own, *returned)
-
-
 def regroup_kernel(after_ref, weights_ref, out_ref, sems):
     del after_ref
     copies = [
@@ -406,51 +385,102 @@
     )(*slots)
 
 
-def project_kernel(
-    tick_ref, h0, h1, h2, h3, down_ref, own_ref, s1_ref, s2_ref, s3_ref, wide_ref, done_ref, total_ref
-):
+def join_kernel(left_ref, right_ref, out_ref):
+    units = left_ref.shape[1]
+    out_ref[:, :units] = left_ref[...]
+    out_ref[:, units:] = right_ref[...]
+
+
+def join(left, right):
+    rows, units = left.shape
+    return pl.pallas_call(
+        join_kernel,
+        in_specs=[VMEM] * 2,
+        out_specs=VMEM,
+        out_shape=jax.ShapeDtypeStruct((rows, 2 * units), left.dtype),
+        compiler_params=params(2),
+        name="join",
+    )(left, right)
+
+
+def project_kernel(tick_ref, here_ref, there_ref, down_ref, near_ref, away_ref, wide_ref, done_ref, total_ref):
     del tick_ref
-    units = h0.shape[1]
-    for k, h_ref in enumerate((h0, h1, h2, h3)):
-        at = pl.multiple_of(quarter_of(k % 2, k // 2) * units, units)
-        wide_ref[:, pl.ds(at, units)] = h_ref[...]
+    units = here_ref.shape[1] // 2
+    for row_flip, pair_ref in enumerate((here_ref, there_ref)):
+        for expert_flip in range(2):
+            at = pl.multiple_of(quarter_of(expert_flip, row_flip) * units, units)
+            wide_ref[:, pl.ds(at, units)] = pair_ref[:, units * expert_flip : units * (expert_flip + 1)]
     done_ref[...] = jnp.zeros_like(done_ref)
-    slots, width = own_ref.shape
+    width = near_ref.shape[1]
+    slots = near_ref.shape[0] // 2
     cut = 512
     for n in range(width // cut):
         total_ref[:, cut * n : cut * (n + 1)] = jnp.dot(
             wide_ref[...], down_ref[:, cut * n : cut * (n + 1)], preferred_element_type=F32
         )
     here = lax.axis_index("col")
-    for slot, out_ref in enumerate((own_ref, s1_ref, s2_ref, s3_ref)):
+    for i, (out_ref, slot) in enumerate(((near_ref, 0), (near_ref, 2), (away_ref, 1), (away_ref, 3))):
         at = pl.multiple_of((here ^ slot) * slots, slots)
-        out_ref[...] = total_ref[pl.ds(at, slots), :].astype(out_ref.dtype)
-
-
-def project(tick, quarters, down):
-    rows, units = quarters[0].shape
+        row = slots * (i % 2)
+        out_ref[row : row + slots, :] = total_ref[pl.ds(at, slots), :].astype(out_ref.dtype)
+
+
+def project(tick, here, there, down):
+    rows, units = here.shape[0], here.shape[1] // 2
     width = down.shape[1]
-    slots = rows // 4
     return pl.pallas_call(
         project_kernel,
-        in_specs=[ANY] + [VMEM] * 5,
-        out_specs=[VMEM] * 6,
-        out_shape=[jax.ShapeDtypeStruct((slots, width), F32)]
-        + [jax.ShapeDtypeStruct((slots, width), BF16)] * 3
-        + [pltpu.VMEM((rows, 4 * units), BF16), pltpu.VMEM((8, 128), F32)],
+        in_specs=[ANY] + [VMEM] * 3,
+        out_specs=[VMEM] * 4,
+        out_shape=[
+            jax.ShapeDtypeStruct((rows // 2, width), F32),
+            jax.ShapeDtypeStruct((rows // 2, width), BF16),
+            pltpu.VMEM((rows, 4 * units), BF16),
+            pltpu.VMEM((8, 128), F32),
+        ],
         scratch_shapes=[pltpu.VMEM((rows, width), F32)],
         compiler_params=params(4),
         cost_estimate=cost(8 * rows * units * width, 0),
         name="project",
-    )(tick, *quarters, in_vmem(down))
-
-
-def gram_kernel(scale, flips, *refs):
+    )(tick, here, there, in_vmem(down))
+
+
+def fold_kernel(near_ref, got_ref, own_ref, onward_ref):
+    slots = own_ref.shape[0]
+    own_ref[...] = near_ref[:slots, :] + got_ref[:slots, :].astype(F32)
+    onward_ref[...] = (near_ref[slots:, :] + got_ref[slots:, :].astype(F32)).astype(BF16)
+
+
+def fold(near, got):
+    slots, width = near.shape[0] // 2, near.shape[1]
+    return pl.pallas_call(
+        fold_kernel,
+        in_specs=[VMEM] * 2,
+        out_specs=[VMEM] * 2,
+        out_shape=[
+            jax.ShapeDtypeStruct((slots, width), F32),
+            jax.ShapeDtypeStruct((slots, width), BF16),
+        ],
+        compiler_params=params(2),
+        name="fold",
+    )(near, got)
+
+
+def unpack_rows(placing_ref, factor_ref, own_ref, got_ref):
+    total = own_ref[...] + got_ref[...].astype(F32)
+    scaled = (total * factor_ref[:, 0:1]).astype(BF16)
+    return lax.dot_general(
+        placing_ref[...], scaled, (((0,), (0,)), ((), ())), preferred_element_type=F32
+    ).astype(BF16)
+
+
+def gram_kernel(scale, flips, last, *refs):
     count = len(flips)
     pieces = refs[1 : 1 + count]
     wide_ref = refs[1 + count]
     out_ref, done_ref, ring_ref, sems = refs[-4:]
-    done_ref[...] = jnp.zeros_like(done_ref)
+    if not last:
+        done_ref[...] = jnp.zeros_like(done_ref)
     units = pieces[0].shape[1]
     depth, _, cut = ring_ref.shape
     copies = []
@@ -469,34 +499,38 @@
             )
             copy.start()
             copies.append(copy)
+            if last and len(copies) == depth:
+                done_ref[...] = unpack_rows(*refs[2 + count : 6 + count])
     for copy in copies[-depth:]:
         copy.wait()
 
 
-def gram_piece(tick, pieces, flips, wide, gram=None):
+def gram_piece(tick, pieces, flips, wide, gram=None, outputs=()):
     rows, units = pieces[0].shape
-    cut, depth = 256, 8
-    operands = [tick, *pieces, in_vmem(wide)]
-    in_specs = [ANY] + [VMEM] * (len(pieces) + 1)
+    cut, depth = 512, 4
+    operands = [tick, *pieces, in_vmem(wide), *outputs]
+    in_specs = [ANY] + [VMEM] * (len(operands) - 1)
     aliases = {}
     if gram is not None:
         aliases = {len(operands): 0}
         operands.append(gram)
         in_specs.append(HBM)
-    return pl.pallas_call(
-        functools.partial(gram_kernel, 2.0 / rows, flips),
+    if outputs:
+        placing, _, own, _ = outputs
+        second = jax.ShapeDtypeStruct((placing.shape[1], own.shape[1]), BF16)
+    else:
+        second = pltpu.VMEM((8, 128), F32)
+    return pl.pallas_call(
+        functools.partial(gram_kernel, 2.0 / rows, flips, bool(outputs)),
         in_specs=in_specs,
         out_specs=[HBM, VMEM],
-        out_shape=[
-            jax.ShapeDtypeStruct((4 * units, 4 * units), F32),
-            pltpu.VMEM((8, 128), F32),
-        ],
+        out_shape=[jax.ShapeDtypeStruct((4 * units, 4 * units), F32), second],
         input_output_aliases=aliases,
         scratch_shapes=[
             pltpu.VMEM((depth, units, cut), F32),
             pltpu.SemaphoreType.DMA((depth,)),
         ],
-        compiler_params=params(10),
+        compiler_params=params(12),
         cost_estimate=cost(8 * rows * units * units * len(pieces), 16 * units * units * len(pieces)),
         name="gram",
     )(*operands)
@@ -540,22 +574,20 @@
     hidden_b, hidden = act(tick, stays[1], got_x[1], hidden_a)
     z1 = across(hidden, 1)
     hidden_x = swap(hidden, "expert")
-    c_near = swap(hidden, "row")
     tick, z2a, hidden_b = tie(tick, z2a, hidden_b)
     z2b = across(hidden_b, 2)
     z3a = across(z2a, 1)
     tick, z2b, z1, hidden_x, z3a = tie(tick, z2b, z1, hidden_x, z3a)
 
     leaves, z2 = choose((z2a, z2b), z1)
-    tick, z2b, leaves, sent_x = tie(tick, z2b, leaves, hidden_x)
+    here = join(hidden, hidden_x)
+    tick, z2b, leaves, here = tie(tick, z2b, leaves, here)
     z3b = across(z2b, 1)
     x2 = swap(leaves, "expert")
-    c_far = swap(sent_x, "row")
-    own, s1, s2, s3, hidden_c, tick = project(
-        tick, [hidden, hidden_x, c_near, c_far], down_held
-    )
-    returned = [across(value, slot) for slot, value in ((1, s1), (2, s2), (3, s3))]
-    tick, z3b = tie(tick, z3b)
+    there = swap(here, "row")
+    tick, there = tie(tick, there)
+    near, away, hidden_c, tick = project(tick, here, there, down_held)
+    tick, z3b, away = tie(tick, z3b, away)
     mine, passed, z3 = pick(hidden, z1, z2, z3a, z3b)
     x3 = lax.ppermute(
         z3,
@@ -563,15 +595,21 @@
         [(ee * 4 + cc, (1 - ee) * 4 + cc) for ee in range(2) for cc in range(4) if cc // 2 == ee],
     )
     mine_near = swap(passed, "row")
+    away = across(away, 1)
     gram, tick = gram_piece(tick, [mine], [(0, 0)], hidden_c)
+    tick, away = tie(tick, away)
+    own, onward = fold(near, away)
+    onward = across(onward, 2)
     tick, x2, x3 = tie(tick, x2, x3)
     mine_x, passed = pick(hidden_x, x2, x2, x3)
     mine_far = swap(passed, "row")
     tick, mine_near = tie(tick, mine_near)
     gram, tick = gram_piece(tick, [mine_near], [(0, 1)], hidden_c, gram)
     tick, mine_far = tie(tick, mine_far)
-    gram, tick = gram_piece(tick, [mine_x, mine_far], [(1, 0), (1, 1)], hidden_c, gram)
-    return (unpack(tick, placing, factor, own, returned), gram)
+    gram, expert_out = gram_piece(
+        tick, [mine_x, mine_far], [(1, 0), (1, 1)], hidden_c, gram, (placing, factor, own, onward)
+    )
+    return (expert_out, gram)
 
 
 def solution(mesh):

time: 74.9 us -> 75.1 us (level)
  waiting for transfers between devices: 7.98 us -> 9.28 us
  Pallas kernels: 37.4 us -> 36.4 us
    ppermute x11 -> x10, waiting for transfers between devices: 7.09 us -> 8.39 us  [across(): return lax.ppermute(value, 'col', [(i, i ^ slot) for i in range(4)])]
    pallas_call x5 -> x6, Pallas kernels: 18.4 us -> 17.4 us  [the longest x3 15.8 us: gram_piece(): pl.pallas_call(functools.partial(gram_kernel, 2.0 / rows, flips, bool(out...]
    ppermute x11 -> x10, starting transfers between devices: 20.5 us -> 20.3 us  [across(): return lax.ppermute(value, 'col', [(i, i ^ slot) for i in range(4)])]
    ppermute x10 -> x9, starting transfers between devices: 5.56 us -> 5.56 us  [swap(): return lax.ppermute(value, axis, [(0, 1), (1, 0)])]
  transfers between devices with their start and end apart: 22 -> 20, of which waited for: 7 -> 8; matrix products, arithmetic and copies ran while one was open for 0% -> 0% of each run, Pallas kernels for 44% -> 34%
where the time goes in v8:
time: 75.1 us; the launch traced here: 74.9 us
  Pallas kernels  36.4 us (48%)
  starting transfers between devices  28.3 us (38%)
  waiting for transfers between devices  9.28 us (12%)
  between operations  1.02 us (1%)
    ppermute x10, starting transfers between devices, across(): return lax.ppermute(value, 'col', [(i, i ^ slot) for i in range(4)])  20.3 us
    pallas_call x3, Pallas kernels, gram_piece(): pl.pallas_call(functools.partial(gram_kernel, 2.0 / rows, flips, bool(out...  15.8 us
    ppermute x10, waiting for transfers between devices, across(): return lax.ppermute(value, 'col', [(i, i ^ slot) for i in range(4)])  8.39 us
    pallas_call x1, Pallas kernels, regroup(): pl.pallas_call(regroup_kernel, in_specs=[ANY, HBM], out_specs=VMEM, out_s...  6.97 us
    pallas_call x4, Pallas kernels, preacts_of(): pl.pallas_call(functools.partial(preact_kernel, first, row_flip, chunk, c...  6.26 us
    ppermute x9, starting transfers between devices, swap(): return lax.ppermute(value, axis, [(0, 1), (1, 0)])  5.56 us
    pallas_call x1, Pallas kernels, fetch(): pl.pallas_call(fetch_kernel, in_specs=[ANY, HBM], out_specs=[VMEM, VMEM],...  3.8 us
    ppermute x1, starting transfers between devices, on_device(): lax.ppermute(z3, ('expert', 'col'), [(ee * 4 + cc, (1 - ee) * 4 + cc) for...  2.43 us
  transfers between devices with their start and end apart: 20, of which 8 were waited for; matrix products, arithmetic and copies ran while one was open for 0% of the time, Pallas kernels for 34%

profile of v8, /device:TPU:0, one launch (start us, length us, event | category | flops | bytes accessed | tf_op | source)
XLA Modules:
  0.0 74.9 jit_solution(7961412776992217844)
XLA Ops:
  0.6 1.3 %pack.1 = (bf16[32,1536]{1,0:T(8,128)(2,1)S(1)}, bf16[32,128]{1,0:T(8,128)(2,1)S(1)}, f32[32,128]{1,0:T(8,128)S(1)}) custom-call(bf16[128,1536]{1,0:T(8,128)(2,1)} %tokens_ref.1, s32[2,128]{1,0:T(2,128)} %bitcast.12, s32[1,128]{1,0:T(1,128)} %bitcast.14, f32[2,128]{1,0:T(2,128)} %bitcast.13), custom_call_target="tpu_custom_call" | custom-call | tf_op jit(solution)/shard_map/pack/pallas_call | solution.py:137
  1.9 3.1 %collective-permute-start = (bf16[32,1536]{1,0:T(8,128)(2,1)S(1)}, bf16[32,1536]{1,0:T(8,128)(2,1)S(1)}, u32[]{:S(2)}, u32[]{:S(2)}) collective-permute-start(bf16[32,1536]{1,0:T(8,128)(2,1)S(1)} %get-tuple-element.69.after_ref.refs_0_), channel_id=1, source_target_pairs={{0,2},{2,0},{4,6},{6,4},{1,3},{3,1},{5,7},{7,5},{8,10},{10,8},{12,... | collective-permute-start | bytes 294920 | tf_op jit(solution)/shard_map/ppermute | solution.py:544
  5.0 2.6 %collective-permute-start.1 = (bf16[32,1536]{1,0:T(8,128)(2,1)S(1)}, bf16[32,1536]{1,0:T(8,128)(2,1)S(1)}, u32[]{:S(2)}, u32[]{:S(2)}) collective-permute-start(bf16[32,1536]{1,0:T(8,128)(2,1)S(1)} %get-tuple-element.69.after_ref.refs_0_), channel_id=1, source_target_pairs={{0,4},{2,6},{4,0},{6,2},{1,5},{3,7},{5,1},{7,3},{8,12},{10,14},{12... | collective-permute-start | bytes 294920 | tf_op jit(solution)/shard_map/ppermute | solution.py:544
  7.6 7.0 %regroup.1 = bf16[24,1536,2,128]{3,2,1,0:T(2,128)(2,1)S(1)} custom-call(bf16[32,1536]{1,0:T(8,128)(2,1)S(1)} %get-tuple-element.69.after_ref.refs_0_, bf16[1536,24,2,128]{3,2,1,0:T(2,128)(2,1)} %bitcast.11), custom_call_target="tpu_custom_call" | custom-call | bytes 37748736 | tf_op jit(solution)/shard_map/regroup/pallas_call | solution.py:167
  15.4 2.0 %preacts_sent.2 = (f32[256,768]{1,0:T(8,128)S(1)}, bf16[256,3072]{1,0:T(8,128)(2,1)S(1)}) custom-call(bf16[32,1536]{1,0:T(8,128)(2,1)S(1)} %get-tuple-element.69.after_ref.refs_0_, bf16[32,1536]{1,0:T(8,128)(2,1)S(1)} %collective-permute-done.refs_1_, bf16[32,1536]{1,0:T(8,128)(2,1)S(1)} %collective-permute-done.1.refs_2_, ...), custom_call_target="tpu_custom_call" | custom-call | flops 1207959552 | tf_op jit(solution)/shard_map/preacts_sent/pallas_call | solution.py:260
  17.5 1.4 %preacts_sent.3 = f32[256,768]{1,0:T(8,128)S(1)} custom-call(bf16[256,3072]{1,0:T(8,128)(2,1)S(1)} %get-tuple-element.75.refs_0_.after_ref, bf16[24,3072,128]{2,1,0:T(8,128)(2,1)S(1)} %bitcast.8), custom_call_target="tpu_custom_call" | custom-call | flops 1207959552 | tf_op jit(solution)/shard_map/preacts_sent/pallas_call | solution.py:260
  19.5 1.4 %preacts_kept.2.kept_ref = f32[256,768]{1,0:T(8,128)S(1)} custom-call(bf16[256,3072]{1,0:T(8,128)(2,1)S(1)} %get-tuple-element.75.refs_0_.after_ref, bf16[24,3072,128]{2,1,0:T(8,128)(2,1)S(1)} %bitcast.9), custom_call_target="tpu_custom_call" | custom-call | flops 1207959552 | tf_op jit(solution)/shard_map/preacts_kept/pallas_call | solution.py:260
  21.0 1.6 %collective-permute-start.5 = (bf16[256,384]{1,0:T(8,128)(2,1)S(1)}, bf16[256,384]{1,0:T(8,128)(2,1)S(1)}, u32[]{:S(2)}, u32[]{:S(2)}) collective-permute-start(bf16[256,384]{1,0:T(8,128)(2,1)S(1)} %get-tuple-element.77), channel_id=1, source_target_pairs={{0,8},{8,0},{1,9},{9,1},{2,10},{10,2},{3,11},{11,3},{4,12},{12,4},... | collective-permute-start | bytes 589832 | tf_op jit(solution)/shard_map/ppermute | solution.py:540
  22.6 1.4 %preacts_kept.3.kept_ref = f32[256,768]{1,0:T(8,128)S(1)} custom-call(bf16[256,3072]{1,0:T(8,128)(2,1)S(1)} %get-tuple-element.75.refs_0_.after_ref, bf16[24,3072,128]{2,1,0:T(8,128)(2,1)S(1)} %bitcast.10), custom_call_target="tpu_custom_call" | custom-call | flops 1207959552 | tf_op jit(solution)/shard_map/preacts_kept/pallas_call | solution.py:260
  24.7 3.8 %fetch_down.1 = (bf16[3072,1536]{1,0:T(8,128)(2,1)S(1)}, f32[8,128]{1,0:T(8,128)S(1)}) custom-call(bf16[256,3072]{1,0:T(8,128)(2,1)S(1)} %get-tuple-element.75.refs_0_.after_ref, bf16[3072,1536]{1,0:T(8,128)(2,1)} %down_ref.1), custom_call_target="tpu_custom_call" | custom-call | bytes 18874368 | tf_op jit(solution)/shard_map/fetch_down/pallas_call | solution.py:198
  28.9 2.7 %collective-permute-start.7 = (bf16[128,384]{1,0:T(8,128)(2,1)S(1)}, bf16[128,384]{1,0:T(8,128)(2,1)S(1)}, u32[]{:S(2)}, u32[]{:S(2)}) collective-permute-start(bf16[128,384]{1,0:T(8,128)(2,1)S(1)} %act.2.refs_0_), channel_id=1, source_target_pairs={{0,4},{2,6},{4,0},{6,2},{1,5},{3,7},{5,1},{7,3},{8,12},{10,14},{12... | collective-permute-start | bytes 294920 | tf_op jit(solution)/shard_map/ppermute | solution.py:544
  32.2 1.6 %collective-permute-start.10 = (bf16[128,768]{1,0:T(8,128)(2,1)S(1)}, bf16[128,768]{1,0:T(8,128)(2,1)S(1)}, u32[]{:S(2)}, u32[]{:S(2)}) collective-permute-start(bf16[128,768]{1,0:T(8,128)(2,1)S(1)} %get-tuple-element.89.left_ref.n0), channel_id=1, source_target_pairs={{0,8},{8,0},{1,9},{9,1},{2,10},{10,2},{3,11},{11,3},{4,12},{12,4},... | collective-permute-start | bytes 589832 | tf_op jit(solution)/shard_map/ppermute | solution.py:540
  33.8 1.6 %collective-permute-start.9 = (bf16[128,768]{1,0:T(8,128)(2,1)S(1)}, bf16[128,768]{1,0:T(8,128)(2,1)S(1)}, u32[]{:S(2)}, u32[]{:S(2)}) collective-permute-start(bf16[128,768]{1,0:T(8,128)(2,1)S(1)} %get-tuple-element.89.left_ref.n0), channel_id=1, source_target_pairs={{0,2},{2,0},{4,6},{6,4},{1,3},{3,1},{5,7},{7,5},{8,10},{10,8},{12,... | collective-permute-start | bytes 589832 | tf_op jit(solution)/shard_map/ppermute | solution.py:544
  36.2 3.2 %collective-permute-start.8 = (bf16[128,384]{1,0:T(8,128)(2,1)S(1)}, bf16[128,384]{1,0:T(8,128)(2,1)S(1)}, u32[]{:S(2)}, u32[]{:S(2)}) collective-permute-start(bf16[128,384]{1,0:T(8,128)(2,1)S(1)} %get-tuple-element.88), channel_id=1, source_target_pairs={{0,4},{2,6},{4,0},{6,2},{1,5},{3,7},{5,1},{7,3},{8,12},{10,14},{12... | collective-permute-start | bytes 294920 | tf_op jit(solution)/shard_map/ppermute | solution.py:544
  39.5 3.4 %collective-permute-done.9.far_ref.n1 = bf16[128,768]{1,0:T(8,128)(2,1)S(1)} collective-permute-done((bf16[128,768]{1,0:T(8,128)(2,1)S(1)}, bf16[128,768]{1,0:T(8,128)(2,1)S(1)}, u32[]{:S(2)}, u32[]{:S(2)}) %collective-permute-start.9) | collective-permute-done | bytes 196640 | tf_op jit(solution)/shard_map/ppermute | solution.py:544
  44.1 2.5 %collective-permute-start.13 = (bf16[128,384]{1,0:T(8,128)(2,1)S(1)}, bf16[128,384]{1,0:T(8,128)(2,1)S(1)}, u32[]{:S(2)}, u32[]{:S(2)}) collective-permute-start(bf16[128,384]{1,0:T(8,128)(2,1)S(1)} %collective-permute-done.8.n1), channel_id=1, source_target_pairs={{0,2},{2,0},{4,6},{6,4},{1,3},{3,1},{5,7},{7,5},{8,10},{10,8},{12,... | collective-permute-start | bytes 294920 | tf_op jit(solution)/shard_map/ppermute | solution.py:544
  47.1 1.6 %project.1 = (f32[64,1536]{1,0:T(8,128)S(1)}, bf16[64,1536]{1,0:T(8,128)(2,1)S(1)}, bf16[128,3072]{1,0:T(8,128)(2,1)S(1)}, f32[8,128]{1,0:T(8,128)S(1)}) custom-call(f32[8,128]{1,0:T(8,128)S(1)} %get-tuple-element.98.tick_ref, bf16[128,1536]{1,0:T(8,128)(2,1)S(1)} %join.1.here_ref, bf16[128,1536]{1,0:T(8,128)(2,1)S(1)} %collective-permute-done.12.there_ref, ...), custom_call_target="tpu_custom_call" | custom-call | flops 1207959552 | tf_op jit(solution)/shard_map/project/pallas_call | solution.py:431
  49.9 1.8 %collective-permute-start.14 = (bf16[64,1536]{1,0:T(8,128)(2,1)S(1)}, bf16[64,1536]{1,0:T(8,128)(2,1)S(1)}, u32[]{:S(2)}, u32[]{:S(2)}) collective-permute-start(bf16[64,1536]{1,0:T(8,128)(2,1)S(1)} %get-tuple-element.111), channel_id=1, source_target_pairs={{0,2},{2,0},{4,6},{6,4},{1,3},{3,1},{5,7},{7,5},{8,10},{10,8},{12,... | collective-permute-start | bytes 589832 | tf_op jit(solution)/shard_map/ppermute | solution.py:544
  51.8 2.4 %collective-permute-start.16 = (bf16[128,768]{1,0:T(8,128)(2,1)S(1)}, bf16[128,768]{1,0:T(8,128)(2,1)S(1)}, u32[]{:S(2)}, u32[]{:S(2)}) collective-permute-start(bf16[128,768]{1,0:T(8,128)(2,1)S(1)} %get-tuple-element.114), channel_id=1, source_target_pairs={{0,8},{2,10},{12,4},{14,6},{1,9},{3,11},{13,5},{15,7},{16,24},{18,... | collective-permute-start | bytes 589832 | tf_op jit(solution)/shard_map/ppermute | solution.py:592
  54.3 4.1 %gram.3 = (f32[3072,3072]{1,0:T(8,128)}, f32[8,128]{1,0:T(8,128)S(1)}) custom-call(f32[8,128]{1,0:T(8,128)S(1)} %get-tuple-element.104.refs_0_, bf16[128,768]{1,0:T(8,128)(2,1)S(1)} %get-tuple-element.108.refs_1_, bf16[128,3072]{1,0:T(8,128)(2,1)S(1)} %get-tuple-element.109.refs_2_.refs_3_), custom_call_target="tpu_custom_call" | custom-call | flops 603979776 | bytes 9437184 | tf_op jit(solution)/shard_map/gram/pallas_call | solution.py:523
  59.2 2.5 %collective-permute-start.19 = (bf16[32,1536]{1,0:T(8,128)(2,1)S(1)}, bf16[32,1536]{1,0:T(8,128)(2,1)S(1)}, u32[]{:S(2)}, u32[]{:S(2)}) collective-permute-start(bf16[32,1536]{1,0:T(8,128)(2,1)S(1)} %get-tuple-element.132), channel_id=1, source_target_pairs={{0,4},{2,6},{4,0},{6,2},{1,5},{3,7},{5,1},{7,3},{8,12},{10,14},{12... | collective-permute-start | bytes 294920 | tf_op jit(solution)/shard_map/ppermute | solution.py:544
  61.8 4.1 %gram.4 = (f32[3072,3072]{1,0:T(8,128)}, f32[8,128]{1,0:T(8,128)S(1)}) custom-call(f32[8,128]{1,0:T(8,128)S(1)} %get-tuple-element.117.refs_0_, bf16[128,768]{1,0:T(8,128)(2,1)S(1)} %collective-permute-done.17.refs_1_, bf16[128,3072]{1,0:T(8,128)(2,1)S(1)} %get-tuple-element.109.refs_2_.refs_3_, ...), custom_call_target="tpu_custom_call", output_to_operand_aliasing={{0}: (3, {})} | custom-call | flops 603979776 | bytes 9437184 | tf_op jit(solution)/shard_map/gram/pallas_call | solution.py:523
  65.9 1.3 %collective-permute-done.19.refs_7_ = bf16[32,1536]{1,0:T(8,128)(2,1)S(1)} collective-permute-done((bf16[32,1536]{1,0:T(8,128)(2,1)S(1)}, bf16[32,1536]{1,0:T(8,128)(2,1)S(1)}, u32[]{:S(2)}, u32[]{:S(2)}) %collective-permute-start.19) | collective-permute-done | bytes 98336 | tf_op jit(solution)/shard_map/ppermute | solution.py:544
  67.1 7.6 %gram.5 = (f32[3072,3072]{1,0:T(8,128)}, bf16[128,1536]{1,0:T(8,128)(2,1)}) custom-call(f32[8,128]{1,0:T(8,128)S(1)} %get-tuple-element.124.refs_0_, bf16[128,768]{1,0:T(8,128)(2,1)S(1)} %get-tuple-element.125.refs_1_, bf16[128,768]{1,0:T(8,128)(2,1)S(1)} %collective-permute-done.18.refs_2_, ...), custom_call_target="tpu_custom_call", output_to_operand_aliasing={{0}: (8, {})} | custom-call | flops 1207959552 | bytes 18874368 | tf_op jit(solution)/shard_map/gram/pallas_call | solution.py:523
  (36 shorter events, 8.0 us)
Async XLA Ops:
  1.9 12.7 %collective-permute-start = (bf16[32,1536]{1,0:T(8,128)(2,1)S(1)}, bf16[32,1536]{1,0:T(8,128)(2,1)S(1)}, u32[]{:S(2)}, u32[]{:S(2)}) collective-permute-start(bf16[32,1536]{1,0:T(8,128)(2,1)S(1)} %get-tuple-element.69.after_ref.refs_0_), channel_id=1, source_target_pairs={{0,2},{2,0},{4,6},{6,4},{1,3},{3,1},{5,7},{7,5},{8,10},{10,8},{12,... | collective-permute-start | bytes 294920 | tf_op jit(solution)/shard_map/ppermute | solution.py:544
  5.0 10.4 %collective-permute-start.1 = (bf16[32,1536]{1,0:T(8,128)(2,1)S(1)}, bf16[32,1536]{1,0:T(8,128)(2,1)S(1)}, u32[]{:S(2)}, u32[]{:S(2)}) collective-permute-start(bf16[32,1536]{1,0:T(8,128)(2,1)S(1)} %get-tuple-element.69.after_ref.refs_0_), channel_id=1, source_target_pairs={{0,4},{2,6},{4,0},{6,2},{1,5},{3,7},{5,1},{7,3},{8,12},{10,14},{12... | collective-permute-start | bytes 294920 | tf_op jit(solution)/shard_map/ppermute | solution.py:544
  7.6 7.8 %collective-permute-start.2 = (bf16[32,1536]{1,0:T(8,128)(2,1)S(1)}, bf16[32,1536]{1,0:T(8,128)(2,1)S(1)}, u32[]{:S(2)}, u32[]{:S(2)}) collective-permute-start(bf16[32,1536]{1,0:T(8,128)(2,1)S(1)} %get-tuple-element.69.after_ref.refs_0_), channel_id=1, source_target_pairs={{0,6},{2,4},{4,2},{6,0},{1,7},{3,5},{5,3},{7,1},{8,14},{10,12},{12... | collective-permute-start | bytes 294920 | tf_op jit(solution)/shard_map/ppermute | solution.py:544
  17.4 3.5 %collective-permute-start.3 = (f32[256,768]{1,0:T(8,128)S(1)}, f32[256,768]{1,0:T(8,128)S(1)}, u32[]{:S(2)}, u32[]{:S(2)}) collective-permute-start(f32[256,768]{1,0:T(8,128)S(1)} %get-tuple-element.71), channel_id=1, source_target_pairs={{0,1},{1,0},{2,3},{3,2},{4,5},{5,4},{6,7},{7,6},{8,9},{9,8},{10,11... | collective-permute-start | bytes 2359304 | tf_op jit(solution)/shard_map/ppermute | solution.py:540
  18.9 5.1 %collective-permute-start.4 = (f32[256,768]{1,0:T(8,128)S(1)}, f32[256,768]{1,0:T(8,128)S(1)}, u32[]{:S(2)}, u32[]{:S(2)}) collective-permute-start(f32[256,768]{1,0:T(8,128)S(1)} %preacts_sent.3), channel_id=1, source_target_pairs={{0,1},{1,0},{2,3},{3,2},{4,5},{5,4},{6,7},{7,6},{8,9},{9,8},{10,11... | collective-permute-start | bytes 2359304 | tf_op jit(solution)/shard_map/ppermute | solution.py:540
  21.0 7.8 %collective-permute-start.5 = (bf16[256,384]{1,0:T(8,128)(2,1)S(1)}, bf16[256,384]{1,0:T(8,128)(2,1)S(1)}, u32[]{:S(2)}, u32[]{:S(2)}) collective-permute-start(bf16[256,384]{1,0:T(8,128)(2,1)S(1)} %get-tuple-element.77), channel_id=1, source_target_pairs={{0,8},{8,0},{1,9},{9,1},{2,10},{10,2},{3,11},{11,3},{4,12},{12,4},... | collective-permute-start | bytes 589832 | tf_op jit(solution)/shard_map/ppermute | solution.py:540
  24.1 8.0 %collective-permute-start.6 = (bf16[256,384]{1,0:T(8,128)(2,1)S(1)}, bf16[256,384]{1,0:T(8,128)(2,1)S(1)}, u32[]{:S(2)}, u32[]{:S(2)}) collective-permute-start(bf16[256,384]{1,0:T(8,128)(2,1)S(1)} %get-tuple-element.79), channel_id=1, source_target_pairs={{0,8},{8,0},{1,9},{9,1},{2,10},{10,2},{3,11},{11,3},{4,12},{12,4},... | collective-permute-start | bytes 589832 | tf_op jit(solution)/shard_map/ppermute | solution.py:540
  28.9 7.0 %collective-permute-start.7 = (bf16[128,384]{1,0:T(8,128)(2,1)S(1)}, bf16[128,384]{1,0:T(8,128)(2,1)S(1)}, u32[]{:S(2)}, u32[]{:S(2)}) collective-permute-start(bf16[128,384]{1,0:T(8,128)(2,1)S(1)} %act.2.refs_0_), channel_id=1, source_target_pairs={{0,4},{2,6},{4,0},{6,2},{1,5},{3,7},{5,1},{7,3},{8,12},{10,14},{12... | collective-permute-start | bytes 294920 | tf_op jit(solution)/shard_map/ppermute | solution.py:544
  32.2 7.3 %collective-permute-start.10 = (bf16[128,768]{1,0:T(8,128)(2,1)S(1)}, bf16[128,768]{1,0:T(8,128)(2,1)S(1)}, u32[]{:S(2)}, u32[]{:S(2)}) collective-permute-start(bf16[128,768]{1,0:T(8,128)(2,1)S(1)} %get-tuple-element.89.left_ref.n0), channel_id=1, source_target_pairs={{0,8},{8,0},{1,9},{9,1},{2,10},{10,2},{3,11},{11,3},{4,12},{12,4},... | collective-permute-start | bytes 589832 | tf_op jit(solution)/shard_map/ppermute | solution.py:540
  33.8 9.1 %collective-permute-start.9 = (bf16[128,768]{1,0:T(8,128)(2,1)S(1)}, bf16[128,768]{1,0:T(8,128)(2,1)S(1)}, u32[]{:S(2)}, u32[]{:S(2)}) collective-permute-start(bf16[128,768]{1,0:T(8,128)(2,1)S(1)} %get-tuple-element.89.left_ref.n0), channel_id=1, source_target_pairs={{0,2},{2,0},{4,6},{6,4},{1,3},{3,1},{5,7},{7,5},{8,10},{10,8},{12,... | collective-permute-start | bytes 589832 | tf_op jit(solution)/shard_map/ppermute | solution.py:544
  35.9 7.9 %collective-permute-start.11 = (bf16[128,384]{1,0:T(8,128)(2,1)S(1)}, bf16[128,384]{1,0:T(8,128)(2,1)S(1)}, u32[]{:S(2)}, u32[]{:S(2)}) collective-permute-start(bf16[128,384]{1,0:T(8,128)(2,1)S(1)} %collective-permute-done.7.n0), channel_id=1, source_target_pairs={{0,2},{2,0},{4,6},{6,4},{1,3},{3,1},{5,7},{7,5},{8,10},{10,8},{12,... | collective-permute-start | bytes 294920 | tf_op jit(solution)/shard_map/ppermute | solution.py:544
  36.2 7.7 %collective-permute-start.8 = (bf16[128,384]{1,0:T(8,128)(2,1)S(1)}, bf16[128,384]{1,0:T(8,128)(2,1)S(1)}, u32[]{:S(2)}, u32[]{:S(2)}) collective-permute-start(bf16[128,384]{1,0:T(8,128)(2,1)S(1)} %get-tuple-element.88), channel_id=1, source_target_pairs={{0,4},{2,6},{4,0},{6,2},{1,5},{3,7},{5,1},{7,3},{8,12},{10,14},{12... | collective-permute-start | bytes 294920 | tf_op jit(solution)/shard_map/ppermute | solution.py:544
  44.0 3.1 %collective-permute-start.12 = (bf16[128,1536]{1,0:T(8,128)(2,1)S(1)}, bf16[128,1536]{1,0:T(8,128)(2,1)S(1)}, u32[]{:S(2)}, u32[]{:S(2)}) collective-permute-start(bf16[128,1536]{1,0:T(8,128)(2,1)S(1)} %join.1.here_ref), channel_id=1, source_target_pairs={{0,1},{1,0},{2,3},{3,2},{4,5},{5,4},{6,7},{7,6},{8,9},{9,8},{10,11... | collective-permute-start | bytes 1179656 | tf_op jit(solution)/shard_map/ppermute | solution.py:540
  44.1 5.9 %collective-permute-start.13 = (bf16[128,384]{1,0:T(8,128)(2,1)S(1)}, bf16[128,384]{1,0:T(8,128)(2,1)S(1)}, u32[]{:S(2)}, u32[]{:S(2)}) collective-permute-start(bf16[128,384]{1,0:T(8,128)(2,1)S(1)} %collective-permute-done.8.n1), channel_id=1, source_target_pairs={{0,2},{2,0},{4,6},{6,4},{1,3},{3,1},{5,7},{7,5},{8,10},{10,8},{12,... | collective-permute-start | bytes 294920 | tf_op jit(solution)/shard_map/ppermute | solution.py:544
  46.6 11.8 %collective-permute-start.15 = (bf16[128,768]{1,0:T(8,128)(2,1)S(1)}, bf16[128,768]{1,0:T(8,128)(2,1)S(1)}, u32[]{:S(2)}, u32[]{:S(2)}) collective-permute-start(bf16[128,768]{1,0:T(8,128)(2,1)S(1)} %get-tuple-element.113), channel_id=1, source_target_pairs={{0,8},{8,0},{1,9},{9,1},{2,10},{10,2},{3,11},{11,3},{4,12},{12,4},... | collective-permute-start | bytes 589832 | tf_op jit(solution)/shard_map/ppermute | solution.py:540
  49.9 8.4 %collective-permute-start.14 = (bf16[64,1536]{1,0:T(8,128)(2,1)S(1)}, bf16[64,1536]{1,0:T(8,128)(2,1)S(1)}, u32[]{:S(2)}, u32[]{:S(2)}) collective-permute-start(bf16[64,1536]{1,0:T(8,128)(2,1)S(1)} %get-tuple-element.111), channel_id=1, source_target_pairs={{0,2},{2,0},{4,6},{6,4},{1,3},{3,1},{5,7},{7,5},{8,10},{10,8},{12,... | collective-permute-start | bytes 589832 | tf_op jit(solution)/shard_map/ppermute | solution.py:544
  51.8 6.6 %collective-permute-start.16 = (bf16[128,768]{1,0:T(8,128)(2,1)S(1)}, bf16[128,768]{1,0:T(8,128)(2,1)S(1)}, u32[]{:S(2)}, u32[]{:S(2)}) collective-permute-start(bf16[128,768]{1,0:T(8,128)(2,1)S(1)} %get-tuple-element.114), channel_id=1, source_target_pairs={{0,8},{2,10},{12,4},{14,6},{1,9},{3,11},{13,5},{15,7},{16,24},{18,... | collective-permute-start | bytes 589832 | tf_op jit(solution)/shard_map/ppermute | solution.py:592
  54.2 7.6 %collective-permute-start.17 = (bf16[128,768]{1,0:T(8,128)(2,1)S(1)}, bf16[128,768]{1,0:T(8,128)(2,1)S(1)}, u32[]{:S(2)}, u32[]{:S(2)}) collective-permute-start(bf16[128,768]{1,0:T(8,128)(2,1)S(1)} %get-tuple-element.116), channel_id=1, source_target_pairs={{0,1},{1,0},{2,3},{3,2},{4,5},{5,4},{6,7},{7,6},{8,9},{9,8},{10,11... | collective-permute-start | bytes 589832 | tf_op jit(solution)/shard_map/ppermute | solution.py:540
  58.6 7.2 %collective-permute-start.18 = (bf16[128,768]{1,0:T(8,128)(2,1)S(1)}, bf16[128,768]{1,0:T(8,128)(2,1)S(1)}, u32[]{:S(2)}, u32[]{:S(2)}) collective-permute-start(bf16[128,768]{1,0:T(8,128)(2,1)S(1)} %get-tuple-element.123), channel_id=1, source_target_pairs={{0,1},{1,0},{2,3},{3,2},{4,5},{5,4},{6,7},{7,6},{8,9},{9,8},{10,11... | collective-permute-start | bytes 589832 | tf_op jit(solution)/shard_map/ppermute | solution.py:540
  59.2 7.9 %collective-permute-start.19 = (bf16[32,1536]{1,0:T(8,128)(2,1)S(1)}, bf16[32,1536]{1,0:T(8,128)(2,1)S(1)}, u32[]{:S(2)}, u32[]{:S(2)}) collective-permute-start(bf16[32,1536]{1,0:T(8,128)(2,1)S(1)} %get-tuple-element.132), channel_id=1, source_target_pairs={{0,4},{2,6},{4,0},{6,2},{1,5},{3,7},{5,1},{7,3},{8,12},{10,14},{12... | collective-permute-start | bytes 294920 | tf_op jit(solution)/shard_map/ppermute | solution.py:544

commit v9 on v8

--- a/solution.py
+++ b/solution.py
@@ -285,6 +285,7 @@
             jax.ShapeDtypeStruct((rows, units), F32),
         ],
         compiler_params=params(2),
+        cost_estimate=cost(0, 1),
         name="leave",
     )(kept, got)
 
@@ -317,6 +318,7 @@
         out_specs=[VMEM] * len(shapes),
         out_shape=[jax.ShapeDtypeStruct(shape, BF16) for shape in shapes],
         compiler_params=params(2),
+        cost_estimate=cost(0, 1),
         name="act",
     )(tick, stays, got, *before)
 
@@ -329,31 +331,33 @@
     return (lax.axis_index("col") % 2) != lax.axis_index("row")
 
 
-def choose_kernel(n0, n1, far_ref, leaves_ref, joined_ref):
+def choose_kernel(n0, n1, f0, f1, leaves_ref, near_ref, far_ref):
     units = n0.shape[1]
-    joined_ref[:, :units] = n0[...]
-    joined_ref[:, units:] = n1[...]
+    for out_ref, parts in ((near_ref, (n0, n1)), (far_ref, (f0, f1))):
+        out_ref[:, :units] = parts[0][...]
+        out_ref[:, units:] = parts[1][...]
 
     @pl.when(is_near())
     def _():
-        leaves_ref[:, :units] = n0[...]
-        leaves_ref[:, units:] = n1[...]
+        leaves_ref[...] = near_ref[...]
 
     @pl.when(jnp.logical_not(is_near()))
     def _():
         leaves_ref[...] = far_ref[...]
 
 
-def choose(near_parts, if_far):
-    same = jax.ShapeDtypeStruct(if_far.shape, if_far.dtype)
+def choose(near_parts, far_parts):
+    rows, units = near_parts[0].shape
+    same = jax.ShapeDtypeStruct((rows, 2 * units), BF16)
     return pl.pallas_call(
         choose_kernel,
-        in_specs=[VMEM] * 3,
-        out_specs=[VMEM] * 2,
-        out_shape=[same, same],
+        in_specs=[VMEM] * 4,
+        out_specs=[VMEM] * 3,
+        out_shape=[same] * 3,
         compiler_params=params(2),
+        cost_estimate=cost(0, 1),
         name="choose",
-    )(*near_parts, if_far)
+    )(*near_parts, *far_parts)
 
 
 def pick_kernel(n0, n1, f2, *refs):
@@ -381,6 +385,7 @@
         out_specs=[VMEM] * (len(slots) - 2),
         out_shape=[same] * (len(slots) - 2),
         compiler_params=params(2),
+        cost_estimate=cost(0, 1),
         name="pick",
     )(*slots)
 
@@ -399,6 +404,7 @@
         out_specs=VMEM,
         out_shape=jax.ShapeDtypeStruct((rows, 2 * units), left.dtype),
         compiler_params=params(2),
+        cost_estimate=cost(0, 1),
         name="join",
     )(left, right)
 
@@ -440,7 +446,7 @@
         ],
         scratch_shapes=[pltpu.VMEM((rows, width), F32)],
         compiler_params=params(4),
-        cost_estimate=cost(8 * rows * units * width, 0),
+        cost_estimate=cost(0, 1),
         name="project",
     )(tick, here, there, in_vmem(down))
 
@@ -462,25 +468,38 @@
             jax.ShapeDtypeStruct((slots, width), BF16),
         ],
         compiler_params=params(2),
+        cost_estimate=cost(0, 1),
         name="fold",
     )(near, got)
 
 
-def unpack_rows(placing_ref, factor_ref, own_ref, got_ref):
+def unpack_kernel(after_ref, placing_ref, factor_ref, own_ref, got_ref, out_ref):
+    del after_ref
     total = own_ref[...] + got_ref[...].astype(F32)
     scaled = (total * factor_ref[:, 0:1]).astype(BF16)
-    return lax.dot_general(
+    out_ref[...] = lax.dot_general(
         placing_ref[...], scaled, (((0,), (0,)), ((), ())), preferred_element_type=F32
     ).astype(BF16)
 
 
-def gram_kernel(scale, flips, last, *refs):
+def unpack(done, placing, factor, own, got):
+    slots, rows = placing.shape
+    return pl.pallas_call(
+        unpack_kernel,
+        in_specs=[ANY] + [VMEM] * 4,
+        out_specs=VMEM,
+        out_shape=jax.ShapeDtypeStruct((rows, own.shape[1]), BF16),
+        compiler_params=params(4),
+        name="unpack",
+    )(done, placing, factor, own, got)
+
+
+def gram_kernel(scale, flips, *refs):
     count = len(flips)
     pieces = refs[1 : 1 + count]
     wide_ref = refs[1 + count]
     out_ref, done_ref, ring_ref, sems = refs[-4:]
-    if not last:
-        done_ref[...] = jnp.zeros_like(done_ref)
+    done_ref[...] = jnp.zeros_like(done_ref)
     units = pieces[0].shape[1]
     depth, _, cut = ring_ref.shape
     copies = []
@@ -499,38 +518,34 @@
             )
             copy.start()
             copies.append(copy)
-            if last and len(copies) == depth:
-                done_ref[...] = unpack_rows(*refs[2 + count : 6 + count])
     for copy in copies[-depth:]:
         copy.wait()
 
 
-def gram_piece(tick, pieces, flips, wide, gram=None, outputs=()):
+def gram_piece(tick, pieces, flips, wide, gram=None):
     rows, units = pieces[0].shape
     cut, depth = 512, 4
-    operands = [tick, *pieces, in_vmem(wide), *outputs]
-    in_specs = [ANY] + [VMEM] * (len(operands) - 1)
+    operands = [tick, *pieces, in_vmem(wide)]
+    in_specs = [ANY] + [VMEM] * (len(pieces) + 1)
     aliases = {}
     if gram is not None:
         aliases = {len(operands): 0}
         operands.append(gram)
         in_specs.append(HBM)
-    if outputs:
-        placing, _, own, _ = outputs
-        second = jax.ShapeDtypeStruct((placing.shape[1], own.shape[1]), BF16)
-    else:
-        second = pltpu.VMEM((8, 128), F32)
-    return pl.pallas_call(
-        functools.partial(gram_kernel, 2.0 / rows, flips, bool(outputs)),
+    return pl.pallas_call(
+        functools.partial(gram_kernel, 2.0 / rows, flips),
         in_specs=in_specs,
         out_specs=[HBM, VMEM],
-        out_shape=[jax.ShapeDtypeStruct((4 * units, 4 * units), F32), second],
+        out_shape=[
+            jax.ShapeDtypeStruct((4 * units, 4 * units), F32),
+            pltpu.VMEM((8, 128), F32),
+        ],
         input_output_aliases=aliases,
         scratch_shapes=[
             pltpu.VMEM((depth, units, cut), F32),
             pltpu.SemaphoreType.DMA((depth,)),
         ],
-        compiler_params=params(12),
+        compiler_params=params(10),
         cost_estimate=cost(8 * rows * units * units * len(pieces), 16 * units * units * len(pieces)),
         name="gram",
     )(*operands)
@@ -570,24 +585,25 @@
     (hidden_a,) = act(tick, stays[0], got_x[0])
 
     z2a = across(hidden_a, 2)
+    z1a = across(hidden_a, 1)
     tick, got_x[1], hidden_a = tie(tick, got_x[1], hidden_a)
     hidden_b, hidden = act(tick, stays[1], got_x[1], hidden_a)
-    z1 = across(hidden, 1)
     hidden_x = swap(hidden, "expert")
-    tick, z2a, hidden_b = tie(tick, z2a, hidden_b)
+    tick, z2a, z1a, hidden_b = tie(tick, z2a, z1a, hidden_b)
     z2b = across(hidden_b, 2)
+    z1b = across(hidden_b, 1)
     z3a = across(z2a, 1)
-    tick, z2b, z1, hidden_x, z3a = tie(tick, z2b, z1, hidden_x, z3a)
-
-    leaves, z2 = choose((z2a, z2b), z1)
+    tick, z2b, z1b, hidden_x, z3a = tie(tick, z2b, z1b, hidden_x, z3a)
+
+    leaves, z2, z1 = choose((z2a, z2b), (z1a, z1b))
     here = join(hidden, hidden_x)
     tick, z2b, leaves, here = tie(tick, z2b, leaves, here)
     z3b = across(z2b, 1)
     x2 = swap(leaves, "expert")
     there = swap(here, "row")
-    tick, there = tie(tick, there)
+    tick, there, here = tie(tick, there, here)
     near, away, hidden_c, tick = project(tick, here, there, down_held)
-    tick, z3b, away = tie(tick, z3b, away)
+    tick, z3b, away, x2 = tie(tick, z3b, away, x2)
     mine, passed, z3 = pick(hidden, z1, z2, z3a, z3b)
     x3 = lax.ppermute(
         z3,
@@ -596,20 +612,17 @@
     )
     mine_near = swap(passed, "row")
     away = across(away, 1)
-    gram, tick = gram_piece(tick, [mine], [(0, 0)], hidden_c)
+    tick, mine_near = tie(tick, mine_near)
+    gram, tick = gram_piece(tick, [mine, mine_near], [(0, 0), (0, 1)], hidden_c)
+    tick, x3 = tie(tick, x3)
+    mine_x, passed = pick(hidden_x, x2, x2, x3)
+    mine_far = swap(passed, "row")
     tick, away = tie(tick, away)
     own, onward = fold(near, away)
     onward = across(onward, 2)
-    tick, x2, x3 = tie(tick, x2, x3)
-    mine_x, passed = pick(hidden_x, x2, x2, x3)
-    mine_far = swap(passed, "row")
-    tick, mine_near = tie(tick, mine_near)
-    gram, tick = gram_piece(tick, [mine_near], [(0, 1)], hidden_c, gram)
     tick, mine_far = tie(tick, mine_far)
-    gram, expert_out = gram_piece(
-        tick, [mine_x, mine_far], [(1, 0), (1, 1)], hidden_c, gram, (placing, factor, own, onward)
-    )
-    return (expert_out, gram)
+    gram, tick = gram_piece(tick, [mine_x, mine_far], [(1, 0), (1, 1)], hidden_c, gram)
+    return (unpack(tick, placing, factor, own, onward), gram)
 
 
 def solution(mesh):

time: 75.1 us -> 73.5 us (0.979)
  starting transfers between devices: 28.3 us -> 25 us
  waiting for transfers between devices: 9.28 us -> 12 us
  Pallas kernels: 36.4 us -> 35.5 us
    ppermute x10 -> x11, starting transfers between devices: 20.3 us -> 15.5 us  [across(): return lax.ppermute(value, 'col', [(i, i ^ slot) for i in range(4)])]
    ppermute x9, waiting for transfers between devices: 0.89 us -> 2.55 us  [swap(): return lax.ppermute(value, axis, [(0, 1), (1, 0)])]
    ppermute x10 -> x11, waiting for transfers between devices: 8.39 us -> 9.44 us  [across(): return lax.ppermute(value, 'col', [(i, i ^ slot) for i in range(4)])]
    ppermute x1, starting transfers between devices: 2.43 us -> 3.4 us  [on_device(): lax.ppermute(z3, ('expert', 'col'), [(ee * 4 + cc, (1 - ee) * 4 + cc) for...]
    pallas_call x4, Pallas kernels: 15.8 us -> 14.9 us  [the longest x2 13.8 us: gram_piece(): pl.pallas_call(functools.partial(gram_kernel, 2.0 / rows, flips), in_spec...]
  transfers between devices with their start and end apart: 20 -> 21, of which waited for: 8 -> 10; matrix products, arithmetic and copies ran while one was open for 0% -> 0% of each run, Pallas kernels for 34% -> 42%
where the time goes in v9:
time: 73.5 us; the launch traced here: 73.3 us
  Pallas kernels  35.5 us (48%)
  starting transfers between devices  25 us (34%)
  waiting for transfers between devices  12 us (16%)
  between operations  0.88 us (1%)
    ppermute x11, starting transfers between devices, across(): return lax.ppermute(value, 'col', [(i, i ^ slot) for i in range(4)])  15.5 us
    pallas_call x2, Pallas kernels, gram_piece(): pl.pallas_call(functools.partial(gram_kernel, 2.0 / rows, flips), in_spec...  13.8 us
    ppermute x11, waiting for transfers between devices, across(): return lax.ppermute(value, 'col', [(i, i ^ slot) for i in range(4)])  9.44 us
    pallas_call x1, Pallas kernels, regroup(): pl.pallas_call(regroup_kernel, in_specs=[ANY, HBM], out_specs=VMEM, out_s...  6.97 us
    pallas_call x4, Pallas kernels, preacts_of(): pl.pallas_call(functools.partial(preact_kernel, first, row_flip, chunk, c...  6.27 us
    ppermute x9, starting transfers between devices, swap(): return lax.ppermute(value, axis, [(0, 1), (1, 0)])  6.09 us
    pallas_call x1, Pallas kernels, fetch(): pl.pallas_call(fetch_kernel, in_specs=[ANY, HBM], out_specs=[VMEM, VMEM],...  3.8 us
    ppermute x1, starting transfers between devices, on_device(): lax.ppermute(z3, ('expert', 'col'), [(ee * 4 + cc, (1 - ee) * 4 + cc) for...  3.4 us
  transfers between devices with their start and end apart: 21, of which 10 were waited for; matrix products, arithmetic and copies ran while one was open for 0% of the time, Pallas kernels for 42%

profile of v9, /device:TPU:0, one launch (start us, length us, event | category | flops | bytes accessed | tf_op | source)
XLA Modules:
  0.0 73.3 jit_solution(13545062184963953575)
XLA Ops:
  0.6 1.3 %pack.1 = (bf16[32,1536]{1,0:T(8,128)(2,1)S(1)}, bf16[32,128]{1,0:T(8,128)(2,1)S(1)}, f32[32,128]{1,0:T(8,128)S(1)}) custom-call(bf16[128,1536]{1,0:T(8,128)(2,1)} %tokens_ref.1, s32[2,128]{1,0:T(2,128)} %bitcast.12, s32[1,128]{1,0:T(1,128)} %bitcast.14, f32[2,128]{1,0:T(2,128)} %bitcast.13), custom_call_target="tpu_custom_call" | custom-call | tf_op jit(solution)/shard_map/pack/pallas_call | solution.py:137
  1.9 5.1 %collective-permute-start.2 = (bf16[32,1536]{1,0:T(8,128)(2,1)S(1)}, bf16[32,1536]{1,0:T(8,128)(2,1)S(1)}, u32[]{:S(2)}, u32[]{:S(2)}) collective-permute-start(bf16[32,1536]{1,0:T(8,128)(2,1)S(1)} %get-tuple-element.70.after_ref.refs_0_), channel_id=1, source_target_pairs={{0,6},{2,4},{4,2},{6,0},{1,7},{3,5},{5,3},{7,1},{8,14},{10,12},{12... | collective-permute-start | bytes 294920 | tf_op jit(solution)/shard_map/ppermute | solution.py:559
  7.7 7.0 %regroup.1 = bf16[24,1536,2,128]{3,2,1,0:T(2,128)(2,1)S(1)} custom-call(bf16[32,1536]{1,0:T(8,128)(2,1)S(1)} %get-tuple-element.70.after_ref.refs_0_, bf16[1536,24,2,128]{3,2,1,0:T(2,128)(2,1)} %bitcast.11), custom_call_target="tpu_custom_call" | custom-call | bytes 37748736 | tf_op jit(solution)/shard_map/regroup/pallas_call | solution.py:167
  15.3 2.0 %preacts_sent.2 = (f32[256,768]{1,0:T(8,128)S(1)}, bf16[256,3072]{1,0:T(8,128)(2,1)S(1)}) custom-call(bf16[32,1536]{1,0:T(8,128)(2,1)S(1)} %get-tuple-element.70.after_ref.refs_0_, bf16[32,1536]{1,0:T(8,128)(2,1)S(1)} %collective-permute-done.refs_1_, bf16[32,1536]{1,0:T(8,128)(2,1)S(1)} %collective-permute-done.1.refs_2_, ...), custom_call_target="tpu_custom_call" | custom-call | flops 1207959552 | tf_op jit(solution)/shard_map/preacts_sent/pallas_call | solution.py:260
  17.4 1.4 %preacts_sent.3 = f32[256,768]{1,0:T(8,128)S(1)} custom-call(bf16[256,3072]{1,0:T(8,128)(2,1)S(1)} %get-tuple-element.76.refs_0_.after_ref, bf16[24,3072,128]{2,1,0:T(8,128)(2,1)S(1)} %bitcast.8), custom_call_target="tpu_custom_call" | custom-call | flops 1207959552 | tf_op jit(solution)/shard_map/preacts_sent/pallas_call | solution.py:260
  19.4 1.4 %preacts_kept.2.kept_ref = f32[256,768]{1,0:T(8,128)S(1)} custom-call(bf16[256,3072]{1,0:T(8,128)(2,1)S(1)} %get-tuple-element.76.refs_0_.after_ref, bf16[24,3072,128]{2,1,0:T(8,128)(2,1)S(1)} %bitcast.9), custom_call_target="tpu_custom_call" | custom-call | flops 1207959552 | tf_op jit(solution)/shard_map/preacts_kept/pallas_call | solution.py:260
  20.9 1.6 %collective-permute-start.5 = (bf16[256,384]{1,0:T(8,128)(2,1)S(1)}, bf16[256,384]{1,0:T(8,128)(2,1)S(1)}, u32[]{:S(2)}, u32[]{:S(2)}) collective-permute-start(bf16[256,384]{1,0:T(8,128)(2,1)S(1)} %get-tuple-element.78), channel_id=1, source_target_pairs={{0,8},{8,0},{1,9},{9,1},{2,10},{10,2},{3,11},{11,3},{4,12},{12,4},... | collective-permute-start | bytes 589832 | tf_op jit(solution)/shard_map/ppermute | solution.py:555
  22.4 1.4 %preacts_kept.3.kept_ref = f32[256,768]{1,0:T(8,128)S(1)} custom-call(bf16[256,3072]{1,0:T(8,128)(2,1)S(1)} %get-tuple-element.76.refs_0_.after_ref, bf16[24,3072,128]{2,1,0:T(8,128)(2,1)S(1)} %bitcast.10), custom_call_target="tpu_custom_call" | custom-call | flops 1207959552 | tf_op jit(solution)/shard_map/preacts_kept/pallas_call | solution.py:260
  24.6 3.8 %fetch_down.1 = (bf16[3072,1536]{1,0:T(8,128)(2,1)S(1)}, f32[8,128]{1,0:T(8,128)S(1)}) custom-call(bf16[256,3072]{1,0:T(8,128)(2,1)S(1)} %get-tuple-element.76.refs_0_.after_ref, bf16[3072,1536]{1,0:T(8,128)(2,1)} %down_ref.1), custom_call_target="tpu_custom_call" | custom-call | bytes 18874368 | tf_op jit(solution)/shard_map/fetch_down/pallas_call | solution.py:198
  29.6 2.9 %collective-permute-start.7 = (bf16[128,384]{1,0:T(8,128)(2,1)S(1)}, bf16[128,384]{1,0:T(8,128)(2,1)S(1)}, u32[]{:S(2)}, u32[]{:S(2)}) collective-permute-start(bf16[128,384]{1,0:T(8,128)(2,1)S(1)} %act.2.refs_0_), channel_id=1, source_target_pairs={{0,4},{2,6},{4,0},{6,2},{1,5},{3,7},{5,1},{7,3},{8,12},{10,14},{12... | collective-permute-start | bytes 294920 | tf_op jit(solution)/shard_map/ppermute | solution.py:559
  32.6 1.6 %collective-permute-start.11 = (bf16[128,768]{1,0:T(8,128)(2,1)S(1)}, bf16[128,768]{1,0:T(8,128)(2,1)S(1)}, u32[]{:S(2)}, u32[]{:S(2)}) collective-permute-start(bf16[128,768]{1,0:T(8,128)(2,1)S(1)} %get-tuple-element.90.left_ref.n0), channel_id=1, source_target_pairs={{0,8},{8,0},{1,9},{9,1},{2,10},{10,2},{3,11},{11,3},{4,12},{12,4},... | collective-permute-start | bytes 589832 | tf_op jit(solution)/shard_map/ppermute | solution.py:555
  34.6 1.9 %collective-permute-done.7.n0 = bf16[128,384]{1,0:T(8,128)(2,1)S(1)} collective-permute-done((bf16[128,384]{1,0:T(8,128)(2,1)S(1)}, bf16[128,384]{1,0:T(8,128)(2,1)S(1)}, u32[]{:S(2)}, u32[]{:S(2)}) %collective-permute-start.7) | collective-permute-done | bytes 98336 | tf_op jit(solution)/shard_map/ppermute | solution.py:559
  36.9 3.0 %collective-permute-start.9 = (bf16[128,384]{1,0:T(8,128)(2,1)S(1)}, bf16[128,384]{1,0:T(8,128)(2,1)S(1)}, u32[]{:S(2)}, u32[]{:S(2)}) collective-permute-start(bf16[128,384]{1,0:T(8,128)(2,1)S(1)} %get-tuple-element.89), channel_id=1, source_target_pairs={{0,4},{2,6},{4,0},{6,2},{1,5},{3,7},{5,1},{7,3},{8,12},{10,14},{12... | collective-permute-start | bytes 294920 | tf_op jit(solution)/shard_map/ppermute | solution.py:559
  40.2 1.1 %collective-permute-done.10.f1 = bf16[128,384]{1,0:T(8,128)(2,1)S(1)} collective-permute-done((bf16[128,384]{1,0:T(8,128)(2,1)S(1)}, bf16[128,384]{1,0:T(8,128)(2,1)S(1)}, u32[]{:S(2)}, u32[]{:S(2)}) %collective-permute-start.10) | collective-permute-done | bytes 98336 | tf_op jit(solution)/shard_map/ppermute | solution.py:559
  41.3 1.1 %collective-permute-done.9.n1 = bf16[128,384]{1,0:T(8,128)(2,1)S(1)} collective-permute-done((bf16[128,384]{1,0:T(8,128)(2,1)S(1)}, bf16[128,384]{1,0:T(8,128)(2,1)S(1)}, u32[]{:S(2)}, u32[]{:S(2)}) %collective-permute-start.9) | collective-permute-done | bytes 98336 | tf_op jit(solution)/shard_map/ppermute | solution.py:559
  42.5 2.0 %collective-permute-done.12.refs_0_ = bf16[128,384]{1,0:T(8,128)(2,1)S(1)} collective-permute-done((bf16[128,384]{1,0:T(8,128)(2,1)S(1)}, bf16[128,384]{1,0:T(8,128)(2,1)S(1)}, u32[]{:S(2)}, u32[]{:S(2)}) %collective-permute-start.12) | collective-permute-done | bytes 98336 | tf_op jit(solution)/shard_map/ppermute | solution.py:559
  44.7 1.5 %collective-permute-start.15 = (bf16[128,768]{1,0:T(8,128)(2,1)S(1)}, bf16[128,768]{1,0:T(8,128)(2,1)S(1)}, u32[]{:S(2)}, u32[]{:S(2)}) collective-permute-start(bf16[128,768]{1,0:T(8,128)(2,1)S(1)} %get-tuple-element.107), channel_id=1, source_target_pairs={{0,8},{8,0},{1,9},{9,1},{2,10},{10,2},{3,11},{11,3},{4,12},{12,4},... | collective-permute-start | bytes 589832 | tf_op jit(solution)/shard_map/ppermute | solution.py:555
  47.3 1.6 %project.1 = (f32[64,1536]{1,0:T(8,128)S(1)}, bf16[64,1536]{1,0:T(8,128)(2,1)S(1)}, bf16[128,3072]{1,0:T(8,128)(2,1)S(1)}, f32[8,128]{1,0:T(8,128)S(1)}) custom-call(f32[8,128]{1,0:T(8,128)S(1)} %get-tuple-element.100.tick_ref, bf16[128,1536]{1,0:T(8,128)(2,1)S(1)} %join.1.here_ref, bf16[128,1536]{1,0:T(8,128)(2,1)S(1)} %collective-permute-done.13.there_ref, ...), custom_call_target="tpu_custom_call" | custom-call | bytes 1 | tf_op jit(solution)/shard_map/project/pallas_call | solution.py:437
  48.9 2.2 %collective-permute-done.14.refs_1_ = bf16[128,384]{1,0:T(8,128)(2,1)S(1)} collective-permute-done((bf16[128,384]{1,0:T(8,128)(2,1)S(1)}, bf16[128,384]{1,0:T(8,128)(2,1)S(1)}, u32[]{:S(2)}, u32[]{:S(2)}) %collective-permute-start.14) | collective-permute-done | bytes 98336 | tf_op jit(solution)/shard_map/ppermute | solution.py:559
  52.1 3.4 %collective-permute-start.17 = (bf16[128,768]{1,0:T(8,128)(2,1)S(1)}, bf16[128,768]{1,0:T(8,128)(2,1)S(1)}, u32[]{:S(2)}, u32[]{:S(2)}) collective-permute-start(bf16[128,768]{1,0:T(8,128)(2,1)S(1)} %get-tuple-element.119), channel_id=1, source_target_pairs={{0,8},{2,10},{12,4},{14,6},{1,9},{3,11},{13,5},{15,7},{16,24},{18,... | collective-permute-start | bytes 589832 | tf_op jit(solution)/shard_map/ppermute | solution.py:608
  55.5 1.1 %collective-permute-start.18 = (bf16[64,1536]{1,0:T(8,128)(2,1)S(1)}, bf16[64,1536]{1,0:T(8,128)(2,1)S(1)}, u32[]{:S(2)}, u32[]{:S(2)}) collective-permute-start(bf16[64,1536]{1,0:T(8,128)(2,1)S(1)} %get-tuple-element.121), channel_id=1, source_target_pairs={{0,2},{2,0},{4,6},{6,4},{1,3},{3,1},{5,7},{7,5},{8,10},{10,8},{12,... | collective-permute-start | bytes 589832 | tf_op jit(solution)/shard_map/ppermute | solution.py:559
  56.7 6.9 %gram.2 = (f32[3072,3072]{1,0:T(8,128)}, f32[8,128]{1,0:T(8,128)S(1)}) custom-call(f32[8,128]{1,0:T(8,128)S(1)} %get-tuple-element.114.refs_0_, bf16[128,768]{1,0:T(8,128)(2,1)S(1)} %get-tuple-element.115.refs_1_, bf16[128,768]{1,0:T(8,128)(2,1)S(1)} %collective-permute-done.16.refs_2_, bf16[128,3072]{1,0:T(8,128)(2,1)S(1)} %get-tuple-element.117.refs_3_), custom_call_target="tpu_custom_call" | custom-call | flops 1207959552 | bytes 18874368 | tf_op jit(solution)/shard_map/gram/pallas_call | solution.py:535
  64.0 1.3 %collective-permute-done.19.refs_2_ = bf16[128,768]{1,0:T(8,128)(2,1)S(1)} collective-permute-done((bf16[128,768]{1,0:T(8,128)(2,1)S(1)}, bf16[128,768]{1,0:T(8,128)(2,1)S(1)}, u32[]{:S(2)}, u32[]{:S(2)}) %collective-permute-start.19) | collective-permute-done | bytes 196640 | tf_op jit(solution)/shard_map/ppermute | solution.py:555
  65.3 6.9 %gram.3 = (f32[3072,3072]{1,0:T(8,128)}, f32[8,128]{1,0:T(8,128)S(1)}) custom-call(f32[8,128]{1,0:T(8,128)S(1)} %get-tuple-element.126.refs_0_, bf16[128,768]{1,0:T(8,128)(2,1)S(1)} %get-tuple-element.127.refs_1_, bf16[128,768]{1,0:T(8,128)(2,1)S(1)} %collective-permute-done.19.refs_2_, ...), custom_call_target="tpu_custom_call", output_to_operand_aliasing={{0}: (4, {})} | custom-call | flops 1207959552 | bytes 18874368 | tf_op jit(solution)/shard_map/gram/pallas_call | solution.py:535
  (38 shorter events, 8.8 us)
Async XLA Ops:
  1.9 12.7 %collective-permute-start.2 = (bf16[32,1536]{1,0:T(8,128)(2,1)S(1)}, bf16[32,1536]{1,0:T(8,128)(2,1)S(1)}, u32[]{:S(2)}, u32[]{:S(2)}) collective-permute-start(bf16[32,1536]{1,0:T(8,128)(2,1)S(1)} %get-tuple-element.70.after_ref.refs_0_), channel_id=1, source_target_pairs={{0,6},{2,4},{4,2},{6,0},{1,7},{3,5},{5,3},{7,1},{8,14},{10,12},{12... | collective-permute-start | bytes 294920 | tf_op jit(solution)/shard_map/ppermute | solution.py:559
  7.0 8.3 %collective-permute-start.1 = (bf16[32,1536]{1,0:T(8,128)(2,1)S(1)}, bf16[32,1536]{1,0:T(8,128)(2,1)S(1)}, u32[]{:S(2)}, u32[]{:S(2)}) collective-permute-start(bf16[32,1536]{1,0:T(8,128)(2,1)S(1)} %get-tuple-element.70.after_ref.refs_0_), channel_id=1, source_target_pairs={{0,4},{2,6},{4,0},{6,2},{1,5},{3,7},{5,1},{7,3},{8,12},{10,14},{12... | collective-permute-start | bytes 294920 | tf_op jit(solution)/shard_map/ppermute | solution.py:559
  7.0 8.3 %collective-permute-start = (bf16[32,1536]{1,0:T(8,128)(2,1)S(1)}, bf16[32,1536]{1,0:T(8,128)(2,1)S(1)}, u32[]{:S(2)}, u32[]{:S(2)}) collective-permute-start(bf16[32,1536]{1,0:T(8,128)(2,1)S(1)} %get-tuple-element.70.after_ref.refs_0_), channel_id=1, source_target_pairs={{0,2},{2,0},{4,6},{6,4},{1,3},{3,1},{5,7},{7,5},{8,10},{10,8},{12,... | collective-permute-start | bytes 294920 | tf_op jit(solution)/shard_map/ppermute | solution.py:559
  17.3 3.5 %collective-permute-start.3 = (f32[256,768]{1,0:T(8,128)S(1)}, f32[256,768]{1,0:T(8,128)S(1)}, u32[]{:S(2)}, u32[]{:S(2)}) collective-permute-start(f32[256,768]{1,0:T(8,128)S(1)} %get-tuple-element.72), channel_id=1, source_target_pairs={{0,1},{1,0},{2,3},{3,2},{4,5},{5,4},{6,7},{7,6},{8,9},{9,8},{10,11... | collective-permute-start | bytes 2359304 | tf_op jit(solution)/shard_map/ppermute | solution.py:555
  18.8 5.1 %collective-permute-start.4 = (f32[256,768]{1,0:T(8,128)S(1)}, f32[256,768]{1,0:T(8,128)S(1)}, u32[]{:S(2)}, u32[]{:S(2)}) collective-permute-start(f32[256,768]{1,0:T(8,128)S(1)} %preacts_sent.3), channel_id=1, source_target_pairs={{0,1},{1,0},{2,3},{3,2},{4,5},{5,4},{6,7},{7,6},{8,9},{9,8},{10,11... | collective-permute-start | bytes 2359304 | tf_op jit(solution)/shard_map/ppermute | solution.py:555
  20.9 7.8 %collective-permute-start.5 = (bf16[256,384]{1,0:T(8,128)(2,1)S(1)}, bf16[256,384]{1,0:T(8,128)(2,1)S(1)}, u32[]{:S(2)}, u32[]{:S(2)}) collective-permute-start(bf16[256,384]{1,0:T(8,128)(2,1)S(1)} %get-tuple-element.78), channel_id=1, source_target_pairs={{0,8},{8,0},{1,9},{9,1},{2,10},{10,2},{3,11},{11,3},{4,12},{12,4},... | collective-permute-start | bytes 589832 | tf_op jit(solution)/shard_map/ppermute | solution.py:555
  24.0 8.6 %collective-permute-start.6 = (bf16[256,384]{1,0:T(8,128)(2,1)S(1)}, bf16[256,384]{1,0:T(8,128)(2,1)S(1)}, u32[]{:S(2)}, u32[]{:S(2)}) collective-permute-start(bf16[256,384]{1,0:T(8,128)(2,1)S(1)} %get-tuple-element.80), channel_id=1, source_target_pairs={{0,8},{8,0},{1,9},{9,1},{2,10},{10,2},{3,11},{11,3},{4,12},{12,4},... | collective-permute-start | bytes 589832 | tf_op jit(solution)/shard_map/ppermute | solution.py:555
  28.8 5.8 %collective-permute-start.8 = (bf16[128,384]{1,0:T(8,128)(2,1)S(1)}, bf16[128,384]{1,0:T(8,128)(2,1)S(1)}, u32[]{:S(2)}, u32[]{:S(2)}) collective-permute-start(bf16[128,384]{1,0:T(8,128)(2,1)S(1)} %act.2.refs_0_), channel_id=1, source_target_pairs={{0,2},{2,0},{4,6},{6,4},{1,3},{3,1},{5,7},{7,5},{8,10},{10,8},{12,... | collective-permute-start | bytes 294920 | tf_op jit(solution)/shard_map/ppermute | solution.py:559
  29.6 6.9 %collective-permute-start.7 = (bf16[128,384]{1,0:T(8,128)(2,1)S(1)}, bf16[128,384]{1,0:T(8,128)(2,1)S(1)}, u32[]{:S(2)}, u32[]{:S(2)}) collective-permute-start(bf16[128,384]{1,0:T(8,128)(2,1)S(1)} %act.2.refs_0_), channel_id=1, source_target_pairs={{0,4},{2,6},{4,0},{6,2},{1,5},{3,7},{5,1},{7,3},{8,12},{10,14},{12... | collective-permute-start | bytes 294920 | tf_op jit(solution)/shard_map/ppermute | solution.py:559
  32.6 7.6 %collective-permute-start.11 = (bf16[128,768]{1,0:T(8,128)(2,1)S(1)}, bf16[128,768]{1,0:T(8,128)(2,1)S(1)}, u32[]{:S(2)}, u32[]{:S(2)}) collective-permute-start(bf16[128,768]{1,0:T(8,128)(2,1)S(1)} %get-tuple-element.90.left_ref.n0), channel_id=1, source_target_pairs={{0,8},{8,0},{1,9},{9,1},{2,10},{10,2},{3,11},{11,3},{4,12},{12,4},... | collective-permute-start | bytes 589832 | tf_op jit(solution)/shard_map/ppermute | solution.py:555
  36.5 4.9 %collective-permute-start.10 = (bf16[128,384]{1,0:T(8,128)(2,1)S(1)}, bf16[128,384]{1,0:T(8,128)(2,1)S(1)}, u32[]{:S(2)}, u32[]{:S(2)}) collective-permute-start(bf16[128,384]{1,0:T(8,128)(2,1)S(1)} %get-tuple-element.89), channel_id=1, source_target_pairs={{0,2},{2,0},{4,6},{6,4},{1,3},{3,1},{5,7},{7,5},{8,10},{10,8},{12,... | collective-permute-start | bytes 294920 | tf_op jit(solution)/shard_map/ppermute | solution.py:559
  36.9 5.6 %collective-permute-start.9 = (bf16[128,384]{1,0:T(8,128)(2,1)S(1)}, bf16[128,384]{1,0:T(8,128)(2,1)S(1)}, u32[]{:S(2)}, u32[]{:S(2)}) collective-permute-start(bf16[128,384]{1,0:T(8,128)(2,1)S(1)} %get-tuple-element.89), channel_id=1, source_target_pairs={{0,4},{2,6},{4,0},{6,2},{1,5},{3,7},{5,1},{7,3},{8,12},{10,14},{12... | collective-permute-start | bytes 294920 | tf_op jit(solution)/shard_map/ppermute | solution.py:559
  39.9 4.6 %collective-permute-start.12 = (bf16[128,384]{1,0:T(8,128)(2,1)S(1)}, bf16[128,384]{1,0:T(8,128)(2,1)S(1)}, u32[]{:S(2)}, u32[]{:S(2)}) collective-permute-start(bf16[128,384]{1,0:T(8,128)(2,1)S(1)} %collective-permute-done.7.n0), channel_id=1, source_target_pairs={{0,2},{2,0},{4,6},{6,4},{1,3},{3,1},{5,7},{7,5},{8,10},{10,8},{12,... | collective-permute-start | bytes 294920 | tf_op jit(solution)/shard_map/ppermute | solution.py:559
  44.6 2.7 %collective-permute-start.13 = (bf16[128,1536]{1,0:T(8,128)(2,1)S(1)}, bf16[128,1536]{1,0:T(8,128)(2,1)S(1)}, u32[]{:S(2)}, u32[]{:S(2)}) collective-permute-start(bf16[128,1536]{1,0:T(8,128)(2,1)S(1)} %join.1.here_ref), channel_id=1, source_target_pairs={{0,1},{1,0},{2,3},{3,2},{4,5},{5,4},{6,7},{7,6},{8,9},{9,8},{10,11... | collective-permute-start | bytes 1179656 | tf_op jit(solution)/shard_map/ppermute | solution.py:555
  44.7 7.3 %collective-permute-start.15 = (bf16[128,768]{1,0:T(8,128)(2,1)S(1)}, bf16[128,768]{1,0:T(8,128)(2,1)S(1)}, u32[]{:S(2)}, u32[]{:S(2)}) collective-permute-start(bf16[128,768]{1,0:T(8,128)(2,1)S(1)} %get-tuple-element.107), channel_id=1, source_target_pairs={{0,8},{8,0},{1,9},{9,1},{2,10},{10,2},{3,11},{11,3},{4,12},{12,4},... | collective-permute-start | bytes 589832 | tf_op jit(solution)/shard_map/ppermute | solution.py:555
  46.2 4.9 %collective-permute-start.14 = (bf16[128,384]{1,0:T(8,128)(2,1)S(1)}, bf16[128,384]{1,0:T(8,128)(2,1)S(1)}, u32[]{:S(2)}, u32[]{:S(2)}) collective-permute-start(bf16[128,384]{1,0:T(8,128)(2,1)S(1)} %collective-permute-done.9.n1), channel_id=1, source_target_pairs={{0,2},{2,0},{4,6},{6,4},{1,3},{3,1},{5,7},{7,5},{8,10},{10,8},{12,... | collective-permute-start | bytes 294920 | tf_op jit(solution)/shard_map/ppermute | solution.py:559
  52.1 4.6 %collective-permute-start.16 = (bf16[128,768]{1,0:T(8,128)(2,1)S(1)}, bf16[128,768]{1,0:T(8,128)(2,1)S(1)}, u32[]{:S(2)}, u32[]{:S(2)}) collective-permute-start(bf16[128,768]{1,0:T(8,128)(2,1)S(1)} %get-tuple-element.113), channel_id=1, source_target_pairs={{0,1},{1,0},{2,3},{3,2},{4,5},{5,4},{6,7},{7,6},{8,9},{9,8},{10,11... | collective-permute-start | bytes 589832 | tf_op jit(solution)/shard_map/ppermute | solution.py:555
  52.1 11.4 %collective-permute-start.17 = (bf16[128,768]{1,0:T(8,128)(2,1)S(1)}, bf16[128,768]{1,0:T(8,128)(2,1)S(1)}, u32[]{:S(2)}, u32[]{:S(2)}) collective-permute-start(bf16[128,768]{1,0:T(8,128)(2,1)S(1)} %get-tuple-element.119), channel_id=1, source_target_pairs={{0,8},{2,10},{12,4},{14,6},{1,9},{3,11},{13,5},{15,7},{16,24},{18,... | collective-permute-start | bytes 589832 | tf_op jit(solution)/shard_map/ppermute | solution.py:608
  55.5 8.4 %collective-permute-start.18 = (bf16[64,1536]{1,0:T(8,128)(2,1)S(1)}, bf16[64,1536]{1,0:T(8,128)(2,1)S(1)}, u32[]{:S(2)}, u32[]{:S(2)}) collective-permute-start(bf16[64,1536]{1,0:T(8,128)(2,1)S(1)} %get-tuple-element.121), channel_id=1, source_target_pairs={{0,2},{2,0},{4,6},{6,4},{1,3},{3,1},{5,7},{7,5},{8,10},{10,8},{12,... | collective-permute-start | bytes 589832 | tf_op jit(solution)/shard_map/ppermute | solution.py:559
  63.8 1.5 %collective-permute-start.19 = (bf16[128,768]{1,0:T(8,128)(2,1)S(1)}, bf16[128,768]{1,0:T(8,128)(2,1)S(1)}, u32[]{:S(2)}, u32[]{:S(2)}) collective-permute-start(bf16[128,768]{1,0:T(8,128)(2,1)S(1)} %get-tuple-element.125), channel_id=1, source_target_pairs={{0,1},{1,0},{2,3},{3,2},{4,5},{5,4},{6,7},{7,6},{8,9},{9,8},{10,11... | collective-permute-start | bytes 589832 | tf_op jit(solution)/shard_map/ppermute | solution.py:555
  64.0 8.3 %collective-permute-start.20 = (bf16[32,1536]{1,0:T(8,128)(2,1)S(1)}, bf16[32,1536]{1,0:T(8,128)(2,1)S(1)}, u32[]{:S(2)}, u32[]{:S(2)}) collective-permute-start(bf16[32,1536]{1,0:T(8,128)(2,1)S(1)} %get-tuple-element.136), channel_id=1, source_target_pairs={{0,4},{2,6},{4,0},{6,2},{1,5},{3,7},{5,1},{7,3},{8,12},{10,14},{12... | collective-permute-start | bytes 294920 | tf_op jit(solution)/shard_map/ppermute | solution.py:559

commit v10 on v9

--- a/solution.py
+++ b/solution.py
@@ -331,63 +331,63 @@
     return (lax.axis_index("col") % 2) != lax.axis_index("row")
 
 
-def choose_kernel(n0, n1, f0, f1, leaves_ref, near_ref, far_ref):
-    units = n0.shape[1]
-    for out_ref, parts in ((near_ref, (n0, n1)), (far_ref, (f0, f1))):
-        out_ref[:, :units] = parts[0][...]
-        out_ref[:, units:] = parts[1][...]
-
+def choose_kernel(near_ref, far_ref, out_ref):
     @pl.when(is_near())
     def _():
-        leaves_ref[...] = near_ref[...]
+        out_ref[...] = near_ref[...]
 
     @pl.when(jnp.logical_not(is_near()))
     def _():
-        leaves_ref[...] = far_ref[...]
-
-
-def choose(near_parts, far_parts):
-    rows, units = near_parts[0].shape
-    same = jax.ShapeDtypeStruct((rows, 2 * units), BF16)
+        out_ref[...] = far_ref[...]
+
+
+def choose(if_near, if_far):
     return pl.pallas_call(
         choose_kernel,
-        in_specs=[VMEM] * 4,
+        in_specs=[VMEM] * 2,
+        out_specs=VMEM,
+        out_shape=jax.ShapeDtypeStruct(if_near.shape, if_near.dtype),
+        compiler_params=params(2),
+        cost_estimate=cost(0, 1),
+        name="choose",
+    )(if_near, if_far)
+
+
+def pick_kernel(counts, *refs):
+    slots, at = [], 0
+    for count in counts:
+        slots.append(refs[at : at + count])
+        at += count
+    mine_ref, other_ref, last_ref = refs[at:]
+
+    def put(out_ref, parts):
+        column = 0
+        for part in parts:
+            out_ref[:, column : column + part.shape[1]] = part[...]
+            column += part.shape[1]
+
+    put(last_ref, slots[3])
+    for near, pair in ((True, slots[:2]), (False, slots[2:])):
+        for odd in (False, True):
+
+            @pl.when((is_near() == near) & (is_odd() == odd))
+            def _():
+                put(mine_ref, pair[int(odd)])
+                put(other_ref, pair[1 - int(odd)])
+
+
+def pick(*slots):
+    parts = [part for slot in slots for part in slot]
+    same = jax.ShapeDtypeStruct(slots[0][0].shape, BF16)
+    return pl.pallas_call(
+        functools.partial(pick_kernel, [len(slot) for slot in slots]),
+        in_specs=[VMEM] * len(parts),
         out_specs=[VMEM] * 3,
         out_shape=[same] * 3,
         compiler_params=params(2),
         cost_estimate=cost(0, 1),
-        name="choose",
-    )(*near_parts, *far_parts)
-
-
-def pick_kernel(n0, n1, f2, *refs):
-    if len(refs) == 3:
-        f3, mine_ref, other_ref = refs
-    else:
-        h0, h1, mine_ref, other_ref, f3 = refs
-        units = h0.shape[1]
-        f3[:, :units] = h0[...]
-        f3[:, units:] = h1[...]
-    for near, pair in ((True, (n0, n1)), (False, (f2, f3))):
-        for odd in (False, True):
-
-            @pl.when((is_near() == near) & (is_odd() == odd))
-            def _():
-                mine_ref[...] = pair[int(odd)][...]
-                other_ref[...] = pair[1 - int(odd)][...]
-
-
-def pick(*slots):
-    same = jax.ShapeDtypeStruct(slots[0].shape, slots[0].dtype)
-    return pl.pallas_call(
-        pick_kernel,
-        in_specs=[VMEM] * len(slots),
-        out_specs=[VMEM] * (len(slots) - 2),
-        out_shape=[same] * (len(slots) - 2),
-        compiler_params=params(2),
-        cost_estimate=cost(0, 1),
         name="pick",
-    )(*slots)
+    )(*parts)
 
 
 def join_kernel(left_ref, right_ref, out_ref):
@@ -591,20 +591,24 @@
     hidden_x = swap(hidden, "expert")
     tick, z2a, z1a, hidden_b = tie(tick, z2a, z1a, hidden_b)
     z2b = across(hidden_b, 2)
+    z3a = across(z2a, 1)
     z1b = across(hidden_b, 1)
-    z3a = across(z2a, 1)
-    tick, z2b, z1b, hidden_x, z3a = tie(tick, z2b, z1b, hidden_x, z3a)
-
-    leaves, z2, z1 = choose((z2a, z2b), (z1a, z1b))
+    x2a = swap(choose(z2a, z1a), "expert")
+    tick, z2b = tie(tick, z2b)
+    tick, z3a = tie(tick, z3a)
+    tick, z1b = tie(tick, z1b)
+    tick, hidden_x = tie(tick, hidden_x)
+    tick, x2a = tie(tick, x2a)
     here = join(hidden, hidden_x)
-    tick, z2b, leaves, here = tie(tick, z2b, leaves, here)
+    tick, z2b, leaves, here = tie(tick, z2b, choose(z2b, z1b), here)
     z3b = across(z2b, 1)
-    x2 = swap(leaves, "expert")
+    x2b = swap(leaves, "expert")
     there = swap(here, "row")
     tick, there, here = tie(tick, there, here)
     near, away, hidden_c, tick = project(tick, here, there, down_held)
-    tick, z3b, away, x2 = tie(tick, z3b, away, x2)
-    mine, passed, z3 = pick(hidden, z1, z2, z3a, z3b)
+    tick, z3b, away = tie(tick, z3b, away)
+    tick, x2b, z3b = tie(tick, x2b, z3b)
+    mine, passed, z3 = pick([hidden], [z1a, z1b], [z2a, z2b], [z3a, z3b])
     x3 = lax.ppermute(
         z3,
         ("expert", "col"),
@@ -615,7 +619,7 @@
     tick, mine_near = tie(tick, mine_near)
     gram, tick = gram_piece(tick, [mine, mine_near], [(0, 0), (0, 1)], hidden_c)
     tick, x3 = tie(tick, x3)
-    mine_x, passed = pick(hidden_x, x2, x2, x3)
+    mine_x, passed, _ = pick([hidden_x], [x2a, x2b], [x2a, x2b], [x3])
     mine_far = swap(passed, "row")
     tick, away = tie(tick, away)
     own, onward = fold(near, away)

time: 73.5 us -> 73 us (level)
  waiting for transfers between devices: 12 us -> 9.53 us
  starting transfers between devices: 25 us -> 26.4 us
    ppermute x11, waiting for transfers between devices: 9.44 us -> 6.22 us  [across(): return lax.ppermute(value, 'col', [(i, i ^ slot) for i in range(4)])]
    ppermute x9 -> x10, starting transfers between devices: 6.09 us -> 7.49 us  [swap(): return lax.ppermute(value, axis, [(0, 1), (1, 0)])]
    ppermute x9 -> x10, waiting for transfers between devices: 2.55 us -> 3.31 us  [swap(): return lax.ppermute(value, axis, [(0, 1), (1, 0)])]
  transfers between devices with their start and end apart: 21 -> 22, of which waited for: 10 -> 11; matrix products, arithmetic and copies ran while one was open for 0% -> 0% of each run, Pallas kernels for 42% -> 43%
where the time goes in v10:
time: 73 us; the launch traced here: 72.9 us
  Pallas kernels  36.1 us (49%)
  starting transfers between devices  26.4 us (36%)
  waiting for transfers between devices  9.53 us (13%)
  between operations  0.86 us (1%)
    ppermute x11, starting transfers between devices, across(): return lax.ppermute(value, 'col', [(i, i ^ slot) for i in range(4)])  15.5 us
    pallas_call x2, Pallas kernels, gram_piece(): pl.pallas_call(functools.partial(gram_kernel, 2.0 / rows, flips), in_spec...  13.8 us
    ppermute x10, starting transfers between devices, swap(): return lax.ppermute(value, axis, [(0, 1), (1, 0)])  7.49 us
    pallas_call x1, Pallas kernels, regroup(): pl.pallas_call(regroup_kernel, in_specs=[ANY, HBM], out_specs=VMEM, out_s...  6.97 us
    pallas_call x4, Pallas kernels, preacts_of(): pl.pallas_call(functools.partial(preact_kernel, first, row_flip, chunk, c...  6.27 us
    ppermute x11, waiting for transfers between devices, across(): return lax.ppermute(value, 'col', [(i, i ^ slot) for i in range(4)])  6.22 us
    pallas_call x1, Pallas kernels, fetch(): pl.pallas_call(fetch_kernel, in_specs=[ANY, HBM], out_specs=[VMEM, VMEM],...  3.8 us
    ppermute x1, starting transfers between devices, on_device(): lax.ppermute(z3, ('expert', 'col'), [(ee * 4 + cc, (1 - ee) * 4 + cc) for...  3.4 us
  transfers between devices with their start and end apart: 22, of which 11 were waited for; matrix products, arithmetic and copies ran while one was open for 0% of the time, Pallas kernels for 43%

profile of v10, /device:TPU:0, one launch (start us, length us, event | category | flops | bytes accessed | tf_op | source)
XLA Modules:
  0.0 72.9 jit_solution(12625140785449294161)
XLA Ops:
  0.6 1.3 %pack.1 = (bf16[32,1536]{1,0:T(8,128)(2,1)S(1)}, bf16[32,128]{1,0:T(8,128)(2,1)S(1)}, f32[32,128]{1,0:T(8,128)S(1)}) custom-call(bf16[128,1536]{1,0:T(8,128)(2,1)} %tokens_ref.1, s32[2,128]{1,0:T(2,128)} %bitcast.12, s32[1,128]{1,0:T(1,128)} %bitcast.14, f32[2,128]{1,0:T(2,128)} %bitcast.13), custom_call_target="tpu_custom_call" | custom-call | tf_op jit(solution)/shard_map/pack/pallas_call | solution.py:137
  1.9 5.1 %collective-permute-start.2 = (bf16[32,1536]{1,0:T(8,128)(2,1)S(1)}, bf16[32,1536]{1,0:T(8,128)(2,1)S(1)}, u32[]{:S(2)}, u32[]{:S(2)}) collective-permute-start(bf16[32,1536]{1,0:T(8,128)(2,1)S(1)} %get-tuple-element.74.after_ref.refs_0_), channel_id=1, source_target_pairs={{0,6},{2,4},{4,2},{6,0},{1,7},{3,5},{5,3},{7,1},{8,14},{10,12},{12... | collective-permute-start | bytes 294920 | tf_op jit(solution)/shard_map/ppermute | solution.py:559
  7.7 7.0 %regroup.1 = bf16[24,1536,2,128]{3,2,1,0:T(2,128)(2,1)S(1)} custom-call(bf16[32,1536]{1,0:T(8,128)(2,1)S(1)} %get-tuple-element.74.after_ref.refs_0_, bf16[1536,24,2,128]{3,2,1,0:T(2,128)(2,1)} %bitcast.11), custom_call_target="tpu_custom_call" | custom-call | bytes 37748736 | tf_op jit(solution)/shard_map/regroup/pallas_call | solution.py:167
  15.3 2.0 %preacts_sent.2 = (f32[256,768]{1,0:T(8,128)S(1)}, bf16[256,3072]{1,0:T(8,128)(2,1)S(1)}) custom-call(bf16[32,1536]{1,0:T(8,128)(2,1)S(1)} %get-tuple-element.74.after_ref.refs_0_, bf16[32,1536]{1,0:T(8,128)(2,1)S(1)} %collective-permute-done.refs_1_, bf16[32,1536]{1,0:T(8,128)(2,1)S(1)} %collective-permute-done.1.refs_2_, ...), custom_call_target="tpu_custom_call" | custom-call | flops 1207959552 | tf_op jit(solution)/shard_map/preacts_sent/pallas_call | solution.py:260
  17.4 1.4 %preacts_sent.3 = f32[256,768]{1,0:T(8,128)S(1)} custom-call(bf16[256,3072]{1,0:T(8,128)(2,1)S(1)} %get-tuple-element.80.refs_0_.after_ref, bf16[24,3072,128]{2,1,0:T(8,128)(2,1)S(1)} %bitcast.8), custom_call_target="tpu_custom_call" | custom-call | flops 1207959552 | tf_op jit(solution)/shard_map/preacts_sent/pallas_call | solution.py:260
  19.4 1.4 %preacts_kept.2.kept_ref = f32[256,768]{1,0:T(8,128)S(1)} custom-call(bf16[256,3072]{1,0:T(8,128)(2,1)S(1)} %get-tuple-element.80.refs_0_.after_ref, bf16[24,3072,128]{2,1,0:T(8,128)(2,1)S(1)} %bitcast.9), custom_call_target="tpu_custom_call" | custom-call | flops 1207959552 | tf_op jit(solution)/shard_map/preacts_kept/pallas_call | solution.py:260
  20.9 1.6 %collective-permute-start.5 = (bf16[256,384]{1,0:T(8,128)(2,1)S(1)}, bf16[256,384]{1,0:T(8,128)(2,1)S(1)}, u32[]{:S(2)}, u32[]{:S(2)}) collective-permute-start(bf16[256,384]{1,0:T(8,128)(2,1)S(1)} %get-tuple-element.82), channel_id=1, source_target_pairs={{0,8},{8,0},{1,9},{9,1},{2,10},{10,2},{3,11},{11,3},{4,12},{12,4},... | collective-permute-start | bytes 589832 | tf_op jit(solution)/shard_map/ppermute | solution.py:555
  22.4 1.4 %preacts_kept.3.kept_ref = f32[256,768]{1,0:T(8,128)S(1)} custom-call(bf16[256,3072]{1,0:T(8,128)(2,1)S(1)} %get-tuple-element.80.refs_0_.after_ref, bf16[24,3072,128]{2,1,0:T(8,128)(2,1)S(1)} %bitcast.10), custom_call_target="tpu_custom_call" | custom-call | flops 1207959552 | tf_op jit(solution)/shard_map/preacts_kept/pallas_call | solution.py:260
  24.6 3.8 %fetch_down.1 = (bf16[3072,1536]{1,0:T(8,128)(2,1)S(1)}, f32[8,128]{1,0:T(8,128)S(1)}) custom-call(bf16[256,3072]{1,0:T(8,128)(2,1)S(1)} %get-tuple-element.80.refs_0_.after_ref, bf16[3072,1536]{1,0:T(8,128)(2,1)} %down_ref.1), custom_call_target="tpu_custom_call" | custom-call | bytes 18874368 | tf_op jit(solution)/shard_map/fetch_down/pallas_call | solution.py:198
  29.6 2.9 %collective-permute-start.7 = (bf16[128,384]{1,0:T(8,128)(2,1)S(1)}, bf16[128,384]{1,0:T(8,128)(2,1)S(1)}, u32[]{:S(2)}, u32[]{:S(2)}) collective-permute-start(bf16[128,384]{1,0:T(8,128)(2,1)S(1)} %act.2.refs_0_), channel_id=1, source_target_pairs={{0,4},{2,6},{4,0},{6,2},{1,5},{3,7},{5,1},{7,3},{8,12},{10,14},{12... | collective-permute-start | bytes 294920 | tf_op jit(solution)/shard_map/ppermute | solution.py:559
  32.6 1.6 %collective-permute-start.12 = (bf16[128,768]{1,0:T(8,128)(2,1)S(1)}, bf16[128,768]{1,0:T(8,128)(2,1)S(1)}, u32[]{:S(2)}, u32[]{:S(2)}) collective-permute-start(bf16[128,768]{1,0:T(8,128)(2,1)S(1)} %get-tuple-element.98.left_ref.refs_0_), channel_id=1, source_target_pairs={{0,8},{8,0},{1,9},{9,1},{2,10},{10,2},{3,11},{11,3},{4,12},{12,4},... | collective-permute-start | bytes 589832 | tf_op jit(solution)/shard_map/ppermute | solution.py:555
  34.6 1.9 %collective-permute-done.7.near_ref.refs_3_ = bf16[128,384]{1,0:T(8,128)(2,1)S(1)} collective-permute-done((bf16[128,384]{1,0:T(8,128)(2,1)S(1)}, bf16[128,384]{1,0:T(8,128)(2,1)S(1)}, u32[]{:S(2)}, u32[]{:S(2)}) %collective-permute-start.7) | collective-permute-done | bytes 98336 | tf_op jit(solution)/shard_map/ppermute | solution.py:559
  36.5 1.7 %collective-permute-start.9 = (bf16[128,384]{1,0:T(8,128)(2,1)S(1)}, bf16[128,384]{1,0:T(8,128)(2,1)S(1)}, u32[]{:S(2)}, u32[]{:S(2)}) collective-permute-start(bf16[128,384]{1,0:T(8,128)(2,1)S(1)} %get-tuple-element.93), channel_id=1, source_target_pairs={{0,4},{2,6},{4,0},{6,2},{1,5},{3,7},{5,1},{7,3},{8,12},{10,14},{12... | collective-permute-start | bytes 294920 | tf_op jit(solution)/shard_map/ppermute | solution.py:559
  38.2 1.6 %collective-permute-start.10 = (bf16[128,384]{1,0:T(8,128)(2,1)S(1)}, bf16[128,384]{1,0:T(8,128)(2,1)S(1)}, u32[]{:S(2)}, u32[]{:S(2)}) collective-permute-start(bf16[128,384]{1,0:T(8,128)(2,1)S(1)} %collective-permute-done.7.near_ref.refs_3_), channel_id=1, source_target_pairs={{0,2},{2,0},{4,6},{6,4},{1,3},{3,1},{5,7},{7,5},{8,10},{10,8},{12,... | collective-permute-start | bytes 294920 | tf_op jit(solution)/shard_map/ppermute | solution.py:559
  40.2 1.5 %collective-permute-start.13 = (bf16[128,384]{1,0:T(8,128)(2,1)S(1)}, bf16[128,384]{1,0:T(8,128)(2,1)S(1)}, u32[]{:S(2)}, u32[]{:S(2)}) collective-permute-start(bf16[128,384]{1,0:T(8,128)(2,1)S(1)} %choose.2), channel_id=1, source_target_pairs={{0,8},{8,0},{1,9},{9,1},{2,10},{10,2},{3,11},{11,3},{4,12},{12,4},... | collective-permute-start | bytes 294920 | tf_op jit(solution)/shard_map/ppermute | solution.py:555
  41.8 1.3 %collective-permute-done.9.near_ref.refs_4_ = bf16[128,384]{1,0:T(8,128)(2,1)S(1)} collective-permute-done((bf16[128,384]{1,0:T(8,128)(2,1)S(1)}, bf16[128,384]{1,0:T(8,128)(2,1)S(1)}, u32[]{:S(2)}, u32[]{:S(2)}) %collective-permute-start.9) | collective-permute-done | bytes 98336 | tf_op jit(solution)/shard_map/ppermute | solution.py:559
  45.0 1.7 %collective-permute-start.15 = (bf16[128,384]{1,0:T(8,128)(2,1)S(1)}, bf16[128,384]{1,0:T(8,128)(2,1)S(1)}, u32[]{:S(2)}, u32[]{:S(2)}) collective-permute-start(bf16[128,384]{1,0:T(8,128)(2,1)S(1)} %collective-permute-done.9.near_ref.refs_4_), channel_id=1, source_target_pairs={{0,2},{2,0},{4,6},{6,4},{1,3},{3,1},{5,7},{7,5},{8,10},{10,8},{12,... | collective-permute-start | bytes 294920 | tf_op jit(solution)/shard_map/ppermute | solution.py:559
  46.7 1.5 %collective-permute-start.16 = (bf16[128,384]{1,0:T(8,128)(2,1)S(1)}, bf16[128,384]{1,0:T(8,128)(2,1)S(1)}, u32[]{:S(2)}, u32[]{:S(2)}) collective-permute-start(bf16[128,384]{1,0:T(8,128)(2,1)S(1)} %choose.3), channel_id=1, source_target_pairs={{0,8},{8,0},{1,9},{9,1},{2,10},{10,2},{3,11},{11,3},{4,12},{12,4},... | collective-permute-start | bytes 294920 | tf_op jit(solution)/shard_map/ppermute | solution.py:555
  48.2 1.6 %project.1 = (f32[64,1536]{1,0:T(8,128)S(1)}, bf16[64,1536]{1,0:T(8,128)(2,1)S(1)}, bf16[128,3072]{1,0:T(8,128)(2,1)S(1)}, f32[8,128]{1,0:T(8,128)S(1)}) custom-call(f32[8,128]{1,0:T(8,128)S(1)} %get-tuple-element.107.tick_ref, bf16[128,1536]{1,0:T(8,128)(2,1)S(1)} %join.1.here_ref, bf16[128,1536]{1,0:T(8,128)(2,1)S(1)} %collective-permute-done.14.there_ref, ...), custom_call_target="tpu_custom_call" | custom-call | bytes 1 | tf_op jit(solution)/shard_map/project/pallas_call | solution.py:437
  50.3 1.3 %collective-permute-done.16.refs_2_.refs_4_ = bf16[128,384]{1,0:T(8,128)(2,1)S(1)} collective-permute-done((bf16[128,384]{1,0:T(8,128)(2,1)S(1)}, bf16[128,384]{1,0:T(8,128)(2,1)S(1)}, u32[]{:S(2)}, u32[]{:S(2)}) %collective-permute-start.16) | collective-permute-done | bytes 98336 | tf_op jit(solution)/shard_map/ppermute | solution.py:555
  51.7 3.4 %collective-permute-start.18 = (bf16[128,768]{1,0:T(8,128)(2,1)S(1)}, bf16[128,768]{1,0:T(8,128)(2,1)S(1)}, u32[]{:S(2)}, u32[]{:S(2)}) collective-permute-start(bf16[128,768]{1,0:T(8,128)(2,1)S(1)} %get-tuple-element.126), channel_id=1, source_target_pairs={{0,8},{2,10},{12,4},{14,6},{1,9},{3,11},{13,5},{15,7},{16,24},{18,... | collective-permute-start | bytes 589832 | tf_op jit(solution)/shard_map/ppermute | solution.py:612
  55.6 6.9 %gram.2 = (f32[3072,3072]{1,0:T(8,128)}, f32[8,128]{1,0:T(8,128)S(1)}) custom-call(f32[8,128]{1,0:T(8,128)S(1)} %get-tuple-element.121.refs_0_, bf16[128,768]{1,0:T(8,128)(2,1)S(1)} %get-tuple-element.122.refs_1_, bf16[128,768]{1,0:T(8,128)(2,1)S(1)} %collective-permute-done.17.refs_2_, bf16[128,3072]{1,0:T(8,128)(2,1)S(1)} %get-tuple-element.124.refs_3_), custom_call_target="tpu_custom_call" | custom-call | flops 1207959552 | bytes 18874368 | tf_op jit(solution)/shard_map/gram/pallas_call | solution.py:535
  63.6 1.3 %collective-permute-done.20.refs_2_ = bf16[128,768]{1,0:T(8,128)(2,1)S(1)} collective-permute-done((bf16[128,768]{1,0:T(8,128)(2,1)S(1)}, bf16[128,768]{1,0:T(8,128)(2,1)S(1)}, u32[]{:S(2)}, u32[]{:S(2)}) %collective-permute-start.20) | collective-permute-done | bytes 196640 | tf_op jit(solution)/shard_map/ppermute | solution.py:555
  64.9 6.9 %gram.3 = (f32[3072,3072]{1,0:T(8,128)}, f32[8,128]{1,0:T(8,128)S(1)}) custom-call(f32[8,128]{1,0:T(8,128)S(1)} %get-tuple-element.134.refs_0_, bf16[128,768]{1,0:T(8,128)(2,1)S(1)} %get-tuple-element.135.refs_1_, bf16[128,768]{1,0:T(8,128)(2,1)S(1)} %collective-permute-done.20.refs_2_, ...), custom_call_target="tpu_custom_call", output_to_operand_aliasing={{0}: (4, {})} | custom-call | flops 1207959552 | bytes 18874368 | tf_op jit(solution)/shard_map/gram/pallas_call | solution.py:535
  (41 shorter events, 9.9 us)
Async XLA Ops:
  1.9 12.7 %collective-permute-start.2 = (bf16[32,1536]{1,0:T(8,128)(2,1)S(1)}, bf16[32,1536]{1,0:T(8,128)(2,1)S(1)}, u32[]{:S(2)}, u32[]{:S(2)}) collective-permute-start(bf16[32,1536]{1,0:T(8,128)(2,1)S(1)} %get-tuple-element.74.after_ref.refs_0_), channel_id=1, source_target_pairs={{0,6},{2,4},{4,2},{6,0},{1,7},{3,5},{5,3},{7,1},{8,14},{10,12},{12... | collective-permute-start | bytes 294920 | tf_op jit(solution)/shard_map/ppermute | solution.py:559
  7.0 8.3 %collective-permute-start.1 = (bf16[32,1536]{1,0:T(8,128)(2,1)S(1)}, bf16[32,1536]{1,0:T(8,128)(2,1)S(1)}, u32[]{:S(2)}, u32[]{:S(2)}) collective-permute-start(bf16[32,1536]{1,0:T(8,128)(2,1)S(1)} %get-tuple-element.74.after_ref.refs_0_), channel_id=1, source_target_pairs={{0,4},{2,6},{4,0},{6,2},{1,5},{3,7},{5,1},{7,3},{8,12},{10,14},{12... | collective-permute-start | bytes 294920 | tf_op jit(solution)/shard_map/ppermute | solution.py:559
  7.0 8.3 %collective-permute-start = (bf16[32,1536]{1,0:T(8,128)(2,1)S(1)}, bf16[32,1536]{1,0:T(8,128)(2,1)S(1)}, u32[]{:S(2)}, u32[]{:S(2)}) collective-permute-start(bf16[32,1536]{1,0:T(8,128)(2,1)S(1)} %get-tuple-element.74.after_ref.refs_0_), channel_id=1, source_target_pairs={{0,2},{2,0},{4,6},{6,4},{1,3},{3,1},{5,7},{7,5},{8,10},{10,8},{12,... | collective-permute-start | bytes 294920 | tf_op jit(solution)/shard_map/ppermute | solution.py:559
  17.3 3.5 %collective-permute-start.3 = (f32[256,768]{1,0:T(8,128)S(1)}, f32[256,768]{1,0:T(8,128)S(1)}, u32[]{:S(2)}, u32[]{:S(2)}) collective-permute-start(f32[256,768]{1,0:T(8,128)S(1)} %get-tuple-element.76), channel_id=1, source_target_pairs={{0,1},{1,0},{2,3},{3,2},{4,5},{5,4},{6,7},{7,6},{8,9},{9,8},{10,11... | collective-permute-start | bytes 2359304 | tf_op jit(solution)/shard_map/ppermute | solution.py:555
  18.8 5.1 %collective-permute-start.4 = (f32[256,768]{1,0:T(8,128)S(1)}, f32[256,768]{1,0:T(8,128)S(1)}, u32[]{:S(2)}, u32[]{:S(2)}) collective-permute-start(f32[256,768]{1,0:T(8,128)S(1)} %preacts_sent.3), channel_id=1, source_target_pairs={{0,1},{1,0},{2,3},{3,2},{4,5},{5,4},{6,7},{7,6},{8,9},{9,8},{10,11... | collective-permute-start | bytes 2359304 | tf_op jit(solution)/shard_map/ppermute | solution.py:555
  20.9 7.8 %collective-permute-start.5 = (bf16[256,384]{1,0:T(8,128)(2,1)S(1)}, bf16[256,384]{1,0:T(8,128)(2,1)S(1)}, u32[]{:S(2)}, u32[]{:S(2)}) collective-permute-start(bf16[256,384]{1,0:T(8,128)(2,1)S(1)} %get-tuple-element.82), channel_id=1, source_target_pairs={{0,8},{8,0},{1,9},{9,1},{2,10},{10,2},{3,11},{11,3},{4,12},{12,4},... | collective-permute-start | bytes 589832 | tf_op jit(solution)/shard_map/ppermute | solution.py:555
  24.0 8.6 %collective-permute-start.6 = (bf16[256,384]{1,0:T(8,128)(2,1)S(1)}, bf16[256,384]{1,0:T(8,128)(2,1)S(1)}, u32[]{:S(2)}, u32[]{:S(2)}) collective-permute-start(bf16[256,384]{1,0:T(8,128)(2,1)S(1)} %get-tuple-element.84), channel_id=1, source_target_pairs={{0,8},{8,0},{1,9},{9,1},{2,10},{10,2},{3,11},{11,3},{4,12},{12,4},... | collective-permute-start | bytes 589832 | tf_op jit(solution)/shard_map/ppermute | solution.py:555
  28.8 5.8 %collective-permute-start.8 = (bf16[128,384]{1,0:T(8,128)(2,1)S(1)}, bf16[128,384]{1,0:T(8,128)(2,1)S(1)}, u32[]{:S(2)}, u32[]{:S(2)}) collective-permute-start(bf16[128,384]{1,0:T(8,128)(2,1)S(1)} %act.2.refs_0_), channel_id=1, source_target_pairs={{0,2},{2,0},{4,6},{6,4},{1,3},{3,1},{5,7},{7,5},{8,10},{10,8},{12,... | collective-permute-start | bytes 294920 | tf_op jit(solution)/shard_map/ppermute | solution.py:559
  29.6 6.9 %collective-permute-start.7 = (bf16[128,384]{1,0:T(8,128)(2,1)S(1)}, bf16[128,384]{1,0:T(8,128)(2,1)S(1)}, u32[]{:S(2)}, u32[]{:S(2)}) collective-permute-start(bf16[128,384]{1,0:T(8,128)(2,1)S(1)} %act.2.refs_0_), channel_id=1, source_target_pairs={{0,4},{2,6},{4,0},{6,2},{1,5},{3,7},{5,1},{7,3},{8,12},{10,14},{12... | collective-permute-start | bytes 294920 | tf_op jit(solution)/shard_map/ppermute | solution.py:559
  32.6 12.0 %collective-permute-start.12 = (bf16[128,768]{1,0:T(8,128)(2,1)S(1)}, bf16[128,768]{1,0:T(8,128)(2,1)S(1)}, u32[]{:S(2)}, u32[]{:S(2)}) collective-permute-start(bf16[128,768]{1,0:T(8,128)(2,1)S(1)} %get-tuple-element.98.left_ref.refs_0_), channel_id=1, source_target_pairs={{0,8},{8,0},{1,9},{9,1},{2,10},{10,2},{3,11},{11,3},{4,12},{12,4},... | collective-permute-start | bytes 589832 | tf_op jit(solution)/shard_map/ppermute | solution.py:555
  36.5 6.6 %collective-permute-start.9 = (bf16[128,384]{1,0:T(8,128)(2,1)S(1)}, bf16[128,384]{1,0:T(8,128)(2,1)S(1)}, u32[]{:S(2)}, u32[]{:S(2)}) collective-permute-start(bf16[128,384]{1,0:T(8,128)(2,1)S(1)} %get-tuple-element.93), channel_id=1, source_target_pairs={{0,4},{2,6},{4,0},{6,2},{1,5},{3,7},{5,1},{7,3},{8,12},{10,14},{12... | collective-permute-start | bytes 294920 | tf_op jit(solution)/shard_map/ppermute | solution.py:559
  38.2 5.3 %collective-permute-start.10 = (bf16[128,384]{1,0:T(8,128)(2,1)S(1)}, bf16[128,384]{1,0:T(8,128)(2,1)S(1)}, u32[]{:S(2)}, u32[]{:S(2)}) collective-permute-start(bf16[128,384]{1,0:T(8,128)(2,1)S(1)} %collective-permute-done.7.near_ref.refs_3_), channel_id=1, source_target_pairs={{0,2},{2,0},{4,6},{6,4},{1,3},{3,1},{5,7},{7,5},{8,10},{10,8},{12,... | collective-permute-start | bytes 294920 | tf_op jit(solution)/shard_map/ppermute | solution.py:559
  39.8 4.8 %collective-permute-start.11 = (bf16[128,384]{1,0:T(8,128)(2,1)S(1)}, bf16[128,384]{1,0:T(8,128)(2,1)S(1)}, u32[]{:S(2)}, u32[]{:S(2)}) collective-permute-start(bf16[128,384]{1,0:T(8,128)(2,1)S(1)} %get-tuple-element.93), channel_id=1, source_target_pairs={{0,2},{2,0},{4,6},{6,4},{1,3},{3,1},{5,7},{7,5},{8,10},{10,8},{12,... | collective-permute-start | bytes 294920 | tf_op jit(solution)/shard_map/ppermute | solution.py:559
  40.2 4.7 %collective-permute-start.13 = (bf16[128,384]{1,0:T(8,128)(2,1)S(1)}, bf16[128,384]{1,0:T(8,128)(2,1)S(1)}, u32[]{:S(2)}, u32[]{:S(2)}) collective-permute-start(bf16[128,384]{1,0:T(8,128)(2,1)S(1)} %choose.2), channel_id=1, source_target_pairs={{0,8},{8,0},{1,9},{9,1},{2,10},{10,2},{3,11},{11,3},{4,12},{12,4},... | collective-permute-start | bytes 294920 | tf_op jit(solution)/shard_map/ppermute | solution.py:555
  45.0 3.2 %collective-permute-start.14 = (bf16[128,1536]{1,0:T(8,128)(2,1)S(1)}, bf16[128,1536]{1,0:T(8,128)(2,1)S(1)}, u32[]{:S(2)}, u32[]{:S(2)}) collective-permute-start(bf16[128,1536]{1,0:T(8,128)(2,1)S(1)} %join.1.here_ref), channel_id=1, source_target_pairs={{0,1},{1,0},{2,3},{3,2},{4,5},{5,4},{6,7},{7,6},{8,9},{9,8},{10,11... | collective-permute-start | bytes 1179656 | tf_op jit(solution)/shard_map/ppermute | solution.py:555
  45.0 5.2 %collective-permute-start.15 = (bf16[128,384]{1,0:T(8,128)(2,1)S(1)}, bf16[128,384]{1,0:T(8,128)(2,1)S(1)}, u32[]{:S(2)}, u32[]{:S(2)}) collective-permute-start(bf16[128,384]{1,0:T(8,128)(2,1)S(1)} %collective-permute-done.9.near_ref.refs_4_), channel_id=1, source_target_pairs={{0,2},{2,0},{4,6},{6,4},{1,3},{3,1},{5,7},{7,5},{8,10},{10,8},{12,... | collective-permute-start | bytes 294920 | tf_op jit(solution)/shard_map/ppermute | solution.py:559
  46.7 4.9 %collective-permute-start.16 = (bf16[128,384]{1,0:T(8,128)(2,1)S(1)}, bf16[128,384]{1,0:T(8,128)(2,1)S(1)}, u32[]{:S(2)}, u32[]{:S(2)}) collective-permute-start(bf16[128,384]{1,0:T(8,128)(2,1)S(1)} %choose.3), channel_id=1, source_target_pairs={{0,8},{8,0},{1,9},{9,1},{2,10},{10,2},{3,11},{11,3},{4,12},{12,4},... | collective-permute-start | bytes 294920 | tf_op jit(solution)/shard_map/ppermute | solution.py:555
  51.6 4.0 %collective-permute-start.17 = (bf16[128,768]{1,0:T(8,128)(2,1)S(1)}, bf16[128,768]{1,0:T(8,128)(2,1)S(1)}, u32[]{:S(2)}, u32[]{:S(2)}) collective-permute-start(bf16[128,768]{1,0:T(8,128)(2,1)S(1)} %get-tuple-element.120), channel_id=1, source_target_pairs={{0,1},{1,0},{2,3},{3,2},{4,5},{5,4},{6,7},{7,6},{8,9},{9,8},{10,11... | collective-permute-start | bytes 589832 | tf_op jit(solution)/shard_map/ppermute | solution.py:555
  51.7 10.8 %collective-permute-start.18 = (bf16[128,768]{1,0:T(8,128)(2,1)S(1)}, bf16[128,768]{1,0:T(8,128)(2,1)S(1)}, u32[]{:S(2)}, u32[]{:S(2)}) collective-permute-start(bf16[128,768]{1,0:T(8,128)(2,1)S(1)} %get-tuple-element.126), channel_id=1, source_target_pairs={{0,8},{2,10},{12,4},{14,6},{1,9},{3,11},{13,5},{15,7},{16,24},{18,... | collective-permute-start | bytes 589832 | tf_op jit(solution)/shard_map/ppermute | solution.py:612
  55.1 8.3 %collective-permute-start.19 = (bf16[64,1536]{1,0:T(8,128)(2,1)S(1)}, bf16[64,1536]{1,0:T(8,128)(2,1)S(1)}, u32[]{:S(2)}, u32[]{:S(2)}) collective-permute-start(bf16[64,1536]{1,0:T(8,128)(2,1)S(1)} %get-tuple-element.128), channel_id=1, source_target_pairs={{0,2},{2,0},{4,6},{6,4},{1,3},{3,1},{5,7},{7,5},{8,10},{10,8},{12,... | collective-permute-start | bytes 589832 | tf_op jit(solution)/shard_map/ppermute | solution.py:559
  63.5 1.4 %collective-permute-start.20 = (bf16[128,768]{1,0:T(8,128)(2,1)S(1)}, bf16[128,768]{1,0:T(8,128)(2,1)S(1)}, u32[]{:S(2)}, u32[]{:S(2)}) collective-permute-start(bf16[128,768]{1,0:T(8,128)(2,1)S(1)} %get-tuple-element.133), channel_id=1, source_target_pairs={{0,1},{1,0},{2,3},{3,2},{4,5},{5,4},{6,7},{7,6},{8,9},{9,8},{10,11... | collective-permute-start | bytes 589832 | tf_op jit(solution)/shard_map/ppermute | solution.py:555
  63.5 8.3 %collective-permute-start.21 = (bf16[32,1536]{1,0:T(8,128)(2,1)S(1)}, bf16[32,1536]{1,0:T(8,128)(2,1)S(1)}, u32[]{:S(2)}, u32[]{:S(2)}) collective-permute-start(bf16[32,1536]{1,0:T(8,128)(2,1)S(1)} %get-tuple-element.144), channel_id=1, source_target_pairs={{0,4},{2,6},{4,0},{6,2},{1,5},{3,7},{5,1},{7,3},{8,12},{10,14},{12... | collective-permute-start | bytes 294920 | tf_op jit(solution)/shard_map/ppermute | solution.py:559

commit v11 on v10

--- a/solution.py
+++ b/solution.py
@@ -353,20 +353,19 @@
     )(if_near, if_far)
 
 
+def put(out_ref, parts):
+    column = 0
+    for part in parts:
+        out_ref[:, column : column + part.shape[1]] = part[...]
+        column += part.shape[1]
+
+
 def pick_kernel(counts, *refs):
     slots, at = [], 0
     for count in counts:
         slots.append(refs[at : at + count])
         at += count
-    mine_ref, other_ref, last_ref = refs[at:]
-
-    def put(out_ref, parts):
-        column = 0
-        for part in parts:
-            out_ref[:, column : column + part.shape[1]] = part[...]
-            column += part.shape[1]
-
-    put(last_ref, slots[3])
+    mine_ref, other_ref = refs[at : at + 2]
     for near, pair in ((True, slots[:2]), (False, slots[2:])):
         for odd in (False, True):
 
@@ -375,19 +374,62 @@
                 put(mine_ref, pair[int(odd)])
                 put(other_ref, pair[1 - int(odd)])
 
-
-def pick(*slots):
+        if len(refs) > at + 2:
+
+            @pl.when(is_near() == near)
+            def _():
+                put(refs[-1], (slots[2][-1] if near else slots[1][-1], *slots[3]))
+
+
+def pick(*slots, leaves=False):
     parts = [part for slot in slots for part in slot]
-    same = jax.ShapeDtypeStruct(slots[0][0].shape, BF16)
+    rows, units = slots[0][0].shape
+    shapes = [(rows, units)] * 2
+    if leaves:
+        shapes.append((rows, units + slots[1][-1].shape[1]))
     return pl.pallas_call(
         functools.partial(pick_kernel, [len(slot) for slot in slots]),
         in_specs=[VMEM] * len(parts),
-        out_specs=[VMEM] * 3,
-        out_shape=[same] * 3,
+        out_specs=[VMEM] * len(shapes),
+        out_shape=[jax.ShapeDtypeStruct(shape, BF16) for shape in shapes],
         compiler_params=params(2),
         cost_estimate=cost(0, 1),
         name="pick",
     )(*parts)
+
+
+def pick_far_kernel(own_ref, first_ref, rest_ref, mine_ref, other_ref):
+    units = first_ref.shape[1]
+
+    def fill(out_ref, slot):
+        if slot == 0:
+            out_ref[...] = own_ref[...]
+        elif slot == 3:
+            out_ref[...] = rest_ref[:, units:]
+        else:
+            out_ref[:, :units] = first_ref[...]
+            out_ref[:, units:] = rest_ref[:, :units]
+
+    for near, pair in ((True, (0, 1)), (False, (2, 3))):
+        for odd in (False, True):
+
+            @pl.when((is_near() == near) & (is_odd() == odd))
+            def _():
+                fill(mine_ref, pair[int(odd)])
+                fill(other_ref, pair[1 - int(odd)])
+
+
+def pick_far(own, first, rest):
+    same = jax.ShapeDtypeStruct(own.shape, BF16)
+    return pl.pallas_call(
+        pick_far_kernel,
+        in_specs=[VMEM] * 3,
+        out_specs=[VMEM] * 2,
+        out_shape=[same] * 2,
+        compiler_params=params(2),
+        cost_estimate=cost(0, 1),
+        name="pick_far",
+    )(own, first, rest)
 
 
 def join_kernel(left_ref, right_ref, out_ref):
@@ -600,26 +642,20 @@
     tick, hidden_x = tie(tick, hidden_x)
     tick, x2a = tie(tick, x2a)
     here = join(hidden, hidden_x)
-    tick, z2b, leaves, here = tie(tick, z2b, choose(z2b, z1b), here)
+    tick, z2b, here = tie(tick, z2b, here)
     z3b = across(z2b, 1)
-    x2b = swap(leaves, "expert")
     there = swap(here, "row")
     tick, there, here = tie(tick, there, here)
     near, away, hidden_c, tick = project(tick, here, there, down_held)
     tick, z3b, away = tie(tick, z3b, away)
-    tick, x2b, z3b = tie(tick, x2b, z3b)
-    mine, passed, z3 = pick([hidden], [z1a, z1b], [z2a, z2b], [z3a, z3b])
-    x3 = lax.ppermute(
-        z3,
-        ("expert", "col"),
-        [(ee * 4 + cc, (1 - ee) * 4 + cc) for ee in range(2) for cc in range(4) if cc // 2 == ee],
-    )
+    mine, passed, leaves = pick([hidden], [z1a, z1b], [z2a, z2b], [z3a, z3b], leaves=True)
+    rest = swap(leaves, "expert")
     mine_near = swap(passed, "row")
     away = across(away, 1)
     tick, mine_near = tie(tick, mine_near)
     gram, tick = gram_piece(tick, [mine, mine_near], [(0, 0), (0, 1)], hidden_c)
-    tick, x3 = tie(tick, x3)
-    mine_x, passed, _ = pick([hidden_x], [x2a, x2b], [x2a, x2b], [x3])
+    tick, rest = tie(tick, rest)
+    mine_x, passed = pick_far(hidden_x, x2a, rest)
     mine_far = swap(passed, "row")
     tick, away = tie(tick, away)
     own, onward = fold(near, away)

time: 73 us -> 70.3 us (0.963)
  starting transfers between devices: 26.4 us -> 24.7 us
    ppermute x1 -> x0, starting transfers between devices: 3.4 us -> none  [on_device(): lax.ppermute(z3, ('expert', 'col'), [(ee * 4 + cc, (1 - ee) * 4 + cc) for...]
    ppermute x10, waiting for transfers between devices: 3.31 us -> 1.46 us  [swap(): return lax.ppermute(value, axis, [(0, 1), (1, 0)])]
    ppermute x11, starting transfers between devices: 15.5 us -> 17.1 us  [across(): return lax.ppermute(value, 'col', [(i, i ^ slot) for i in range(4)])]
    ppermute x11, waiting for transfers between devices: 6.22 us -> 7.65 us  [across(): return lax.ppermute(value, 'col', [(i, i ^ slot) for i in range(4)])]
    pallas_call x2 -> x1, Pallas kernels: 0.99 us -> 0.07 us  [pick(): pl.pallas_call(functools.partial(pick_kernel, [len(slot) for slot in slot...]
  transfers between devices with their start and end apart: 22 -> 21, of which waited for: 11 -> 10; matrix products, arithmetic and copies ran while one was open for 0% -> 0% of each run, Pallas kernels for 43% -> 44%
where the time goes in v11:
time: 70.3 us; the launch traced here: 70.2 us
  Pallas kernels  35.4 us (50%)
  starting transfers between devices  24.7 us (35%)
  waiting for transfers between devices  9.11 us (13%)
  between operations  0.86 us (1%)
    ppermute x11, starting transfers between devices, across(): return lax.ppermute(value, 'col', [(i, i ^ slot) for i in range(4)])  17.1 us
    pallas_call x2, Pallas kernels, gram_piece(): pl.pallas_call(functools.partial(gram_kernel, 2.0 / rows, flips), in_spec...  13.8 us
    ppermute x11, waiting for transfers between devices, across(): return lax.ppermute(value, 'col', [(i, i ^ slot) for i in range(4)])  7.65 us
    ppermute x10, starting transfers between devices, swap(): return lax.ppermute(value, axis, [(0, 1), (1, 0)])  7.62 us
    pallas_call x1, Pallas kernels, regroup(): pl.pallas_call(regroup_kernel, in_specs=[ANY, HBM], out_specs=VMEM, out_s...  6.97 us
    pallas_call x4, Pallas kernels, preacts_of(): pl.pallas_call(functools.partial(preact_kernel, first, row_flip, chunk, c...  6.27 us
    pallas_call x1, Pallas kernels, fetch(): pl.pallas_call(fetch_kernel, in_specs=[ANY, HBM], out_specs=[VMEM, VMEM],...  3.8 us
    pallas_call x1, Pallas kernels, project(): pl.pallas_call(project_kernel, in_specs=[ANY] + [VMEM] * 3, out_specs=[VM...  1.6 us
  transfers between devices with their start and end apart: 21, of which 10 were waited for; matrix products, arithmetic and copies ran while one was open for 0% of the time, Pallas kernels for 44%

profile of v11, /device:TPU:0, one launch (start us, length us, event | category | flops | bytes accessed | tf_op | source)
XLA Modules:
  0.0 70.2 jit_solution(10985300817011665132)
XLA Ops:
  0.6 1.3 %pack.1 = (bf16[32,1536]{1,0:T(8,128)(2,1)S(1)}, bf16[32,128]{1,0:T(8,128)(2,1)S(1)}, f32[32,128]{1,0:T(8,128)S(1)}) custom-call(bf16[128,1536]{1,0:T(8,128)(2,1)} %tokens_ref.1, s32[2,128]{1,0:T(2,128)} %bitcast.12, s32[1,128]{1,0:T(1,128)} %bitcast.14, f32[2,128]{1,0:T(2,128)} %bitcast.13), custom_call_target="tpu_custom_call" | custom-call | tf_op jit(solution)/shard_map/pack/pallas_call | solution.py:137
  1.9 5.1 %collective-permute-start.2 = (bf16[32,1536]{1,0:T(8,128)(2,1)S(1)}, bf16[32,1536]{1,0:T(8,128)(2,1)S(1)}, u32[]{:S(2)}, u32[]{:S(2)}) collective-permute-start(bf16[32,1536]{1,0:T(8,128)(2,1)S(1)} %get-tuple-element.70.after_ref.refs_0_), channel_id=1, source_target_pairs={{0,6},{2,4},{4,2},{6,0},{1,7},{3,5},{5,3},{7,1},{8,14},{10,12},{12... | collective-permute-start | bytes 294920 | tf_op jit(solution)/shard_map/ppermute | solution.py:601
  7.7 7.0 %regroup.1 = bf16[24,1536,2,128]{3,2,1,0:T(2,128)(2,1)S(1)} custom-call(bf16[32,1536]{1,0:T(8,128)(2,1)S(1)} %get-tuple-element.70.after_ref.refs_0_, bf16[1536,24,2,128]{3,2,1,0:T(2,128)(2,1)} %bitcast.11), custom_call_target="tpu_custom_call" | custom-call | bytes 37748736 | tf_op jit(solution)/shard_map/regroup/pallas_call | solution.py:167
  15.3 2.0 %preacts_sent.2 = (f32[256,768]{1,0:T(8,128)S(1)}, bf16[256,3072]{1,0:T(8,128)(2,1)S(1)}) custom-call(bf16[32,1536]{1,0:T(8,128)(2,1)S(1)} %get-tuple-element.70.after_ref.refs_0_, bf16[32,1536]{1,0:T(8,128)(2,1)S(1)} %collective-permute-done.refs_1_, bf16[32,1536]{1,0:T(8,128)(2,1)S(1)} %collective-permute-done.1.refs_2_, ...), custom_call_target="tpu_custom_call" | custom-call | flops 1207959552 | tf_op jit(solution)/shard_map/preacts_sent/pallas_call | solution.py:260
  17.4 1.4 %preacts_sent.3 = f32[256,768]{1,0:T(8,128)S(1)} custom-call(bf16[256,3072]{1,0:T(8,128)(2,1)S(1)} %get-tuple-element.76.refs_0_.after_ref, bf16[24,3072,128]{2,1,0:T(8,128)(2,1)S(1)} %bitcast.8), custom_call_target="tpu_custom_call" | custom-call | flops 1207959552 | tf_op jit(solution)/shard_map/preacts_sent/pallas_call | solution.py:260
  19.4 1.4 %preacts_kept.2.kept_ref = f32[256,768]{1,0:T(8,128)S(1)} custom-call(bf16[256,3072]{1,0:T(8,128)(2,1)S(1)} %get-tuple-element.76.refs_0_.after_ref, bf16[24,3072,128]{2,1,0:T(8,128)(2,1)S(1)} %bitcast.9), custom_call_target="tpu_custom_call" | custom-call | flops 1207959552 | tf_op jit(solution)/shard_map/preacts_kept/pallas_call | solution.py:260
  20.9 1.6 %collective-permute-start.5 = (bf16[256,384]{1,0:T(8,128)(2,1)S(1)}, bf16[256,384]{1,0:T(8,128)(2,1)S(1)}, u32[]{:S(2)}, u32[]{:S(2)}) collective-permute-start(bf16[256,384]{1,0:T(8,128)(2,1)S(1)} %get-tuple-element.78), channel_id=1, source_target_pairs={{0,8},{8,0},{1,9},{9,1},{2,10},{10,2},{3,11},{11,3},{4,12},{12,4},... | collective-permute-start | bytes 589832 | tf_op jit(solution)/shard_map/ppermute | solution.py:597
  22.4 1.4 %preacts_kept.3.kept_ref = f32[256,768]{1,0:T(8,128)S(1)} custom-call(bf16[256,3072]{1,0:T(8,128)(2,1)S(1)} %get-tuple-element.76.refs_0_.after_ref, bf16[24,3072,128]{2,1,0:T(8,128)(2,1)S(1)} %bitcast.10), custom_call_target="tpu_custom_call" | custom-call | flops 1207959552 | tf_op jit(solution)/shard_map/preacts_kept/pallas_call | solution.py:260
  24.6 3.8 %fetch_down.1 = (bf16[3072,1536]{1,0:T(8,128)(2,1)S(1)}, f32[8,128]{1,0:T(8,128)S(1)}) custom-call(bf16[256,3072]{1,0:T(8,128)(2,1)S(1)} %get-tuple-element.76.refs_0_.after_ref, bf16[3072,1536]{1,0:T(8,128)(2,1)} %down_ref.1), custom_call_target="tpu_custom_call" | custom-call | bytes 18874368 | tf_op jit(solution)/shard_map/fetch_down/pallas_call | solution.py:198
  29.6 2.9 %collective-permute-start.7 = (bf16[128,384]{1,0:T(8,128)(2,1)S(1)}, bf16[128,384]{1,0:T(8,128)(2,1)S(1)}, u32[]{:S(2)}, u32[]{:S(2)}) collective-permute-start(bf16[128,384]{1,0:T(8,128)(2,1)S(1)} %act.2.refs_0_), channel_id=1, source_target_pairs={{0,4},{2,6},{4,0},{6,2},{1,5},{3,7},{5,1},{7,3},{8,12},{10,14},{12... | collective-permute-start | bytes 294920 | tf_op jit(solution)/shard_map/ppermute | solution.py:601
  32.6 1.6 %collective-permute-start.12 = (bf16[128,768]{1,0:T(8,128)(2,1)S(1)}, bf16[128,768]{1,0:T(8,128)(2,1)S(1)}, u32[]{:S(2)}, u32[]{:S(2)}) collective-permute-start(bf16[128,768]{1,0:T(8,128)(2,1)S(1)} %get-tuple-element.94.left_ref.refs_0_), channel_id=1, source_target_pairs={{0,8},{8,0},{1,9},{9,1},{2,10},{10,2},{3,11},{11,3},{4,12},{12,4},... | collective-permute-start | bytes 589832 | tf_op jit(solution)/shard_map/ppermute | solution.py:597
  34.6 1.9 %collective-permute-done.7.near_ref.refs_3_ = bf16[128,384]{1,0:T(8,128)(2,1)S(1)} collective-permute-done((bf16[128,384]{1,0:T(8,128)(2,1)S(1)}, bf16[128,384]{1,0:T(8,128)(2,1)S(1)}, u32[]{:S(2)}, u32[]{:S(2)}) %collective-permute-start.7) | collective-permute-done | bytes 98336 | tf_op jit(solution)/shard_map/ppermute | solution.py:601
  36.5 1.7 %collective-permute-start.9 = (bf16[128,384]{1,0:T(8,128)(2,1)S(1)}, bf16[128,384]{1,0:T(8,128)(2,1)S(1)}, u32[]{:S(2)}, u32[]{:S(2)}) collective-permute-start(bf16[128,384]{1,0:T(8,128)(2,1)S(1)} %get-tuple-element.89), channel_id=1, source_target_pairs={{0,4},{2,6},{4,0},{6,2},{1,5},{3,7},{5,1},{7,3},{8,12},{10,14},{12... | collective-permute-start | bytes 294920 | tf_op jit(solution)/shard_map/ppermute | solution.py:601
  38.2 1.6 %collective-permute-start.10 = (bf16[128,384]{1,0:T(8,128)(2,1)S(1)}, bf16[128,384]{1,0:T(8,128)(2,1)S(1)}, u32[]{:S(2)}, u32[]{:S(2)}) collective-permute-start(bf16[128,384]{1,0:T(8,128)(2,1)S(1)} %collective-permute-done.7.near_ref.refs_3_), channel_id=1, source_target_pairs={{0,2},{2,0},{4,6},{6,4},{1,3},{3,1},{5,7},{7,5},{8,10},{10,8},{12,... | collective-permute-start | bytes 294920 | tf_op jit(solution)/shard_map/ppermute | solution.py:601
  40.2 1.5 %collective-permute-start.13 = (bf16[128,384]{1,0:T(8,128)(2,1)S(1)}, bf16[128,384]{1,0:T(8,128)(2,1)S(1)}, u32[]{:S(2)}, u32[]{:S(2)}) collective-permute-start(bf16[128,384]{1,0:T(8,128)(2,1)S(1)} %choose.1), channel_id=1, source_target_pairs={{0,8},{8,0},{1,9},{9,1},{2,10},{10,2},{3,11},{11,3},{4,12},{12,4},... | collective-permute-start | bytes 294920 | tf_op jit(solution)/shard_map/ppermute | solution.py:597
  41.8 1.3 %collective-permute-done.9.refs_4_ = bf16[128,384]{1,0:T(8,128)(2,1)S(1)} collective-permute-done((bf16[128,384]{1,0:T(8,128)(2,1)S(1)}, bf16[128,384]{1,0:T(8,128)(2,1)S(1)}, u32[]{:S(2)}, u32[]{:S(2)}) %collective-permute-start.9) | collective-permute-done | bytes 98336 | tf_op jit(solution)/shard_map/ppermute | solution.py:601
  45.0 1.7 %collective-permute-start.15 = (bf16[128,384]{1,0:T(8,128)(2,1)S(1)}, bf16[128,384]{1,0:T(8,128)(2,1)S(1)}, u32[]{:S(2)}, u32[]{:S(2)}) collective-permute-start(bf16[128,384]{1,0:T(8,128)(2,1)S(1)} %collective-permute-done.9.refs_4_), channel_id=1, source_target_pairs={{0,2},{2,0},{4,6},{6,4},{1,3},{3,1},{5,7},{7,5},{8,10},{10,8},{12,... | collective-permute-start | bytes 294920 | tf_op jit(solution)/shard_map/ppermute | solution.py:601
  46.7 1.6 %project.1 = (f32[64,1536]{1,0:T(8,128)S(1)}, bf16[64,1536]{1,0:T(8,128)(2,1)S(1)}, bf16[128,3072]{1,0:T(8,128)(2,1)S(1)}, f32[8,128]{1,0:T(8,128)S(1)}) custom-call(f32[8,128]{1,0:T(8,128)S(1)} %get-tuple-element.102.tick_ref, bf16[128,1536]{1,0:T(8,128)(2,1)S(1)} %join.1.here_ref, bf16[128,1536]{1,0:T(8,128)(2,1)S(1)} %collective-permute-done.14.there_ref, ...), custom_call_target="tpu_custom_call" | custom-call | bytes 1 | tf_op jit(solution)/shard_map/project/pallas_call | solution.py:479
  48.3 1.9 %collective-permute-done.15.refs_6_ = bf16[128,384]{1,0:T(8,128)(2,1)S(1)} collective-permute-done((bf16[128,384]{1,0:T(8,128)(2,1)S(1)}, bf16[128,384]{1,0:T(8,128)(2,1)S(1)}, u32[]{:S(2)}, u32[]{:S(2)}) %collective-permute-start.15) | collective-permute-done | bytes 98336 | tf_op jit(solution)/shard_map/ppermute | solution.py:601
  50.4 1.5 %collective-permute-start.17 = (bf16[128,1152]{1,0:T(8,128)(2,1)S(1)}, bf16[128,1152]{1,0:T(8,128)(2,1)S(1)}, u32[]{:S(2)}, u32[]{:S(2)}) collective-permute-start(bf16[128,1152]{1,0:T(8,128)(2,1)S(1)} %get-tuple-element.119), channel_id=1, source_target_pairs={{0,8},{8,0},{1,9},{9,1},{2,10},{10,2},{3,11},{11,3},{4,12},{12,4},... | collective-permute-start | bytes 884744 | tf_op jit(solution)/shard_map/ppermute | solution.py:597
  51.9 1.6 %collective-permute-start.18 = (bf16[64,1536]{1,0:T(8,128)(2,1)S(1)}, bf16[64,1536]{1,0:T(8,128)(2,1)S(1)}, u32[]{:S(2)}, u32[]{:S(2)}) collective-permute-start(bf16[64,1536]{1,0:T(8,128)(2,1)S(1)} %get-tuple-element.121), channel_id=1, source_target_pairs={{0,2},{2,0},{4,6},{6,4},{1,3},{3,1},{5,7},{7,5},{8,10},{10,8},{12,... | collective-permute-start | bytes 589832 | tf_op jit(solution)/shard_map/ppermute | solution.py:601
  53.5 6.9 %gram.2 = (f32[3072,3072]{1,0:T(8,128)}, f32[8,128]{1,0:T(8,128)S(1)}) custom-call(f32[8,128]{1,0:T(8,128)S(1)} %get-tuple-element.114.refs_0_, bf16[128,768]{1,0:T(8,128)(2,1)S(1)} %get-tuple-element.115.refs_1_, bf16[128,768]{1,0:T(8,128)(2,1)S(1)} %collective-permute-done.16.refs_2_, bf16[128,3072]{1,0:T(8,128)(2,1)S(1)} %get-tuple-element.117.refs_3_), custom_call_target="tpu_custom_call" | custom-call | flops 1207959552 | bytes 18874368 | tf_op jit(solution)/shard_map/gram/pallas_call | solution.py:577
  62.2 6.9 %gram.3 = (f32[3072,3072]{1,0:T(8,128)}, f32[8,128]{1,0:T(8,128)S(1)}) custom-call(f32[8,128]{1,0:T(8,128)S(1)} %get-tuple-element.126.refs_0_, bf16[128,768]{1,0:T(8,128)(2,1)S(1)} %get-tuple-element.127.refs_1_, bf16[128,768]{1,0:T(8,128)(2,1)S(1)} %collective-permute-done.19.refs_2_, ...), custom_call_target="tpu_custom_call", output_to_operand_aliasing={{0}: (4, {})} | custom-call | flops 1207959552 | bytes 18874368 | tf_op jit(solution)/shard_map/gram/pallas_call | solution.py:577
  69.1 1.1 %unpack.1 = bf16[128,1536]{1,0:T(8,128)(2,1)} custom-call(f32[8,128]{1,0:T(8,128)S(1)} %get-tuple-element.130.after_ref, bf16[32,128]{1,0:T(8,128)(2,1)S(1)} %get-tuple-element.131.placing_ref, f32[32,128]{1,0:T(8,128)S(1)} %get-tuple-element.132.factor_ref, f32[32,1536]{1,0:T(8,128)S(1)} %get-tuple-element.135.own_ref, ...), custom_call_target="tpu_custom_call" | custom-call | tf_op jit(solution)/shard_map/unpack/pallas_call | solution.py:529
  (38 shorter events, 8.6 us)
Async XLA Ops:
  1.9 12.7 %collective-permute-start.2 = (bf16[32,1536]{1,0:T(8,128)(2,1)S(1)}, bf16[32,1536]{1,0:T(8,128)(2,1)S(1)}, u32[]{:S(2)}, u32[]{:S(2)}) collective-permute-start(bf16[32,1536]{1,0:T(8,128)(2,1)S(1)} %get-tuple-element.70.after_ref.refs_0_), channel_id=1, source_target_pairs={{0,6},{2,4},{4,2},{6,0},{1,7},{3,5},{5,3},{7,1},{8,14},{10,12},{12... | collective-permute-start | bytes 294920 | tf_op jit(solution)/shard_map/ppermute | solution.py:601
  7.0 8.3 %collective-permute-start.1 = (bf16[32,1536]{1,0:T(8,128)(2,1)S(1)}, bf16[32,1536]{1,0:T(8,128)(2,1)S(1)}, u32[]{:S(2)}, u32[]{:S(2)}) collective-permute-start(bf16[32,1536]{1,0:T(8,128)(2,1)S(1)} %get-tuple-element.70.after_ref.refs_0_), channel_id=1, source_target_pairs={{0,4},{2,6},{4,0},{6,2},{1,5},{3,7},{5,1},{7,3},{8,12},{10,14},{12... | collective-permute-start | bytes 294920 | tf_op jit(solution)/shard_map/ppermute | solution.py:601
  7.0 8.3 %collective-permute-start = (bf16[32,1536]{1,0:T(8,128)(2,1)S(1)}, bf16[32,1536]{1,0:T(8,128)(2,1)S(1)}, u32[]{:S(2)}, u32[]{:S(2)}) collective-permute-start(bf16[32,1536]{1,0:T(8,128)(2,1)S(1)} %get-tuple-element.70.after_ref.refs_0_), channel_id=1, source_target_pairs={{0,2},{2,0},{4,6},{6,4},{1,3},{3,1},{5,7},{7,5},{8,10},{10,8},{12,... | collective-permute-start | bytes 294920 | tf_op jit(solution)/shard_map/ppermute | solution.py:601
  17.3 3.5 %collective-permute-start.3 = (f32[256,768]{1,0:T(8,128)S(1)}, f32[256,768]{1,0:T(8,128)S(1)}, u32[]{:S(2)}, u32[]{:S(2)}) collective-permute-start(f32[256,768]{1,0:T(8,128)S(1)} %get-tuple-element.72), channel_id=1, source_target_pairs={{0,1},{1,0},{2,3},{3,2},{4,5},{5,4},{6,7},{7,6},{8,9},{9,8},{10,11... | collective-permute-start | bytes 2359304 | tf_op jit(solution)/shard_map/ppermute | solution.py:597
  18.8 5.1 %collective-permute-start.4 = (f32[256,768]{1,0:T(8,128)S(1)}, f32[256,768]{1,0:T(8,128)S(1)}, u32[]{:S(2)}, u32[]{:S(2)}) collective-permute-start(f32[256,768]{1,0:T(8,128)S(1)} %preacts_sent.3), channel_id=1, source_target_pairs={{0,1},{1,0},{2,3},{3,2},{4,5},{5,4},{6,7},{7,6},{8,9},{9,8},{10,11... | collective-permute-start | bytes 2359304 | tf_op jit(solution)/shard_map/ppermute | solution.py:597
  20.9 7.8 %collective-permute-start.5 = (bf16[256,384]{1,0:T(8,128)(2,1)S(1)}, bf16[256,384]{1,0:T(8,128)(2,1)S(1)}, u32[]{:S(2)}, u32[]{:S(2)}) collective-permute-start(bf16[256,384]{1,0:T(8,128)(2,1)S(1)} %get-tuple-element.78), channel_id=1, source_target_pairs={{0,8},{8,0},{1,9},{9,1},{2,10},{10,2},{3,11},{11,3},{4,12},{12,4},... | collective-permute-start | bytes 589832 | tf_op jit(solution)/shard_map/ppermute | solution.py:597
  24.0 8.6 %collective-permute-start.6 = (bf16[256,384]{1,0:T(8,128)(2,1)S(1)}, bf16[256,384]{1,0:T(8,128)(2,1)S(1)}, u32[]{:S(2)}, u32[]{:S(2)}) collective-permute-start(bf16[256,384]{1,0:T(8,128)(2,1)S(1)} %get-tuple-element.80), channel_id=1, source_target_pairs={{0,8},{8,0},{1,9},{9,1},{2,10},{10,2},{3,11},{11,3},{4,12},{12,4},... | collective-permute-start | bytes 589832 | tf_op jit(solution)/shard_map/ppermute | solution.py:597
  28.8 5.8 %collective-permute-start.8 = (bf16[128,384]{1,0:T(8,128)(2,1)S(1)}, bf16[128,384]{1,0:T(8,128)(2,1)S(1)}, u32[]{:S(2)}, u32[]{:S(2)}) collective-permute-start(bf16[128,384]{1,0:T(8,128)(2,1)S(1)} %act.2.refs_0_), channel_id=1, source_target_pairs={{0,2},{2,0},{4,6},{6,4},{1,3},{3,1},{5,7},{7,5},{8,10},{10,8},{12,... | collective-permute-start | bytes 294920 | tf_op jit(solution)/shard_map/ppermute | solution.py:601
  29.6 6.9 %collective-permute-start.7 = (bf16[128,384]{1,0:T(8,128)(2,1)S(1)}, bf16[128,384]{1,0:T(8,128)(2,1)S(1)}, u32[]{:S(2)}, u32[]{:S(2)}) collective-permute-start(bf16[128,384]{1,0:T(8,128)(2,1)S(1)} %act.2.refs_0_), channel_id=1, source_target_pairs={{0,4},{2,6},{4,0},{6,2},{1,5},{3,7},{5,1},{7,3},{8,12},{10,14},{12... | collective-permute-start | bytes 294920 | tf_op jit(solution)/shard_map/ppermute | solution.py:601
  32.6 12.0 %collective-permute-start.12 = (bf16[128,768]{1,0:T(8,128)(2,1)S(1)}, bf16[128,768]{1,0:T(8,128)(2,1)S(1)}, u32[]{:S(2)}, u32[]{:S(2)}) collective-permute-start(bf16[128,768]{1,0:T(8,128)(2,1)S(1)} %get-tuple-element.94.left_ref.refs_0_), channel_id=1, source_target_pairs={{0,8},{8,0},{1,9},{9,1},{2,10},{10,2},{3,11},{11,3},{4,12},{12,4},... | collective-permute-start | bytes 589832 | tf_op jit(solution)/shard_map/ppermute | solution.py:597
  36.5 6.6 %collective-permute-start.9 = (bf16[128,384]{1,0:T(8,128)(2,1)S(1)}, bf16[128,384]{1,0:T(8,128)(2,1)S(1)}, u32[]{:S(2)}, u32[]{:S(2)}) collective-permute-start(bf16[128,384]{1,0:T(8,128)(2,1)S(1)} %get-tuple-element.89), channel_id=1, source_target_pairs={{0,4},{2,6},{4,0},{6,2},{1,5},{3,7},{5,1},{7,3},{8,12},{10,14},{12... | collective-permute-start | bytes 294920 | tf_op jit(solution)/shard_map/ppermute | solution.py:601
  38.2 5.3 %collective-permute-start.10 = (bf16[128,384]{1,0:T(8,128)(2,1)S(1)}, bf16[128,384]{1,0:T(8,128)(2,1)S(1)}, u32[]{:S(2)}, u32[]{:S(2)}) collective-permute-start(bf16[128,384]{1,0:T(8,128)(2,1)S(1)} %collective-permute-done.7.near_ref.refs_3_), channel_id=1, source_target_pairs={{0,2},{2,0},{4,6},{6,4},{1,3},{3,1},{5,7},{7,5},{8,10},{10,8},{12,... | collective-permute-start | bytes 294920 | tf_op jit(solution)/shard_map/ppermute | solution.py:601
  39.8 4.8 %collective-permute-start.11 = (bf16[128,384]{1,0:T(8,128)(2,1)S(1)}, bf16[128,384]{1,0:T(8,128)(2,1)S(1)}, u32[]{:S(2)}, u32[]{:S(2)}) collective-permute-start(bf16[128,384]{1,0:T(8,128)(2,1)S(1)} %get-tuple-element.89), channel_id=1, source_target_pairs={{0,2},{2,0},{4,6},{6,4},{1,3},{3,1},{5,7},{7,5},{8,10},{10,8},{12,... | collective-permute-start | bytes 294920 | tf_op jit(solution)/shard_map/ppermute | solution.py:601
  40.2 4.7 %collective-permute-start.13 = (bf16[128,384]{1,0:T(8,128)(2,1)S(1)}, bf16[128,384]{1,0:T(8,128)(2,1)S(1)}, u32[]{:S(2)}, u32[]{:S(2)}) collective-permute-start(bf16[128,384]{1,0:T(8,128)(2,1)S(1)} %choose.1), channel_id=1, source_target_pairs={{0,8},{8,0},{1,9},{9,1},{2,10},{10,2},{3,11},{11,3},{4,12},{12,4},... | collective-permute-start | bytes 294920 | tf_op jit(solution)/shard_map/ppermute | solution.py:597
  44.9 1.8 %collective-permute-start.14 = (bf16[128,1536]{1,0:T(8,128)(2,1)S(1)}, bf16[128,1536]{1,0:T(8,128)(2,1)S(1)}, u32[]{:S(2)}, u32[]{:S(2)}) collective-permute-start(bf16[128,1536]{1,0:T(8,128)(2,1)S(1)} %join.1.here_ref), channel_id=1, source_target_pairs={{0,1},{1,0},{2,3},{3,2},{4,5},{5,4},{6,7},{7,6},{8,9},{9,8},{10,11... | collective-permute-start | bytes 1179656 | tf_op jit(solution)/shard_map/ppermute | solution.py:597
  45.0 5.2 %collective-permute-start.15 = (bf16[128,384]{1,0:T(8,128)(2,1)S(1)}, bf16[128,384]{1,0:T(8,128)(2,1)S(1)}, u32[]{:S(2)}, u32[]{:S(2)}) collective-permute-start(bf16[128,384]{1,0:T(8,128)(2,1)S(1)} %collective-permute-done.9.refs_4_), channel_id=1, source_target_pairs={{0,2},{2,0},{4,6},{6,4},{1,3},{3,1},{5,7},{7,5},{8,10},{10,8},{12,... | collective-permute-start | bytes 294920 | tf_op jit(solution)/shard_map/ppermute | solution.py:601
  50.3 3.2 %collective-permute-start.16 = (bf16[128,768]{1,0:T(8,128)(2,1)S(1)}, bf16[128,768]{1,0:T(8,128)(2,1)S(1)}, u32[]{:S(2)}, u32[]{:S(2)}) collective-permute-start(bf16[128,768]{1,0:T(8,128)(2,1)S(1)} %get-tuple-element.113), channel_id=1, source_target_pairs={{0,1},{1,0},{2,3},{3,2},{4,5},{5,4},{6,7},{7,6},{8,9},{9,8},{10,11... | collective-permute-start | bytes 589832 | tf_op jit(solution)/shard_map/ppermute | solution.py:597
  50.4 10.0 %collective-permute-start.17 = (bf16[128,1152]{1,0:T(8,128)(2,1)S(1)}, bf16[128,1152]{1,0:T(8,128)(2,1)S(1)}, u32[]{:S(2)}, u32[]{:S(2)}) collective-permute-start(bf16[128,1152]{1,0:T(8,128)(2,1)S(1)} %get-tuple-element.119), channel_id=1, source_target_pairs={{0,8},{8,0},{1,9},{9,1},{2,10},{10,2},{3,11},{11,3},{4,12},{12,4},... | collective-permute-start | bytes 884744 | tf_op jit(solution)/shard_map/ppermute | solution.py:597
  51.9 8.8 %collective-permute-start.18 = (bf16[64,1536]{1,0:T(8,128)(2,1)S(1)}, bf16[64,1536]{1,0:T(8,128)(2,1)S(1)}, u32[]{:S(2)}, u32[]{:S(2)}) collective-permute-start(bf16[64,1536]{1,0:T(8,128)(2,1)S(1)} %get-tuple-element.121), channel_id=1, source_target_pairs={{0,2},{2,0},{4,6},{6,4},{1,3},{3,1},{5,7},{7,5},{8,10},{10,8},{12,... | collective-permute-start | bytes 589832 | tf_op jit(solution)/shard_map/ppermute | solution.py:601
  60.7 1.5 %collective-permute-start.19 = (bf16[128,768]{1,0:T(8,128)(2,1)S(1)}, bf16[128,768]{1,0:T(8,128)(2,1)S(1)}, u32[]{:S(2)}, u32[]{:S(2)}) collective-permute-start(bf16[128,768]{1,0:T(8,128)(2,1)S(1)} %get-tuple-element.125), channel_id=1, source_target_pairs={{0,1},{1,0},{2,3},{3,2},{4,5},{5,4},{6,7},{7,6},{8,9},{9,8},{10,11... | collective-permute-start | bytes 589832 | tf_op jit(solution)/shard_map/ppermute | solution.py:597
  60.8 8.3 %collective-permute-start.20 = (bf16[32,1536]{1,0:T(8,128)(2,1)S(1)}, bf16[32,1536]{1,0:T(8,128)(2,1)S(1)}, u32[]{:S(2)}, u32[]{:S(2)}) collective-permute-start(bf16[32,1536]{1,0:T(8,128)(2,1)S(1)} %get-tuple-element.136), channel_id=1, source_target_pairs={{0,4},{2,6},{4,0},{6,2},{1,5},{3,7},{5,1},{7,3},{8,12},{10,14},{12... | collective-permute-start | bytes 294920 | tf_op jit(solution)/shard_map/ppermute | solution.py:601

commit v12 on v11

--- a/solution.py
+++ b/solution.py
@@ -631,9 +631,10 @@
     tick, got_x[1], hidden_a = tie(tick, got_x[1], hidden_a)
     hidden_b, hidden = act(tick, stays[1], got_x[1], hidden_a)
     hidden_x = swap(hidden, "expert")
-    tick, z2a, z1a, hidden_b = tie(tick, z2a, z1a, hidden_b)
     z2b = across(hidden_b, 2)
+    tick, z2a = tie(tick, z2a)
     z3a = across(z2a, 1)
+    tick, z1a, hidden_b = tie(tick, z1a, hidden_b)
     z1b = across(hidden_b, 1)
     x2a = swap(choose(z2a, z1a), "expert")
     tick, z2b = tie(tick, z2b)

time: 70.3 us -> 68.9 us (0.980)
  waiting for transfers between devices: 9.11 us -> 6.62 us
  starting transfers between devices: 24.7 us -> 25.8 us
    ppermute x11, waiting for transfers between devices: 7.65 us -> 5.51 us  [across(): return lax.ppermute(value, 'col', [(i, i ^ slot) for i in range(4)])]
    ppermute x10, starting transfers between devices: 7.62 us -> 8.81 us  [swap(): return lax.ppermute(value, axis, [(0, 1), (1, 0)])]
  transfers between devices with their start and end apart: 21 -> 21, of which waited for: 10 -> 10; matrix products, arithmetic and copies ran while one was open for 0% -> 0% of each run, Pallas kernels for 44% -> 45%
where the time goes in v12:
time: 68.9 us; the launch traced here: 68.7 us
  Pallas kernels  35.4 us (51%)
  starting transfers between devices  25.8 us (37%)
  waiting for transfers between devices  6.62 us (10%)
  between operations  0.85 us (1%)
    ppermute x11, starting transfers between devices, across(): return lax.ppermute(value, 'col', [(i, i ^ slot) for i in range(4)])  17 us
    pallas_call x2, Pallas kernels, gram_piece(): pl.pallas_call(functools.partial(gram_kernel, 2.0 / rows, flips), in_spec...  13.8 us
    ppermute x10, starting transfers between devices, swap(): return lax.ppermute(value, axis, [(0, 1), (1, 0)])  8.81 us
    pallas_call x1, Pallas kernels, regroup(): pl.pallas_call(regroup_kernel, in_specs=[ANY, HBM], out_specs=VMEM, out_s...  6.97 us
    pallas_call x4, Pallas kernels, preacts_of(): pl.pallas_call(functools.partial(preact_kernel, first, row_flip, chunk, c...  6.27 us
    ppermute x11, waiting for transfers between devices, across(): return lax.ppermute(value, 'col', [(i, i ^ slot) for i in range(4)])  5.51 us
    pallas_call x1, Pallas kernels, fetch(): pl.pallas_call(fetch_kernel, in_specs=[ANY, HBM], out_specs=[VMEM, VMEM],...  3.8 us
    pallas_call x1, Pallas kernels, project(): pl.pallas_call(project_kernel, in_specs=[ANY] + [VMEM] * 3, out_specs=[VM...  1.6 us
  transfers between devices with their start and end apart: 21, of which 10 were waited for; matrix products, arithmetic and copies ran while one was open for 0% of the time, Pallas kernels for 45%

profile of v12, /device:TPU:0, one launch (start us, length us, event | category | flops | bytes accessed | tf_op | source)
XLA Modules:
  0.0 68.7 jit_solution(12461278704049244914)
XLA Ops:
  0.6 1.3 %pack.1 = (bf16[32,1536]{1,0:T(8,128)(2,1)S(1)}, bf16[32,128]{1,0:T(8,128)(2,1)S(1)}, f32[32,128]{1,0:T(8,128)S(1)}) custom-call(bf16[128,1536]{1,0:T(8,128)(2,1)} %tokens_ref.1, s32[2,128]{1,0:T(2,128)} %bitcast.12, s32[1,128]{1,0:T(1,128)} %bitcast.14, f32[2,128]{1,0:T(2,128)} %bitcast.13), custom_call_target="tpu_custom_call" | custom-call | tf_op jit(solution)/shard_map/pack/pallas_call | solution.py:137
  1.9 5.1 %collective-permute-start.2 = (bf16[32,1536]{1,0:T(8,128)(2,1)S(1)}, bf16[32,1536]{1,0:T(8,128)(2,1)S(1)}, u32[]{:S(2)}, u32[]{:S(2)}) collective-permute-start(bf16[32,1536]{1,0:T(8,128)(2,1)S(1)} %get-tuple-element.71.after_ref.refs_0_), channel_id=1, source_target_pairs={{0,6},{2,4},{4,2},{6,0},{1,7},{3,5},{5,3},{7,1},{8,14},{10,12},{12... | collective-permute-start | bytes 294920 | tf_op jit(solution)/shard_map/ppermute | solution.py:601
  7.7 7.0 %regroup.1 = bf16[24,1536,2,128]{3,2,1,0:T(2,128)(2,1)S(1)} custom-call(bf16[32,1536]{1,0:T(8,128)(2,1)S(1)} %get-tuple-element.71.after_ref.refs_0_, bf16[1536,24,2,128]{3,2,1,0:T(2,128)(2,1)} %bitcast.11), custom_call_target="tpu_custom_call" | custom-call | bytes 37748736 | tf_op jit(solution)/shard_map/regroup/pallas_call | solution.py:167
  15.3 2.0 %preacts_sent.2 = (f32[256,768]{1,0:T(8,128)S(1)}, bf16[256,3072]{1,0:T(8,128)(2,1)S(1)}) custom-call(bf16[32,1536]{1,0:T(8,128)(2,1)S(1)} %get-tuple-element.71.after_ref.refs_0_, bf16[32,1536]{1,0:T(8,128)(2,1)S(1)} %collective-permute-done.refs_1_, bf16[32,1536]{1,0:T(8,128)(2,1)S(1)} %collective-permute-done.1.refs_2_, ...), custom_call_target="tpu_custom_call" | custom-call | flops 1207959552 | tf_op jit(solution)/shard_map/preacts_sent/pallas_call | solution.py:260
  17.4 1.4 %preacts_sent.3 = f32[256,768]{1,0:T(8,128)S(1)} custom-call(bf16[256,3072]{1,0:T(8,128)(2,1)S(1)} %get-tuple-element.77.refs_0_.after_ref, bf16[24,3072,128]{2,1,0:T(8,128)(2,1)S(1)} %bitcast.8), custom_call_target="tpu_custom_call" | custom-call | flops 1207959552 | tf_op jit(solution)/shard_map/preacts_sent/pallas_call | solution.py:260
  19.4 1.4 %preacts_kept.2.kept_ref = f32[256,768]{1,0:T(8,128)S(1)} custom-call(bf16[256,3072]{1,0:T(8,128)(2,1)S(1)} %get-tuple-element.77.refs_0_.after_ref, bf16[24,3072,128]{2,1,0:T(8,128)(2,1)S(1)} %bitcast.9), custom_call_target="tpu_custom_call" | custom-call | flops 1207959552 | tf_op jit(solution)/shard_map/preacts_kept/pallas_call | solution.py:260
  20.9 1.6 %collective-permute-start.5 = (bf16[256,384]{1,0:T(8,128)(2,1)S(1)}, bf16[256,384]{1,0:T(8,128)(2,1)S(1)}, u32[]{:S(2)}, u32[]{:S(2)}) collective-permute-start(bf16[256,384]{1,0:T(8,128)(2,1)S(1)} %get-tuple-element.79), channel_id=1, source_target_pairs={{0,8},{8,0},{1,9},{9,1},{2,10},{10,2},{3,11},{11,3},{4,12},{12,4},... | collective-permute-start | bytes 589832 | tf_op jit(solution)/shard_map/ppermute | solution.py:597
  22.4 1.4 %preacts_kept.3.kept_ref = f32[256,768]{1,0:T(8,128)S(1)} custom-call(bf16[256,3072]{1,0:T(8,128)(2,1)S(1)} %get-tuple-element.77.refs_0_.after_ref, bf16[24,3072,128]{2,1,0:T(8,128)(2,1)S(1)} %bitcast.10), custom_call_target="tpu_custom_call" | custom-call | flops 1207959552 | tf_op jit(solution)/shard_map/preacts_kept/pallas_call | solution.py:260
  24.6 3.8 %fetch_down.1 = (bf16[3072,1536]{1,0:T(8,128)(2,1)S(1)}, f32[8,128]{1,0:T(8,128)S(1)}) custom-call(bf16[256,3072]{1,0:T(8,128)(2,1)S(1)} %get-tuple-element.77.refs_0_.after_ref, bf16[3072,1536]{1,0:T(8,128)(2,1)} %down_ref.1), custom_call_target="tpu_custom_call" | custom-call | bytes 18874368 | tf_op jit(solution)/shard_map/fetch_down/pallas_call | solution.py:198
  28.8 1.7 %collective-permute-start.7 = (bf16[128,384]{1,0:T(8,128)(2,1)S(1)}, bf16[128,384]{1,0:T(8,128)(2,1)S(1)}, u32[]{:S(2)}, u32[]{:S(2)}) collective-permute-start(bf16[128,384]{1,0:T(8,128)(2,1)S(1)} %act.2.refs_0_), channel_id=1, source_target_pairs={{0,4},{2,6},{4,0},{6,2},{1,5},{3,7},{5,1},{7,3},{8,12},{10,14},{12... | collective-permute-start | bytes 294920 | tf_op jit(solution)/shard_map/ppermute | solution.py:601
  30.5 2.0 %collective-permute-start.8 = (bf16[128,384]{1,0:T(8,128)(2,1)S(1)}, bf16[128,384]{1,0:T(8,128)(2,1)S(1)}, u32[]{:S(2)}, u32[]{:S(2)}) collective-permute-start(bf16[128,384]{1,0:T(8,128)(2,1)S(1)} %act.2.refs_0_), channel_id=1, source_target_pairs={{0,2},{2,0},{4,6},{6,4},{1,3},{3,1},{5,7},{7,5},{8,10},{10,8},{12,... | collective-permute-start | bytes 294920 | tf_op jit(solution)/shard_map/ppermute | solution.py:601
  32.6 1.6 %collective-permute-start.12 = (bf16[128,768]{1,0:T(8,128)(2,1)S(1)}, bf16[128,768]{1,0:T(8,128)(2,1)S(1)}, u32[]{:S(2)}, u32[]{:S(2)}) collective-permute-start(bf16[128,768]{1,0:T(8,128)(2,1)S(1)} %get-tuple-element.96.left_ref.refs_0_), channel_id=1, source_target_pairs={{0,8},{8,0},{1,9},{9,1},{2,10},{10,2},{3,11},{11,3},{4,12},{12,4},... | collective-permute-start | bytes 589832 | tf_op jit(solution)/shard_map/ppermute | solution.py:597
  34.2 1.1 %collective-permute-start.9 = (bf16[128,384]{1,0:T(8,128)(2,1)S(1)}, bf16[128,384]{1,0:T(8,128)(2,1)S(1)}, u32[]{:S(2)}, u32[]{:S(2)}) collective-permute-start(bf16[128,384]{1,0:T(8,128)(2,1)S(1)} %get-tuple-element.94), channel_id=1, source_target_pairs={{0,4},{2,6},{4,0},{6,2},{1,5},{3,7},{5,1},{7,3},{8,12},{10,14},{12... | collective-permute-start | bytes 294920 | tf_op jit(solution)/shard_map/ppermute | solution.py:601
  35.8 1.5 %collective-permute-start.10 = (bf16[128,384]{1,0:T(8,128)(2,1)S(1)}, bf16[128,384]{1,0:T(8,128)(2,1)S(1)}, u32[]{:S(2)}, u32[]{:S(2)}) collective-permute-start(bf16[128,384]{1,0:T(8,128)(2,1)S(1)} %collective-permute-done.7.near_ref.refs_3_), channel_id=1, source_target_pairs={{0,2},{2,0},{4,6},{6,4},{1,3},{3,1},{5,7},{7,5},{8,10},{10,8},{12,... | collective-permute-start | bytes 294920 | tf_op jit(solution)/shard_map/ppermute | solution.py:601
  37.9 2.2 %collective-permute-start.13 = (bf16[128,384]{1,0:T(8,128)(2,1)S(1)}, bf16[128,384]{1,0:T(8,128)(2,1)S(1)}, u32[]{:S(2)}, u32[]{:S(2)}) collective-permute-start(bf16[128,384]{1,0:T(8,128)(2,1)S(1)} %choose.1), channel_id=1, source_target_pairs={{0,8},{8,0},{1,9},{9,1},{2,10},{10,2},{3,11},{11,3},{4,12},{12,4},... | collective-permute-start | bytes 294920 | tf_op jit(solution)/shard_map/ppermute | solution.py:597
  41.5 1.1 %collective-permute-done.11.refs_2_ = bf16[128,384]{1,0:T(8,128)(2,1)S(1)} collective-permute-done((bf16[128,384]{1,0:T(8,128)(2,1)S(1)}, bf16[128,384]{1,0:T(8,128)(2,1)S(1)}, u32[]{:S(2)}, u32[]{:S(2)}) %collective-permute-start.11) | collective-permute-done | bytes 98336 | tf_op jit(solution)/shard_map/ppermute | solution.py:601
  42.8 1.5 %collective-permute-start.15 = (bf16[128,384]{1,0:T(8,128)(2,1)S(1)}, bf16[128,384]{1,0:T(8,128)(2,1)S(1)}, u32[]{:S(2)}, u32[]{:S(2)}) collective-permute-start(bf16[128,384]{1,0:T(8,128)(2,1)S(1)} %collective-permute-done.9.refs_4_), channel_id=1, source_target_pairs={{0,2},{2,0},{4,6},{6,4},{1,3},{3,1},{5,7},{7,5},{8,10},{10,8},{12,... | collective-permute-start | bytes 294920 | tf_op jit(solution)/shard_map/ppermute | solution.py:601
  44.5 1.6 %project.1 = (f32[64,1536]{1,0:T(8,128)S(1)}, bf16[64,1536]{1,0:T(8,128)(2,1)S(1)}, bf16[128,3072]{1,0:T(8,128)(2,1)S(1)}, f32[8,128]{1,0:T(8,128)S(1)}) custom-call(f32[8,128]{1,0:T(8,128)S(1)} %get-tuple-element.104.tick_ref, bf16[128,1536]{1,0:T(8,128)(2,1)S(1)} %join.1.here_ref, bf16[128,1536]{1,0:T(8,128)(2,1)S(1)} %collective-permute-done.14.there_ref, ...), custom_call_target="tpu_custom_call" | custom-call | bytes 1 | tf_op jit(solution)/shard_map/project/pallas_call | solution.py:479
  46.1 1.9 %collective-permute-done.15.refs_6_ = bf16[128,384]{1,0:T(8,128)(2,1)S(1)} collective-permute-done((bf16[128,384]{1,0:T(8,128)(2,1)S(1)}, bf16[128,384]{1,0:T(8,128)(2,1)S(1)}, u32[]{:S(2)}, u32[]{:S(2)}) %collective-permute-start.15) | collective-permute-done | bytes 98336 | tf_op jit(solution)/shard_map/ppermute | solution.py:601
  48.1 2.1 %collective-permute-start.17 = (bf16[128,1152]{1,0:T(8,128)(2,1)S(1)}, bf16[128,1152]{1,0:T(8,128)(2,1)S(1)}, u32[]{:S(2)}, u32[]{:S(2)}) collective-permute-start(bf16[128,1152]{1,0:T(8,128)(2,1)S(1)} %get-tuple-element.121), channel_id=1, source_target_pairs={{0,8},{8,0},{1,9},{9,1},{2,10},{10,2},{3,11},{11,3},{4,12},{12,4},... | collective-permute-start | bytes 884744 | tf_op jit(solution)/shard_map/ppermute | solution.py:597
  50.5 6.9 %gram.2 = (f32[3072,3072]{1,0:T(8,128)}, f32[8,128]{1,0:T(8,128)S(1)}) custom-call(f32[8,128]{1,0:T(8,128)S(1)} %get-tuple-element.116.refs_0_, bf16[128,768]{1,0:T(8,128)(2,1)S(1)} %get-tuple-element.117.refs_1_, bf16[128,768]{1,0:T(8,128)(2,1)S(1)} %collective-permute-done.16.refs_2_, bf16[128,3072]{1,0:T(8,128)(2,1)S(1)} %get-tuple-element.119.refs_3_), custom_call_target="tpu_custom_call" | custom-call | flops 1207959552 | bytes 18874368 | tf_op jit(solution)/shard_map/gram/pallas_call | solution.py:577
  58.2 2.6 %collective-permute-start.20 = (bf16[32,1536]{1,0:T(8,128)(2,1)S(1)}, bf16[32,1536]{1,0:T(8,128)(2,1)S(1)}, u32[]{:S(2)}, u32[]{:S(2)}) collective-permute-start(bf16[32,1536]{1,0:T(8,128)(2,1)S(1)} %get-tuple-element.138), channel_id=1, source_target_pairs={{0,4},{2,6},{4,0},{6,2},{1,5},{3,7},{5,1},{7,3},{8,12},{10,14},{12... | collective-permute-start | bytes 294920 | tf_op jit(solution)/shard_map/ppermute | solution.py:601
  60.8 6.9 %gram.3 = (f32[3072,3072]{1,0:T(8,128)}, f32[8,128]{1,0:T(8,128)S(1)}) custom-call(f32[8,128]{1,0:T(8,128)S(1)} %get-tuple-element.128.refs_0_, bf16[128,768]{1,0:T(8,128)(2,1)S(1)} %get-tuple-element.129.refs_1_, bf16[128,768]{1,0:T(8,128)(2,1)S(1)} %collective-permute-done.19.refs_2_, ...), custom_call_target="tpu_custom_call", output_to_operand_aliasing={{0}: (4, {})} | custom-call | flops 1207959552 | bytes 18874368 | tf_op jit(solution)/shard_map/gram/pallas_call | solution.py:577
  67.7 1.1 %unpack.1 = bf16[128,1536]{1,0:T(8,128)(2,1)} custom-call(f32[8,128]{1,0:T(8,128)S(1)} %get-tuple-element.132.after_ref, bf16[32,128]{1,0:T(8,128)(2,1)S(1)} %get-tuple-element.133.placing_ref, f32[32,128]{1,0:T(8,128)S(1)} %get-tuple-element.134.factor_ref, f32[32,1536]{1,0:T(8,128)S(1)} %get-tuple-element.137.own_ref, ...), custom_call_target="tpu_custom_call" | custom-call | tf_op jit(solution)/shard_map/unpack/pallas_call | solution.py:529
  (38 shorter events, 7.2 us)
Async XLA Ops:
  1.9 12.7 %collective-permute-start.2 = (bf16[32,1536]{1,0:T(8,128)(2,1)S(1)}, bf16[32,1536]{1,0:T(8,128)(2,1)S(1)}, u32[]{:S(2)}, u32[]{:S(2)}) collective-permute-start(bf16[32,1536]{1,0:T(8,128)(2,1)S(1)} %get-tuple-element.71.after_ref.refs_0_), channel_id=1, source_target_pairs={{0,6},{2,4},{4,2},{6,0},{1,7},{3,5},{5,3},{7,1},{8,14},{10,12},{12... | collective-permute-start | bytes 294920 | tf_op jit(solution)/shard_map/ppermute | solution.py:601
  7.0 8.3 %collective-permute-start.1 = (bf16[32,1536]{1,0:T(8,128)(2,1)S(1)}, bf16[32,1536]{1,0:T(8,128)(2,1)S(1)}, u32[]{:S(2)}, u32[]{:S(2)}) collective-permute-start(bf16[32,1536]{1,0:T(8,128)(2,1)S(1)} %get-tuple-element.71.after_ref.refs_0_), channel_id=1, source_target_pairs={{0,4},{2,6},{4,0},{6,2},{1,5},{3,7},{5,1},{7,3},{8,12},{10,14},{12... | collective-permute-start | bytes 294920 | tf_op jit(solution)/shard_map/ppermute | solution.py:601
  7.0 8.3 %collective-permute-start = (bf16[32,1536]{1,0:T(8,128)(2,1)S(1)}, bf16[32,1536]{1,0:T(8,128)(2,1)S(1)}, u32[]{:S(2)}, u32[]{:S(2)}) collective-permute-start(bf16[32,1536]{1,0:T(8,128)(2,1)S(1)} %get-tuple-element.71.after_ref.refs_0_), channel_id=1, source_target_pairs={{0,2},{2,0},{4,6},{6,4},{1,3},{3,1},{5,7},{7,5},{8,10},{10,8},{12,... | collective-permute-start | bytes 294920 | tf_op jit(solution)/shard_map/ppermute | solution.py:601
  17.3 3.5 %collective-permute-start.3 = (f32[256,768]{1,0:T(8,128)S(1)}, f32[256,768]{1,0:T(8,128)S(1)}, u32[]{:S(2)}, u32[]{:S(2)}) collective-permute-start(f32[256,768]{1,0:T(8,128)S(1)} %get-tuple-element.73), channel_id=1, source_target_pairs={{0,1},{1,0},{2,3},{3,2},{4,5},{5,4},{6,7},{7,6},{8,9},{9,8},{10,11... | collective-permute-start | bytes 2359304 | tf_op jit(solution)/shard_map/ppermute | solution.py:597
  18.8 5.1 %collective-permute-start.4 = (f32[256,768]{1,0:T(8,128)S(1)}, f32[256,768]{1,0:T(8,128)S(1)}, u32[]{:S(2)}, u32[]{:S(2)}) collective-permute-start(f32[256,768]{1,0:T(8,128)S(1)} %preacts_sent.3), channel_id=1, source_target_pairs={{0,1},{1,0},{2,3},{3,2},{4,5},{5,4},{6,7},{7,6},{8,9},{9,8},{10,11... | collective-permute-start | bytes 2359304 | tf_op jit(solution)/shard_map/ppermute | solution.py:597
  20.9 7.8 %collective-permute-start.5 = (bf16[256,384]{1,0:T(8,128)(2,1)S(1)}, bf16[256,384]{1,0:T(8,128)(2,1)S(1)}, u32[]{:S(2)}, u32[]{:S(2)}) collective-permute-start(bf16[256,384]{1,0:T(8,128)(2,1)S(1)} %get-tuple-element.79), channel_id=1, source_target_pairs={{0,8},{8,0},{1,9},{9,1},{2,10},{10,2},{3,11},{11,3},{4,12},{12,4},... | collective-permute-start | bytes 589832 | tf_op jit(solution)/shard_map/ppermute | solution.py:597
  24.0 8.6 %collective-permute-start.6 = (bf16[256,384]{1,0:T(8,128)(2,1)S(1)}, bf16[256,384]{1,0:T(8,128)(2,1)S(1)}, u32[]{:S(2)}, u32[]{:S(2)}) collective-permute-start(bf16[256,384]{1,0:T(8,128)(2,1)S(1)} %get-tuple-element.81), channel_id=1, source_target_pairs={{0,8},{8,0},{1,9},{9,1},{2,10},{10,2},{3,11},{11,3},{4,12},{12,4},... | collective-permute-start | bytes 589832 | tf_op jit(solution)/shard_map/ppermute | solution.py:597
  28.8 7.0 %collective-permute-start.7 = (bf16[128,384]{1,0:T(8,128)(2,1)S(1)}, bf16[128,384]{1,0:T(8,128)(2,1)S(1)}, u32[]{:S(2)}, u32[]{:S(2)}) collective-permute-start(bf16[128,384]{1,0:T(8,128)(2,1)S(1)} %act.2.refs_0_), channel_id=1, source_target_pairs={{0,4},{2,6},{4,0},{6,2},{1,5},{3,7},{5,1},{7,3},{8,12},{10,14},{12... | collective-permute-start | bytes 294920 | tf_op jit(solution)/shard_map/ppermute | solution.py:601
  30.5 6.8 %collective-permute-start.8 = (bf16[128,384]{1,0:T(8,128)(2,1)S(1)}, bf16[128,384]{1,0:T(8,128)(2,1)S(1)}, u32[]{:S(2)}, u32[]{:S(2)}) collective-permute-start(bf16[128,384]{1,0:T(8,128)(2,1)S(1)} %act.2.refs_0_), channel_id=1, source_target_pairs={{0,2},{2,0},{4,6},{6,4},{1,3},{3,1},{5,7},{7,5},{8,10},{10,8},{12,... | collective-permute-start | bytes 294920 | tf_op jit(solution)/shard_map/ppermute | solution.py:601
  32.6 9.9 %collective-permute-start.12 = (bf16[128,768]{1,0:T(8,128)(2,1)S(1)}, bf16[128,768]{1,0:T(8,128)(2,1)S(1)}, u32[]{:S(2)}, u32[]{:S(2)}) collective-permute-start(bf16[128,768]{1,0:T(8,128)(2,1)S(1)} %get-tuple-element.96.left_ref.refs_0_), channel_id=1, source_target_pairs={{0,8},{8,0},{1,9},{9,1},{2,10},{10,2},{3,11},{11,3},{4,12},{12,4},... | collective-permute-start | bytes 589832 | tf_op jit(solution)/shard_map/ppermute | solution.py:597
  34.2 6.4 %collective-permute-start.9 = (bf16[128,384]{1,0:T(8,128)(2,1)S(1)}, bf16[128,384]{1,0:T(8,128)(2,1)S(1)}, u32[]{:S(2)}, u32[]{:S(2)}) collective-permute-start(bf16[128,384]{1,0:T(8,128)(2,1)S(1)} %get-tuple-element.94), channel_id=1, source_target_pairs={{0,4},{2,6},{4,0},{6,2},{1,5},{3,7},{5,1},{7,3},{8,12},{10,14},{12... | collective-permute-start | bytes 294920 | tf_op jit(solution)/shard_map/ppermute | solution.py:601
  35.8 5.7 %collective-permute-start.10 = (bf16[128,384]{1,0:T(8,128)(2,1)S(1)}, bf16[128,384]{1,0:T(8,128)(2,1)S(1)}, u32[]{:S(2)}, u32[]{:S(2)}) collective-permute-start(bf16[128,384]{1,0:T(8,128)(2,1)S(1)} %collective-permute-done.7.near_ref.refs_3_), channel_id=1, source_target_pairs={{0,2},{2,0},{4,6},{6,4},{1,3},{3,1},{5,7},{7,5},{8,10},{10,8},{12,... | collective-permute-start | bytes 294920 | tf_op jit(solution)/shard_map/ppermute | solution.py:601
  37.3 5.2 %collective-permute-start.11 = (bf16[128,384]{1,0:T(8,128)(2,1)S(1)}, bf16[128,384]{1,0:T(8,128)(2,1)S(1)}, u32[]{:S(2)}, u32[]{:S(2)}) collective-permute-start(bf16[128,384]{1,0:T(8,128)(2,1)S(1)} %get-tuple-element.94), channel_id=1, source_target_pairs={{0,2},{2,0},{4,6},{6,4},{1,3},{3,1},{5,7},{7,5},{8,10},{10,8},{12,... | collective-permute-start | bytes 294920 | tf_op jit(solution)/shard_map/ppermute | solution.py:601
  37.9 4.8 %collective-permute-start.13 = (bf16[128,384]{1,0:T(8,128)(2,1)S(1)}, bf16[128,384]{1,0:T(8,128)(2,1)S(1)}, u32[]{:S(2)}, u32[]{:S(2)}) collective-permute-start(bf16[128,384]{1,0:T(8,128)(2,1)S(1)} %choose.1), channel_id=1, source_target_pairs={{0,8},{8,0},{1,9},{9,1},{2,10},{10,2},{3,11},{11,3},{4,12},{12,4},... | collective-permute-start | bytes 294920 | tf_op jit(solution)/shard_map/ppermute | solution.py:597
  42.7 1.8 %collective-permute-start.14 = (bf16[128,1536]{1,0:T(8,128)(2,1)S(1)}, bf16[128,1536]{1,0:T(8,128)(2,1)S(1)}, u32[]{:S(2)}, u32[]{:S(2)}) collective-permute-start(bf16[128,1536]{1,0:T(8,128)(2,1)S(1)} %join.1.here_ref), channel_id=1, source_target_pairs={{0,1},{1,0},{2,3},{3,2},{4,5},{5,4},{6,7},{7,6},{8,9},{9,8},{10,11... | collective-permute-start | bytes 1179656 | tf_op jit(solution)/shard_map/ppermute | solution.py:597
  42.8 5.2 %collective-permute-start.15 = (bf16[128,384]{1,0:T(8,128)(2,1)S(1)}, bf16[128,384]{1,0:T(8,128)(2,1)S(1)}, u32[]{:S(2)}, u32[]{:S(2)}) collective-permute-start(bf16[128,384]{1,0:T(8,128)(2,1)S(1)} %collective-permute-done.9.refs_4_), channel_id=1, source_target_pairs={{0,2},{2,0},{4,6},{6,4},{1,3},{3,1},{5,7},{7,5},{8,10},{10,8},{12,... | collective-permute-start | bytes 294920 | tf_op jit(solution)/shard_map/ppermute | solution.py:601
  48.1 2.5 %collective-permute-start.16 = (bf16[128,768]{1,0:T(8,128)(2,1)S(1)}, bf16[128,768]{1,0:T(8,128)(2,1)S(1)}, u32[]{:S(2)}, u32[]{:S(2)}) collective-permute-start(bf16[128,768]{1,0:T(8,128)(2,1)S(1)} %get-tuple-element.115), channel_id=1, source_target_pairs={{0,1},{1,0},{2,3},{3,2},{4,5},{5,4},{6,7},{7,6},{8,9},{9,8},{10,11... | collective-permute-start | bytes 589832 | tf_op jit(solution)/shard_map/ppermute | solution.py:597
  48.1 9.7 %collective-permute-start.17 = (bf16[128,1152]{1,0:T(8,128)(2,1)S(1)}, bf16[128,1152]{1,0:T(8,128)(2,1)S(1)}, u32[]{:S(2)}, u32[]{:S(2)}) collective-permute-start(bf16[128,1152]{1,0:T(8,128)(2,1)S(1)} %get-tuple-element.121), channel_id=1, source_target_pairs={{0,8},{8,0},{1,9},{9,1},{2,10},{10,2},{3,11},{11,3},{4,12},{12,4},... | collective-permute-start | bytes 884744 | tf_op jit(solution)/shard_map/ppermute | solution.py:597
  50.2 7.9 %collective-permute-start.18 = (bf16[64,1536]{1,0:T(8,128)(2,1)S(1)}, bf16[64,1536]{1,0:T(8,128)(2,1)S(1)}, u32[]{:S(2)}, u32[]{:S(2)}) collective-permute-start(bf16[64,1536]{1,0:T(8,128)(2,1)S(1)} %get-tuple-element.123), channel_id=1, source_target_pairs={{0,2},{2,0},{4,6},{6,4},{1,3},{3,1},{5,7},{7,5},{8,10},{10,8},{12,... | collective-permute-start | bytes 589832 | tf_op jit(solution)/shard_map/ppermute | solution.py:601
  58.0 2.7 %collective-permute-start.19 = (bf16[128,768]{1,0:T(8,128)(2,1)S(1)}, bf16[128,768]{1,0:T(8,128)(2,1)S(1)}, u32[]{:S(2)}, u32[]{:S(2)}) collective-permute-start(bf16[128,768]{1,0:T(8,128)(2,1)S(1)} %get-tuple-element.127), channel_id=1, source_target_pairs={{0,1},{1,0},{2,3},{3,2},{4,5},{5,4},{6,7},{7,6},{8,9},{9,8},{10,11... | collective-permute-start | bytes 589832 | tf_op jit(solution)/shard_map/ppermute | solution.py:597
  58.2 9.5 %collective-permute-start.20 = (bf16[32,1536]{1,0:T(8,128)(2,1)S(1)}, bf16[32,1536]{1,0:T(8,128)(2,1)S(1)}, u32[]{:S(2)}, u32[]{:S(2)}) collective-permute-start(bf16[32,1536]{1,0:T(8,128)(2,1)S(1)} %get-tuple-element.138), channel_id=1, source_target_pairs={{0,4},{2,6},{4,0},{6,2},{1,5},{3,7},{5,1},{7,3},{8,12},{10,14},{12... | collective-permute-start | bytes 294920 | tf_op jit(solution)/shard_map/ppermute | solution.py:601

commit v13 on v12

--- a/solution.py
+++ b/solution.py
@@ -323,6 +323,22 @@
     )(tick, stays, got, *before)
 
 
+def relay_kernel(in_ref, out_ref):
+    out_ref[...] = in_ref[...]
+
+
+def relay(value):
+    return pl.pallas_call(
+        relay_kernel,
+        in_specs=[VMEM],
+        out_specs=VMEM,
+        out_shape=jax.ShapeDtypeStruct(value.shape, value.dtype),
+        compiler_params=params(2),
+        cost_estimate=cost(1e10, 1),
+        name="relay",
+    )(value)
+
+
 def is_near():
     return (lax.axis_index("col") // 2) == lax.axis_index("expert")
 
@@ -348,7 +364,7 @@
         out_specs=VMEM,
         out_shape=jax.ShapeDtypeStruct(if_near.shape, if_near.dtype),
         compiler_params=params(2),
-        cost_estimate=cost(0, 1),
+        cost_estimate=cost(1e10, 1),
         name="choose",
     )(if_near, if_far)
 
@@ -633,22 +649,20 @@
     hidden_x = swap(hidden, "expert")
     z2b = across(hidden_b, 2)
     tick, z2a = tie(tick, z2a)
-    z3a = across(z2a, 1)
+    z3a = across(relay(z2a), 1)
     tick, z1a, hidden_b = tie(tick, z1a, hidden_b)
     z1b = across(hidden_b, 1)
     x2a = swap(choose(z2a, z1a), "expert")
     tick, z2b = tie(tick, z2b)
+    z3b = across(z2b, 1)
     tick, z3a = tie(tick, z3a)
     tick, z1b = tie(tick, z1b)
-    tick, hidden_x = tie(tick, hidden_x)
-    tick, x2a = tie(tick, x2a)
     here = join(hidden, hidden_x)
-    tick, z2b, here = tie(tick, z2b, here)
-    z3b = across(z2b, 1)
     there = swap(here, "row")
     tick, there, here = tie(tick, there, here)
     near, away, hidden_c, tick = project(tick, here, there, down_held)
-    tick, z3b, away = tie(tick, z3b, away)
+    tick, x2a = tie(tick, x2a)
+    tick, z3b = tie(tick, z3b)
     mine, passed, leaves = pick([hidden], [z1a, z1b], [z2a, z2b], [z3a, z3b], leaves=True)
     rest = swap(leaves, "expert")
     mine_near = swap(passed, "row")

time: 68.9 us -> 66 us (0.958)
  waiting for transfers between devices: 6.62 us -> 4.79 us
  starting transfers between devices: 25.8 us -> 24.7 us
    ppermute x10, starting transfers between devices: 8.81 us -> 6.66 us  [swap(): return lax.ppermute(value, axis, [(0, 1), (1, 0)])]
    ppermute x11, waiting for transfers between devices: 5.51 us -> 3.6 us  [across(): return lax.ppermute(value, 'col', [(i, i ^ slot) for i in range(4)])]
    ppermute x11, starting transfers between devices: 17 us -> 18.1 us  [across(): return lax.ppermute(value, 'col', [(i, i ^ slot) for i in range(4)])]
  transfers between devices with their start and end apart: 21 -> 21, of which waited for: 10 -> 6; matrix products, arithmetic and copies ran while one was open for 0% -> 0% of each run, Pallas kernels for 45% -> 47%
where the time goes in v13:
time: 66 us; the launch traced here: 65.9 us
  Pallas kernels  35.5 us (54%)
  starting transfers between devices  24.7 us (37%)
  waiting for transfers between devices  4.79 us (7%)
  between operations  0.87 us (1%)
    ppermute x11, starting transfers between devices, across(): return lax.ppermute(value, 'col', [(i, i ^ slot) for i in range(4)])  18.1 us
    pallas_call x2, Pallas kernels, gram_piece(): pl.pallas_call(functools.partial(gram_kernel, 2.0 / rows, flips), in_spec...  13.8 us
    pallas_call x1, Pallas kernels, regroup(): pl.pallas_call(regroup_kernel, in_specs=[ANY, HBM], out_specs=VMEM, out_s...  6.97 us
    ppermute x10, starting transfers between devices, swap(): return lax.ppermute(value, axis, [(0, 1), (1, 0)])  6.66 us
    pallas_call x4, Pallas kernels, preacts_of(): pl.pallas_call(functools.partial(preact_kernel, first, row_flip, chunk, c...  6.27 us
    pallas_call x1, Pallas kernels, fetch(): pl.pallas_call(fetch_kernel, in_specs=[ANY, HBM], out_specs=[VMEM, VMEM],...  3.8 us
    ppermute x11, waiting for transfers between devices, across(): return lax.ppermute(value, 'col', [(i, i ^ slot) for i in range(4)])  3.6 us
    pallas_call x1, Pallas kernels, project(): pl.pallas_call(project_kernel, in_specs=[ANY] + [VMEM] * 3, out_specs=[VM...  1.61 us
  transfers between devices with their start and end apart: 21, of which 6 were waited for; matrix products, arithmetic and copies ran while one was open for 0% of the time, Pallas kernels for 47%

profile of v13, /device:TPU:0, one launch (start us, length us, event | category | flops | bytes accessed | tf_op | source)
XLA Modules:
  0.0 65.9 jit_solution(8977794353369052115)
XLA Ops:
  0.6 1.3 %pack.1 = (bf16[32,1536]{1,0:T(8,128)(2,1)S(1)}, bf16[32,128]{1,0:T(8,128)(2,1)S(1)}, f32[32,128]{1,0:T(8,128)S(1)}) custom-call(bf16[128,1536]{1,0:T(8,128)(2,1)} %tokens_ref.1, s32[2,128]{1,0:T(2,128)} %bitcast.12, s32[1,128]{1,0:T(1,128)} %bitcast.14, f32[2,128]{1,0:T(2,128)} %bitcast.13), custom_call_target="tpu_custom_call" | custom-call | tf_op jit(solution)/shard_map/pack/pallas_call | solution.py:137
  1.9 5.1 %collective-permute-start.2 = (bf16[32,1536]{1,0:T(8,128)(2,1)S(1)}, bf16[32,1536]{1,0:T(8,128)(2,1)S(1)}, u32[]{:S(2)}, u32[]{:S(2)}) collective-permute-start(bf16[32,1536]{1,0:T(8,128)(2,1)S(1)} %get-tuple-element.65.after_ref.refs_0_), channel_id=1, source_target_pairs={{0,6},{2,4},{4,2},{6,0},{1,7},{3,5},{5,3},{7,1},{8,14},{10,12},{12... | collective-permute-start | bytes 294920 | tf_op jit(solution)/shard_map/ppermute | solution.py:617
  7.7 7.0 %regroup.1 = bf16[24,1536,2,128]{3,2,1,0:T(2,128)(2,1)S(1)} custom-call(bf16[32,1536]{1,0:T(8,128)(2,1)S(1)} %get-tuple-element.65.after_ref.refs_0_, bf16[1536,24,2,128]{3,2,1,0:T(2,128)(2,1)} %bitcast.11), custom_call_target="tpu_custom_call" | custom-call | bytes 37748736 | tf_op jit(solution)/shard_map/regroup/pallas_call | solution.py:167
  15.3 2.0 %preacts_sent.2 = (f32[256,768]{1,0:T(8,128)S(1)}, bf16[256,3072]{1,0:T(8,128)(2,1)S(1)}) custom-call(bf16[32,1536]{1,0:T(8,128)(2,1)S(1)} %get-tuple-element.65.after_ref.refs_0_, bf16[32,1536]{1,0:T(8,128)(2,1)S(1)} %collective-permute-done.refs_1_, bf16[32,1536]{1,0:T(8,128)(2,1)S(1)} %collective-permute-done.1.refs_2_, ...), custom_call_target="tpu_custom_call" | custom-call | flops 1207959552 | tf_op jit(solution)/shard_map/preacts_sent/pallas_call | solution.py:260
  17.4 1.4 %preacts_sent.3 = f32[256,768]{1,0:T(8,128)S(1)} custom-call(bf16[256,3072]{1,0:T(8,128)(2,1)S(1)} %get-tuple-element.71.refs_0_.after_ref, bf16[24,3072,128]{2,1,0:T(8,128)(2,1)S(1)} %bitcast.8), custom_call_target="tpu_custom_call" | custom-call | flops 1207959552 | tf_op jit(solution)/shard_map/preacts_sent/pallas_call | solution.py:260
  19.4 1.4 %preacts_kept.2.kept_ref = f32[256,768]{1,0:T(8,128)S(1)} custom-call(bf16[256,3072]{1,0:T(8,128)(2,1)S(1)} %get-tuple-element.71.refs_0_.after_ref, bf16[24,3072,128]{2,1,0:T(8,128)(2,1)S(1)} %bitcast.9), custom_call_target="tpu_custom_call" | custom-call | flops 1207959552 | tf_op jit(solution)/shard_map/preacts_kept/pallas_call | solution.py:260
  20.9 1.6 %collective-permute-start.5 = (bf16[256,384]{1,0:T(8,128)(2,1)S(1)}, bf16[256,384]{1,0:T(8,128)(2,1)S(1)}, u32[]{:S(2)}, u32[]{:S(2)}) collective-permute-start(bf16[256,384]{1,0:T(8,128)(2,1)S(1)} %get-tuple-element.73), channel_id=1, source_target_pairs={{0,8},{8,0},{1,9},{9,1},{2,10},{10,2},{3,11},{11,3},{4,12},{12,4},... | collective-permute-start | bytes 589832 | tf_op jit(solution)/shard_map/ppermute | solution.py:613
  22.4 1.4 %preacts_kept.3.kept_ref = f32[256,768]{1,0:T(8,128)S(1)} custom-call(bf16[256,3072]{1,0:T(8,128)(2,1)S(1)} %get-tuple-element.71.refs_0_.after_ref, bf16[24,3072,128]{2,1,0:T(8,128)(2,1)S(1)} %bitcast.10), custom_call_target="tpu_custom_call" | custom-call | flops 1207959552 | tf_op jit(solution)/shard_map/preacts_kept/pallas_call | solution.py:260
  24.6 3.8 %fetch_down.1 = (bf16[3072,1536]{1,0:T(8,128)(2,1)S(1)}, f32[8,128]{1,0:T(8,128)S(1)}) custom-call(bf16[256,3072]{1,0:T(8,128)(2,1)S(1)} %get-tuple-element.71.refs_0_.after_ref, bf16[3072,1536]{1,0:T(8,128)(2,1)} %down_ref.1), custom_call_target="tpu_custom_call" | custom-call | bytes 18874368 | tf_op jit(solution)/shard_map/fetch_down/pallas_call | solution.py:198
  28.8 1.7 %collective-permute-start.7 = (bf16[128,384]{1,0:T(8,128)(2,1)S(1)}, bf16[128,384]{1,0:T(8,128)(2,1)S(1)}, u32[]{:S(2)}, u32[]{:S(2)}) collective-permute-start(bf16[128,384]{1,0:T(8,128)(2,1)S(1)} %act.2.refs_0_), channel_id=1, source_target_pairs={{0,4},{2,6},{4,0},{6,2},{1,5},{3,7},{5,1},{7,3},{8,12},{10,14},{12... | collective-permute-start | bytes 294920 | tf_op jit(solution)/shard_map/ppermute | solution.py:617
  30.5 2.0 %collective-permute-start.8 = (bf16[128,384]{1,0:T(8,128)(2,1)S(1)}, bf16[128,384]{1,0:T(8,128)(2,1)S(1)}, u32[]{:S(2)}, u32[]{:S(2)}) collective-permute-start(bf16[128,384]{1,0:T(8,128)(2,1)S(1)} %act.2.refs_0_), channel_id=1, source_target_pairs={{0,2},{2,0},{4,6},{6,4},{1,3},{3,1},{5,7},{7,5},{8,10},{10,8},{12,... | collective-permute-start | bytes 294920 | tf_op jit(solution)/shard_map/ppermute | solution.py:617
  32.6 1.2 %collective-permute-start.9 = (bf16[128,384]{1,0:T(8,128)(2,1)S(1)}, bf16[128,384]{1,0:T(8,128)(2,1)S(1)}, u32[]{:S(2)}, u32[]{:S(2)}) collective-permute-start(bf16[128,384]{1,0:T(8,128)(2,1)S(1)} %get-tuple-element.88), channel_id=1, source_target_pairs={{0,4},{2,6},{4,0},{6,2},{1,5},{3,7},{5,1},{7,3},{8,12},{10,14},{12... | collective-permute-start | bytes 294920 | tf_op jit(solution)/shard_map/ppermute | solution.py:617
  33.8 1.5 %collective-permute-start.12 = (bf16[128,768]{1,0:T(8,128)(2,1)S(1)}, bf16[128,768]{1,0:T(8,128)(2,1)S(1)}, u32[]{:S(2)}, u32[]{:S(2)}) collective-permute-start(bf16[128,768]{1,0:T(8,128)(2,1)S(1)} %get-tuple-element.90.left_ref.refs_0_), channel_id=1, source_target_pairs={{0,8},{8,0},{1,9},{9,1},{2,10},{10,2},{3,11},{11,3},{4,12},{12,4},... | collective-permute-start | bytes 589832 | tf_op jit(solution)/shard_map/ppermute | solution.py:613
  35.3 1.4 %collective-permute-done.7.in_ref.near_ref.refs_3_ = bf16[128,384]{1,0:T(8,128)(2,1)S(1)} collective-permute-done((bf16[128,384]{1,0:T(8,128)(2,1)S(1)}, bf16[128,384]{1,0:T(8,128)(2,1)S(1)}, u32[]{:S(2)}, u32[]{:S(2)}) %collective-permute-start.7) | collective-permute-done | bytes 98336 | tf_op jit(solution)/shard_map/ppermute | solution.py:617
  36.8 1.5 %collective-permute-start.10 = (bf16[128,384]{1,0:T(8,128)(2,1)S(1)}, bf16[128,384]{1,0:T(8,128)(2,1)S(1)}, u32[]{:S(2)}, u32[]{:S(2)}) collective-permute-start(bf16[128,384]{1,0:T(8,128)(2,1)S(1)} %relay.1), channel_id=1, source_target_pairs={{0,2},{2,0},{4,6},{6,4},{1,3},{3,1},{5,7},{7,5},{8,10},{10,8},{12,... | collective-permute-start | bytes 294920 | tf_op jit(solution)/shard_map/ppermute | solution.py:617
  39.7 1.6 %collective-permute-start.14 = (bf16[128,384]{1,0:T(8,128)(2,1)S(1)}, bf16[128,384]{1,0:T(8,128)(2,1)S(1)}, u32[]{:S(2)}, u32[]{:S(2)}) collective-permute-start(bf16[128,384]{1,0:T(8,128)(2,1)S(1)} %choose.1), channel_id=1, source_target_pairs={{0,8},{8,0},{1,9},{9,1},{2,10},{10,2},{3,11},{11,3},{4,12},{12,4},... | collective-permute-start | bytes 294920 | tf_op jit(solution)/shard_map/ppermute | solution.py:613
  41.2 2.0 %collective-permute-start.15 = (bf16[128,384]{1,0:T(8,128)(2,1)S(1)}, bf16[128,384]{1,0:T(8,128)(2,1)S(1)}, u32[]{:S(2)}, u32[]{:S(2)}) collective-permute-start(bf16[128,384]{1,0:T(8,128)(2,1)S(1)} %collective-permute-done.9.refs_4_), channel_id=1, source_target_pairs={{0,2},{2,0},{4,6},{6,4},{1,3},{3,1},{5,7},{7,5},{8,10},{10,8},{12,... | collective-permute-start | bytes 294920 | tf_op jit(solution)/shard_map/ppermute | solution.py:617
  43.3 1.6 %project.1 = (f32[64,1536]{1,0:T(8,128)S(1)}, bf16[64,1536]{1,0:T(8,128)(2,1)S(1)}, bf16[128,3072]{1,0:T(8,128)(2,1)S(1)}, f32[8,128]{1,0:T(8,128)S(1)}) custom-call(f32[8,128]{1,0:T(8,128)S(1)} %get-tuple-element.91.tick_ref, bf16[128,1536]{1,0:T(8,128)(2,1)S(1)} %join.1.here_ref, bf16[128,1536]{1,0:T(8,128)(2,1)S(1)} %collective-permute-done.13.there_ref, ...), custom_call_target="tpu_custom_call" | custom-call | bytes 1 | tf_op jit(solution)/shard_map/project/pallas_call | solution.py:495
  44.9 1.5 %collective-permute-done.15.refs_6_ = bf16[128,384]{1,0:T(8,128)(2,1)S(1)} collective-permute-done((bf16[128,384]{1,0:T(8,128)(2,1)S(1)}, bf16[128,384]{1,0:T(8,128)(2,1)S(1)}, u32[]{:S(2)}, u32[]{:S(2)}) %collective-permute-start.15) | collective-permute-done | bytes 98336 | tf_op jit(solution)/shard_map/ppermute | solution.py:617
  47.2 1.7 %collective-permute-start.18 = (bf16[64,1536]{1,0:T(8,128)(2,1)S(1)}, bf16[64,1536]{1,0:T(8,128)(2,1)S(1)}, u32[]{:S(2)}, u32[]{:S(2)}) collective-permute-start(bf16[64,1536]{1,0:T(8,128)(2,1)S(1)} %get-tuple-element.111), channel_id=1, source_target_pairs={{0,2},{2,0},{4,6},{6,4},{1,3},{3,1},{5,7},{7,5},{8,10},{10,8},{12,... | collective-permute-start | bytes 589832 | tf_op jit(solution)/shard_map/ppermute | solution.py:617
  48.9 6.9 %gram.2 = (f32[3072,3072]{1,0:T(8,128)}, f32[8,128]{1,0:T(8,128)S(1)}) custom-call(f32[8,128]{1,0:T(8,128)S(1)} %get-tuple-element.104.refs_0_, bf16[128,768]{1,0:T(8,128)(2,1)S(1)} %get-tuple-element.105.refs_1_, bf16[128,768]{1,0:T(8,128)(2,1)S(1)} %collective-permute-done.16.refs_2_, bf16[128,3072]{1,0:T(8,128)(2,1)S(1)} %get-tuple-element.107.refs_3_), custom_call_target="tpu_custom_call" | custom-call | flops 1207959552 | bytes 18874368 | tf_op jit(solution)/shard_map/gram/pallas_call | solution.py:593
  56.3 1.5 %collective-permute-start.20 = (bf16[32,1536]{1,0:T(8,128)(2,1)S(1)}, bf16[32,1536]{1,0:T(8,128)(2,1)S(1)}, u32[]{:S(2)}, u32[]{:S(2)}) collective-permute-start(bf16[32,1536]{1,0:T(8,128)(2,1)S(1)} %get-tuple-element.126), channel_id=1, source_target_pairs={{0,4},{2,6},{4,0},{6,2},{1,5},{3,7},{5,1},{7,3},{8,12},{10,14},{12... | collective-permute-start | bytes 294920 | tf_op jit(solution)/shard_map/ppermute | solution.py:617
  57.9 6.9 %gram.3 = (f32[3072,3072]{1,0:T(8,128)}, f32[8,128]{1,0:T(8,128)S(1)}) custom-call(f32[8,128]{1,0:T(8,128)S(1)} %get-tuple-element.116.refs_0_, bf16[128,768]{1,0:T(8,128)(2,1)S(1)} %get-tuple-element.117.refs_1_, bf16[128,768]{1,0:T(8,128)(2,1)S(1)} %collective-permute-done.19.refs_2_, ...), custom_call_target="tpu_custom_call", output_to_operand_aliasing={{0}: (4, {})} | custom-call | flops 1207959552 | bytes 18874368 | tf_op jit(solution)/shard_map/gram/pallas_call | solution.py:593
  64.8 1.1 %unpack.1 = bf16[128,1536]{1,0:T(8,128)(2,1)} custom-call(f32[8,128]{1,0:T(8,128)S(1)} %get-tuple-element.120.after_ref, bf16[32,128]{1,0:T(8,128)(2,1)S(1)} %get-tuple-element.121.placing_ref, f32[32,128]{1,0:T(8,128)S(1)} %get-tuple-element.122.factor_ref, f32[32,1536]{1,0:T(8,128)S(1)} %get-tuple-element.125.own_ref, ...), custom_call_target="tpu_custom_call" | custom-call | tf_op jit(solution)/shard_map/unpack/pallas_call | solution.py:545
  (39 shorter events, 5.8 us)
Async XLA Ops:
  1.9 12.7 %collective-permute-start.2 = (bf16[32,1536]{1,0:T(8,128)(2,1)S(1)}, bf16[32,1536]{1,0:T(8,128)(2,1)S(1)}, u32[]{:S(2)}, u32[]{:S(2)}) collective-permute-start(bf16[32,1536]{1,0:T(8,128)(2,1)S(1)} %get-tuple-element.65.after_ref.refs_0_), channel_id=1, source_target_pairs={{0,6},{2,4},{4,2},{6,0},{1,7},{3,5},{5,3},{7,1},{8,14},{10,12},{12... | collective-permute-start | bytes 294920 | tf_op jit(solution)/shard_map/ppermute | solution.py:617
  7.0 8.3 %collective-permute-start.1 = (bf16[32,1536]{1,0:T(8,128)(2,1)S(1)}, bf16[32,1536]{1,0:T(8,128)(2,1)S(1)}, u32[]{:S(2)}, u32[]{:S(2)}) collective-permute-start(bf16[32,1536]{1,0:T(8,128)(2,1)S(1)} %get-tuple-element.65.after_ref.refs_0_), channel_id=1, source_target_pairs={{0,4},{2,6},{4,0},{6,2},{1,5},{3,7},{5,1},{7,3},{8,12},{10,14},{12... | collective-permute-start | bytes 294920 | tf_op jit(solution)/shard_map/ppermute | solution.py:617
  7.0 8.3 %collective-permute-start = (bf16[32,1536]{1,0:T(8,128)(2,1)S(1)}, bf16[32,1536]{1,0:T(8,128)(2,1)S(1)}, u32[]{:S(2)}, u32[]{:S(2)}) collective-permute-start(bf16[32,1536]{1,0:T(8,128)(2,1)S(1)} %get-tuple-element.65.after_ref.refs_0_), channel_id=1, source_target_pairs={{0,2},{2,0},{4,6},{6,4},{1,3},{3,1},{5,7},{7,5},{8,10},{10,8},{12,... | collective-permute-start | bytes 294920 | tf_op jit(solution)/shard_map/ppermute | solution.py:617
  17.3 3.5 %collective-permute-start.3 = (f32[256,768]{1,0:T(8,128)S(1)}, f32[256,768]{1,0:T(8,128)S(1)}, u32[]{:S(2)}, u32[]{:S(2)}) collective-permute-start(f32[256,768]{1,0:T(8,128)S(1)} %get-tuple-element.67), channel_id=1, source_target_pairs={{0,1},{1,0},{2,3},{3,2},{4,5},{5,4},{6,7},{7,6},{8,9},{9,8},{10,11... | collective-permute-start | bytes 2359304 | tf_op jit(solution)/shard_map/ppermute | solution.py:613
  18.8 5.1 %collective-permute-start.4 = (f32[256,768]{1,0:T(8,128)S(1)}, f32[256,768]{1,0:T(8,128)S(1)}, u32[]{:S(2)}, u32[]{:S(2)}) collective-permute-start(f32[256,768]{1,0:T(8,128)S(1)} %preacts_sent.3), channel_id=1, source_target_pairs={{0,1},{1,0},{2,3},{3,2},{4,5},{5,4},{6,7},{7,6},{8,9},{9,8},{10,11... | collective-permute-start | bytes 2359304 | tf_op jit(solution)/shard_map/ppermute | solution.py:613
  20.9 7.8 %collective-permute-start.5 = (bf16[256,384]{1,0:T(8,128)(2,1)S(1)}, bf16[256,384]{1,0:T(8,128)(2,1)S(1)}, u32[]{:S(2)}, u32[]{:S(2)}) collective-permute-start(bf16[256,384]{1,0:T(8,128)(2,1)S(1)} %get-tuple-element.73), channel_id=1, source_target_pairs={{0,8},{8,0},{1,9},{9,1},{2,10},{10,2},{3,11},{11,3},{4,12},{12,4},... | collective-permute-start | bytes 589832 | tf_op jit(solution)/shard_map/ppermute | solution.py:613
  24.0 8.6 %collective-permute-start.6 = (bf16[256,384]{1,0:T(8,128)(2,1)S(1)}, bf16[256,384]{1,0:T(8,128)(2,1)S(1)}, u32[]{:S(2)}, u32[]{:S(2)}) collective-permute-start(bf16[256,384]{1,0:T(8,128)(2,1)S(1)} %get-tuple-element.75), channel_id=1, source_target_pairs={{0,8},{8,0},{1,9},{9,1},{2,10},{10,2},{3,11},{11,3},{4,12},{12,4},... | collective-permute-start | bytes 589832 | tf_op jit(solution)/shard_map/ppermute | solution.py:613
  28.8 8.0 %collective-permute-start.7 = (bf16[128,384]{1,0:T(8,128)(2,1)S(1)}, bf16[128,384]{1,0:T(8,128)(2,1)S(1)}, u32[]{:S(2)}, u32[]{:S(2)}) collective-permute-start(bf16[128,384]{1,0:T(8,128)(2,1)S(1)} %act.2.refs_0_), channel_id=1, source_target_pairs={{0,4},{2,6},{4,0},{6,2},{1,5},{3,7},{5,1},{7,3},{8,12},{10,14},{12... | collective-permute-start | bytes 294920 | tf_op jit(solution)/shard_map/ppermute | solution.py:617
  30.5 6.2 %collective-permute-start.8 = (bf16[128,384]{1,0:T(8,128)(2,1)S(1)}, bf16[128,384]{1,0:T(8,128)(2,1)S(1)}, u32[]{:S(2)}, u32[]{:S(2)}) collective-permute-start(bf16[128,384]{1,0:T(8,128)(2,1)S(1)} %act.2.refs_0_), channel_id=1, source_target_pairs={{0,2},{2,0},{4,6},{6,4},{1,3},{3,1},{5,7},{7,5},{8,10},{10,8},{12,... | collective-permute-start | bytes 294920 | tf_op jit(solution)/shard_map/ppermute | solution.py:617
  32.6 8.6 %collective-permute-start.9 = (bf16[128,384]{1,0:T(8,128)(2,1)S(1)}, bf16[128,384]{1,0:T(8,128)(2,1)S(1)}, u32[]{:S(2)}, u32[]{:S(2)}) collective-permute-start(bf16[128,384]{1,0:T(8,128)(2,1)S(1)} %get-tuple-element.88), channel_id=1, source_target_pairs={{0,4},{2,6},{4,0},{6,2},{1,5},{3,7},{5,1},{7,3},{8,12},{10,14},{12... | collective-permute-start | bytes 294920 | tf_op jit(solution)/shard_map/ppermute | solution.py:617
  33.8 5.7 %collective-permute-start.12 = (bf16[128,768]{1,0:T(8,128)(2,1)S(1)}, bf16[128,768]{1,0:T(8,128)(2,1)S(1)}, u32[]{:S(2)}, u32[]{:S(2)}) collective-permute-start(bf16[128,768]{1,0:T(8,128)(2,1)S(1)} %get-tuple-element.90.left_ref.refs_0_), channel_id=1, source_target_pairs={{0,8},{8,0},{1,9},{9,1},{2,10},{10,2},{3,11},{11,3},{4,12},{12,4},... | collective-permute-start | bytes 589832 | tf_op jit(solution)/shard_map/ppermute | solution.py:613
  36.8 6.5 %collective-permute-start.10 = (bf16[128,384]{1,0:T(8,128)(2,1)S(1)}, bf16[128,384]{1,0:T(8,128)(2,1)S(1)}, u32[]{:S(2)}, u32[]{:S(2)}) collective-permute-start(bf16[128,384]{1,0:T(8,128)(2,1)S(1)} %relay.1), channel_id=1, source_target_pairs={{0,2},{2,0},{4,6},{6,4},{1,3},{3,1},{5,7},{7,5},{8,10},{10,8},{12,... | collective-permute-start | bytes 294920 | tf_op jit(solution)/shard_map/ppermute | solution.py:617
  38.2 5.0 %collective-permute-start.11 = (bf16[128,384]{1,0:T(8,128)(2,1)S(1)}, bf16[128,384]{1,0:T(8,128)(2,1)S(1)}, u32[]{:S(2)}, u32[]{:S(2)}) collective-permute-start(bf16[128,384]{1,0:T(8,128)(2,1)S(1)} %get-tuple-element.88), channel_id=1, source_target_pairs={{0,2},{2,0},{4,6},{6,4},{1,3},{3,1},{5,7},{7,5},{8,10},{10,8},{12,... | collective-permute-start | bytes 294920 | tf_op jit(solution)/shard_map/ppermute | solution.py:617
  39.5 3.7 %collective-permute-start.13 = (bf16[128,1536]{1,0:T(8,128)(2,1)S(1)}, bf16[128,1536]{1,0:T(8,128)(2,1)S(1)}, u32[]{:S(2)}, u32[]{:S(2)}) collective-permute-start(bf16[128,1536]{1,0:T(8,128)(2,1)S(1)} %join.1.here_ref), channel_id=1, source_target_pairs={{0,1},{1,0},{2,3},{3,2},{4,5},{5,4},{6,7},{7,6},{8,9},{9,8},{10,11... | collective-permute-start | bytes 1179656 | tf_op jit(solution)/shard_map/ppermute | solution.py:613
  39.7 5.2 %collective-permute-start.14 = (bf16[128,384]{1,0:T(8,128)(2,1)S(1)}, bf16[128,384]{1,0:T(8,128)(2,1)S(1)}, u32[]{:S(2)}, u32[]{:S(2)}) collective-permute-start(bf16[128,384]{1,0:T(8,128)(2,1)S(1)} %choose.1), channel_id=1, source_target_pairs={{0,8},{8,0},{1,9},{9,1},{2,10},{10,2},{3,11},{11,3},{4,12},{12,4},... | collective-permute-start | bytes 294920 | tf_op jit(solution)/shard_map/ppermute | solution.py:613
  41.2 5.2 %collective-permute-start.15 = (bf16[128,384]{1,0:T(8,128)(2,1)S(1)}, bf16[128,384]{1,0:T(8,128)(2,1)S(1)}, u32[]{:S(2)}, u32[]{:S(2)}) collective-permute-start(bf16[128,384]{1,0:T(8,128)(2,1)S(1)} %collective-permute-done.9.refs_4_), channel_id=1, source_target_pairs={{0,2},{2,0},{4,6},{6,4},{1,3},{3,1},{5,7},{7,5},{8,10},{10,8},{12,... | collective-permute-start | bytes 294920 | tf_op jit(solution)/shard_map/ppermute | solution.py:617
  46.5 2.4 %collective-permute-start.16 = (bf16[128,768]{1,0:T(8,128)(2,1)S(1)}, bf16[128,768]{1,0:T(8,128)(2,1)S(1)}, u32[]{:S(2)}, u32[]{:S(2)}) collective-permute-start(bf16[128,768]{1,0:T(8,128)(2,1)S(1)} %get-tuple-element.103), channel_id=1, source_target_pairs={{0,1},{1,0},{2,3},{3,2},{4,5},{5,4},{6,7},{7,6},{8,9},{9,8},{10,11... | collective-permute-start | bytes 589832 | tf_op jit(solution)/shard_map/ppermute | solution.py:613
  46.6 9.4 %collective-permute-start.17 = (bf16[128,1152]{1,0:T(8,128)(2,1)S(1)}, bf16[128,1152]{1,0:T(8,128)(2,1)S(1)}, u32[]{:S(2)}, u32[]{:S(2)}) collective-permute-start(bf16[128,1152]{1,0:T(8,128)(2,1)S(1)} %get-tuple-element.109), channel_id=1, source_target_pairs={{0,8},{8,0},{1,9},{9,1},{2,10},{10,2},{3,11},{11,3},{4,12},{12,4},... | collective-permute-start | bytes 884744 | tf_op jit(solution)/shard_map/ppermute | solution.py:613
  47.2 9.1 %collective-permute-start.18 = (bf16[64,1536]{1,0:T(8,128)(2,1)S(1)}, bf16[64,1536]{1,0:T(8,128)(2,1)S(1)}, u32[]{:S(2)}, u32[]{:S(2)}) collective-permute-start(bf16[64,1536]{1,0:T(8,128)(2,1)S(1)} %get-tuple-element.111), channel_id=1, source_target_pairs={{0,2},{2,0},{4,6},{6,4},{1,3},{3,1},{5,7},{7,5},{8,10},{10,8},{12,... | collective-permute-start | bytes 589832 | tf_op jit(solution)/shard_map/ppermute | solution.py:617
  56.2 1.7 %collective-permute-start.19 = (bf16[128,768]{1,0:T(8,128)(2,1)S(1)}, bf16[128,768]{1,0:T(8,128)(2,1)S(1)}, u32[]{:S(2)}, u32[]{:S(2)}) collective-permute-start(bf16[128,768]{1,0:T(8,128)(2,1)S(1)} %get-tuple-element.115), channel_id=1, source_target_pairs={{0,1},{1,0},{2,3},{3,2},{4,5},{5,4},{6,7},{7,6},{8,9},{9,8},{10,11... | collective-permute-start | bytes 589832 | tf_op jit(solution)/shard_map/ppermute | solution.py:613
  56.3 8.4 %collective-permute-start.20 = (bf16[32,1536]{1,0:T(8,128)(2,1)S(1)}, bf16[32,1536]{1,0:T(8,128)(2,1)S(1)}, u32[]{:S(2)}, u32[]{:S(2)}) collective-permute-start(bf16[32,1536]{1,0:T(8,128)(2,1)S(1)} %get-tuple-element.126), channel_id=1, source_target_pairs={{0,4},{2,6},{4,0},{6,2},{1,5},{3,7},{5,1},{7,3},{8,12},{10,14},{12... | collective-permute-start | bytes 294920 | tf_op jit(solution)/shard_map/ppermute | solution.py:617

commit v14 on v13

--- a/solution.py
+++ b/solution.py
@@ -559,30 +559,35 @@
     out_ref, done_ref, ring_ref, sems = refs[-4:]
     done_ref[...] = jnp.zeros_like(done_ref)
     units = pieces[0].shape[1]
-    depth, _, cut = ring_ref.shape
+    depth, height, cut = ring_ref.shape
+    half = cut // 2
     copies = []
     for (expert_flip, row_flip), a_ref in zip(flips, pieces):
-        at = pl.multiple_of(quarter_of(expert_flip, row_flip) * units, units)
-        left = a_ref[...].T
-        for n in range(4 * units // cut):
-            spot = len(copies) % depth
-            if len(copies) >= depth:
-                copies[-depth].wait()
-            ring_ref[spot] = scale * jnp.dot(
-                left, wide_ref[:, cut * n : cut * (n + 1)], preferred_element_type=F32
-            )
-            copy = pltpu.make_async_copy(
-                ring_ref.at[spot], out_ref.at[pl.ds(at, units), pl.ds(cut * n, cut)], sems.at[spot]
-            )
-            copy.start()
-            copies.append(copy)
+        start = quarter_of(expert_flip, row_flip) * units
+        for m in range(units // height):
+            rows = pl.ds(pl.multiple_of(start + height * m, height), height)
+            left = a_ref[:, height * m : height * (m + 1)].T
+            for n in range(4 * units // cut):
+                spot = len(copies) % depth
+                if len(copies) >= depth:
+                    copies[-depth].wait()
+                for i in range(2):
+                    column = cut * n + half * i
+                    ring_ref[spot, :, half * i : half * (i + 1)] = scale * jnp.dot(
+                        left, wide_ref[:, column : column + half], preferred_element_type=F32
+                    )
+                copy = pltpu.make_async_copy(
+                    ring_ref.at[spot], out_ref.at[rows, pl.ds(cut * n, cut)], sems.at[spot]
+                )
+                copy.start()
+                copies.append(copy)
     for copy in copies[-depth:]:
         copy.wait()
 
 
 def gram_piece(tick, pieces, flips, wide, gram=None):
     rows, units = pieces[0].shape
-    cut, depth = 512, 4
+    cut, height, depth = 1024, 256, 6
     operands = [tick, *pieces, in_vmem(wide)]
     in_specs = [ANY] + [VMEM] * (len(pieces) + 1)
     aliases = {}
@@ -600,7 +605,7 @@
         ],
         input_output_aliases=aliases,
         scratch_shapes=[
-            pltpu.VMEM((depth, units, cut), F32),
+            pltpu.VMEM((depth, height, cut), F32),
             pltpu.SemaphoreType.DMA((depth,)),
         ],
         compiler_params=params(10),

time: 66 us -> 65.9 us (level)
  no operation moved by 1% of the time
where the time goes in v14:
time: 65.9 us; the launch traced here: 65.8 us
  Pallas kernels  35.3 us (54%)
  starting transfers between devices  24.7 us (37%)
  waiting for transfers between devices  4.87 us (7%)
  between operations  0.87 us (1%)
    ppermute x11, starting transfers between devices, across(): return lax.ppermute(value, 'col', [(i, i ^ slot) for i in range(4)])  18.1 us
    pallas_call x2, Pallas kernels, gram_piece(): pl.pallas_call(functools.partial(gram_kernel, 2.0 / rows, flips), in_spec...  13.6 us
    pallas_call x1, Pallas kernels, regroup(): pl.pallas_call(regroup_kernel, in_specs=[ANY, HBM], out_specs=VMEM, out_s...  6.97 us
    ppermute x10, starting transfers between devices, swap(): return lax.ppermute(value, axis, [(0, 1), (1, 0)])  6.66 us
    pallas_call x4, Pallas kernels, preacts_of(): pl.pallas_call(functools.partial(preact_kernel, first, row_flip, chunk, c...  6.27 us
    pallas_call x1, Pallas kernels, fetch(): pl.pallas_call(fetch_kernel, in_specs=[ANY, HBM], out_specs=[VMEM, VMEM],...  3.8 us
    ppermute x11, waiting for transfers between devices, across(): return lax.ppermute(value, 'col', [(i, i ^ slot) for i in range(4)])  3.6 us
    pallas_call x1, Pallas kernels, project(): pl.pallas_call(project_kernel, in_specs=[ANY] + [VMEM] * 3, out_specs=[VM...  1.61 us
  transfers between devices with their start and end apart: 21, of which 6 were waited for; matrix products, arithmetic and copies ran while one was open for 0% of the time, Pallas kernels for 47%

profile of v14, /device:TPU:0, one launch (start us, length us, event | category | flops | bytes accessed | tf_op | source)
XLA Modules:
  0.0 65.8 jit_solution(3522234383429284889)
XLA Ops:
  0.6 1.3 %pack.1 = (bf16[32,1536]{1,0:T(8,128)(2,1)S(1)}, bf16[32,128]{1,0:T(8,128)(2,1)S(1)}, f32[32,128]{1,0:T(8,128)S(1)}) custom-call(bf16[128,1536]{1,0:T(8,128)(2,1)} %tokens_ref.1, s32[2,128]{1,0:T(2,128)} %bitcast.12, s32[1,128]{1,0:T(1,128)} %bitcast.14, f32[2,128]{1,0:T(2,128)} %bitcast.13), custom_call_target="tpu_custom_call" | custom-call | tf_op jit(solution)/shard_map/pack/pallas_call | solution.py:137
  1.9 5.1 %collective-permute-start.2 = (bf16[32,1536]{1,0:T(8,128)(2,1)S(1)}, bf16[32,1536]{1,0:T(8,128)(2,1)S(1)}, u32[]{:S(2)}, u32[]{:S(2)}) collective-permute-start(bf16[32,1536]{1,0:T(8,128)(2,1)S(1)} %get-tuple-element.65.after_ref.refs_0_), channel_id=1, source_target_pairs={{0,6},{2,4},{4,2},{6,0},{1,7},{3,5},{5,3},{7,1},{8,14},{10,12},{12... | collective-permute-start | bytes 294920 | tf_op jit(solution)/shard_map/ppermute | solution.py:622
  7.7 7.0 %regroup.1 = bf16[24,1536,2,128]{3,2,1,0:T(2,128)(2,1)S(1)} custom-call(bf16[32,1536]{1,0:T(8,128)(2,1)S(1)} %get-tuple-element.65.after_ref.refs_0_, bf16[1536,24,2,128]{3,2,1,0:T(2,128)(2,1)} %bitcast.11), custom_call_target="tpu_custom_call" | custom-call | bytes 37748736 | tf_op jit(solution)/shard_map/regroup/pallas_call | solution.py:167
  15.3 2.0 %preacts_sent.2 = (f32[256,768]{1,0:T(8,128)S(1)}, bf16[256,3072]{1,0:T(8,128)(2,1)S(1)}) custom-call(bf16[32,1536]{1,0:T(8,128)(2,1)S(1)} %get-tuple-element.65.after_ref.refs_0_, bf16[32,1536]{1,0:T(8,128)(2,1)S(1)} %collective-permute-done.refs_1_, bf16[32,1536]{1,0:T(8,128)(2,1)S(1)} %collective-permute-done.1.refs_2_, ...), custom_call_target="tpu_custom_call" | custom-call | flops 1207959552 | tf_op jit(solution)/shard_map/preacts_sent/pallas_call | solution.py:260
  17.4 1.4 %preacts_sent.3 = f32[256,768]{1,0:T(8,128)S(1)} custom-call(bf16[256,3072]{1,0:T(8,128)(2,1)S(1)} %get-tuple-element.71.refs_0_.after_ref, bf16[24,3072,128]{2,1,0:T(8,128)(2,1)S(1)} %bitcast.8), custom_call_target="tpu_custom_call" | custom-call | flops 1207959552 | tf_op jit(solution)/shard_map/preacts_sent/pallas_call | solution.py:260
  19.4 1.4 %preacts_kept.2.kept_ref = f32[256,768]{1,0:T(8,128)S(1)} custom-call(bf16[256,3072]{1,0:T(8,128)(2,1)S(1)} %get-tuple-element.71.refs_0_.after_ref, bf16[24,3072,128]{2,1,0:T(8,128)(2,1)S(1)} %bitcast.9), custom_call_target="tpu_custom_call" | custom-call | flops 1207959552 | tf_op jit(solution)/shard_map/preacts_kept/pallas_call | solution.py:260
  20.9 1.6 %collective-permute-start.5 = (bf16[256,384]{1,0:T(8,128)(2,1)S(1)}, bf16[256,384]{1,0:T(8,128)(2,1)S(1)}, u32[]{:S(2)}, u32[]{:S(2)}) collective-permute-start(bf16[256,384]{1,0:T(8,128)(2,1)S(1)} %get-tuple-element.73), channel_id=1, source_target_pairs={{0,8},{8,0},{1,9},{9,1},{2,10},{10,2},{3,11},{11,3},{4,12},{12,4},... | collective-permute-start | bytes 589832 | tf_op jit(solution)/shard_map/ppermute | solution.py:618
  22.4 1.4 %preacts_kept.3.kept_ref = f32[256,768]{1,0:T(8,128)S(1)} custom-call(bf16[256,3072]{1,0:T(8,128)(2,1)S(1)} %get-tuple-element.71.refs_0_.after_ref, bf16[24,3072,128]{2,1,0:T(8,128)(2,1)S(1)} %bitcast.10), custom_call_target="tpu_custom_call" | custom-call | flops 1207959552 | tf_op jit(solution)/shard_map/preacts_kept/pallas_call | solution.py:260
  24.6 3.8 %fetch_down.1 = (bf16[3072,1536]{1,0:T(8,128)(2,1)S(1)}, f32[8,128]{1,0:T(8,128)S(1)}) custom-call(bf16[256,3072]{1,0:T(8,128)(2,1)S(1)} %get-tuple-element.71.refs_0_.after_ref, bf16[3072,1536]{1,0:T(8,128)(2,1)} %down_ref.1), custom_call_target="tpu_custom_call" | custom-call | bytes 18874368 | tf_op jit(solution)/shard_map/fetch_down/pallas_call | solution.py:198
  28.8 1.7 %collective-permute-start.7 = (bf16[128,384]{1,0:T(8,128)(2,1)S(1)}, bf16[128,384]{1,0:T(8,128)(2,1)S(1)}, u32[]{:S(2)}, u32[]{:S(2)}) collective-permute-start(bf16[128,384]{1,0:T(8,128)(2,1)S(1)} %act.2.refs_0_), channel_id=1, source_target_pairs={{0,4},{2,6},{4,0},{6,2},{1,5},{3,7},{5,1},{7,3},{8,12},{10,14},{12... | collective-permute-start | bytes 294920 | tf_op jit(solution)/shard_map/ppermute | solution.py:622
  30.5 2.0 %collective-permute-start.8 = (bf16[128,384]{1,0:T(8,128)(2,1)S(1)}, bf16[128,384]{1,0:T(8,128)(2,1)S(1)}, u32[]{:S(2)}, u32[]{:S(2)}) collective-permute-start(bf16[128,384]{1,0:T(8,128)(2,1)S(1)} %act.2.refs_0_), channel_id=1, source_target_pairs={{0,2},{2,0},{4,6},{6,4},{1,3},{3,1},{5,7},{7,5},{8,10},{10,8},{12,... | collective-permute-start | bytes 294920 | tf_op jit(solution)/shard_map/ppermute | solution.py:622
  32.6 1.2 %collective-permute-start.9 = (bf16[128,384]{1,0:T(8,128)(2,1)S(1)}, bf16[128,384]{1,0:T(8,128)(2,1)S(1)}, u32[]{:S(2)}, u32[]{:S(2)}) collective-permute-start(bf16[128,384]{1,0:T(8,128)(2,1)S(1)} %get-tuple-element.88), channel_id=1, source_target_pairs={{0,4},{2,6},{4,0},{6,2},{1,5},{3,7},{5,1},{7,3},{8,12},{10,14},{12... | collective-permute-start | bytes 294920 | tf_op jit(solution)/shard_map/ppermute | solution.py:622
  33.8 1.5 %collective-permute-start.12 = (bf16[128,768]{1,0:T(8,128)(2,1)S(1)}, bf16[128,768]{1,0:T(8,128)(2,1)S(1)}, u32[]{:S(2)}, u32[]{:S(2)}) collective-permute-start(bf16[128,768]{1,0:T(8,128)(2,1)S(1)} %get-tuple-element.90.left_ref.refs_0_), channel_id=1, source_target_pairs={{0,8},{8,0},{1,9},{9,1},{2,10},{10,2},{3,11},{11,3},{4,12},{12,4},... | collective-permute-start | bytes 589832 | tf_op jit(solution)/shard_map/ppermute | solution.py:618
  35.3 1.4 %collective-permute-done.7.in_ref.near_ref.refs_3_ = bf16[128,384]{1,0:T(8,128)(2,1)S(1)} collective-permute-done((bf16[128,384]{1,0:T(8,128)(2,1)S(1)}, bf16[128,384]{1,0:T(8,128)(2,1)S(1)}, u32[]{:S(2)}, u32[]{:S(2)}) %collective-permute-start.7) | collective-permute-done | bytes 98336 | tf_op jit(solution)/shard_map/ppermute | solution.py:622
  36.8 1.5 %collective-permute-start.10 = (bf16[128,384]{1,0:T(8,128)(2,1)S(1)}, bf16[128,384]{1,0:T(8,128)(2,1)S(1)}, u32[]{:S(2)}, u32[]{:S(2)}) collective-permute-start(bf16[128,384]{1,0:T(8,128)(2,1)S(1)} %relay.1), channel_id=1, source_target_pairs={{0,2},{2,0},{4,6},{6,4},{1,3},{3,1},{5,7},{7,5},{8,10},{10,8},{12,... | collective-permute-start | bytes 294920 | tf_op jit(solution)/shard_map/ppermute | solution.py:622
  39.7 1.6 %collective-permute-start.14 = (bf16[128,384]{1,0:T(8,128)(2,1)S(1)}, bf16[128,384]{1,0:T(8,128)(2,1)S(1)}, u32[]{:S(2)}, u32[]{:S(2)}) collective-permute-start(bf16[128,384]{1,0:T(8,128)(2,1)S(1)} %choose.1), channel_id=1, source_target_pairs={{0,8},{8,0},{1,9},{9,1},{2,10},{10,2},{3,11},{11,3},{4,12},{12,4},... | collective-permute-start | bytes 294920 | tf_op jit(solution)/shard_map/ppermute | solution.py:618
  41.2 2.0 %collective-permute-start.15 = (bf16[128,384]{1,0:T(8,128)(2,1)S(1)}, bf16[128,384]{1,0:T(8,128)(2,1)S(1)}, u32[]{:S(2)}, u32[]{:S(2)}) collective-permute-start(bf16[128,384]{1,0:T(8,128)(2,1)S(1)} %collective-permute-done.9.refs_4_), channel_id=1, source_target_pairs={{0,2},{2,0},{4,6},{6,4},{1,3},{3,1},{5,7},{7,5},{8,10},{10,8},{12,... | collective-permute-start | bytes 294920 | tf_op jit(solution)/shard_map/ppermute | solution.py:622
  43.3 1.6 %project.1 = (f32[64,1536]{1,0:T(8,128)S(1)}, bf16[64,1536]{1,0:T(8,128)(2,1)S(1)}, bf16[128,3072]{1,0:T(8,128)(2,1)S(1)}, f32[8,128]{1,0:T(8,128)S(1)}) custom-call(f32[8,128]{1,0:T(8,128)S(1)} %get-tuple-element.91.tick_ref, bf16[128,1536]{1,0:T(8,128)(2,1)S(1)} %join.1.here_ref, bf16[128,1536]{1,0:T(8,128)(2,1)S(1)} %collective-permute-done.13.there_ref, ...), custom_call_target="tpu_custom_call" | custom-call | bytes 1 | tf_op jit(solution)/shard_map/project/pallas_call | solution.py:495
  44.9 1.5 %collective-permute-done.15.refs_6_ = bf16[128,384]{1,0:T(8,128)(2,1)S(1)} collective-permute-done((bf16[128,384]{1,0:T(8,128)(2,1)S(1)}, bf16[128,384]{1,0:T(8,128)(2,1)S(1)}, u32[]{:S(2)}, u32[]{:S(2)}) %collective-permute-start.15) | collective-permute-done | bytes 98336 | tf_op jit(solution)/shard_map/ppermute | solution.py:622
  47.2 1.7 %collective-permute-start.18 = (bf16[64,1536]{1,0:T(8,128)(2,1)S(1)}, bf16[64,1536]{1,0:T(8,128)(2,1)S(1)}, u32[]{:S(2)}, u32[]{:S(2)}) collective-permute-start(bf16[64,1536]{1,0:T(8,128)(2,1)S(1)} %get-tuple-element.111), channel_id=1, source_target_pairs={{0,2},{2,0},{4,6},{6,4},{1,3},{3,1},{5,7},{7,5},{8,10},{10,8},{12,... | collective-permute-start | bytes 589832 | tf_op jit(solution)/shard_map/ppermute | solution.py:622
  48.9 6.8 %gram.2 = (f32[3072,3072]{1,0:T(8,128)}, f32[8,128]{1,0:T(8,128)S(1)}) custom-call(f32[8,128]{1,0:T(8,128)S(1)} %get-tuple-element.104.refs_0_, bf16[128,768]{1,0:T(8,128)(2,1)S(1)} %get-tuple-element.105.refs_1_, bf16[128,768]{1,0:T(8,128)(2,1)S(1)} %collective-permute-done.16.refs_2_, bf16[128,3072]{1,0:T(8,128)(2,1)S(1)} %get-tuple-element.107.refs_3_), custom_call_target="tpu_custom_call" | custom-call | flops 1207959552 | bytes 18874368 | tf_op jit(solution)/shard_map/gram/pallas_call | solution.py:598
  56.3 1.5 %collective-permute-start.20 = (bf16[32,1536]{1,0:T(8,128)(2,1)S(1)}, bf16[32,1536]{1,0:T(8,128)(2,1)S(1)}, u32[]{:S(2)}, u32[]{:S(2)}) collective-permute-start(bf16[32,1536]{1,0:T(8,128)(2,1)S(1)} %get-tuple-element.126), channel_id=1, source_target_pairs={{0,4},{2,6},{4,0},{6,2},{1,5},{3,7},{5,1},{7,3},{8,12},{10,14},{12... | collective-permute-start | bytes 294920 | tf_op jit(solution)/shard_map/ppermute | solution.py:622
  57.9 6.8 %gram.3 = (f32[3072,3072]{1,0:T(8,128)}, f32[8,128]{1,0:T(8,128)S(1)}) custom-call(f32[8,128]{1,0:T(8,128)S(1)} %get-tuple-element.116.refs_0_, bf16[128,768]{1,0:T(8,128)(2,1)S(1)} %get-tuple-element.117.refs_1_, bf16[128,768]{1,0:T(8,128)(2,1)S(1)} %collective-permute-done.19.refs_2_, ...), custom_call_target="tpu_custom_call", output_to_operand_aliasing={{0}: (4, {})} | custom-call | flops 1207959552 | bytes 18874368 | tf_op jit(solution)/shard_map/gram/pallas_call | solution.py:598
  64.7 1.1 %unpack.1 = bf16[128,1536]{1,0:T(8,128)(2,1)} custom-call(f32[8,128]{1,0:T(8,128)S(1)} %get-tuple-element.120.after_ref, bf16[32,128]{1,0:T(8,128)(2,1)S(1)} %get-tuple-element.121.placing_ref, f32[32,128]{1,0:T(8,128)S(1)} %get-tuple-element.122.factor_ref, f32[32,1536]{1,0:T(8,128)S(1)} %get-tuple-element.125.own_ref, ...), custom_call_target="tpu_custom_call" | custom-call | tf_op jit(solution)/shard_map/unpack/pallas_call | solution.py:545
  (39 shorter events, 5.9 us)
Async XLA Ops:
  1.9 12.7 %collective-permute-start.2 = (bf16[32,1536]{1,0:T(8,128)(2,1)S(1)}, bf16[32,1536]{1,0:T(8,128)(2,1)S(1)}, u32[]{:S(2)}, u32[]{:S(2)}) collective-permute-start(bf16[32,1536]{1,0:T(8,128)(2,1)S(1)} %get-tuple-element.65.after_ref.refs_0_), channel_id=1, source_target_pairs={{0,6},{2,4},{4,2},{6,0},{1,7},{3,5},{5,3},{7,1},{8,14},{10,12},{12... | collective-permute-start | bytes 294920 | tf_op jit(solution)/shard_map/ppermute | solution.py:622
  7.0 8.3 %collective-permute-start.1 = (bf16[32,1536]{1,0:T(8,128)(2,1)S(1)}, bf16[32,1536]{1,0:T(8,128)(2,1)S(1)}, u32[]{:S(2)}, u32[]{:S(2)}) collective-permute-start(bf16[32,1536]{1,0:T(8,128)(2,1)S(1)} %get-tuple-element.65.after_ref.refs_0_), channel_id=1, source_target_pairs={{0,4},{2,6},{4,0},{6,2},{1,5},{3,7},{5,1},{7,3},{8,12},{10,14},{12... | collective-permute-start | bytes 294920 | tf_op jit(solution)/shard_map/ppermute | solution.py:622
  7.0 8.3 %collective-permute-start = (bf16[32,1536]{1,0:T(8,128)(2,1)S(1)}, bf16[32,1536]{1,0:T(8,128)(2,1)S(1)}, u32[]{:S(2)}, u32[]{:S(2)}) collective-permute-start(bf16[32,1536]{1,0:T(8,128)(2,1)S(1)} %get-tuple-element.65.after_ref.refs_0_), channel_id=1, source_target_pairs={{0,2},{2,0},{4,6},{6,4},{1,3},{3,1},{5,7},{7,5},{8,10},{10,8},{12,... | collective-permute-start | bytes 294920 | tf_op jit(solution)/shard_map/ppermute | solution.py:622
  17.3 3.5 %collective-permute-start.3 = (f32[256,768]{1,0:T(8,128)S(1)}, f32[256,768]{1,0:T(8,128)S(1)}, u32[]{:S(2)}, u32[]{:S(2)}) collective-permute-start(f32[256,768]{1,0:T(8,128)S(1)} %get-tuple-element.67), channel_id=1, source_target_pairs={{0,1},{1,0},{2,3},{3,2},{4,5},{5,4},{6,7},{7,6},{8,9},{9,8},{10,11... | collective-permute-start | bytes 2359304 | tf_op jit(solution)/shard_map/ppermute | solution.py:618
  18.8 5.1 %collective-permute-start.4 = (f32[256,768]{1,0:T(8,128)S(1)}, f32[256,768]{1,0:T(8,128)S(1)}, u32[]{:S(2)}, u32[]{:S(2)}) collective-permute-start(f32[256,768]{1,0:T(8,128)S(1)} %preacts_sent.3), channel_id=1, source_target_pairs={{0,1},{1,0},{2,3},{3,2},{4,5},{5,4},{6,7},{7,6},{8,9},{9,8},{10,11... | collective-permute-start | bytes 2359304 | tf_op jit(solution)/shard_map/ppermute | solution.py:618
  20.9 7.8 %collective-permute-start.5 = (bf16[256,384]{1,0:T(8,128)(2,1)S(1)}, bf16[256,384]{1,0:T(8,128)(2,1)S(1)}, u32[]{:S(2)}, u32[]{:S(2)}) collective-permute-start(bf16[256,384]{1,0:T(8,128)(2,1)S(1)} %get-tuple-element.73), channel_id=1, source_target_pairs={{0,8},{8,0},{1,9},{9,1},{2,10},{10,2},{3,11},{11,3},{4,12},{12,4},... | collective-permute-start | bytes 589832 | tf_op jit(solution)/shard_map/ppermute | solution.py:618
  24.0 8.6 %collective-permute-start.6 = (bf16[256,384]{1,0:T(8,128)(2,1)S(1)}, bf16[256,384]{1,0:T(8,128)(2,1)S(1)}, u32[]{:S(2)}, u32[]{:S(2)}) collective-permute-start(bf16[256,384]{1,0:T(8,128)(2,1)S(1)} %get-tuple-element.75), channel_id=1, source_target_pairs={{0,8},{8,0},{1,9},{9,1},{2,10},{10,2},{3,11},{11,3},{4,12},{12,4},... | collective-permute-start | bytes 589832 | tf_op jit(solution)/shard_map/ppermute | solution.py:618
  28.8 8.0 %collective-permute-start.7 = (bf16[128,384]{1,0:T(8,128)(2,1)S(1)}, bf16[128,384]{1,0:T(8,128)(2,1)S(1)}, u32[]{:S(2)}, u32[]{:S(2)}) collective-permute-start(bf16[128,384]{1,0:T(8,128)(2,1)S(1)} %act.2.refs_0_), channel_id=1, source_target_pairs={{0,4},{2,6},{4,0},{6,2},{1,5},{3,7},{5,1},{7,3},{8,12},{10,14},{12... | collective-permute-start | bytes 294920 | tf_op jit(solution)/shard_map/ppermute | solution.py:622
  30.5 6.2 %collective-permute-start.8 = (bf16[128,384]{1,0:T(8,128)(2,1)S(1)}, bf16[128,384]{1,0:T(8,128)(2,1)S(1)}, u32[]{:S(2)}, u32[]{:S(2)}) collective-permute-start(bf16[128,384]{1,0:T(8,128)(2,1)S(1)} %act.2.refs_0_), channel_id=1, source_target_pairs={{0,2},{2,0},{4,6},{6,4},{1,3},{3,1},{5,7},{7,5},{8,10},{10,8},{12,... | collective-permute-start | bytes 294920 | tf_op jit(solution)/shard_map/ppermute | solution.py:622
  32.6 8.6 %collective-permute-start.9 = (bf16[128,384]{1,0:T(8,128)(2,1)S(1)}, bf16[128,384]{1,0:T(8,128)(2,1)S(1)}, u32[]{:S(2)}, u32[]{:S(2)}) collective-permute-start(bf16[128,384]{1,0:T(8,128)(2,1)S(1)} %get-tuple-element.88), channel_id=1, source_target_pairs={{0,4},{2,6},{4,0},{6,2},{1,5},{3,7},{5,1},{7,3},{8,12},{10,14},{12... | collective-permute-start | bytes 294920 | tf_op jit(solution)/shard_map/ppermute | solution.py:622
  33.8 5.7 %collective-permute-start.12 = (bf16[128,768]{1,0:T(8,128)(2,1)S(1)}, bf16[128,768]{1,0:T(8,128)(2,1)S(1)}, u32[]{:S(2)}, u32[]{:S(2)}) collective-permute-start(bf16[128,768]{1,0:T(8,128)(2,1)S(1)} %get-tuple-element.90.left_ref.refs_0_), channel_id=1, source_target_pairs={{0,8},{8,0},{1,9},{9,1},{2,10},{10,2},{3,11},{11,3},{4,12},{12,4},... | collective-permute-start | bytes 589832 | tf_op jit(solution)/shard_map/ppermute | solution.py:618
  36.8 6.5 %collective-permute-start.10 = (bf16[128,384]{1,0:T(8,128)(2,1)S(1)}, bf16[128,384]{1,0:T(8,128)(2,1)S(1)}, u32[]{:S(2)}, u32[]{:S(2)}) collective-permute-start(bf16[128,384]{1,0:T(8,128)(2,1)S(1)} %relay.1), channel_id=1, source_target_pairs={{0,2},{2,0},{4,6},{6,4},{1,3},{3,1},{5,7},{7,5},{8,10},{10,8},{12,... | collective-permute-start | bytes 294920 | tf_op jit(solution)/shard_map/ppermute | solution.py:622
  38.2 5.0 %collective-permute-start.11 = (bf16[128,384]{1,0:T(8,128)(2,1)S(1)}, bf16[128,384]{1,0:T(8,128)(2,1)S(1)}, u32[]{:S(2)}, u32[]{:S(2)}) collective-permute-start(bf16[128,384]{1,0:T(8,128)(2,1)S(1)} %get-tuple-element.88), channel_id=1, source_target_pairs={{0,2},{2,0},{4,6},{6,4},{1,3},{3,1},{5,7},{7,5},{8,10},{10,8},{12,... | collective-permute-start | bytes 294920 | tf_op jit(solution)/shard_map/ppermute | solution.py:622
  39.5 3.7 %collective-permute-start.13 = (bf16[128,1536]{1,0:T(8,128)(2,1)S(1)}, bf16[128,1536]{1,0:T(8,128)(2,1)S(1)}, u32[]{:S(2)}, u32[]{:S(2)}) collective-permute-start(bf16[128,1536]{1,0:T(8,128)(2,1)S(1)} %join.1.here_ref), channel_id=1, source_target_pairs={{0,1},{1,0},{2,3},{3,2},{4,5},{5,4},{6,7},{7,6},{8,9},{9,8},{10,11... | collective-permute-start | bytes 1179656 | tf_op jit(solution)/shard_map/ppermute | solution.py:618
  39.7 5.2 %collective-permute-start.14 = (bf16[128,384]{1,0:T(8,128)(2,1)S(1)}, bf16[128,384]{1,0:T(8,128)(2,1)S(1)}, u32[]{:S(2)}, u32[]{:S(2)}) collective-permute-start(bf16[128,384]{1,0:T(8,128)(2,1)S(1)} %choose.1), channel_id=1, source_target_pairs={{0,8},{8,0},{1,9},{9,1},{2,10},{10,2},{3,11},{11,3},{4,12},{12,4},... | collective-permute-start | bytes 294920 | tf_op jit(solution)/shard_map/ppermute | solution.py:618
  41.2 5.2 %collective-permute-start.15 = (bf16[128,384]{1,0:T(8,128)(2,1)S(1)}, bf16[128,384]{1,0:T(8,128)(2,1)S(1)}, u32[]{:S(2)}, u32[]{:S(2)}) collective-permute-start(bf16[128,384]{1,0:T(8,128)(2,1)S(1)} %collective-permute-done.9.refs_4_), channel_id=1, source_target_pairs={{0,2},{2,0},{4,6},{6,4},{1,3},{3,1},{5,7},{7,5},{8,10},{10,8},{12,... | collective-permute-start | bytes 294920 | tf_op jit(solution)/shard_map/ppermute | solution.py:622
  46.5 2.4 %collective-permute-start.16 = (bf16[128,768]{1,0:T(8,128)(2,1)S(1)}, bf16[128,768]{1,0:T(8,128)(2,1)S(1)}, u32[]{:S(2)}, u32[]{:S(2)}) collective-permute-start(bf16[128,768]{1,0:T(8,128)(2,1)S(1)} %get-tuple-element.103), channel_id=1, source_target_pairs={{0,1},{1,0},{2,3},{3,2},{4,5},{5,4},{6,7},{7,6},{8,9},{9,8},{10,11... | collective-permute-start | bytes 589832 | tf_op jit(solution)/shard_map/ppermute | solution.py:618
  46.6 9.4 %collective-permute-start.17 = (bf16[128,1152]{1,0:T(8,128)(2,1)S(1)}, bf16[128,1152]{1,0:T(8,128)(2,1)S(1)}, u32[]{:S(2)}, u32[]{:S(2)}) collective-permute-start(bf16[128,1152]{1,0:T(8,128)(2,1)S(1)} %get-tuple-element.109), channel_id=1, source_target_pairs={{0,8},{8,0},{1,9},{9,1},{2,10},{10,2},{3,11},{11,3},{4,12},{12,4},... | collective-permute-start | bytes 884744 | tf_op jit(solution)/shard_map/ppermute | solution.py:618
  47.2 9.1 %collective-permute-start.18 = (bf16[64,1536]{1,0:T(8,128)(2,1)S(1)}, bf16[64,1536]{1,0:T(8,128)(2,1)S(1)}, u32[]{:S(2)}, u32[]{:S(2)}) collective-permute-start(bf16[64,1536]{1,0:T(8,128)(2,1)S(1)} %get-tuple-element.111), channel_id=1, source_target_pairs={{0,2},{2,0},{4,6},{6,4},{1,3},{3,1},{5,7},{7,5},{8,10},{10,8},{12,... | collective-permute-start | bytes 589832 | tf_op jit(solution)/shard_map/ppermute | solution.py:622
  56.2 1.7 %collective-permute-start.19 = (bf16[128,768]{1,0:T(8,128)(2,1)S(1)}, bf16[128,768]{1,0:T(8,128)(2,1)S(1)}, u32[]{:S(2)}, u32[]{:S(2)}) collective-permute-start(bf16[128,768]{1,0:T(8,128)(2,1)S(1)} %get-tuple-element.115), channel_id=1, source_target_pairs={{0,1},{1,0},{2,3},{3,2},{4,5},{5,4},{6,7},{7,6},{8,9},{9,8},{10,11... | collective-permute-start | bytes 589832 | tf_op jit(solution)/shard_map/ppermute | solution.py:618
  56.3 8.4 %collective-permute-start.20 = (bf16[32,1536]{1,0:T(8,128)(2,1)S(1)}, bf16[32,1536]{1,0:T(8,128)(2,1)S(1)}, u32[]{:S(2)}, u32[]{:S(2)}) collective-permute-start(bf16[32,1536]{1,0:T(8,128)(2,1)S(1)} %get-tuple-element.126), channel_id=1, source_target_pairs={{0,4},{2,6},{4,0},{6,2},{1,5},{3,7},{5,1},{7,3},{8,12},{10,14},{12... | collective-permute-start | bytes 294920 | tf_op jit(solution)/shard_map/ppermute | solution.py:622

commit v15 on v14

--- a/solution.py
+++ b/solution.py
@@ -150,7 +150,7 @@
     )(*(in_hbm(x) for x in operands))
 
 
-def regroup_kernel(after_ref, weights_ref, out_ref, sems):
+def regroup_kernel(after_ref, weights_ref, out_ref, widen_ref, sems):
     del after_ref
     copies = [
         pltpu.make_async_copy(weights_ref.at[:, t], out_ref.at[t], sems.at[t])
@@ -158,23 +158,31 @@
     ]
     for copy in copies:
         copy.start()
+    cut = widen_ref.shape[0]
+    into = lax.broadcasted_iota(jnp.int32, (cut, 4 * cut), 1)
+    out_of = lax.broadcasted_iota(jnp.int32, (cut, 4 * cut), 0)
+    half = jnp.where(into < 2 * cut, 0, 1)
+    widen_ref[...] = jnp.where(into - 2 * cut * half == 2 * out_of + half, 1.0, 0.0).astype(BF16)
     for copy in copies:
         copy.wait()
 
 
 def regroup(behind, weights):
     depth, tiles, two, lanes = weights.shape
-    grouped = pl.pallas_call(
+    grouped, widen = pl.pallas_call(
         regroup_kernel,
         in_specs=[ANY, HBM],
-        out_specs=VMEM,
-        out_shape=pltpu.VMEM((tiles, depth, two, lanes), BF16),
+        out_specs=[VMEM] * 2,
+        out_shape=[
+            pltpu.VMEM((tiles, depth, two, lanes), BF16),
+            pltpu.VMEM((256, 1024), BF16),
+        ],
         scratch_shapes=[pltpu.SemaphoreType.DMA((tiles,))],
         compiler_params=params(4),
         cost_estimate=cost(0, 4 * weights.size),
         name="regroup",
     )(behind, in_hbm(weights))
-    return grouped.reshape(tiles, depth * two, lanes)
+    return grouped.reshape(tiles, depth * two, lanes), widen
 
 
 def fetch_kernel(after_ref, down_ref, out_ref, done_ref, sems):
@@ -207,32 +215,30 @@
     )(behind, in_hbm(down))
 
 
-def widen_tokens(x_refs, wide_ref):
+def widen_tokens(x_refs, widen_ref, wide_ref):
     slots, depth = x_refs[0].shape
     rows = 4 * slots
     here = lax.axis_index("col")
-    cut = 256
-    into = lax.broadcasted_iota(jnp.int32, (cut, 4 * cut), 1)
-    out_of = lax.broadcasted_iota(jnp.int32, (cut, 4 * cut), 0)
-    half = jnp.where(into < 2 * cut, 0, 1)
-    widen = jnp.where(into - 2 * cut * half == 2 * out_of + half, 1.0, 0.0).astype(BF16)
-    for slot, x_ref in enumerate(x_refs):
-        stacked = jnp.concatenate(
-            [x_ref[:, cut * k : cut * (k + 1)] for k in range(depth // cut)], axis=0
-        )
-        spaced = jnp.dot(stacked, widen, preferred_element_type=F32).astype(BF16)
+    cut = widen_ref.shape[0]
+    parts = depth // cut
+    stacked = jnp.concatenate(
+        [x_ref[:, cut * k : cut * (k + 1)] for x_ref in x_refs for k in range(parts)], axis=0
+    )
+    spaced = jnp.dot(stacked, widen_ref[...], preferred_element_type=F32).astype(BF16)
+    for slot in range(len(x_refs)):
         for h in range(2):
             at = pl.multiple_of(h * rows + (here ^ slot) * slots, slots)
-            for k in range(depth // cut):
+            for k in range(parts):
+                row = slots * (slot * parts + k)
                 wide_ref[pl.ds(at, slots), 2 * cut * k : 2 * cut * (k + 1)] = spaced[
-                    slots * k : slots * (k + 1), 2 * cut * h : 2 * cut * (h + 1)
+                    row : row + slots, 2 * cut * h : 2 * cut * (h + 1)
                 ]
 
 
 def preact_kernel(first, row_flip, chunk, chunks, *refs):
     if first:
-        x0, x1, x2, x3, w_ref, out_ref, wide_ref = refs
-        widen_tokens((x0, x1, x2, x3), wide_ref)
+        x0, x1, x2, x3, widen_ref, w_ref, out_ref, wide_ref = refs
+        widen_tokens((x0, x1, x2, x3), widen_ref, wide_ref)
     else:
         wide_ref, w_ref, out_ref = refs
     tiles, _, lanes = w_ref.shape
@@ -631,9 +637,9 @@
 
     packed, placing, factor = pack(tokens, routes.T, pad_mask[None, :], route_weight.T)
     lefts = [packed] + [across(packed, slot) for slot in (1, 2, 3)]
-    grouped = regroup(packed, weights)
-
-    first_sent, wide = preacts_of(lefts, grouped, 1, 0, chunks)
+    grouped, widen = regroup(packed, weights)
+
+    first_sent, wide = preacts_of([*lefts, widen], grouped, 1, 0, chunks)
     (last_sent,) = preacts_of([wide], grouped, 1, 1, chunks)
     got = [swap(first_sent, "row"), swap(last_sent, "row")]
     stays, got_x = [], []

time: 65.9 us -> 66.7 us (1.012)
  Pallas kernels: 35.3 us -> 36.1 us
    pallas_call x4, Pallas kernels: 6.27 us -> 7.04 us  [preacts_of(): pl.pallas_call(functools.partial(preact_kernel, first, row_flip, chunk, c...]
  transfers between devices with their start and end apart: 21 -> 21, of which waited for: 6 -> 6; matrix products, arithmetic and copies ran while one was open for 0% -> 0% of each run, Pallas kernels for 47% -> 46%
where the time goes in v15:
time: 66.7 us; the launch traced here: 66.6 us
  Pallas kernels  36.1 us (54%)
  starting transfers between devices  24.7 us (37%)
  waiting for transfers between devices  4.88 us (7%)
  between operations  0.86 us (1%)
    ppermute x11, starting transfers between devices, across(): return lax.ppermute(value, 'col', [(i, i ^ slot) for i in range(4)])  18.1 us
    pallas_call x2, Pallas kernels, gram_piece(): pl.pallas_call(functools.partial(gram_kernel, 2.0 / rows, flips), in_spec...  13.6 us
    pallas_call x4, Pallas kernels, preacts_of(): pl.pallas_call(functools.partial(preact_kernel, first, row_flip, chunk, c...  7.04 us
    pallas_call x1, Pallas kernels, regroup(): pl.pallas_call(regroup_kernel, in_specs=[ANY, HBM], out_specs=[VMEM] * 2,...  6.97 us
    ppermute x10, starting transfers between devices, swap(): return lax.ppermute(value, axis, [(0, 1), (1, 0)])  6.63 us
    pallas_call x1, Pallas kernels, fetch(): pl.pallas_call(fetch_kernel, in_specs=[ANY, HBM], out_specs=[VMEM, VMEM],...  3.8 us
    ppermute x11, waiting for transfers between devices, across(): return lax.ppermute(value, 'col', [(i, i ^ slot) for i in range(4)])  3.54 us
    pallas_call x1, Pallas kernels, project(): pl.pallas_call(project_kernel, in_specs=[ANY] + [VMEM] * 3, out_specs=[VM...  1.61 us
  transfers between devices with their start and end apart: 21, of which 6 were waited for; matrix products, arithmetic and copies ran while one was open for 0% of the time, Pallas kernels for 46%

profile of v15, /device:TPU:0, one launch (start us, length us, event | category | flops | bytes accessed | tf_op | source)
XLA Modules:
  0.0 66.6 jit_solution(991103311382932431)
XLA Ops:
  0.6 1.3 %pack.1 = (bf16[32,1536]{1,0:T(8,128)(2,1)S(1)}, bf16[32,128]{1,0:T(8,128)(2,1)S(1)}, f32[32,128]{1,0:T(8,128)S(1)}) custom-call(bf16[128,1536]{1,0:T(8,128)(2,1)} %tokens_ref.1, s32[2,128]{1,0:T(2,128)} %bitcast.12, s32[1,128]{1,0:T(1,128)} %bitcast.14, f32[2,128]{1,0:T(2,128)} %bitcast.13), custom_call_target="tpu_custom_call" | custom-call | tf_op jit(solution)/shard_map/pack/pallas_call | solution.py:137
  1.9 5.1 %collective-permute-start.2 = (bf16[32,1536]{1,0:T(8,128)(2,1)S(1)}, bf16[32,1536]{1,0:T(8,128)(2,1)S(1)}, u32[]{:S(2)}, u32[]{:S(2)}) collective-permute-start(bf16[32,1536]{1,0:T(8,128)(2,1)S(1)} %get-tuple-element.67.after_ref.refs_0_), channel_id=1, source_target_pairs={{0,6},{2,4},{4,2},{6,0},{1,7},{3,5},{5,3},{7,1},{8,14},{10,12},{12... | collective-permute-start | bytes 294920 | tf_op jit(solution)/shard_map/ppermute | solution.py:628
  7.7 7.0 %regroup.1 = (bf16[24,1536,2,128]{3,2,1,0:T(2,128)(2,1)S(1)}, bf16[256,1024]{1,0:T(8,128)(2,1)S(1)}) custom-call(bf16[32,1536]{1,0:T(8,128)(2,1)S(1)} %get-tuple-element.67.after_ref.refs_0_, bf16[1536,24,2,128]{3,2,1,0:T(2,128)(2,1)} %bitcast.11), custom_call_target="tpu_custom_call" | custom-call | bytes 37748736 | tf_op jit(solution)/shard_map/regroup/pallas_call | solution.py:172
  15.3 2.8 %preacts_sent.2 = (f32[256,768]{1,0:T(8,128)S(1)}, bf16[256,3072]{1,0:T(8,128)(2,1)S(1)}) custom-call(bf16[32,1536]{1,0:T(8,128)(2,1)S(1)} %get-tuple-element.67.after_ref.refs_0_, bf16[32,1536]{1,0:T(8,128)(2,1)S(1)} %collective-permute-done.refs_1_, bf16[32,1536]{1,0:T(8,128)(2,1)S(1)} %collective-permute-done.1.refs_2_, ...), custom_call_target="tpu_custom_call" | custom-call | flops 1207959552 | tf_op jit(solution)/shard_map/preacts_sent/pallas_call | solution.py:266
  18.1 1.4 %preacts_sent.3 = f32[256,768]{1,0:T(8,128)S(1)} custom-call(bf16[256,3072]{1,0:T(8,128)(2,1)S(1)} %get-tuple-element.75.refs_0_.after_ref, bf16[24,3072,128]{2,1,0:T(8,128)(2,1)S(1)} %bitcast.8), custom_call_target="tpu_custom_call" | custom-call | flops 1207959552 | tf_op jit(solution)/shard_map/preacts_sent/pallas_call | solution.py:266
  20.1 1.4 %preacts_kept.2.kept_ref = f32[256,768]{1,0:T(8,128)S(1)} custom-call(bf16[256,3072]{1,0:T(8,128)(2,1)S(1)} %get-tuple-element.75.refs_0_.after_ref, bf16[24,3072,128]{2,1,0:T(8,128)(2,1)S(1)} %bitcast.9), custom_call_target="tpu_custom_call" | custom-call | flops 1207959552 | tf_op jit(solution)/shard_map/preacts_kept/pallas_call | solution.py:266
  21.7 1.6 %collective-permute-start.5 = (bf16[256,384]{1,0:T(8,128)(2,1)S(1)}, bf16[256,384]{1,0:T(8,128)(2,1)S(1)}, u32[]{:S(2)}, u32[]{:S(2)}) collective-permute-start(bf16[256,384]{1,0:T(8,128)(2,1)S(1)} %get-tuple-element.77), channel_id=1, source_target_pairs={{0,8},{8,0},{1,9},{9,1},{2,10},{10,2},{3,11},{11,3},{4,12},{12,4},... | collective-permute-start | bytes 589832 | tf_op jit(solution)/shard_map/ppermute | solution.py:624
  23.3 1.4 %preacts_kept.3.kept_ref = f32[256,768]{1,0:T(8,128)S(1)} custom-call(bf16[256,3072]{1,0:T(8,128)(2,1)S(1)} %get-tuple-element.75.refs_0_.after_ref, bf16[24,3072,128]{2,1,0:T(8,128)(2,1)S(1)} %bitcast.10), custom_call_target="tpu_custom_call" | custom-call | flops 1207959552 | tf_op jit(solution)/shard_map/preacts_kept/pallas_call | solution.py:266
  25.4 3.8 %fetch_down.1 = (bf16[3072,1536]{1,0:T(8,128)(2,1)S(1)}, f32[8,128]{1,0:T(8,128)S(1)}) custom-call(bf16[256,3072]{1,0:T(8,128)(2,1)S(1)} %get-tuple-element.75.refs_0_.after_ref, bf16[3072,1536]{1,0:T(8,128)(2,1)} %down_ref.1), custom_call_target="tpu_custom_call" | custom-call | bytes 18874368 | tf_op jit(solution)/shard_map/fetch_down/pallas_call | solution.py:206
  29.6 1.7 %collective-permute-start.7 = (bf16[128,384]{1,0:T(8,128)(2,1)S(1)}, bf16[128,384]{1,0:T(8,128)(2,1)S(1)}, u32[]{:S(2)}, u32[]{:S(2)}) collective-permute-start(bf16[128,384]{1,0:T(8,128)(2,1)S(1)} %act.2.refs_0_), channel_id=1, source_target_pairs={{0,4},{2,6},{4,0},{6,2},{1,5},{3,7},{5,1},{7,3},{8,12},{10,14},{12... | collective-permute-start | bytes 294920 | tf_op jit(solution)/shard_map/ppermute | solution.py:628
  31.3 2.0 %collective-permute-start.8 = (bf16[128,384]{1,0:T(8,128)(2,1)S(1)}, bf16[128,384]{1,0:T(8,128)(2,1)S(1)}, u32[]{:S(2)}, u32[]{:S(2)}) collective-permute-start(bf16[128,384]{1,0:T(8,128)(2,1)S(1)} %act.2.refs_0_), channel_id=1, source_target_pairs={{0,2},{2,0},{4,6},{6,4},{1,3},{3,1},{5,7},{7,5},{8,10},{10,8},{12,... | collective-permute-start | bytes 294920 | tf_op jit(solution)/shard_map/ppermute | solution.py:628
  33.4 1.2 %collective-permute-start.9 = (bf16[128,384]{1,0:T(8,128)(2,1)S(1)}, bf16[128,384]{1,0:T(8,128)(2,1)S(1)}, u32[]{:S(2)}, u32[]{:S(2)}) collective-permute-start(bf16[128,384]{1,0:T(8,128)(2,1)S(1)} %get-tuple-element.92), channel_id=1, source_target_pairs={{0,4},{2,6},{4,0},{6,2},{1,5},{3,7},{5,1},{7,3},{8,12},{10,14},{12... | collective-permute-start | bytes 294920 | tf_op jit(solution)/shard_map/ppermute | solution.py:628
  34.6 1.5 %collective-permute-start.12 = (bf16[128,768]{1,0:T(8,128)(2,1)S(1)}, bf16[128,768]{1,0:T(8,128)(2,1)S(1)}, u32[]{:S(2)}, u32[]{:S(2)}) collective-permute-start(bf16[128,768]{1,0:T(8,128)(2,1)S(1)} %get-tuple-element.94.left_ref.refs_0_), channel_id=1, source_target_pairs={{0,8},{8,0},{1,9},{9,1},{2,10},{10,2},{3,11},{11,3},{4,12},{12,4},... | collective-permute-start | bytes 589832 | tf_op jit(solution)/shard_map/ppermute | solution.py:624
  36.1 1.4 %collective-permute-done.7.in_ref.near_ref.refs_3_ = bf16[128,384]{1,0:T(8,128)(2,1)S(1)} collective-permute-done((bf16[128,384]{1,0:T(8,128)(2,1)S(1)}, bf16[128,384]{1,0:T(8,128)(2,1)S(1)}, u32[]{:S(2)}, u32[]{:S(2)}) %collective-permute-start.7) | collective-permute-done | bytes 98336 | tf_op jit(solution)/shard_map/ppermute | solution.py:628
  37.5 1.5 %collective-permute-start.10 = (bf16[128,384]{1,0:T(8,128)(2,1)S(1)}, bf16[128,384]{1,0:T(8,128)(2,1)S(1)}, u32[]{:S(2)}, u32[]{:S(2)}) collective-permute-start(bf16[128,384]{1,0:T(8,128)(2,1)S(1)} %relay.1), channel_id=1, source_target_pairs={{0,2},{2,0},{4,6},{6,4},{1,3},{3,1},{5,7},{7,5},{8,10},{10,8},{12,... | collective-permute-start | bytes 294920 | tf_op jit(solution)/shard_map/ppermute | solution.py:628
  40.5 1.6 %collective-permute-start.14 = (bf16[128,384]{1,0:T(8,128)(2,1)S(1)}, bf16[128,384]{1,0:T(8,128)(2,1)S(1)}, u32[]{:S(2)}, u32[]{:S(2)}) collective-permute-start(bf16[128,384]{1,0:T(8,128)(2,1)S(1)} %choose.1), channel_id=1, source_target_pairs={{0,8},{8,0},{1,9},{9,1},{2,10},{10,2},{3,11},{11,3},{4,12},{12,4},... | collective-permute-start | bytes 294920 | tf_op jit(solution)/shard_map/ppermute | solution.py:624
  42.0 2.0 %collective-permute-start.15 = (bf16[128,384]{1,0:T(8,128)(2,1)S(1)}, bf16[128,384]{1,0:T(8,128)(2,1)S(1)}, u32[]{:S(2)}, u32[]{:S(2)}) collective-permute-start(bf16[128,384]{1,0:T(8,128)(2,1)S(1)} %collective-permute-done.9.refs_4_), channel_id=1, source_target_pairs={{0,2},{2,0},{4,6},{6,4},{1,3},{3,1},{5,7},{7,5},{8,10},{10,8},{12,... | collective-permute-start | bytes 294920 | tf_op jit(solution)/shard_map/ppermute | solution.py:628
  44.1 1.6 %project.1 = (f32[64,1536]{1,0:T(8,128)S(1)}, bf16[64,1536]{1,0:T(8,128)(2,1)S(1)}, bf16[128,3072]{1,0:T(8,128)(2,1)S(1)}, f32[8,128]{1,0:T(8,128)S(1)}) custom-call(f32[8,128]{1,0:T(8,128)S(1)} %get-tuple-element.95.tick_ref, bf16[128,1536]{1,0:T(8,128)(2,1)S(1)} %join.1.here_ref, bf16[128,1536]{1,0:T(8,128)(2,1)S(1)} %collective-permute-done.13.there_ref, ...), custom_call_target="tpu_custom_call" | custom-call | bytes 1 | tf_op jit(solution)/shard_map/project/pallas_call | solution.py:501
  45.7 1.5 %collective-permute-done.15.refs_6_ = bf16[128,384]{1,0:T(8,128)(2,1)S(1)} collective-permute-done((bf16[128,384]{1,0:T(8,128)(2,1)S(1)}, bf16[128,384]{1,0:T(8,128)(2,1)S(1)}, u32[]{:S(2)}, u32[]{:S(2)}) %collective-permute-start.15) | collective-permute-done | bytes 98336 | tf_op jit(solution)/shard_map/ppermute | solution.py:628
  48.0 1.7 %collective-permute-start.18 = (bf16[64,1536]{1,0:T(8,128)(2,1)S(1)}, bf16[64,1536]{1,0:T(8,128)(2,1)S(1)}, u32[]{:S(2)}, u32[]{:S(2)}) collective-permute-start(bf16[64,1536]{1,0:T(8,128)(2,1)S(1)} %get-tuple-element.115), channel_id=1, source_target_pairs={{0,2},{2,0},{4,6},{6,4},{1,3},{3,1},{5,7},{7,5},{8,10},{10,8},{12,... | collective-permute-start | bytes 589832 | tf_op jit(solution)/shard_map/ppermute | solution.py:628
  49.7 6.8 %gram.2 = (f32[3072,3072]{1,0:T(8,128)}, f32[8,128]{1,0:T(8,128)S(1)}) custom-call(f32[8,128]{1,0:T(8,128)S(1)} %get-tuple-element.108.refs_0_, bf16[128,768]{1,0:T(8,128)(2,1)S(1)} %get-tuple-element.109.refs_1_, bf16[128,768]{1,0:T(8,128)(2,1)S(1)} %collective-permute-done.16.refs_2_, bf16[128,3072]{1,0:T(8,128)(2,1)S(1)} %get-tuple-element.111.refs_3_), custom_call_target="tpu_custom_call" | custom-call | flops 1207959552 | bytes 18874368 | tf_op jit(solution)/shard_map/gram/pallas_call | solution.py:604
  57.2 1.5 %collective-permute-start.20 = (bf16[32,1536]{1,0:T(8,128)(2,1)S(1)}, bf16[32,1536]{1,0:T(8,128)(2,1)S(1)}, u32[]{:S(2)}, u32[]{:S(2)}) collective-permute-start(bf16[32,1536]{1,0:T(8,128)(2,1)S(1)} %get-tuple-element.130), channel_id=1, source_target_pairs={{0,4},{2,6},{4,0},{6,2},{1,5},{3,7},{5,1},{7,3},{8,12},{10,14},{12... | collective-permute-start | bytes 294920 | tf_op jit(solution)/shard_map/ppermute | solution.py:628
  58.7 6.8 %gram.3 = (f32[3072,3072]{1,0:T(8,128)}, f32[8,128]{1,0:T(8,128)S(1)}) custom-call(f32[8,128]{1,0:T(8,128)S(1)} %get-tuple-element.120.refs_0_, bf16[128,768]{1,0:T(8,128)(2,1)S(1)} %get-tuple-element.121.refs_1_, bf16[128,768]{1,0:T(8,128)(2,1)S(1)} %collective-permute-done.19.refs_2_, ...), custom_call_target="tpu_custom_call", output_to_operand_aliasing={{0}: (4, {})} | custom-call | flops 1207959552 | bytes 18874368 | tf_op jit(solution)/shard_map/gram/pallas_call | solution.py:604
  65.5 1.1 %unpack.1 = bf16[128,1536]{1,0:T(8,128)(2,1)} custom-call(f32[8,128]{1,0:T(8,128)S(1)} %get-tuple-element.124.after_ref, bf16[32,128]{1,0:T(8,128)(2,1)S(1)} %get-tuple-element.125.placing_ref, f32[32,128]{1,0:T(8,128)S(1)} %get-tuple-element.126.factor_ref, f32[32,1536]{1,0:T(8,128)S(1)} %get-tuple-element.129.own_ref, ...), custom_call_target="tpu_custom_call" | custom-call | tf_op jit(solution)/shard_map/unpack/pallas_call | solution.py:551
  (39 shorter events, 5.9 us)
Async XLA Ops:
  1.9 12.7 %collective-permute-start.2 = (bf16[32,1536]{1,0:T(8,128)(2,1)S(1)}, bf16[32,1536]{1,0:T(8,128)(2,1)S(1)}, u32[]{:S(2)}, u32[]{:S(2)}) collective-permute-start(bf16[32,1536]{1,0:T(8,128)(2,1)S(1)} %get-tuple-element.67.after_ref.refs_0_), channel_id=1, source_target_pairs={{0,6},{2,4},{4,2},{6,0},{1,7},{3,5},{5,3},{7,1},{8,14},{10,12},{12... | collective-permute-start | bytes 294920 | tf_op jit(solution)/shard_map/ppermute | solution.py:628
  7.0 8.3 %collective-permute-start.1 = (bf16[32,1536]{1,0:T(8,128)(2,1)S(1)}, bf16[32,1536]{1,0:T(8,128)(2,1)S(1)}, u32[]{:S(2)}, u32[]{:S(2)}) collective-permute-start(bf16[32,1536]{1,0:T(8,128)(2,1)S(1)} %get-tuple-element.67.after_ref.refs_0_), channel_id=1, source_target_pairs={{0,4},{2,6},{4,0},{6,2},{1,5},{3,7},{5,1},{7,3},{8,12},{10,14},{12... | collective-permute-start | bytes 294920 | tf_op jit(solution)/shard_map/ppermute | solution.py:628
  7.0 8.3 %collective-permute-start = (bf16[32,1536]{1,0:T(8,128)(2,1)S(1)}, bf16[32,1536]{1,0:T(8,128)(2,1)S(1)}, u32[]{:S(2)}, u32[]{:S(2)}) collective-permute-start(bf16[32,1536]{1,0:T(8,128)(2,1)S(1)} %get-tuple-element.67.after_ref.refs_0_), channel_id=1, source_target_pairs={{0,2},{2,0},{4,6},{6,4},{1,3},{3,1},{5,7},{7,5},{8,10},{10,8},{12,... | collective-permute-start | bytes 294920 | tf_op jit(solution)/shard_map/ppermute | solution.py:628
  18.1 3.5 %collective-permute-start.3 = (f32[256,768]{1,0:T(8,128)S(1)}, f32[256,768]{1,0:T(8,128)S(1)}, u32[]{:S(2)}, u32[]{:S(2)}) collective-permute-start(f32[256,768]{1,0:T(8,128)S(1)} %get-tuple-element.71), channel_id=1, source_target_pairs={{0,1},{1,0},{2,3},{3,2},{4,5},{5,4},{6,7},{7,6},{8,9},{9,8},{10,11... | collective-permute-start | bytes 2359304 | tf_op jit(solution)/shard_map/ppermute | solution.py:624
  19.6 5.1 %collective-permute-start.4 = (f32[256,768]{1,0:T(8,128)S(1)}, f32[256,768]{1,0:T(8,128)S(1)}, u32[]{:S(2)}, u32[]{:S(2)}) collective-permute-start(f32[256,768]{1,0:T(8,128)S(1)} %preacts_sent.3), channel_id=1, source_target_pairs={{0,1},{1,0},{2,3},{3,2},{4,5},{5,4},{6,7},{7,6},{8,9},{9,8},{10,11... | collective-permute-start | bytes 2359304 | tf_op jit(solution)/shard_map/ppermute | solution.py:624
  21.7 7.8 %collective-permute-start.5 = (bf16[256,384]{1,0:T(8,128)(2,1)S(1)}, bf16[256,384]{1,0:T(8,128)(2,1)S(1)}, u32[]{:S(2)}, u32[]{:S(2)}) collective-permute-start(bf16[256,384]{1,0:T(8,128)(2,1)S(1)} %get-tuple-element.77), channel_id=1, source_target_pairs={{0,8},{8,0},{1,9},{9,1},{2,10},{10,2},{3,11},{11,3},{4,12},{12,4},... | collective-permute-start | bytes 589832 | tf_op jit(solution)/shard_map/ppermute | solution.py:624
  24.8 8.6 %collective-permute-start.6 = (bf16[256,384]{1,0:T(8,128)(2,1)S(1)}, bf16[256,384]{1,0:T(8,128)(2,1)S(1)}, u32[]{:S(2)}, u32[]{:S(2)}) collective-permute-start(bf16[256,384]{1,0:T(8,128)(2,1)S(1)} %get-tuple-element.79), channel_id=1, source_target_pairs={{0,8},{8,0},{1,9},{9,1},{2,10},{10,2},{3,11},{11,3},{4,12},{12,4},... | collective-permute-start | bytes 589832 | tf_op jit(solution)/shard_map/ppermute | solution.py:624
  29.6 7.9 %collective-permute-start.7 = (bf16[128,384]{1,0:T(8,128)(2,1)S(1)}, bf16[128,384]{1,0:T(8,128)(2,1)S(1)}, u32[]{:S(2)}, u32[]{:S(2)}) collective-permute-start(bf16[128,384]{1,0:T(8,128)(2,1)S(1)} %act.2.refs_0_), channel_id=1, source_target_pairs={{0,4},{2,6},{4,0},{6,2},{1,5},{3,7},{5,1},{7,3},{8,12},{10,14},{12... | collective-permute-start | bytes 294920 | tf_op jit(solution)/shard_map/ppermute | solution.py:628
  31.3 6.2 %collective-permute-start.8 = (bf16[128,384]{1,0:T(8,128)(2,1)S(1)}, bf16[128,384]{1,0:T(8,128)(2,1)S(1)}, u32[]{:S(2)}, u32[]{:S(2)}) collective-permute-start(bf16[128,384]{1,0:T(8,128)(2,1)S(1)} %act.2.refs_0_), channel_id=1, source_target_pairs={{0,2},{2,0},{4,6},{6,4},{1,3},{3,1},{5,7},{7,5},{8,10},{10,8},{12,... | collective-permute-start | bytes 294920 | tf_op jit(solution)/shard_map/ppermute | solution.py:628
  33.4 8.6 %collective-permute-start.9 = (bf16[128,384]{1,0:T(8,128)(2,1)S(1)}, bf16[128,384]{1,0:T(8,128)(2,1)S(1)}, u32[]{:S(2)}, u32[]{:S(2)}) collective-permute-start(bf16[128,384]{1,0:T(8,128)(2,1)S(1)} %get-tuple-element.92), channel_id=1, source_target_pairs={{0,4},{2,6},{4,0},{6,2},{1,5},{3,7},{5,1},{7,3},{8,12},{10,14},{12... | collective-permute-start | bytes 294920 | tf_op jit(solution)/shard_map/ppermute | solution.py:628
  34.6 5.7 %collective-permute-start.12 = (bf16[128,768]{1,0:T(8,128)(2,1)S(1)}, bf16[128,768]{1,0:T(8,128)(2,1)S(1)}, u32[]{:S(2)}, u32[]{:S(2)}) collective-permute-start(bf16[128,768]{1,0:T(8,128)(2,1)S(1)} %get-tuple-element.94.left_ref.refs_0_), channel_id=1, source_target_pairs={{0,8},{8,0},{1,9},{9,1},{2,10},{10,2},{3,11},{11,3},{4,12},{12,4},... | collective-permute-start | bytes 589832 | tf_op jit(solution)/shard_map/ppermute | solution.py:624
  37.5 6.6 %collective-permute-start.10 = (bf16[128,384]{1,0:T(8,128)(2,1)S(1)}, bf16[128,384]{1,0:T(8,128)(2,1)S(1)}, u32[]{:S(2)}, u32[]{:S(2)}) collective-permute-start(bf16[128,384]{1,0:T(8,128)(2,1)S(1)} %relay.1), channel_id=1, source_target_pairs={{0,2},{2,0},{4,6},{6,4},{1,3},{3,1},{5,7},{7,5},{8,10},{10,8},{12,... | collective-permute-start | bytes 294920 | tf_op jit(solution)/shard_map/ppermute | solution.py:628
  39.0 5.0 %collective-permute-start.11 = (bf16[128,384]{1,0:T(8,128)(2,1)S(1)}, bf16[128,384]{1,0:T(8,128)(2,1)S(1)}, u32[]{:S(2)}, u32[]{:S(2)}) collective-permute-start(bf16[128,384]{1,0:T(8,128)(2,1)S(1)} %get-tuple-element.92), channel_id=1, source_target_pairs={{0,2},{2,0},{4,6},{6,4},{1,3},{3,1},{5,7},{7,5},{8,10},{10,8},{12,... | collective-permute-start | bytes 294920 | tf_op jit(solution)/shard_map/ppermute | solution.py:628
  40.4 3.7 %collective-permute-start.13 = (bf16[128,1536]{1,0:T(8,128)(2,1)S(1)}, bf16[128,1536]{1,0:T(8,128)(2,1)S(1)}, u32[]{:S(2)}, u32[]{:S(2)}) collective-permute-start(bf16[128,1536]{1,0:T(8,128)(2,1)S(1)} %join.1.here_ref), channel_id=1, source_target_pairs={{0,1},{1,0},{2,3},{3,2},{4,5},{5,4},{6,7},{7,6},{8,9},{9,8},{10,11... | collective-permute-start | bytes 1179656 | tf_op jit(solution)/shard_map/ppermute | solution.py:624
  40.5 5.2 %collective-permute-start.14 = (bf16[128,384]{1,0:T(8,128)(2,1)S(1)}, bf16[128,384]{1,0:T(8,128)(2,1)S(1)}, u32[]{:S(2)}, u32[]{:S(2)}) collective-permute-start(bf16[128,384]{1,0:T(8,128)(2,1)S(1)} %choose.1), channel_id=1, source_target_pairs={{0,8},{8,0},{1,9},{9,1},{2,10},{10,2},{3,11},{11,3},{4,12},{12,4},... | collective-permute-start | bytes 294920 | tf_op jit(solution)/shard_map/ppermute | solution.py:624
  42.0 5.2 %collective-permute-start.15 = (bf16[128,384]{1,0:T(8,128)(2,1)S(1)}, bf16[128,384]{1,0:T(8,128)(2,1)S(1)}, u32[]{:S(2)}, u32[]{:S(2)}) collective-permute-start(bf16[128,384]{1,0:T(8,128)(2,1)S(1)} %collective-permute-done.9.refs_4_), channel_id=1, source_target_pairs={{0,2},{2,0},{4,6},{6,4},{1,3},{3,1},{5,7},{7,5},{8,10},{10,8},{12,... | collective-permute-start | bytes 294920 | tf_op jit(solution)/shard_map/ppermute | solution.py:628
  47.3 2.4 %collective-permute-start.16 = (bf16[128,768]{1,0:T(8,128)(2,1)S(1)}, bf16[128,768]{1,0:T(8,128)(2,1)S(1)}, u32[]{:S(2)}, u32[]{:S(2)}) collective-permute-start(bf16[128,768]{1,0:T(8,128)(2,1)S(1)} %get-tuple-element.107), channel_id=1, source_target_pairs={{0,1},{1,0},{2,3},{3,2},{4,5},{5,4},{6,7},{7,6},{8,9},{9,8},{10,11... | collective-permute-start | bytes 589832 | tf_op jit(solution)/shard_map/ppermute | solution.py:624
  47.4 9.4 %collective-permute-start.17 = (bf16[128,1152]{1,0:T(8,128)(2,1)S(1)}, bf16[128,1152]{1,0:T(8,128)(2,1)S(1)}, u32[]{:S(2)}, u32[]{:S(2)}) collective-permute-start(bf16[128,1152]{1,0:T(8,128)(2,1)S(1)} %get-tuple-element.113), channel_id=1, source_target_pairs={{0,8},{8,0},{1,9},{9,1},{2,10},{10,2},{3,11},{11,3},{4,12},{12,4},... | collective-permute-start | bytes 884744 | tf_op jit(solution)/shard_map/ppermute | solution.py:624
  48.0 9.2 %collective-permute-start.18 = (bf16[64,1536]{1,0:T(8,128)(2,1)S(1)}, bf16[64,1536]{1,0:T(8,128)(2,1)S(1)}, u32[]{:S(2)}, u32[]{:S(2)}) collective-permute-start(bf16[64,1536]{1,0:T(8,128)(2,1)S(1)} %get-tuple-element.115), channel_id=1, source_target_pairs={{0,2},{2,0},{4,6},{6,4},{1,3},{3,1},{5,7},{7,5},{8,10},{10,8},{12,... | collective-permute-start | bytes 589832 | tf_op jit(solution)/shard_map/ppermute | solution.py:628
  57.0 1.7 %collective-permute-start.19 = (bf16[128,768]{1,0:T(8,128)(2,1)S(1)}, bf16[128,768]{1,0:T(8,128)(2,1)S(1)}, u32[]{:S(2)}, u32[]{:S(2)}) collective-permute-start(bf16[128,768]{1,0:T(8,128)(2,1)S(1)} %get-tuple-element.119), channel_id=1, source_target_pairs={{0,1},{1,0},{2,3},{3,2},{4,5},{5,4},{6,7},{7,6},{8,9},{9,8},{10,11... | collective-permute-start | bytes 589832 | tf_op jit(solution)/shard_map/ppermute | solution.py:624
  57.2 8.4 %collective-permute-start.20 = (bf16[32,1536]{1,0:T(8,128)(2,1)S(1)}, bf16[32,1536]{1,0:T(8,128)(2,1)S(1)}, u32[]{:S(2)}, u32[]{:S(2)}) collective-permute-start(bf16[32,1536]{1,0:T(8,128)(2,1)S(1)} %get-tuple-element.130), channel_id=1, source_target_pairs={{0,4},{2,6},{4,0},{6,2},{1,5},{3,7},{5,1},{7,3},{8,12},{10,14},{12... | collective-permute-start | bytes 294920 | tf_op jit(solution)/shard_map/ppermute | solution.py:628

commit v16 on v15

--- a/solution.py
+++ b/solution.py
@@ -221,17 +221,16 @@
     here = lax.axis_index("col")
     cut = widen_ref.shape[0]
     parts = depth // cut
-    stacked = jnp.concatenate(
-        [x_ref[:, cut * k : cut * (k + 1)] for x_ref in x_refs for k in range(parts)], axis=0
-    )
-    spaced = jnp.dot(stacked, widen_ref[...], preferred_element_type=F32).astype(BF16)
-    for slot in range(len(x_refs)):
+    for slot, x_ref in enumerate(x_refs):
+        stacked = jnp.concatenate(
+            [x_ref[:, cut * k : cut * (k + 1)] for k in range(parts)], axis=0
+        )
+        spaced = jnp.dot(stacked, widen_ref[...], preferred_element_type=F32).astype(BF16)
         for h in range(2):
             at = pl.multiple_of(h * rows + (here ^ slot) * slots, slots)
             for k in range(parts):
-                row = slots * (slot * parts + k)
                 wide_ref[pl.ds(at, slots), 2 * cut * k : 2 * cut * (k + 1)] = spaced[
-                    row : row + slots, 2 * cut * h : 2 * cut * (h + 1)
+                    slots * k : slots * (k + 1), 2 * cut * h : 2 * cut * (h + 1)
                 ]
 
 

time: 66.7 us -> 65.9 us (0.988)
  Pallas kernels: 36.1 us -> 35.3 us
    pallas_call x4, Pallas kernels: 7.04 us -> 6.26 us  [preacts_of(): pl.pallas_call(functools.partial(preact_kernel, first, row_flip, chunk, c...]
  transfers between devices with their start and end apart: 21 -> 21, of which waited for: 6 -> 6; matrix products, arithmetic and copies ran while one was open for 0% -> 0% of each run, Pallas kernels for 46% -> 47%
where the time goes in v16:
time: 65.9 us; the launch traced here: 65.8 us
  Pallas kernels  35.3 us (54%)
  starting transfers between devices  24.7 us (37%)
  waiting for transfers between devices  4.9 us (7%)
  between operations  0.86 us (1%)
    ppermute x11, starting transfers between devices, across(): return lax.ppermute(value, 'col', [(i, i ^ slot) for i in range(4)])  18.1 us
    pallas_call x2, Pallas kernels, gram_piece(): pl.pallas_call(functools.partial(gram_kernel, 2.0 / rows, flips), in_spec...  13.6 us
    pallas_call x1, Pallas kernels, regroup(): pl.pallas_call(regroup_kernel, in_specs=[ANY, HBM], out_specs=[VMEM] * 2,...  6.97 us
    ppermute x10, starting transfers between devices, swap(): return lax.ppermute(value, axis, [(0, 1), (1, 0)])  6.61 us
    pallas_call x4, Pallas kernels, preacts_of(): pl.pallas_call(functools.partial(preact_kernel, first, row_flip, chunk, c...  6.26 us
    pallas_call x1, Pallas kernels, fetch(): pl.pallas_call(fetch_kernel, in_specs=[ANY, HBM], out_specs=[VMEM, VMEM],...  3.8 us
    ppermute x11, waiting for transfers between devices, across(): return lax.ppermute(value, 'col', [(i, i ^ slot) for i in range(4)])  3.62 us
    pallas_call x1, Pallas kernels, project(): pl.pallas_call(project_kernel, in_specs=[ANY] + [VMEM] * 3, out_specs=[VM...  1.61 us
  transfers between devices with their start and end apart: 21, of which 6 were waited for; matrix products, arithmetic and copies ran while one was open for 0% of the time, Pallas kernels for 47%

profile of v16, /device:TPU:0, one launch (start us, length us, event | category | flops | bytes accessed | tf_op | source)
XLA Modules:
  0.0 65.8 jit_solution(5107104814994210802)
XLA Ops:
  0.6 1.3 %pack.1 = (bf16[32,1536]{1,0:T(8,128)(2,1)S(1)}, bf16[32,128]{1,0:T(8,128)(2,1)S(1)}, f32[32,128]{1,0:T(8,128)S(1)}) custom-call(bf16[128,1536]{1,0:T(8,128)(2,1)} %tokens_ref.1, s32[2,128]{1,0:T(2,128)} %bitcast.12, s32[1,128]{1,0:T(1,128)} %bitcast.14, f32[2,128]{1,0:T(2,128)} %bitcast.13), custom_call_target="tpu_custom_call" | custom-call | tf_op jit(solution)/shard_map/pack/pallas_call | solution.py:137
  1.9 5.1 %collective-permute-start.2 = (bf16[32,1536]{1,0:T(8,128)(2,1)S(1)}, bf16[32,1536]{1,0:T(8,128)(2,1)S(1)}, u32[]{:S(2)}, u32[]{:S(2)}) collective-permute-start(bf16[32,1536]{1,0:T(8,128)(2,1)S(1)} %get-tuple-element.67.after_ref.refs_0_), channel_id=1, source_target_pairs={{0,6},{2,4},{4,2},{6,0},{1,7},{3,5},{5,3},{7,1},{8,14},{10,12},{12... | collective-permute-start | bytes 294920 | tf_op jit(solution)/shard_map/ppermute | solution.py:627
  7.7 7.0 %regroup.1 = (bf16[24,1536,2,128]{3,2,1,0:T(2,128)(2,1)S(1)}, bf16[256,1024]{1,0:T(8,128)(2,1)S(1)}) custom-call(bf16[32,1536]{1,0:T(8,128)(2,1)S(1)} %get-tuple-element.67.after_ref.refs_0_, bf16[1536,24,2,128]{3,2,1,0:T(2,128)(2,1)} %bitcast.11), custom_call_target="tpu_custom_call" | custom-call | bytes 37748736 | tf_op jit(solution)/shard_map/regroup/pallas_call | solution.py:172
  15.3 2.0 %preacts_sent.2 = (f32[256,768]{1,0:T(8,128)S(1)}, bf16[256,3072]{1,0:T(8,128)(2,1)S(1)}) custom-call(bf16[32,1536]{1,0:T(8,128)(2,1)S(1)} %get-tuple-element.67.after_ref.refs_0_, bf16[32,1536]{1,0:T(8,128)(2,1)S(1)} %collective-permute-done.refs_1_, bf16[32,1536]{1,0:T(8,128)(2,1)S(1)} %collective-permute-done.1.refs_2_, ...), custom_call_target="tpu_custom_call" | custom-call | flops 1207959552 | tf_op jit(solution)/shard_map/preacts_sent/pallas_call | solution.py:265
  17.4 1.4 %preacts_sent.3 = f32[256,768]{1,0:T(8,128)S(1)} custom-call(bf16[256,3072]{1,0:T(8,128)(2,1)S(1)} %get-tuple-element.75.refs_0_.after_ref, bf16[24,3072,128]{2,1,0:T(8,128)(2,1)S(1)} %bitcast.8), custom_call_target="tpu_custom_call" | custom-call | flops 1207959552 | tf_op jit(solution)/shard_map/preacts_sent/pallas_call | solution.py:265
  19.3 1.4 %preacts_kept.2.kept_ref = f32[256,768]{1,0:T(8,128)S(1)} custom-call(bf16[256,3072]{1,0:T(8,128)(2,1)S(1)} %get-tuple-element.75.refs_0_.after_ref, bf16[24,3072,128]{2,1,0:T(8,128)(2,1)S(1)} %bitcast.9), custom_call_target="tpu_custom_call" | custom-call | flops 1207959552 | tf_op jit(solution)/shard_map/preacts_kept/pallas_call | solution.py:265
  20.9 1.6 %collective-permute-start.5 = (bf16[256,384]{1,0:T(8,128)(2,1)S(1)}, bf16[256,384]{1,0:T(8,128)(2,1)S(1)}, u32[]{:S(2)}, u32[]{:S(2)}) collective-permute-start(bf16[256,384]{1,0:T(8,128)(2,1)S(1)} %get-tuple-element.77), channel_id=1, source_target_pairs={{0,8},{8,0},{1,9},{9,1},{2,10},{10,2},{3,11},{11,3},{4,12},{12,4},... | collective-permute-start | bytes 589832 | tf_op jit(solution)/shard_map/ppermute | solution.py:623
  22.5 1.4 %preacts_kept.3.kept_ref = f32[256,768]{1,0:T(8,128)S(1)} custom-call(bf16[256,3072]{1,0:T(8,128)(2,1)S(1)} %get-tuple-element.75.refs_0_.after_ref, bf16[24,3072,128]{2,1,0:T(8,128)(2,1)S(1)} %bitcast.10), custom_call_target="tpu_custom_call" | custom-call | flops 1207959552 | tf_op jit(solution)/shard_map/preacts_kept/pallas_call | solution.py:265
  24.6 3.8 %fetch_down.1 = (bf16[3072,1536]{1,0:T(8,128)(2,1)S(1)}, f32[8,128]{1,0:T(8,128)S(1)}) custom-call(bf16[256,3072]{1,0:T(8,128)(2,1)S(1)} %get-tuple-element.75.refs_0_.after_ref, bf16[3072,1536]{1,0:T(8,128)(2,1)} %down_ref.1), custom_call_target="tpu_custom_call" | custom-call | bytes 18874368 | tf_op jit(solution)/shard_map/fetch_down/pallas_call | solution.py:206
  28.8 1.7 %collective-permute-start.7 = (bf16[128,384]{1,0:T(8,128)(2,1)S(1)}, bf16[128,384]{1,0:T(8,128)(2,1)S(1)}, u32[]{:S(2)}, u32[]{:S(2)}) collective-permute-start(bf16[128,384]{1,0:T(8,128)(2,1)S(1)} %act.2.refs_0_), channel_id=1, source_target_pairs={{0,4},{2,6},{4,0},{6,2},{1,5},{3,7},{5,1},{7,3},{8,12},{10,14},{12... | collective-permute-start | bytes 294920 | tf_op jit(solution)/shard_map/ppermute | solution.py:627
  30.5 2.0 %collective-permute-start.8 = (bf16[128,384]{1,0:T(8,128)(2,1)S(1)}, bf16[128,384]{1,0:T(8,128)(2,1)S(1)}, u32[]{:S(2)}, u32[]{:S(2)}) collective-permute-start(bf16[128,384]{1,0:T(8,128)(2,1)S(1)} %act.2.refs_0_), channel_id=1, source_target_pairs={{0,2},{2,0},{4,6},{6,4},{1,3},{3,1},{5,7},{7,5},{8,10},{10,8},{12,... | collective-permute-start | bytes 294920 | tf_op jit(solution)/shard_map/ppermute | solution.py:627
  32.6 1.2 %collective-permute-start.9 = (bf16[128,384]{1,0:T(8,128)(2,1)S(1)}, bf16[128,384]{1,0:T(8,128)(2,1)S(1)}, u32[]{:S(2)}, u32[]{:S(2)}) collective-permute-start(bf16[128,384]{1,0:T(8,128)(2,1)S(1)} %get-tuple-element.92), channel_id=1, source_target_pairs={{0,4},{2,6},{4,0},{6,2},{1,5},{3,7},{5,1},{7,3},{8,12},{10,14},{12... | collective-permute-start | bytes 294920 | tf_op jit(solution)/shard_map/ppermute | solution.py:627
  33.8 1.5 %collective-permute-start.12 = (bf16[128,768]{1,0:T(8,128)(2,1)S(1)}, bf16[128,768]{1,0:T(8,128)(2,1)S(1)}, u32[]{:S(2)}, u32[]{:S(2)}) collective-permute-start(bf16[128,768]{1,0:T(8,128)(2,1)S(1)} %get-tuple-element.94.left_ref.refs_0_), channel_id=1, source_target_pairs={{0,8},{8,0},{1,9},{9,1},{2,10},{10,2},{3,11},{11,3},{4,12},{12,4},... | collective-permute-start | bytes 589832 | tf_op jit(solution)/shard_map/ppermute | solution.py:623
  35.3 1.5 %collective-permute-done.7.in_ref.near_ref.refs_3_ = bf16[128,384]{1,0:T(8,128)(2,1)S(1)} collective-permute-done((bf16[128,384]{1,0:T(8,128)(2,1)S(1)}, bf16[128,384]{1,0:T(8,128)(2,1)S(1)}, u32[]{:S(2)}, u32[]{:S(2)}) %collective-permute-start.7) | collective-permute-done | bytes 98336 | tf_op jit(solution)/shard_map/ppermute | solution.py:627
  36.8 1.4 %collective-permute-start.10 = (bf16[128,384]{1,0:T(8,128)(2,1)S(1)}, bf16[128,384]{1,0:T(8,128)(2,1)S(1)}, u32[]{:S(2)}, u32[]{:S(2)}) collective-permute-start(bf16[128,384]{1,0:T(8,128)(2,1)S(1)} %relay.1), channel_id=1, source_target_pairs={{0,2},{2,0},{4,6},{6,4},{1,3},{3,1},{5,7},{7,5},{8,10},{10,8},{12,... | collective-permute-start | bytes 294920 | tf_op jit(solution)/shard_map/ppermute | solution.py:627
  39.7 1.5 %collective-permute-start.14 = (bf16[128,384]{1,0:T(8,128)(2,1)S(1)}, bf16[128,384]{1,0:T(8,128)(2,1)S(1)}, u32[]{:S(2)}, u32[]{:S(2)}) collective-permute-start(bf16[128,384]{1,0:T(8,128)(2,1)S(1)} %choose.1), channel_id=1, source_target_pairs={{0,8},{8,0},{1,9},{9,1},{2,10},{10,2},{3,11},{11,3},{4,12},{12,4},... | collective-permute-start | bytes 294920 | tf_op jit(solution)/shard_map/ppermute | solution.py:623
  41.2 2.0 %collective-permute-start.15 = (bf16[128,384]{1,0:T(8,128)(2,1)S(1)}, bf16[128,384]{1,0:T(8,128)(2,1)S(1)}, u32[]{:S(2)}, u32[]{:S(2)}) collective-permute-start(bf16[128,384]{1,0:T(8,128)(2,1)S(1)} %collective-permute-done.9.refs_4_), channel_id=1, source_target_pairs={{0,2},{2,0},{4,6},{6,4},{1,3},{3,1},{5,7},{7,5},{8,10},{10,8},{12,... | collective-permute-start | bytes 294920 | tf_op jit(solution)/shard_map/ppermute | solution.py:627
  43.3 1.6 %project.1 = (f32[64,1536]{1,0:T(8,128)S(1)}, bf16[64,1536]{1,0:T(8,128)(2,1)S(1)}, bf16[128,3072]{1,0:T(8,128)(2,1)S(1)}, f32[8,128]{1,0:T(8,128)S(1)}) custom-call(f32[8,128]{1,0:T(8,128)S(1)} %get-tuple-element.95.tick_ref, bf16[128,1536]{1,0:T(8,128)(2,1)S(1)} %join.1.here_ref, bf16[128,1536]{1,0:T(8,128)(2,1)S(1)} %collective-permute-done.13.there_ref, ...), custom_call_target="tpu_custom_call" | custom-call | bytes 1 | tf_op jit(solution)/shard_map/project/pallas_call | solution.py:500
  44.9 1.5 %collective-permute-done.15.refs_6_ = bf16[128,384]{1,0:T(8,128)(2,1)S(1)} collective-permute-done((bf16[128,384]{1,0:T(8,128)(2,1)S(1)}, bf16[128,384]{1,0:T(8,128)(2,1)S(1)}, u32[]{:S(2)}, u32[]{:S(2)}) %collective-permute-start.15) | collective-permute-done | bytes 98336 | tf_op jit(solution)/shard_map/ppermute | solution.py:627
  47.2 1.7 %collective-permute-start.18 = (bf16[64,1536]{1,0:T(8,128)(2,1)S(1)}, bf16[64,1536]{1,0:T(8,128)(2,1)S(1)}, u32[]{:S(2)}, u32[]{:S(2)}) collective-permute-start(bf16[64,1536]{1,0:T(8,128)(2,1)S(1)} %get-tuple-element.115), channel_id=1, source_target_pairs={{0,2},{2,0},{4,6},{6,4},{1,3},{3,1},{5,7},{7,5},{8,10},{10,8},{12,... | collective-permute-start | bytes 589832 | tf_op jit(solution)/shard_map/ppermute | solution.py:627
  48.9 6.8 %gram.2 = (f32[3072,3072]{1,0:T(8,128)}, f32[8,128]{1,0:T(8,128)S(1)}) custom-call(f32[8,128]{1,0:T(8,128)S(1)} %get-tuple-element.108.refs_0_, bf16[128,768]{1,0:T(8,128)(2,1)S(1)} %get-tuple-element.109.refs_1_, bf16[128,768]{1,0:T(8,128)(2,1)S(1)} %collective-permute-done.16.refs_2_, bf16[128,3072]{1,0:T(8,128)(2,1)S(1)} %get-tuple-element.111.refs_3_), custom_call_target="tpu_custom_call" | custom-call | flops 1207959552 | bytes 18874368 | tf_op jit(solution)/shard_map/gram/pallas_call | solution.py:603
  56.4 1.5 %collective-permute-start.20 = (bf16[32,1536]{1,0:T(8,128)(2,1)S(1)}, bf16[32,1536]{1,0:T(8,128)(2,1)S(1)}, u32[]{:S(2)}, u32[]{:S(2)}) collective-permute-start(bf16[32,1536]{1,0:T(8,128)(2,1)S(1)} %get-tuple-element.130), channel_id=1, source_target_pairs={{0,4},{2,6},{4,0},{6,2},{1,5},{3,7},{5,1},{7,3},{8,12},{10,14},{12... | collective-permute-start | bytes 294920 | tf_op jit(solution)/shard_map/ppermute | solution.py:627
  57.9 6.8 %gram.3 = (f32[3072,3072]{1,0:T(8,128)}, f32[8,128]{1,0:T(8,128)S(1)}) custom-call(f32[8,128]{1,0:T(8,128)S(1)} %get-tuple-element.120.refs_0_, bf16[128,768]{1,0:T(8,128)(2,1)S(1)} %get-tuple-element.121.refs_1_, bf16[128,768]{1,0:T(8,128)(2,1)S(1)} %collective-permute-done.19.refs_2_, ...), custom_call_target="tpu_custom_call", output_to_operand_aliasing={{0}: (4, {})} | custom-call | flops 1207959552 | bytes 18874368 | tf_op jit(solution)/shard_map/gram/pallas_call | solution.py:603
  64.7 1.0 %unpack.1 = bf16[128,1536]{1,0:T(8,128)(2,1)} custom-call(f32[8,128]{1,0:T(8,128)S(1)} %get-tuple-element.124.after_ref, bf16[32,128]{1,0:T(8,128)(2,1)S(1)} %get-tuple-element.125.placing_ref, f32[32,128]{1,0:T(8,128)S(1)} %get-tuple-element.126.factor_ref, f32[32,1536]{1,0:T(8,128)S(1)} %get-tuple-element.129.own_ref, ...), custom_call_target="tpu_custom_call" | custom-call | tf_op jit(solution)/shard_map/unpack/pallas_call | solution.py:550
  (39 shorter events, 6.0 us)
Async XLA Ops:
  1.9 12.7 %collective-permute-start.2 = (bf16[32,1536]{1,0:T(8,128)(2,1)S(1)}, bf16[32,1536]{1,0:T(8,128)(2,1)S(1)}, u32[]{:S(2)}, u32[]{:S(2)}) collective-permute-start(bf16[32,1536]{1,0:T(8,128)(2,1)S(1)} %get-tuple-element.67.after_ref.refs_0_), channel_id=1, source_target_pairs={{0,6},{2,4},{4,2},{6,0},{1,7},{3,5},{5,3},{7,1},{8,14},{10,12},{12... | collective-permute-start | bytes 294920 | tf_op jit(solution)/shard_map/ppermute | solution.py:627
  7.0 8.3 %collective-permute-start.1 = (bf16[32,1536]{1,0:T(8,128)(2,1)S(1)}, bf16[32,1536]{1,0:T(8,128)(2,1)S(1)}, u32[]{:S(2)}, u32[]{:S(2)}) collective-permute-start(bf16[32,1536]{1,0:T(8,128)(2,1)S(1)} %get-tuple-element.67.after_ref.refs_0_), channel_id=1, source_target_pairs={{0,4},{2,6},{4,0},{6,2},{1,5},{3,7},{5,1},{7,3},{8,12},{10,14},{12... | collective-permute-start | bytes 294920 | tf_op jit(solution)/shard_map/ppermute | solution.py:627
  7.0 8.3 %collective-permute-start = (bf16[32,1536]{1,0:T(8,128)(2,1)S(1)}, bf16[32,1536]{1,0:T(8,128)(2,1)S(1)}, u32[]{:S(2)}, u32[]{:S(2)}) collective-permute-start(bf16[32,1536]{1,0:T(8,128)(2,1)S(1)} %get-tuple-element.67.after_ref.refs_0_), channel_id=1, source_target_pairs={{0,2},{2,0},{4,6},{6,4},{1,3},{3,1},{5,7},{7,5},{8,10},{10,8},{12,... | collective-permute-start | bytes 294920 | tf_op jit(solution)/shard_map/ppermute | solution.py:627
  17.3 3.5 %collective-permute-start.3 = (f32[256,768]{1,0:T(8,128)S(1)}, f32[256,768]{1,0:T(8,128)S(1)}, u32[]{:S(2)}, u32[]{:S(2)}) collective-permute-start(f32[256,768]{1,0:T(8,128)S(1)} %get-tuple-element.71), channel_id=1, source_target_pairs={{0,1},{1,0},{2,3},{3,2},{4,5},{5,4},{6,7},{7,6},{8,9},{9,8},{10,11... | collective-permute-start | bytes 2359304 | tf_op jit(solution)/shard_map/ppermute | solution.py:623
  18.8 5.1 %collective-permute-start.4 = (f32[256,768]{1,0:T(8,128)S(1)}, f32[256,768]{1,0:T(8,128)S(1)}, u32[]{:S(2)}, u32[]{:S(2)}) collective-permute-start(f32[256,768]{1,0:T(8,128)S(1)} %preacts_sent.3), channel_id=1, source_target_pairs={{0,1},{1,0},{2,3},{3,2},{4,5},{5,4},{6,7},{7,6},{8,9},{9,8},{10,11... | collective-permute-start | bytes 2359304 | tf_op jit(solution)/shard_map/ppermute | solution.py:623
  20.9 7.8 %collective-permute-start.5 = (bf16[256,384]{1,0:T(8,128)(2,1)S(1)}, bf16[256,384]{1,0:T(8,128)(2,1)S(1)}, u32[]{:S(2)}, u32[]{:S(2)}) collective-permute-start(bf16[256,384]{1,0:T(8,128)(2,1)S(1)} %get-tuple-element.77), channel_id=1, source_target_pairs={{0,8},{8,0},{1,9},{9,1},{2,10},{10,2},{3,11},{11,3},{4,12},{12,4},... | collective-permute-start | bytes 589832 | tf_op jit(solution)/shard_map/ppermute | solution.py:623
  24.0 8.6 %collective-permute-start.6 = (bf16[256,384]{1,0:T(8,128)(2,1)S(1)}, bf16[256,384]{1,0:T(8,128)(2,1)S(1)}, u32[]{:S(2)}, u32[]{:S(2)}) collective-permute-start(bf16[256,384]{1,0:T(8,128)(2,1)S(1)} %get-tuple-element.79), channel_id=1, source_target_pairs={{0,8},{8,0},{1,9},{9,1},{2,10},{10,2},{3,11},{11,3},{4,12},{12,4},... | collective-permute-start | bytes 589832 | tf_op jit(solution)/shard_map/ppermute | solution.py:623
  28.8 8.0 %collective-permute-start.7 = (bf16[128,384]{1,0:T(8,128)(2,1)S(1)}, bf16[128,384]{1,0:T(8,128)(2,1)S(1)}, u32[]{:S(2)}, u32[]{:S(2)}) collective-permute-start(bf16[128,384]{1,0:T(8,128)(2,1)S(1)} %act.2.refs_0_), channel_id=1, source_target_pairs={{0,4},{2,6},{4,0},{6,2},{1,5},{3,7},{5,1},{7,3},{8,12},{10,14},{12... | collective-permute-start | bytes 294920 | tf_op jit(solution)/shard_map/ppermute | solution.py:627
  30.5 6.3 %collective-permute-start.8 = (bf16[128,384]{1,0:T(8,128)(2,1)S(1)}, bf16[128,384]{1,0:T(8,128)(2,1)S(1)}, u32[]{:S(2)}, u32[]{:S(2)}) collective-permute-start(bf16[128,384]{1,0:T(8,128)(2,1)S(1)} %act.2.refs_0_), channel_id=1, source_target_pairs={{0,2},{2,0},{4,6},{6,4},{1,3},{3,1},{5,7},{7,5},{8,10},{10,8},{12,... | collective-permute-start | bytes 294920 | tf_op jit(solution)/shard_map/ppermute | solution.py:627
  32.6 8.6 %collective-permute-start.9 = (bf16[128,384]{1,0:T(8,128)(2,1)S(1)}, bf16[128,384]{1,0:T(8,128)(2,1)S(1)}, u32[]{:S(2)}, u32[]{:S(2)}) collective-permute-start(bf16[128,384]{1,0:T(8,128)(2,1)S(1)} %get-tuple-element.92), channel_id=1, source_target_pairs={{0,4},{2,6},{4,0},{6,2},{1,5},{3,7},{5,1},{7,3},{8,12},{10,14},{12... | collective-permute-start | bytes 294920 | tf_op jit(solution)/shard_map/ppermute | solution.py:627
  33.8 5.7 %collective-permute-start.12 = (bf16[128,768]{1,0:T(8,128)(2,1)S(1)}, bf16[128,768]{1,0:T(8,128)(2,1)S(1)}, u32[]{:S(2)}, u32[]{:S(2)}) collective-permute-start(bf16[128,768]{1,0:T(8,128)(2,1)S(1)} %get-tuple-element.94.left_ref.refs_0_), channel_id=1, source_target_pairs={{0,8},{8,0},{1,9},{9,1},{2,10},{10,2},{3,11},{11,3},{4,12},{12,4},... | collective-permute-start | bytes 589832 | tf_op jit(solution)/shard_map/ppermute | solution.py:623
  36.8 6.4 %collective-permute-start.10 = (bf16[128,384]{1,0:T(8,128)(2,1)S(1)}, bf16[128,384]{1,0:T(8,128)(2,1)S(1)}, u32[]{:S(2)}, u32[]{:S(2)}) collective-permute-start(bf16[128,384]{1,0:T(8,128)(2,1)S(1)} %relay.1), channel_id=1, source_target_pairs={{0,2},{2,0},{4,6},{6,4},{1,3},{3,1},{5,7},{7,5},{8,10},{10,8},{12,... | collective-permute-start | bytes 294920 | tf_op jit(solution)/shard_map/ppermute | solution.py:627
  38.2 5.0 %collective-permute-start.11 = (bf16[128,384]{1,0:T(8,128)(2,1)S(1)}, bf16[128,384]{1,0:T(8,128)(2,1)S(1)}, u32[]{:S(2)}, u32[]{:S(2)}) collective-permute-start(bf16[128,384]{1,0:T(8,128)(2,1)S(1)} %get-tuple-element.92), channel_id=1, source_target_pairs={{0,2},{2,0},{4,6},{6,4},{1,3},{3,1},{5,7},{7,5},{8,10},{10,8},{12,... | collective-permute-start | bytes 294920 | tf_op jit(solution)/shard_map/ppermute | solution.py:627
  39.6 3.7 %collective-permute-start.13 = (bf16[128,1536]{1,0:T(8,128)(2,1)S(1)}, bf16[128,1536]{1,0:T(8,128)(2,1)S(1)}, u32[]{:S(2)}, u32[]{:S(2)}) collective-permute-start(bf16[128,1536]{1,0:T(8,128)(2,1)S(1)} %join.1.here_ref), channel_id=1, source_target_pairs={{0,1},{1,0},{2,3},{3,2},{4,5},{5,4},{6,7},{7,6},{8,9},{9,8},{10,11... | collective-permute-start | bytes 1179656 | tf_op jit(solution)/shard_map/ppermute | solution.py:623
  39.7 5.2 %collective-permute-start.14 = (bf16[128,384]{1,0:T(8,128)(2,1)S(1)}, bf16[128,384]{1,0:T(8,128)(2,1)S(1)}, u32[]{:S(2)}, u32[]{:S(2)}) collective-permute-start(bf16[128,384]{1,0:T(8,128)(2,1)S(1)} %choose.1), channel_id=1, source_target_pairs={{0,8},{8,0},{1,9},{9,1},{2,10},{10,2},{3,11},{11,3},{4,12},{12,4},... | collective-permute-start | bytes 294920 | tf_op jit(solution)/shard_map/ppermute | solution.py:623
  41.2 5.2 %collective-permute-start.15 = (bf16[128,384]{1,0:T(8,128)(2,1)S(1)}, bf16[128,384]{1,0:T(8,128)(2,1)S(1)}, u32[]{:S(2)}, u32[]{:S(2)}) collective-permute-start(bf16[128,384]{1,0:T(8,128)(2,1)S(1)} %collective-permute-done.9.refs_4_), channel_id=1, source_target_pairs={{0,2},{2,0},{4,6},{6,4},{1,3},{3,1},{5,7},{7,5},{8,10},{10,8},{12,... | collective-permute-start | bytes 294920 | tf_op jit(solution)/shard_map/ppermute | solution.py:627
  46.5 2.4 %collective-permute-start.16 = (bf16[128,768]{1,0:T(8,128)(2,1)S(1)}, bf16[128,768]{1,0:T(8,128)(2,1)S(1)}, u32[]{:S(2)}, u32[]{:S(2)}) collective-permute-start(bf16[128,768]{1,0:T(8,128)(2,1)S(1)} %get-tuple-element.107), channel_id=1, source_target_pairs={{0,1},{1,0},{2,3},{3,2},{4,5},{5,4},{6,7},{7,6},{8,9},{9,8},{10,11... | collective-permute-start | bytes 589832 | tf_op jit(solution)/shard_map/ppermute | solution.py:623
  46.6 9.4 %collective-permute-start.17 = (bf16[128,1152]{1,0:T(8,128)(2,1)S(1)}, bf16[128,1152]{1,0:T(8,128)(2,1)S(1)}, u32[]{:S(2)}, u32[]{:S(2)}) collective-permute-start(bf16[128,1152]{1,0:T(8,128)(2,1)S(1)} %get-tuple-element.113), channel_id=1, source_target_pairs={{0,8},{8,0},{1,9},{9,1},{2,10},{10,2},{3,11},{11,3},{4,12},{12,4},... | collective-permute-start | bytes 884744 | tf_op jit(solution)/shard_map/ppermute | solution.py:623
  47.2 9.2 %collective-permute-start.18 = (bf16[64,1536]{1,0:T(8,128)(2,1)S(1)}, bf16[64,1536]{1,0:T(8,128)(2,1)S(1)}, u32[]{:S(2)}, u32[]{:S(2)}) collective-permute-start(bf16[64,1536]{1,0:T(8,128)(2,1)S(1)} %get-tuple-element.115), channel_id=1, source_target_pairs={{0,2},{2,0},{4,6},{6,4},{1,3},{3,1},{5,7},{7,5},{8,10},{10,8},{12,... | collective-permute-start | bytes 589832 | tf_op jit(solution)/shard_map/ppermute | solution.py:627
  56.2 1.7 %collective-permute-start.19 = (bf16[128,768]{1,0:T(8,128)(2,1)S(1)}, bf16[128,768]{1,0:T(8,128)(2,1)S(1)}, u32[]{:S(2)}, u32[]{:S(2)}) collective-permute-start(bf16[128,768]{1,0:T(8,128)(2,1)S(1)} %get-tuple-element.119), channel_id=1, source_target_pairs={{0,1},{1,0},{2,3},{3,2},{4,5},{5,4},{6,7},{7,6},{8,9},{9,8},{10,11... | collective-permute-start | bytes 589832 | tf_op jit(solution)/shard_map/ppermute | solution.py:623
  56.4 8.4 %collective-permute-start.20 = (bf16[32,1536]{1,0:T(8,128)(2,1)S(1)}, bf16[32,1536]{1,0:T(8,128)(2,1)S(1)}, u32[]{:S(2)}, u32[]{:S(2)}) collective-permute-start(bf16[32,1536]{1,0:T(8,128)(2,1)S(1)} %get-tuple-element.130), channel_id=1, source_target_pairs={{0,4},{2,6},{4,0},{6,2},{1,5},{3,7},{5,1},{7,3},{8,12},{10,14},{12... | collective-permute-start | bytes 294920 | tf_op jit(solution)/shard_map/ppermute | solution.py:627

commit v17 on v16

--- a/solution.py
+++ b/solution.py
@@ -536,22 +536,41 @@
     )(near, got)
 
 
-def unpack_kernel(after_ref, placing_ref, factor_ref, own_ref, got_ref, out_ref):
+def unpack_kernel(
+    after_ref, placing_ref, factor_ref, own_ref, got_ref, out_ref, held_ref, sems
+):
     del after_ref
-    total = own_ref[...] + got_ref[...].astype(F32)
-    scaled = (total * factor_ref[:, 0:1]).astype(BF16)
-    out_ref[...] = lax.dot_general(
-        placing_ref[...], scaled, (((0,), (0,)), ((), ())), preferred_element_type=F32
-    ).astype(BF16)
+    parts, _, cut = held_ref.shape
+    copies = []
+    for n in range(parts):
+        columns = slice(cut * n, cut * (n + 1))
+        total = own_ref[:, columns] + got_ref[:, columns].astype(F32)
+        scaled = (total * factor_ref[:, 0:1]).astype(BF16)
+        held_ref[n] = lax.dot_general(
+            placing_ref[...], scaled, (((0,), (0,)), ((), ())), preferred_element_type=F32
+        ).astype(BF16)
+        copy = pltpu.make_async_copy(
+            held_ref.at[n], out_ref.at[:, pl.ds(cut * n, cut)], sems.at[n]
+        )
+        copy.start()
+        copies.append(copy)
+    for copy in copies:
+        copy.wait()
 
 
 def unpack(done, placing, factor, own, got):
     slots, rows = placing.shape
+    width = own.shape[1]
+    parts = 3
     return pl.pallas_call(
         unpack_kernel,
         in_specs=[ANY] + [VMEM] * 4,
-        out_specs=VMEM,
-        out_shape=jax.ShapeDtypeStruct((rows, own.shape[1]), BF16),
+        out_specs=HBM,
+        out_shape=jax.ShapeDtypeStruct((rows, width), BF16),
+        scratch_shapes=[
+            pltpu.VMEM((parts, rows, width // parts), BF16),
+            pltpu.SemaphoreType.DMA((parts,)),
+        ],
         compiler_params=params(4),
         name="unpack",
     )(done, placing, factor, own, got)

time: 65.9 us -> 66 us (level)
  no operation moved by 1% of the time
where the time goes in v17:
time: 66 us; the launch traced here: 65.9 us
  Pallas kernels  35.3 us (53%)
  starting transfers between devices  24.7 us (37%)
  waiting for transfers between devices  4.9 us (7%)
  between operations  1.02 us (2%)
    ppermute x11, starting transfers between devices, across(): return lax.ppermute(value, 'col', [(i, i ^ slot) for i in range(4)])  18.1 us
    pallas_call x2, Pallas kernels, gram_piece(): pl.pallas_call(functools.partial(gram_kernel, 2.0 / rows, flips), in_spec...  13.6 us
    pallas_call x1, Pallas kernels, regroup(): pl.pallas_call(regroup_kernel, in_specs=[ANY, HBM], out_specs=[VMEM] * 2,...  6.97 us
    ppermute x10, starting transfers between devices, swap(): return lax.ppermute(value, axis, [(0, 1), (1, 0)])  6.61 us
    pallas_call x4, Pallas kernels, preacts_of(): pl.pallas_call(functools.partial(preact_kernel, first, row_flip, chunk, c...  6.26 us
    pallas_call x1, Pallas kernels, fetch(): pl.pallas_call(fetch_kernel, in_specs=[ANY, HBM], out_specs=[VMEM, VMEM],...  3.8 us
    ppermute x11, waiting for transfers between devices, across(): return lax.ppermute(value, 'col', [(i, i ^ slot) for i in range(4)])  3.62 us
    pallas_call x1, Pallas kernels, project(): pl.pallas_call(project_kernel, in_specs=[ANY] + [VMEM] * 3, out_specs=[VM...  1.61 us
  transfers between devices with their start and end apart: 21, of which 6 were waited for; matrix products, arithmetic and copies ran while one was open for 0% of the time, Pallas kernels for 47%

profile of v17, /device:TPU:0, one launch (start us, length us, event | category | flops | bytes accessed | tf_op | source)
XLA Modules:
  0.0 65.9 jit_solution(7245529403101951690)
XLA Ops:
  0.6 1.3 %pack.1 = (bf16[32,1536]{1,0:T(8,128)(2,1)S(1)}, bf16[32,128]{1,0:T(8,128)(2,1)S(1)}, f32[32,128]{1,0:T(8,128)S(1)}) custom-call(bf16[128,1536]{1,0:T(8,128)(2,1)} %tokens_ref.1, s32[2,128]{1,0:T(2,128)} %bitcast.12, s32[1,128]{1,0:T(1,128)} %bitcast.14, f32[2,128]{1,0:T(2,128)} %bitcast.13), custom_call_target="tpu_custom_call" | custom-call | tf_op jit(solution)/shard_map/pack/pallas_call | solution.py:137
  1.9 5.1 %collective-permute-start.2 = (bf16[32,1536]{1,0:T(8,128)(2,1)S(1)}, bf16[32,1536]{1,0:T(8,128)(2,1)S(1)}, u32[]{:S(2)}, u32[]{:S(2)}) collective-permute-start(bf16[32,1536]{1,0:T(8,128)(2,1)S(1)} %get-tuple-element.67.after_ref.refs_0_), channel_id=1, source_target_pairs={{0,6},{2,4},{4,2},{6,0},{1,7},{3,5},{5,3},{7,1},{8,14},{10,12},{12... | collective-permute-start | bytes 294920 | tf_op jit(solution)/shard_map/ppermute | solution.py:646
  7.7 7.0 %regroup.1 = (bf16[24,1536,2,128]{3,2,1,0:T(2,128)(2,1)S(1)}, bf16[256,1024]{1,0:T(8,128)(2,1)S(1)}) custom-call(bf16[32,1536]{1,0:T(8,128)(2,1)S(1)} %get-tuple-element.67.after_ref.refs_0_, bf16[1536,24,2,128]{3,2,1,0:T(2,128)(2,1)} %bitcast.11), custom_call_target="tpu_custom_call" | custom-call | bytes 37748736 | tf_op jit(solution)/shard_map/regroup/pallas_call | solution.py:172
  15.3 2.0 %preacts_sent.2 = (f32[256,768]{1,0:T(8,128)S(1)}, bf16[256,3072]{1,0:T(8,128)(2,1)S(1)}) custom-call(bf16[32,1536]{1,0:T(8,128)(2,1)S(1)} %get-tuple-element.67.after_ref.refs_0_, bf16[32,1536]{1,0:T(8,128)(2,1)S(1)} %collective-permute-done.refs_1_, bf16[32,1536]{1,0:T(8,128)(2,1)S(1)} %collective-permute-done.1.refs_2_, ...), custom_call_target="tpu_custom_call" | custom-call | flops 1207959552 | tf_op jit(solution)/shard_map/preacts_sent/pallas_call | solution.py:265
  17.4 1.4 %preacts_sent.3 = f32[256,768]{1,0:T(8,128)S(1)} custom-call(bf16[256,3072]{1,0:T(8,128)(2,1)S(1)} %get-tuple-element.75.refs_0_.after_ref, bf16[24,3072,128]{2,1,0:T(8,128)(2,1)S(1)} %bitcast.8), custom_call_target="tpu_custom_call" | custom-call | flops 1207959552 | tf_op jit(solution)/shard_map/preacts_sent/pallas_call | solution.py:265
  19.3 1.4 %preacts_kept.2.kept_ref = f32[256,768]{1,0:T(8,128)S(1)} custom-call(bf16[256,3072]{1,0:T(8,128)(2,1)S(1)} %get-tuple-element.75.refs_0_.after_ref, bf16[24,3072,128]{2,1,0:T(8,128)(2,1)S(1)} %bitcast.9), custom_call_target="tpu_custom_call" | custom-call | flops 1207959552 | tf_op jit(solution)/shard_map/preacts_kept/pallas_call | solution.py:265
  20.9 1.6 %collective-permute-start.5 = (bf16[256,384]{1,0:T(8,128)(2,1)S(1)}, bf16[256,384]{1,0:T(8,128)(2,1)S(1)}, u32[]{:S(2)}, u32[]{:S(2)}) collective-permute-start(bf16[256,384]{1,0:T(8,128)(2,1)S(1)} %get-tuple-element.77), channel_id=1, source_target_pairs={{0,8},{8,0},{1,9},{9,1},{2,10},{10,2},{3,11},{11,3},{4,12},{12,4},... | collective-permute-start | bytes 589832 | tf_op jit(solution)/shard_map/ppermute | solution.py:642
  22.5 1.4 %preacts_kept.3.kept_ref = f32[256,768]{1,0:T(8,128)S(1)} custom-call(bf16[256,3072]{1,0:T(8,128)(2,1)S(1)} %get-tuple-element.75.refs_0_.after_ref, bf16[24,3072,128]{2,1,0:T(8,128)(2,1)S(1)} %bitcast.10), custom_call_target="tpu_custom_call" | custom-call | flops 1207959552 | tf_op jit(solution)/shard_map/preacts_kept/pallas_call | solution.py:265
  24.6 3.8 %fetch_down.1 = (bf16[3072,1536]{1,0:T(8,128)(2,1)S(1)}, f32[8,128]{1,0:T(8,128)S(1)}) custom-call(bf16[256,3072]{1,0:T(8,128)(2,1)S(1)} %get-tuple-element.75.refs_0_.after_ref, bf16[3072,1536]{1,0:T(8,128)(2,1)} %down_ref.1), custom_call_target="tpu_custom_call" | custom-call | bytes 18874368 | tf_op jit(solution)/shard_map/fetch_down/pallas_call | solution.py:206
  28.8 1.7 %collective-permute-start.7 = (bf16[128,384]{1,0:T(8,128)(2,1)S(1)}, bf16[128,384]{1,0:T(8,128)(2,1)S(1)}, u32[]{:S(2)}, u32[]{:S(2)}) collective-permute-start(bf16[128,384]{1,0:T(8,128)(2,1)S(1)} %act.2.refs_0_), channel_id=1, source_target_pairs={{0,4},{2,6},{4,0},{6,2},{1,5},{3,7},{5,1},{7,3},{8,12},{10,14},{12... | collective-permute-start | bytes 294920 | tf_op jit(solution)/shard_map/ppermute | solution.py:646
  30.5 2.0 %collective-permute-start.8 = (bf16[128,384]{1,0:T(8,128)(2,1)S(1)}, bf16[128,384]{1,0:T(8,128)(2,1)S(1)}, u32[]{:S(2)}, u32[]{:S(2)}) collective-permute-start(bf16[128,384]{1,0:T(8,128)(2,1)S(1)} %act.2.refs_0_), channel_id=1, source_target_pairs={{0,2},{2,0},{4,6},{6,4},{1,3},{3,1},{5,7},{7,5},{8,10},{10,8},{12,... | collective-permute-start | bytes 294920 | tf_op jit(solution)/shard_map/ppermute | solution.py:646
  32.6 1.2 %collective-permute-start.9 = (bf16[128,384]{1,0:T(8,128)(2,1)S(1)}, bf16[128,384]{1,0:T(8,128)(2,1)S(1)}, u32[]{:S(2)}, u32[]{:S(2)}) collective-permute-start(bf16[128,384]{1,0:T(8,128)(2,1)S(1)} %get-tuple-element.92), channel_id=1, source_target_pairs={{0,4},{2,6},{4,0},{6,2},{1,5},{3,7},{5,1},{7,3},{8,12},{10,14},{12... | collective-permute-start | bytes 294920 | tf_op jit(solution)/shard_map/ppermute | solution.py:646
  33.8 1.5 %collective-permute-start.12 = (bf16[128,768]{1,0:T(8,128)(2,1)S(1)}, bf16[128,768]{1,0:T(8,128)(2,1)S(1)}, u32[]{:S(2)}, u32[]{:S(2)}) collective-permute-start(bf16[128,768]{1,0:T(8,128)(2,1)S(1)} %get-tuple-element.94.left_ref.refs_0_), channel_id=1, source_target_pairs={{0,8},{8,0},{1,9},{9,1},{2,10},{10,2},{3,11},{11,3},{4,12},{12,4},... | collective-permute-start | bytes 589832 | tf_op jit(solution)/shard_map/ppermute | solution.py:642
  35.3 1.5 %collective-permute-done.7.in_ref.near_ref.refs_3_ = bf16[128,384]{1,0:T(8,128)(2,1)S(1)} collective-permute-done((bf16[128,384]{1,0:T(8,128)(2,1)S(1)}, bf16[128,384]{1,0:T(8,128)(2,1)S(1)}, u32[]{:S(2)}, u32[]{:S(2)}) %collective-permute-start.7) | collective-permute-done | bytes 98336 | tf_op jit(solution)/shard_map/ppermute | solution.py:646
  36.8 1.4 %collective-permute-start.10 = (bf16[128,384]{1,0:T(8,128)(2,1)S(1)}, bf16[128,384]{1,0:T(8,128)(2,1)S(1)}, u32[]{:S(2)}, u32[]{:S(2)}) collective-permute-start(bf16[128,384]{1,0:T(8,128)(2,1)S(1)} %relay.1), channel_id=1, source_target_pairs={{0,2},{2,0},{4,6},{6,4},{1,3},{3,1},{5,7},{7,5},{8,10},{10,8},{12,... | collective-permute-start | bytes 294920 | tf_op jit(solution)/shard_map/ppermute | solution.py:646
  39.7 1.5 %collective-permute-start.14 = (bf16[128,384]{1,0:T(8,128)(2,1)S(1)}, bf16[128,384]{1,0:T(8,128)(2,1)S(1)}, u32[]{:S(2)}, u32[]{:S(2)}) collective-permute-start(bf16[128,384]{1,0:T(8,128)(2,1)S(1)} %choose.1), channel_id=1, source_target_pairs={{0,8},{8,0},{1,9},{9,1},{2,10},{10,2},{3,11},{11,3},{4,12},{12,4},... | collective-permute-start | bytes 294920 | tf_op jit(solution)/shard_map/ppermute | solution.py:642
  41.2 2.0 %collective-permute-start.15 = (bf16[128,384]{1,0:T(8,128)(2,1)S(1)}, bf16[128,384]{1,0:T(8,128)(2,1)S(1)}, u32[]{:S(2)}, u32[]{:S(2)}) collective-permute-start(bf16[128,384]{1,0:T(8,128)(2,1)S(1)} %collective-permute-done.9.refs_4_), channel_id=1, source_target_pairs={{0,2},{2,0},{4,6},{6,4},{1,3},{3,1},{5,7},{7,5},{8,10},{10,8},{12,... | collective-permute-start | bytes 294920 | tf_op jit(solution)/shard_map/ppermute | solution.py:646
  43.3 1.6 %project.1 = (f32[64,1536]{1,0:T(8,128)S(1)}, bf16[64,1536]{1,0:T(8,128)(2,1)S(1)}, bf16[128,3072]{1,0:T(8,128)(2,1)S(1)}, f32[8,128]{1,0:T(8,128)S(1)}) custom-call(f32[8,128]{1,0:T(8,128)S(1)} %get-tuple-element.95.tick_ref, bf16[128,1536]{1,0:T(8,128)(2,1)S(1)} %join.1.here_ref, bf16[128,1536]{1,0:T(8,128)(2,1)S(1)} %collective-permute-done.13.there_ref, ...), custom_call_target="tpu_custom_call" | custom-call | bytes 1 | tf_op jit(solution)/shard_map/project/pallas_call | solution.py:500
  44.9 1.5 %collective-permute-done.15.refs_6_ = bf16[128,384]{1,0:T(8,128)(2,1)S(1)} collective-permute-done((bf16[128,384]{1,0:T(8,128)(2,1)S(1)}, bf16[128,384]{1,0:T(8,128)(2,1)S(1)}, u32[]{:S(2)}, u32[]{:S(2)}) %collective-permute-start.15) | collective-permute-done | bytes 98336 | tf_op jit(solution)/shard_map/ppermute | solution.py:646
  47.2 1.7 %collective-permute-start.18 = (bf16[64,1536]{1,0:T(8,128)(2,1)S(1)}, bf16[64,1536]{1,0:T(8,128)(2,1)S(1)}, u32[]{:S(2)}, u32[]{:S(2)}) collective-permute-start(bf16[64,1536]{1,0:T(8,128)(2,1)S(1)} %get-tuple-element.115), channel_id=1, source_target_pairs={{0,2},{2,0},{4,6},{6,4},{1,3},{3,1},{5,7},{7,5},{8,10},{10,8},{12,... | collective-permute-start | bytes 589832 | tf_op jit(solution)/shard_map/ppermute | solution.py:646
  48.9 6.8 %gram.2 = (f32[3072,3072]{1,0:T(8,128)}, f32[8,128]{1,0:T(8,128)S(1)}) custom-call(f32[8,128]{1,0:T(8,128)S(1)} %get-tuple-element.108.refs_0_, bf16[128,768]{1,0:T(8,128)(2,1)S(1)} %get-tuple-element.109.refs_1_, bf16[128,768]{1,0:T(8,128)(2,1)S(1)} %collective-permute-done.16.refs_2_, bf16[128,3072]{1,0:T(8,128)(2,1)S(1)} %get-tuple-element.111.refs_3_), custom_call_target="tpu_custom_call" | custom-call | flops 1207959552 | bytes 18874368 | tf_op jit(solution)/shard_map/gram/pallas_call | solution.py:622
  56.4 1.5 %collective-permute-start.20 = (bf16[32,1536]{1,0:T(8,128)(2,1)S(1)}, bf16[32,1536]{1,0:T(8,128)(2,1)S(1)}, u32[]{:S(2)}, u32[]{:S(2)}) collective-permute-start(bf16[32,1536]{1,0:T(8,128)(2,1)S(1)} %get-tuple-element.130), channel_id=1, source_target_pairs={{0,4},{2,6},{4,0},{6,2},{1,5},{3,7},{5,1},{7,3},{8,12},{10,14},{12... | collective-permute-start | bytes 294920 | tf_op jit(solution)/shard_map/ppermute | solution.py:646
  57.9 6.8 %gram.3 = (f32[3072,3072]{1,0:T(8,128)}, f32[8,128]{1,0:T(8,128)S(1)}) custom-call(f32[8,128]{1,0:T(8,128)S(1)} %get-tuple-element.120.refs_0_, bf16[128,768]{1,0:T(8,128)(2,1)S(1)} %get-tuple-element.121.refs_1_, bf16[128,768]{1,0:T(8,128)(2,1)S(1)} %collective-permute-done.19.refs_2_, ...), custom_call_target="tpu_custom_call", output_to_operand_aliasing={{0}: (4, {})} | custom-call | flops 1207959552 | bytes 18874368 | tf_op jit(solution)/shard_map/gram/pallas_call | solution.py:622
  64.7 1.0 %unpack.1 = bf16[128,1536]{1,0:T(8,128)(2,1)} custom-call(f32[8,128]{1,0:T(8,128)S(1)} %get-tuple-element.124.after_ref, bf16[32,128]{1,0:T(8,128)(2,1)S(1)} %get-tuple-element.125.placing_ref, f32[32,128]{1,0:T(8,128)S(1)} %get-tuple-element.126.factor_ref, f32[32,1536]{1,0:T(8,128)S(1)} %get-tuple-element.129.own_ref, ...), custom_call_target="tpu_custom_call" | custom-call | tf_op jit(solution)/shard_map/unpack/pallas_call | solution.py:565
  (39 shorter events, 6.0 us)
Async XLA Ops:
  1.9 12.7 %collective-permute-start.2 = (bf16[32,1536]{1,0:T(8,128)(2,1)S(1)}, bf16[32,1536]{1,0:T(8,128)(2,1)S(1)}, u32[]{:S(2)}, u32[]{:S(2)}) collective-permute-start(bf16[32,1536]{1,0:T(8,128)(2,1)S(1)} %get-tuple-element.67.after_ref.refs_0_), channel_id=1, source_target_pairs={{0,6},{2,4},{4,2},{6,0},{1,7},{3,5},{5,3},{7,1},{8,14},{10,12},{12... | collective-permute-start | bytes 294920 | tf_op jit(solution)/shard_map/ppermute | solution.py:646
  7.0 8.3 %collective-permute-start.1 = (bf16[32,1536]{1,0:T(8,128)(2,1)S(1)}, bf16[32,1536]{1,0:T(8,128)(2,1)S(1)}, u32[]{:S(2)}, u32[]{:S(2)}) collective-permute-start(bf16[32,1536]{1,0:T(8,128)(2,1)S(1)} %get-tuple-element.67.after_ref.refs_0_), channel_id=1, source_target_pairs={{0,4},{2,6},{4,0},{6,2},{1,5},{3,7},{5,1},{7,3},{8,12},{10,14},{12... | collective-permute-start | bytes 294920 | tf_op jit(solution)/shard_map/ppermute | solution.py:646
  7.0 8.3 %collective-permute-start = (bf16[32,1536]{1,0:T(8,128)(2,1)S(1)}, bf16[32,1536]{1,0:T(8,128)(2,1)S(1)}, u32[]{:S(2)}, u32[]{:S(2)}) collective-permute-start(bf16[32,1536]{1,0:T(8,128)(2,1)S(1)} %get-tuple-element.67.after_ref.refs_0_), channel_id=1, source_target_pairs={{0,2},{2,0},{4,6},{6,4},{1,3},{3,1},{5,7},{7,5},{8,10},{10,8},{12,... | collective-permute-start | bytes 294920 | tf_op jit(solution)/shard_map/ppermute | solution.py:646
  17.3 3.5 %collective-permute-start.3 = (f32[256,768]{1,0:T(8,128)S(1)}, f32[256,768]{1,0:T(8,128)S(1)}, u32[]{:S(2)}, u32[]{:S(2)}) collective-permute-start(f32[256,768]{1,0:T(8,128)S(1)} %get-tuple-element.71), channel_id=1, source_target_pairs={{0,1},{1,0},{2,3},{3,2},{4,5},{5,4},{6,7},{7,6},{8,9},{9,8},{10,11... | collective-permute-start | bytes 2359304 | tf_op jit(solution)/shard_map/ppermute | solution.py:642
  18.8 5.1 %collective-permute-start.4 = (f32[256,768]{1,0:T(8,128)S(1)}, f32[256,768]{1,0:T(8,128)S(1)}, u32[]{:S(2)}, u32[]{:S(2)}) collective-permute-start(f32[256,768]{1,0:T(8,128)S(1)} %preacts_sent.3), channel_id=1, source_target_pairs={{0,1},{1,0},{2,3},{3,2},{4,5},{5,4},{6,7},{7,6},{8,9},{9,8},{10,11... | collective-permute-start | bytes 2359304 | tf_op jit(solution)/shard_map/ppermute | solution.py:642
  20.9 7.8 %collective-permute-start.5 = (bf16[256,384]{1,0:T(8,128)(2,1)S(1)}, bf16[256,384]{1,0:T(8,128)(2,1)S(1)}, u32[]{:S(2)}, u32[]{:S(2)}) collective-permute-start(bf16[256,384]{1,0:T(8,128)(2,1)S(1)} %get-tuple-element.77), channel_id=1, source_target_pairs={{0,8},{8,0},{1,9},{9,1},{2,10},{10,2},{3,11},{11,3},{4,12},{12,4},... | collective-permute-start | bytes 589832 | tf_op jit(solution)/shard_map/ppermute | solution.py:642
  24.0 8.6 %collective-permute-start.6 = (bf16[256,384]{1,0:T(8,128)(2,1)S(1)}, bf16[256,384]{1,0:T(8,128)(2,1)S(1)}, u32[]{:S(2)}, u32[]{:S(2)}) collective-permute-start(bf16[256,384]{1,0:T(8,128)(2,1)S(1)} %get-tuple-element.79), channel_id=1, source_target_pairs={{0,8},{8,0},{1,9},{9,1},{2,10},{10,2},{3,11},{11,3},{4,12},{12,4},... | collective-permute-start | bytes 589832 | tf_op jit(solution)/shard_map/ppermute | solution.py:642
  28.8 8.0 %collective-permute-start.7 = (bf16[128,384]{1,0:T(8,128)(2,1)S(1)}, bf16[128,384]{1,0:T(8,128)(2,1)S(1)}, u32[]{:S(2)}, u32[]{:S(2)}) collective-permute-start(bf16[128,384]{1,0:T(8,128)(2,1)S(1)} %act.2.refs_0_), channel_id=1, source_target_pairs={{0,4},{2,6},{4,0},{6,2},{1,5},{3,7},{5,1},{7,3},{8,12},{10,14},{12... | collective-permute-start | bytes 294920 | tf_op jit(solution)/shard_map/ppermute | solution.py:646
  30.5 6.3 %collective-permute-start.8 = (bf16[128,384]{1,0:T(8,128)(2,1)S(1)}, bf16[128,384]{1,0:T(8,128)(2,1)S(1)}, u32[]{:S(2)}, u32[]{:S(2)}) collective-permute-start(bf16[128,384]{1,0:T(8,128)(2,1)S(1)} %act.2.refs_0_), channel_id=1, source_target_pairs={{0,2},{2,0},{4,6},{6,4},{1,3},{3,1},{5,7},{7,5},{8,10},{10,8},{12,... | collective-permute-start | bytes 294920 | tf_op jit(solution)/shard_map/ppermute | solution.py:646
  32.6 8.6 %collective-permute-start.9 = (bf16[128,384]{1,0:T(8,128)(2,1)S(1)}, bf16[128,384]{1,0:T(8,128)(2,1)S(1)}, u32[]{:S(2)}, u32[]{:S(2)}) collective-permute-start(bf16[128,384]{1,0:T(8,128)(2,1)S(1)} %get-tuple-element.92), channel_id=1, source_target_pairs={{0,4},{2,6},{4,0},{6,2},{1,5},{3,7},{5,1},{7,3},{8,12},{10,14},{12... | collective-permute-start | bytes 294920 | tf_op jit(solution)/shard_map/ppermute | solution.py:646
  33.8 5.7 %collective-permute-start.12 = (bf16[128,768]{1,0:T(8,128)(2,1)S(1)}, bf16[128,768]{1,0:T(8,128)(2,1)S(1)}, u32[]{:S(2)}, u32[]{:S(2)}) collective-permute-start(bf16[128,768]{1,0:T(8,128)(2,1)S(1)} %get-tuple-element.94.left_ref.refs_0_), channel_id=1, source_target_pairs={{0,8},{8,0},{1,9},{9,1},{2,10},{10,2},{3,11},{11,3},{4,12},{12,4},... | collective-permute-start | bytes 589832 | tf_op jit(solution)/shard_map/ppermute | solution.py:642
  36.8 6.4 %collective-permute-start.10 = (bf16[128,384]{1,0:T(8,128)(2,1)S(1)}, bf16[128,384]{1,0:T(8,128)(2,1)S(1)}, u32[]{:S(2)}, u32[]{:S(2)}) collective-permute-start(bf16[128,384]{1,0:T(8,128)(2,1)S(1)} %relay.1), channel_id=1, source_target_pairs={{0,2},{2,0},{4,6},{6,4},{1,3},{3,1},{5,7},{7,5},{8,10},{10,8},{12,... | collective-permute-start | bytes 294920 | tf_op jit(solution)/shard_map/ppermute | solution.py:646
  38.2 5.0 %collective-permute-start.11 = (bf16[128,384]{1,0:T(8,128)(2,1)S(1)}, bf16[128,384]{1,0:T(8,128)(2,1)S(1)}, u32[]{:S(2)}, u32[]{:S(2)}) collective-permute-start(bf16[128,384]{1,0:T(8,128)(2,1)S(1)} %get-tuple-element.92), channel_id=1, source_target_pairs={{0,2},{2,0},{4,6},{6,4},{1,3},{3,1},{5,7},{7,5},{8,10},{10,8},{12,... | collective-permute-start | bytes 294920 | tf_op jit(solution)/shard_map/ppermute | solution.py:646
  39.6 3.7 %collective-permute-start.13 = (bf16[128,1536]{1,0:T(8,128)(2,1)S(1)}, bf16[128,1536]{1,0:T(8,128)(2,1)S(1)}, u32[]{:S(2)}, u32[]{:S(2)}) collective-permute-start(bf16[128,1536]{1,0:T(8,128)(2,1)S(1)} %join.1.here_ref), channel_id=1, source_target_pairs={{0,1},{1,0},{2,3},{3,2},{4,5},{5,4},{6,7},{7,6},{8,9},{9,8},{10,11... | collective-permute-start | bytes 1179656 | tf_op jit(solution)/shard_map/ppermute | solution.py:642
  39.7 5.2 %collective-permute-start.14 = (bf16[128,384]{1,0:T(8,128)(2,1)S(1)}, bf16[128,384]{1,0:T(8,128)(2,1)S(1)}, u32[]{:S(2)}, u32[]{:S(2)}) collective-permute-start(bf16[128,384]{1,0:T(8,128)(2,1)S(1)} %choose.1), channel_id=1, source_target_pairs={{0,8},{8,0},{1,9},{9,1},{2,10},{10,2},{3,11},{11,3},{4,12},{12,4},... | collective-permute-start | bytes 294920 | tf_op jit(solution)/shard_map/ppermute | solution.py:642
  41.2 5.2 %collective-permute-start.15 = (bf16[128,384]{1,0:T(8,128)(2,1)S(1)}, bf16[128,384]{1,0:T(8,128)(2,1)S(1)}, u32[]{:S(2)}, u32[]{:S(2)}) collective-permute-start(bf16[128,384]{1,0:T(8,128)(2,1)S(1)} %collective-permute-done.9.refs_4_), channel_id=1, source_target_pairs={{0,2},{2,0},{4,6},{6,4},{1,3},{3,1},{5,7},{7,5},{8,10},{10,8},{12,... | collective-permute-start | bytes 294920 | tf_op jit(solution)/shard_map/ppermute | solution.py:646
  46.5 2.4 %collective-permute-start.16 = (bf16[128,768]{1,0:T(8,128)(2,1)S(1)}, bf16[128,768]{1,0:T(8,128)(2,1)S(1)}, u32[]{:S(2)}, u32[]{:S(2)}) collective-permute-start(bf16[128,768]{1,0:T(8,128)(2,1)S(1)} %get-tuple-element.107), channel_id=1, source_target_pairs={{0,1},{1,0},{2,3},{3,2},{4,5},{5,4},{6,7},{7,6},{8,9},{9,8},{10,11... | collective-permute-start | bytes 589832 | tf_op jit(solution)/shard_map/ppermute | solution.py:642
  46.6 9.4 %collective-permute-start.17 = (bf16[128,1152]{1,0:T(8,128)(2,1)S(1)}, bf16[128,1152]{1,0:T(8,128)(2,1)S(1)}, u32[]{:S(2)}, u32[]{:S(2)}) collective-permute-start(bf16[128,1152]{1,0:T(8,128)(2,1)S(1)} %get-tuple-element.113), channel_id=1, source_target_pairs={{0,8},{8,0},{1,9},{9,1},{2,10},{10,2},{3,11},{11,3},{4,12},{12,4},... | collective-permute-start | bytes 884744 | tf_op jit(solution)/shard_map/ppermute | solution.py:642
  47.2 9.2 %collective-permute-start.18 = (bf16[64,1536]{1,0:T(8,128)(2,1)S(1)}, bf16[64,1536]{1,0:T(8,128)(2,1)S(1)}, u32[]{:S(2)}, u32[]{:S(2)}) collective-permute-start(bf16[64,1536]{1,0:T(8,128)(2,1)S(1)} %get-tuple-element.115), channel_id=1, source_target_pairs={{0,2},{2,0},{4,6},{6,4},{1,3},{3,1},{5,7},{7,5},{8,10},{10,8},{12,... | collective-permute-start | bytes 589832 | tf_op jit(solution)/shard_map/ppermute | solution.py:646
  56.2 1.7 %collective-permute-start.19 = (bf16[128,768]{1,0:T(8,128)(2,1)S(1)}, bf16[128,768]{1,0:T(8,128)(2,1)S(1)}, u32[]{:S(2)}, u32[]{:S(2)}) collective-permute-start(bf16[128,768]{1,0:T(8,128)(2,1)S(1)} %get-tuple-element.119), channel_id=1, source_target_pairs={{0,1},{1,0},{2,3},{3,2},{4,5},{5,4},{6,7},{7,6},{8,9},{9,8},{10,11... | collective-permute-start | bytes 589832 | tf_op jit(solution)/shard_map/ppermute | solution.py:642
  56.4 8.4 %collective-permute-start.20 = (bf16[32,1536]{1,0:T(8,128)(2,1)S(1)}, bf16[32,1536]{1,0:T(8,128)(2,1)S(1)}, u32[]{:S(2)}, u32[]{:S(2)}) collective-permute-start(bf16[32,1536]{1,0:T(8,128)(2,1)S(1)} %get-tuple-element.130), channel_id=1, source_target_pairs={{0,4},{2,6},{4,0},{6,2},{1,5},{3,7},{5,1},{7,3},{8,12},{10,14},{12... | collective-permute-start | bytes 294920 | tf_op jit(solution)/shard_map/ppermute | solution.py:646

commit v18 on v16

--- a/solution.py
+++ b/solution.py
@@ -592,7 +592,7 @@
 
 def gram_piece(tick, pieces, flips, wide, gram=None):
     rows, units = pieces[0].shape
-    cut, height, depth = 1024, 256, 6
+    cut, height, depth = 512, 256, 12
     operands = [tick, *pieces, in_vmem(wide)]
     in_specs = [ANY] + [VMEM] * (len(pieces) + 1)
     aliases = {}

time: 65.9 us -> 66.3 us (level)
  Pallas kernels: 35.3 us -> 36.1 us
    pallas_call x2, Pallas kernels: 13.6 us -> 14.4 us  [gram_piece(): pl.pallas_call(functools.partial(gram_kernel, 2.0 / rows, flips), in_spec...]
  transfers between devices with their start and end apart: 21 -> 21, of which waited for: 6 -> 5; matrix products, arithmetic and copies ran while one was open for 0% -> 0% of each run, Pallas kernels for 47% -> 48%
where the time goes in v18:
time: 66.3 us; the launch traced here: 66.2 us
  Pallas kernels  36.1 us (54%)
  starting transfers between devices  24.6 us (37%)
  waiting for transfers between devices  4.63 us (7%)
  between operations  0.87 us (1%)
    ppermute x11, starting transfers between devices, across(): return lax.ppermute(value, 'col', [(i, i ^ slot) for i in range(4)])  18 us
    pallas_call x2, Pallas kernels, gram_piece(): pl.pallas_call(functools.partial(gram_kernel, 2.0 / rows, flips), in_spec...  14.4 us
    pallas_call x1, Pallas kernels, regroup(): pl.pallas_call(regroup_kernel, in_specs=[ANY, HBM], out_specs=[VMEM] * 2,...  6.97 us
    ppermute x10, starting transfers between devices, swap(): return lax.ppermute(value, axis, [(0, 1), (1, 0)])  6.61 us
    pallas_call x4, Pallas kernels, preacts_of(): pl.pallas_call(functools.partial(preact_kernel, first, row_flip, chunk, c...  6.26 us
    pallas_call x1, Pallas kernels, fetch(): pl.pallas_call(fetch_kernel, in_specs=[ANY, HBM], out_specs=[VMEM, VMEM],...  3.8 us
    ppermute x11, waiting for transfers between devices, across(): return lax.ppermute(value, 'col', [(i, i ^ slot) for i in range(4)])  3.62 us
    pallas_call x1, Pallas kernels, project(): pl.pallas_call(project_kernel, in_specs=[ANY] + [VMEM] * 3, out_specs=[VM...  1.61 us
  transfers between devices with their start and end apart: 21, of which 5 were waited for; matrix products, arithmetic and copies ran while one was open for 0% of the time, Pallas kernels for 48%

profile of v18, /device:TPU:0, one launch (start us, length us, event | category | flops | bytes accessed | tf_op | source)
XLA Modules:
  0.0 66.2 jit_solution(4360375197587715203)
XLA Ops:
  0.6 1.3 %pack.1 = (bf16[32,1536]{1,0:T(8,128)(2,1)S(1)}, bf16[32,128]{1,0:T(8,128)(2,1)S(1)}, f32[32,128]{1,0:T(8,128)S(1)}) custom-call(bf16[128,1536]{1,0:T(8,128)(2,1)} %tokens_ref.1, s32[2,128]{1,0:T(2,128)} %bitcast.12, s32[1,128]{1,0:T(1,128)} %bitcast.14, f32[2,128]{1,0:T(2,128)} %bitcast.13), custom_call_target="tpu_custom_call" | custom-call | tf_op jit(solution)/shard_map/pack/pallas_call | solution.py:137
  1.9 5.1 %collective-permute-start.2 = (bf16[32,1536]{1,0:T(8,128)(2,1)S(1)}, bf16[32,1536]{1,0:T(8,128)(2,1)S(1)}, u32[]{:S(2)}, u32[]{:S(2)}) collective-permute-start(bf16[32,1536]{1,0:T(8,128)(2,1)S(1)} %get-tuple-element.67.after_ref.refs_0_), channel_id=1, source_target_pairs={{0,6},{2,4},{4,2},{6,0},{1,7},{3,5},{5,3},{7,1},{8,14},{10,12},{12... | collective-permute-start | bytes 294920 | tf_op jit(solution)/shard_map/ppermute | solution.py:627
  7.7 7.0 %regroup.1 = (bf16[24,1536,2,128]{3,2,1,0:T(2,128)(2,1)S(1)}, bf16[256,1024]{1,0:T(8,128)(2,1)S(1)}) custom-call(bf16[32,1536]{1,0:T(8,128)(2,1)S(1)} %get-tuple-element.67.after_ref.refs_0_, bf16[1536,24,2,128]{3,2,1,0:T(2,128)(2,1)} %bitcast.11), custom_call_target="tpu_custom_call" | custom-call | bytes 37748736 | tf_op jit(solution)/shard_map/regroup/pallas_call | solution.py:172
  15.3 2.0 %preacts_sent.2 = (f32[256,768]{1,0:T(8,128)S(1)}, bf16[256,3072]{1,0:T(8,128)(2,1)S(1)}) custom-call(bf16[32,1536]{1,0:T(8,128)(2,1)S(1)} %get-tuple-element.67.after_ref.refs_0_, bf16[32,1536]{1,0:T(8,128)(2,1)S(1)} %collective-permute-done.refs_1_, bf16[32,1536]{1,0:T(8,128)(2,1)S(1)} %collective-permute-done.1.refs_2_, ...), custom_call_target="tpu_custom_call" | custom-call | flops 1207959552 | tf_op jit(solution)/shard_map/preacts_sent/pallas_call | solution.py:265
  17.4 1.4 %preacts_sent.3 = f32[256,768]{1,0:T(8,128)S(1)} custom-call(bf16[256,3072]{1,0:T(8,128)(2,1)S(1)} %get-tuple-element.75.refs_0_.after_ref, bf16[24,3072,128]{2,1,0:T(8,128)(2,1)S(1)} %bitcast.8), custom_call_target="tpu_custom_call" | custom-call | flops 1207959552 | tf_op jit(solution)/shard_map/preacts_sent/pallas_call | solution.py:265
  19.3 1.4 %preacts_kept.2.kept_ref = f32[256,768]{1,0:T(8,128)S(1)} custom-call(bf16[256,3072]{1,0:T(8,128)(2,1)S(1)} %get-tuple-element.75.refs_0_.after_ref, bf16[24,3072,128]{2,1,0:T(8,128)(2,1)S(1)} %bitcast.9), custom_call_target="tpu_custom_call" | custom-call | flops 1207959552 | tf_op jit(solution)/shard_map/preacts_kept/pallas_call | solution.py:265
  20.9 1.6 %collective-permute-start.5 = (bf16[256,384]{1,0:T(8,128)(2,1)S(1)}, bf16[256,384]{1,0:T(8,128)(2,1)S(1)}, u32[]{:S(2)}, u32[]{:S(2)}) collective-permute-start(bf16[256,384]{1,0:T(8,128)(2,1)S(1)} %get-tuple-element.77), channel_id=1, source_target_pairs={{0,8},{8,0},{1,9},{9,1},{2,10},{10,2},{3,11},{11,3},{4,12},{12,4},... | collective-permute-start | bytes 589832 | tf_op jit(solution)/shard_map/ppermute | solution.py:623
  22.5 1.4 %preacts_kept.3.kept_ref = f32[256,768]{1,0:T(8,128)S(1)} custom-call(bf16[256,3072]{1,0:T(8,128)(2,1)S(1)} %get-tuple-element.75.refs_0_.after_ref, bf16[24,3072,128]{2,1,0:T(8,128)(2,1)S(1)} %bitcast.10), custom_call_target="tpu_custom_call" | custom-call | flops 1207959552 | tf_op jit(solution)/shard_map/preacts_kept/pallas_call | solution.py:265
  24.6 3.8 %fetch_down.1 = (bf16[3072,1536]{1,0:T(8,128)(2,1)S(1)}, f32[8,128]{1,0:T(8,128)S(1)}) custom-call(bf16[256,3072]{1,0:T(8,128)(2,1)S(1)} %get-tuple-element.75.refs_0_.after_ref, bf16[3072,1536]{1,0:T(8,128)(2,1)} %down_ref.1), custom_call_target="tpu_custom_call" | custom-call | bytes 18874368 | tf_op jit(solution)/shard_map/fetch_down/pallas_call | solution.py:206
  28.8 1.7 %collective-permute-start.7 = (bf16[128,384]{1,0:T(8,128)(2,1)S(1)}, bf16[128,384]{1,0:T(8,128)(2,1)S(1)}, u32[]{:S(2)}, u32[]{:S(2)}) collective-permute-start(bf16[128,384]{1,0:T(8,128)(2,1)S(1)} %act.2.refs_0_), channel_id=1, source_target_pairs={{0,4},{2,6},{4,0},{6,2},{1,5},{3,7},{5,1},{7,3},{8,12},{10,14},{12... | collective-permute-start | bytes 294920 | tf_op jit(solution)/shard_map/ppermute | solution.py:627
  30.5 2.0 %collective-permute-start.8 = (bf16[128,384]{1,0:T(8,128)(2,1)S(1)}, bf16[128,384]{1,0:T(8,128)(2,1)S(1)}, u32[]{:S(2)}, u32[]{:S(2)}) collective-permute-start(bf16[128,384]{1,0:T(8,128)(2,1)S(1)} %act.2.refs_0_), channel_id=1, source_target_pairs={{0,2},{2,0},{4,6},{6,4},{1,3},{3,1},{5,7},{7,5},{8,10},{10,8},{12,... | collective-permute-start | bytes 294920 | tf_op jit(solution)/shard_map/ppermute | solution.py:627
  32.6 1.2 %collective-permute-start.9 = (bf16[128,384]{1,0:T(8,128)(2,1)S(1)}, bf16[128,384]{1,0:T(8,128)(2,1)S(1)}, u32[]{:S(2)}, u32[]{:S(2)}) collective-permute-start(bf16[128,384]{1,0:T(8,128)(2,1)S(1)} %get-tuple-element.92), channel_id=1, source_target_pairs={{0,4},{2,6},{4,0},{6,2},{1,5},{3,7},{5,1},{7,3},{8,12},{10,14},{12... | collective-permute-start | bytes 294920 | tf_op jit(solution)/shard_map/ppermute | solution.py:627
  33.8 1.5 %collective-permute-start.12 = (bf16[128,768]{1,0:T(8,128)(2,1)S(1)}, bf16[128,768]{1,0:T(8,128)(2,1)S(1)}, u32[]{:S(2)}, u32[]{:S(2)}) collective-permute-start(bf16[128,768]{1,0:T(8,128)(2,1)S(1)} %get-tuple-element.94.left_ref.refs_0_), channel_id=1, source_target_pairs={{0,8},{8,0},{1,9},{9,1},{2,10},{10,2},{3,11},{11,3},{4,12},{12,4},... | collective-permute-start | bytes 589832 | tf_op jit(solution)/shard_map/ppermute | solution.py:623
  35.3 1.5 %collective-permute-done.7.in_ref.near_ref.refs_3_ = bf16[128,384]{1,0:T(8,128)(2,1)S(1)} collective-permute-done((bf16[128,384]{1,0:T(8,128)(2,1)S(1)}, bf16[128,384]{1,0:T(8,128)(2,1)S(1)}, u32[]{:S(2)}, u32[]{:S(2)}) %collective-permute-start.7) | collective-permute-done | bytes 98336 | tf_op jit(solution)/shard_map/ppermute | solution.py:627
  36.8 1.4 %collective-permute-start.10 = (bf16[128,384]{1,0:T(8,128)(2,1)S(1)}, bf16[128,384]{1,0:T(8,128)(2,1)S(1)}, u32[]{:S(2)}, u32[]{:S(2)}) collective-permute-start(bf16[128,384]{1,0:T(8,128)(2,1)S(1)} %relay.1), channel_id=1, source_target_pairs={{0,2},{2,0},{4,6},{6,4},{1,3},{3,1},{5,7},{7,5},{8,10},{10,8},{12,... | collective-permute-start | bytes 294920 | tf_op jit(solution)/shard_map/ppermute | solution.py:627
  39.7 1.5 %collective-permute-start.14 = (bf16[128,384]{1,0:T(8,128)(2,1)S(1)}, bf16[128,384]{1,0:T(8,128)(2,1)S(1)}, u32[]{:S(2)}, u32[]{:S(2)}) collective-permute-start(bf16[128,384]{1,0:T(8,128)(2,1)S(1)} %choose.1), channel_id=1, source_target_pairs={{0,8},{8,0},{1,9},{9,1},{2,10},{10,2},{3,11},{11,3},{4,12},{12,4},... | collective-permute-start | bytes 294920 | tf_op jit(solution)/shard_map/ppermute | solution.py:623
  41.2 2.0 %collective-permute-start.15 = (bf16[128,384]{1,0:T(8,128)(2,1)S(1)}, bf16[128,384]{1,0:T(8,128)(2,1)S(1)}, u32[]{:S(2)}, u32[]{:S(2)}) collective-permute-start(bf16[128,384]{1,0:T(8,128)(2,1)S(1)} %collective-permute-done.9.refs_4_), channel_id=1, source_target_pairs={{0,2},{2,0},{4,6},{6,4},{1,3},{3,1},{5,7},{7,5},{8,10},{10,8},{12,... | collective-permute-start | bytes 294920 | tf_op jit(solution)/shard_map/ppermute | solution.py:627
  43.3 1.6 %project.1 = (f32[64,1536]{1,0:T(8,128)S(1)}, bf16[64,1536]{1,0:T(8,128)(2,1)S(1)}, bf16[128,3072]{1,0:T(8,128)(2,1)S(1)}, f32[8,128]{1,0:T(8,128)S(1)}) custom-call(f32[8,128]{1,0:T(8,128)S(1)} %get-tuple-element.95.tick_ref, bf16[128,1536]{1,0:T(8,128)(2,1)S(1)} %join.1.here_ref, bf16[128,1536]{1,0:T(8,128)(2,1)S(1)} %collective-permute-done.13.there_ref, ...), custom_call_target="tpu_custom_call" | custom-call | bytes 1 | tf_op jit(solution)/shard_map/project/pallas_call | solution.py:500
  44.9 1.5 %collective-permute-done.15.refs_6_ = bf16[128,384]{1,0:T(8,128)(2,1)S(1)} collective-permute-done((bf16[128,384]{1,0:T(8,128)(2,1)S(1)}, bf16[128,384]{1,0:T(8,128)(2,1)S(1)}, u32[]{:S(2)}, u32[]{:S(2)}) %collective-permute-start.15) | collective-permute-done | bytes 98336 | tf_op jit(solution)/shard_map/ppermute | solution.py:627
  47.2 1.7 %collective-permute-start.18 = (bf16[64,1536]{1,0:T(8,128)(2,1)S(1)}, bf16[64,1536]{1,0:T(8,128)(2,1)S(1)}, u32[]{:S(2)}, u32[]{:S(2)}) collective-permute-start(bf16[64,1536]{1,0:T(8,128)(2,1)S(1)} %get-tuple-element.115), channel_id=1, source_target_pairs={{0,2},{2,0},{4,6},{6,4},{1,3},{3,1},{5,7},{7,5},{8,10},{10,8},{12,... | collective-permute-start | bytes 589832 | tf_op jit(solution)/shard_map/ppermute | solution.py:627
  48.9 7.2 %gram.2 = (f32[3072,3072]{1,0:T(8,128)}, f32[8,128]{1,0:T(8,128)S(1)}) custom-call(f32[8,128]{1,0:T(8,128)S(1)} %get-tuple-element.108.refs_0_, bf16[128,768]{1,0:T(8,128)(2,1)S(1)} %get-tuple-element.109.refs_1_, bf16[128,768]{1,0:T(8,128)(2,1)S(1)} %collective-permute-done.16.refs_2_, bf16[128,3072]{1,0:T(8,128)(2,1)S(1)} %get-tuple-element.111.refs_3_), custom_call_target="tpu_custom_call" | custom-call | flops 1207959552 | bytes 18874368 | tf_op jit(solution)/shard_map/gram/pallas_call | solution.py:603
  56.5 1.4 %collective-permute-start.20 = (bf16[32,1536]{1,0:T(8,128)(2,1)S(1)}, bf16[32,1536]{1,0:T(8,128)(2,1)S(1)}, u32[]{:S(2)}, u32[]{:S(2)}) collective-permute-start(bf16[32,1536]{1,0:T(8,128)(2,1)S(1)} %get-tuple-element.130), channel_id=1, source_target_pairs={{0,4},{2,6},{4,0},{6,2},{1,5},{3,7},{5,1},{7,3},{8,12},{10,14},{12... | collective-permute-start | bytes 294920 | tf_op jit(solution)/shard_map/ppermute | solution.py:627
  57.9 7.2 %gram.3 = (f32[3072,3072]{1,0:T(8,128)}, f32[8,128]{1,0:T(8,128)S(1)}) custom-call(f32[8,128]{1,0:T(8,128)S(1)} %get-tuple-element.120.refs_0_, bf16[128,768]{1,0:T(8,128)(2,1)S(1)} %get-tuple-element.121.refs_1_, bf16[128,768]{1,0:T(8,128)(2,1)S(1)} %collective-permute-done.19.refs_2_, ...), custom_call_target="tpu_custom_call", output_to_operand_aliasing={{0}: (4, {})} | custom-call | flops 1207959552 | bytes 18874368 | tf_op jit(solution)/shard_map/gram/pallas_call | solution.py:603
  65.1 1.1 %unpack.1 = bf16[128,1536]{1,0:T(8,128)(2,1)} custom-call(f32[8,128]{1,0:T(8,128)S(1)} %get-tuple-element.124.after_ref, bf16[32,128]{1,0:T(8,128)(2,1)S(1)} %get-tuple-element.125.placing_ref, f32[32,128]{1,0:T(8,128)S(1)} %get-tuple-element.126.factor_ref, f32[32,1536]{1,0:T(8,128)S(1)} %get-tuple-element.129.own_ref, ...), custom_call_target="tpu_custom_call" | custom-call | tf_op jit(solution)/shard_map/unpack/pallas_call | solution.py:550
  (39 shorter events, 5.7 us)
Async XLA Ops:
  1.9 12.7 %collective-permute-start.2 = (bf16[32,1536]{1,0:T(8,128)(2,1)S(1)}, bf16[32,1536]{1,0:T(8,128)(2,1)S(1)}, u32[]{:S(2)}, u32[]{:S(2)}) collective-permute-start(bf16[32,1536]{1,0:T(8,128)(2,1)S(1)} %get-tuple-element.67.after_ref.refs_0_), channel_id=1, source_target_pairs={{0,6},{2,4},{4,2},{6,0},{1,7},{3,5},{5,3},{7,1},{8,14},{10,12},{12... | collective-permute-start | bytes 294920 | tf_op jit(solution)/shard_map/ppermute | solution.py:627
  7.0 8.3 %collective-permute-start.1 = (bf16[32,1536]{1,0:T(8,128)(2,1)S(1)}, bf16[32,1536]{1,0:T(8,128)(2,1)S(1)}, u32[]{:S(2)}, u32[]{:S(2)}) collective-permute-start(bf16[32,1536]{1,0:T(8,128)(2,1)S(1)} %get-tuple-element.67.after_ref.refs_0_), channel_id=1, source_target_pairs={{0,4},{2,6},{4,0},{6,2},{1,5},{3,7},{5,1},{7,3},{8,12},{10,14},{12... | collective-permute-start | bytes 294920 | tf_op jit(solution)/shard_map/ppermute | solution.py:627
  7.0 8.3 %collective-permute-start = (bf16[32,1536]{1,0:T(8,128)(2,1)S(1)}, bf16[32,1536]{1,0:T(8,128)(2,1)S(1)}, u32[]{:S(2)}, u32[]{:S(2)}) collective-permute-start(bf16[32,1536]{1,0:T(8,128)(2,1)S(1)} %get-tuple-element.67.after_ref.refs_0_), channel_id=1, source_target_pairs={{0,2},{2,0},{4,6},{6,4},{1,3},{3,1},{5,7},{7,5},{8,10},{10,8},{12,... | collective-permute-start | bytes 294920 | tf_op jit(solution)/shard_map/ppermute | solution.py:627
  17.3 3.5 %collective-permute-start.3 = (f32[256,768]{1,0:T(8,128)S(1)}, f32[256,768]{1,0:T(8,128)S(1)}, u32[]{:S(2)}, u32[]{:S(2)}) collective-permute-start(f32[256,768]{1,0:T(8,128)S(1)} %get-tuple-element.71), channel_id=1, source_target_pairs={{0,1},{1,0},{2,3},{3,2},{4,5},{5,4},{6,7},{7,6},{8,9},{9,8},{10,11... | collective-permute-start | bytes 2359304 | tf_op jit(solution)/shard_map/ppermute | solution.py:623
  18.8 5.1 %collective-permute-start.4 = (f32[256,768]{1,0:T(8,128)S(1)}, f32[256,768]{1,0:T(8,128)S(1)}, u32[]{:S(2)}, u32[]{:S(2)}) collective-permute-start(f32[256,768]{1,0:T(8,128)S(1)} %preacts_sent.3), channel_id=1, source_target_pairs={{0,1},{1,0},{2,3},{3,2},{4,5},{5,4},{6,7},{7,6},{8,9},{9,8},{10,11... | collective-permute-start | bytes 2359304 | tf_op jit(solution)/shard_map/ppermute | solution.py:623
  20.9 7.8 %collective-permute-start.5 = (bf16[256,384]{1,0:T(8,128)(2,1)S(1)}, bf16[256,384]{1,0:T(8,128)(2,1)S(1)}, u32[]{:S(2)}, u32[]{:S(2)}) collective-permute-start(bf16[256,384]{1,0:T(8,128)(2,1)S(1)} %get-tuple-element.77), channel_id=1, source_target_pairs={{0,8},{8,0},{1,9},{9,1},{2,10},{10,2},{3,11},{11,3},{4,12},{12,4},... | collective-permute-start | bytes 589832 | tf_op jit(solution)/shard_map/ppermute | solution.py:623
  24.0 8.6 %collective-permute-start.6 = (bf16[256,384]{1,0:T(8,128)(2,1)S(1)}, bf16[256,384]{1,0:T(8,128)(2,1)S(1)}, u32[]{:S(2)}, u32[]{:S(2)}) collective-permute-start(bf16[256,384]{1,0:T(8,128)(2,1)S(1)} %get-tuple-element.79), channel_id=1, source_target_pairs={{0,8},{8,0},{1,9},{9,1},{2,10},{10,2},{3,11},{11,3},{4,12},{12,4},... | collective-permute-start | bytes 589832 | tf_op jit(solution)/shard_map/ppermute | solution.py:623
  28.8 8.0 %collective-permute-start.7 = (bf16[128,384]{1,0:T(8,128)(2,1)S(1)}, bf16[128,384]{1,0:T(8,128)(2,1)S(1)}, u32[]{:S(2)}, u32[]{:S(2)}) collective-permute-start(bf16[128,384]{1,0:T(8,128)(2,1)S(1)} %act.2.refs_0_), channel_id=1, source_target_pairs={{0,4},{2,6},{4,0},{6,2},{1,5},{3,7},{5,1},{7,3},{8,12},{10,14},{12... | collective-permute-start | bytes 294920 | tf_op jit(solution)/shard_map/ppermute | solution.py:627
  30.5 6.3 %collective-permute-start.8 = (bf16[128,384]{1,0:T(8,128)(2,1)S(1)}, bf16[128,384]{1,0:T(8,128)(2,1)S(1)}, u32[]{:S(2)}, u32[]{:S(2)}) collective-permute-start(bf16[128,384]{1,0:T(8,128)(2,1)S(1)} %act.2.refs_0_), channel_id=1, source_target_pairs={{0,2},{2,0},{4,6},{6,4},{1,3},{3,1},{5,7},{7,5},{8,10},{10,8},{12,... | collective-permute-start | bytes 294920 | tf_op jit(solution)/shard_map/ppermute | solution.py:627
  32.6 8.6 %collective-permute-start.9 = (bf16[128,384]{1,0:T(8,128)(2,1)S(1)}, bf16[128,384]{1,0:T(8,128)(2,1)S(1)}, u32[]{:S(2)}, u32[]{:S(2)}) collective-permute-start(bf16[128,384]{1,0:T(8,128)(2,1)S(1)} %get-tuple-element.92), channel_id=1, source_target_pairs={{0,4},{2,6},{4,0},{6,2},{1,5},{3,7},{5,1},{7,3},{8,12},{10,14},{12... | collective-permute-start | bytes 294920 | tf_op jit(solution)/shard_map/ppermute | solution.py:627
  33.8 5.7 %collective-permute-start.12 = (bf16[128,768]{1,0:T(8,128)(2,1)S(1)}, bf16[128,768]{1,0:T(8,128)(2,1)S(1)}, u32[]{:S(2)}, u32[]{:S(2)}) collective-permute-start(bf16[128,768]{1,0:T(8,128)(2,1)S(1)} %get-tuple-element.94.left_ref.refs_0_), channel_id=1, source_target_pairs={{0,8},{8,0},{1,9},{9,1},{2,10},{10,2},{3,11},{11,3},{4,12},{12,4},... | collective-permute-start | bytes 589832 | tf_op jit(solution)/shard_map/ppermute | solution.py:623
  36.8 6.4 %collective-permute-start.10 = (bf16[128,384]{1,0:T(8,128)(2,1)S(1)}, bf16[128,384]{1,0:T(8,128)(2,1)S(1)}, u32[]{:S(2)}, u32[]{:S(2)}) collective-permute-start(bf16[128,384]{1,0:T(8,128)(2,1)S(1)} %relay.1), channel_id=1, source_target_pairs={{0,2},{2,0},{4,6},{6,4},{1,3},{3,1},{5,7},{7,5},{8,10},{10,8},{12,... | collective-permute-start | bytes 294920 | tf_op jit(solution)/shard_map/ppermute | solution.py:627
  38.2 5.0 %collective-permute-start.11 = (bf16[128,384]{1,0:T(8,128)(2,1)S(1)}, bf16[128,384]{1,0:T(8,128)(2,1)S(1)}, u32[]{:S(2)}, u32[]{:S(2)}) collective-permute-start(bf16[128,384]{1,0:T(8,128)(2,1)S(1)} %get-tuple-element.92), channel_id=1, source_target_pairs={{0,2},{2,0},{4,6},{6,4},{1,3},{3,1},{5,7},{7,5},{8,10},{10,8},{12,... | collective-permute-start | bytes 294920 | tf_op jit(solution)/shard_map/ppermute | solution.py:627
  39.6 3.7 %collective-permute-start.13 = (bf16[128,1536]{1,0:T(8,128)(2,1)S(1)}, bf16[128,1536]{1,0:T(8,128)(2,1)S(1)}, u32[]{:S(2)}, u32[]{:S(2)}) collective-permute-start(bf16[128,1536]{1,0:T(8,128)(2,1)S(1)} %join.1.here_ref), channel_id=1, source_target_pairs={{0,1},{1,0},{2,3},{3,2},{4,5},{5,4},{6,7},{7,6},{8,9},{9,8},{10,11... | collective-permute-start | bytes 1179656 | tf_op jit(solution)/shard_map/ppermute | solution.py:623
  39.7 5.2 %collective-permute-start.14 = (bf16[128,384]{1,0:T(8,128)(2,1)S(1)}, bf16[128,384]{1,0:T(8,128)(2,1)S(1)}, u32[]{:S(2)}, u32[]{:S(2)}) collective-permute-start(bf16[128,384]{1,0:T(8,128)(2,1)S(1)} %choose.1), channel_id=1, source_target_pairs={{0,8},{8,0},{1,9},{9,1},{2,10},{10,2},{3,11},{11,3},{4,12},{12,4},... | collective-permute-start | bytes 294920 | tf_op jit(solution)/shard_map/ppermute | solution.py:623
  41.2 5.2 %collective-permute-start.15 = (bf16[128,384]{1,0:T(8,128)(2,1)S(1)}, bf16[128,384]{1,0:T(8,128)(2,1)S(1)}, u32[]{:S(2)}, u32[]{:S(2)}) collective-permute-start(bf16[128,384]{1,0:T(8,128)(2,1)S(1)} %collective-permute-done.9.refs_4_), channel_id=1, source_target_pairs={{0,2},{2,0},{4,6},{6,4},{1,3},{3,1},{5,7},{7,5},{8,10},{10,8},{12,... | collective-permute-start | bytes 294920 | tf_op jit(solution)/shard_map/ppermute | solution.py:627
  46.5 2.4 %collective-permute-start.16 = (bf16[128,768]{1,0:T(8,128)(2,1)S(1)}, bf16[128,768]{1,0:T(8,128)(2,1)S(1)}, u32[]{:S(2)}, u32[]{:S(2)}) collective-permute-start(bf16[128,768]{1,0:T(8,128)(2,1)S(1)} %get-tuple-element.107), channel_id=1, source_target_pairs={{0,1},{1,0},{2,3},{3,2},{4,5},{5,4},{6,7},{7,6},{8,9},{9,8},{10,11... | collective-permute-start | bytes 589832 | tf_op jit(solution)/shard_map/ppermute | solution.py:623
  46.6 9.5 %collective-permute-start.17 = (bf16[128,1152]{1,0:T(8,128)(2,1)S(1)}, bf16[128,1152]{1,0:T(8,128)(2,1)S(1)}, u32[]{:S(2)}, u32[]{:S(2)}) collective-permute-start(bf16[128,1152]{1,0:T(8,128)(2,1)S(1)} %get-tuple-element.113), channel_id=1, source_target_pairs={{0,8},{8,0},{1,9},{9,1},{2,10},{10,2},{3,11},{11,3},{4,12},{12,4},... | collective-permute-start | bytes 884744 | tf_op jit(solution)/shard_map/ppermute | solution.py:623
  47.2 9.3 %collective-permute-start.18 = (bf16[64,1536]{1,0:T(8,128)(2,1)S(1)}, bf16[64,1536]{1,0:T(8,128)(2,1)S(1)}, u32[]{:S(2)}, u32[]{:S(2)}) collective-permute-start(bf16[64,1536]{1,0:T(8,128)(2,1)S(1)} %get-tuple-element.115), channel_id=1, source_target_pairs={{0,2},{2,0},{4,6},{6,4},{1,3},{3,1},{5,7},{7,5},{8,10},{10,8},{12,... | collective-permute-start | bytes 589832 | tf_op jit(solution)/shard_map/ppermute | solution.py:627
  56.4 1.5 %collective-permute-start.19 = (bf16[128,768]{1,0:T(8,128)(2,1)S(1)}, bf16[128,768]{1,0:T(8,128)(2,1)S(1)}, u32[]{:S(2)}, u32[]{:S(2)}) collective-permute-start(bf16[128,768]{1,0:T(8,128)(2,1)S(1)} %get-tuple-element.119), channel_id=1, source_target_pairs={{0,1},{1,0},{2,3},{3,2},{4,5},{5,4},{6,7},{7,6},{8,9},{9,8},{10,11... | collective-permute-start | bytes 589832 | tf_op jit(solution)/shard_map/ppermute | solution.py:623
  56.5 8.6 %collective-permute-start.20 = (bf16[32,1536]{1,0:T(8,128)(2,1)S(1)}, bf16[32,1536]{1,0:T(8,128)(2,1)S(1)}, u32[]{:S(2)}, u32[]{:S(2)}) collective-permute-start(bf16[32,1536]{1,0:T(8,128)(2,1)S(1)} %get-tuple-element.130), channel_id=1, source_target_pairs={{0,4},{2,6},{4,0},{6,2},{1,5},{3,7},{5,1},{7,3},{8,12},{10,14},{12... | collective-permute-start | bytes 294920 | tf_op jit(solution)/shard_map/ppermute | solution.py:627
